TPU v7x, 32 devices: a whole 2x2x4 slice. The times are simulated.
32 devices in a mesh: groups: 2 (over y), dp: 2 (over core), tensor: 8 (over z, x).
Axes of the slice: x: 2, y: 2, z: 4, core: 2. Of those that a mesh axis runs over, the one named last changes fastest.
Arguments:
- attended: bfloat16 [256, 8192], P(('groups', 'dp'), 'tensor'), parts along dimension 0, may hold values from -12 to 12
- out_weight: bfloat16 [8192, 16384], P('tensor'), may hold values from -0.09375 to 0.09375
- residual: bfloat16 [256, 16384], P(('groups', 'dp'), 'tensor'), parts along dimension 0, may hold values from -40 to 40
- norm_gain: bfloat16 [16384], P('tensor'), may hold values from 0.099609375 to 1.8984375
- norm_bias: bfloat16 [16384], P('tensor'), may hold values from -3 to 3
Outputs:
- stream_out: bfloat16 [256, 16384], P(('groups', 'dp'), 'tensor'), parts along dimension 0
- normed: bfloat16 [256, 16384], P(('groups', 'dp')), parts along dimension 0
There are 2 independent parts, one for each index of `groups`. A program takes and returns all parts, laid end to end along the dimension named above; an argument that names none is the same for every part. Nothing has to cross between parts.
All inputs are finite; a program needn't handle non-finite values.
Results may differ from a plain program's by a relative error of at most 0.008.
Values may be sent and summed in bfloat16 or wider, within the bound.
No kernel may reach another device: no remote copies, remote signals or barrier semaphores. Data moves between devices by JAX's collectives and lax.ppermute only.
A program may use at most 128 MiB of HBM per device.

v0:
```python
import math

import jax
import jax.numpy as jnp
from jax import lax
from jax.sharding import PartitionSpec as P

BLOCK_LEN = 128


def hadamard(length):
    indices = lax.iota(jnp.int32, length)
    parity = jnp.zeros((length, length), jnp.int32)
    for bit_index in range(length.bit_length() - 1):
        column = jnp.bitwise_and(jnp.right_shift(indices, bit_index), 1)
        parity = parity + column[:, None] * column[None, :]
    sign_table = 1 - 2 * jnp.bitwise_and(parity, 1)
    return sign_table.astype(jnp.float32) / math.sqrt(length)


def rotate(values, rotation):
    length = rotation.shape[0]
    flat = jnp.dot(values.reshape(-1, length), rotation, precision=lax.Precision.HIGHEST)
    return flat.reshape(values.shape)


def encode(values, length):
    blocks = values.reshape(values.shape[0], -1, length)
    largest = jnp.max(jnp.abs(blocks), axis=2)
    scales = (largest / 448.0 + 1e-06).astype(jnp.bfloat16)
    quanta = (blocks / scales.astype(jnp.float32)[:, :, None]).astype(jnp.bfloat16)
    return (quanta.reshape(values.shape), scales)


def decode(quanta, scales, rotation):
    length = rotation.shape[0]
    blocks = quanta.astype(jnp.float32).reshape(quanta.shape[0], -1, length)
    blocks = blocks * scales.astype(jnp.float32)[:, :, None]
    return rotate(blocks.reshape(quanta.shape), rotation).astype(jnp.bfloat16)


def normalize(stream, centre, spread, gain_part, bias_part):
    scaled = (stream - centre) * lax.rsqrt(spread + 1e-05)
    return scaled * gain_part.astype(jnp.float32) + bias_part.astype(jnp.float32)


def body(attended, out_weight, residual, norm_gain, norm_bias):
    rotation = hadamard(BLOCK_LEN)
    full_width = out_weight.shape[1]
    devices = lax.axis_size("tensor")
    local_width = full_width // devices
    projected = jnp.dot(attended, out_weight, preferred_element_type=jnp.float32)
    summed = lax.psum(projected, "tensor")
    stream_in, gain_all, bias_all = (
        lax.all_gather(residual, "tensor", axis=1, tiled=True),
        lax.all_gather(norm_gain, "tensor", axis=0, tiled=True),
        lax.all_gather(norm_bias, "tensor", axis=0, tiled=True),
    )
    stream = stream_in.astype(jnp.float32) + summed
    centre = jnp.mean(stream, axis=1, keepdims=True)
    offsets = stream - centre
    spread = jnp.mean(offsets * offsets, axis=1, keepdims=True)
    normal_rows = normalize(stream, centre, spread, gain_all, bias_all)
    quanta, scales = encode(rotate(normal_rows, rotation), BLOCK_LEN)
    own_slice = lax.dynamic_slice_in_dim(
        stream, lax.axis_index("tensor") * local_width, local_width, 1
    )
    stream_out = own_slice.astype(jnp.bfloat16)
    normed = decode(quanta, scales, rotation)
    return (stream_out, normed)


def solution(mesh):
    placed = (
        P(("groups", "dp"), "tensor"),
        P("tensor", None),
        P(("groups", "dp"), "tensor"),
        P("tensor"),
        P("tensor"),
    )
    return jax.shard_map(
        body,
        mesh=mesh,
        in_specs=placed,
        out_specs=(P(("groups", "dp"), "tensor"), P(("groups", "dp"), None)),
        check_vma=False,
    )
```

profile of v0, /device:TPU:0, one launch (start us, length us, event | category | flops | bytes accessed | tf_op | source)
XLA Modules:
  0.0 245.8 jit_solution(5313719250603915427)
XLA Ops:
  7.2 0.0 copy-start
  7.2 0.0 all-gather.2.cloned.1.call-start
  7.2 0.7 all-gather.2.cloned.1.call-update
  7.9 0.0 all-reduce.2.cloned.1.call-start
  8.0 0.1 copy-done
  8.1 15.5 %fusion.10 = f32[64,16384]{1,0:T(8,128)} fusion(bf16[64,1024]{1,0:T(8,128)(2,1)S(1)} %copy-done, bf16[1024,16384]{1,0:T(8,128)(2,1)} %param.6), kind=kOutput, calls=%fused_computation.29 | convolution fusion | flops 2147483648 | bytes 37879808 | tf_op jit(solution)/shard_map/dot_general | solution.py:52
  23.6 0.0 copy-start.2
  23.6 0.0 copy-start.3
  23.6 0.0 all-reduce.2.cloned.1.call-update
  23.6 0.7 copy-done.2
  24.3 32.4 %all_gather.11 = bf16[16384]{0:T(1024)(128)(2,1)S(1)} all-gather(bf16[2048]{0:T(1024)(128)(2,1)S(1)} %copy-done.2), channel_id=1, replica_groups=mesh['groups'=2,'dp'=2,'tensor'=8] {'tensor'}, dimensions={0}, use_global_device_ids=true | all-gather | bytes 36864 | tf_op jit(solution)/shard_map/all_gather | solution.py:57
  56.7 0.0 copy-done.3
  56.7 30.9 %all_gather.10 = bf16[16384]{0:T(1024)(128)(2,1)S(1)} all-gather(bf16[2048]{0:T(1024)(128)(2,1)S(1)} %copy-done.3), channel_id=1, replica_groups=mesh['groups'=2,'dp'=2,'tensor'=8] {'tensor'}, dimensions={0}, use_global_device_ids=true | all-gather | bytes 36864 | tf_op jit(solution)/shard_map/all_gather | solution.py:56
  87.7 0.0 all-gather.2.cloned.1.call-done
  87.7 133.4 %all-reduce.2.cloned.1.call-done = f32[64,16384]{1,0:T(8,128)} async-done(((f32[64,16384]{1,0:T(8,128)}), f32[64,16384]{1,0:T(8,128)}) %all-reduce.2.cloned.1.call-update) | async-done | bytes 4194320 | tf_op jit(solution)/shard_map/psum | solution.py:53
  221.2 3.4 %fusion.9 = (f32[64]{0:T(128)S(1)}, f32[64,16384]{1,0:T(8,128)S(1)}) fusion(f32[64,16384]{1,0:T(8,128)} %all-reduce.2.cloned.1.call-done, bf16[64,16384]{1,0:T(8,128)(2,1)} %all-gather.2.cloned.1.call-done), kind=kLoop, calls=%fused_computation.28 | loop fusion | flops 3145664 | bytes 10486016 | tf_op jit(solution)/shard_map/reduce_sum | solution.py:60
  224.6 0.7 dynamic-slice_convert_fusion
  225.3 0.7 multiply_reduce_fusion
  226.0 0.7 add_bitcast_fusion
  226.8 0.7 copy.7
  227.5 3.7 %abs_reduce_fusion = (f32[64,128]{1,0:T(8,128)S(1)}, f32[64,128,128]{2,1,0:T(8,128)S(1)}) fusion(f32[64,128,128]{2,1,0:T(8,128)S(1)} %bitcast.14, s32[128]{0:T(128)S(1)} %get-tuple-element.6, s32[128]{0:T(128)S(1)} %get-tuple-element.7, s32[128]{0:T(128)S(1)} %get-tuple-element.8, s32[128]{0:T(128)S(1)} %get-tuple-element.9, s32[128]{0:T(128)S(1)} %get-tuple-element.10, ...), kind=kOutput, calls=%fused_computation.3 | convolution fusion | flops 1612996608 | bytes 8424960 | tf_op jit(solution)/shard_map/dot_general | solution.py:23
  231.2 1.4 convert_multiply_fusion
  232.7 0.0 copy-start.1
  232.7 4.0 %convolution_convert_fusion = bf16[8192,128]{1,0:T(8,128)(2,1)S(1)} fusion(f32[8192,128]{1,0:T(8,128)S(1)} %bitcast.13, s32[128]{0:T(128)S(1)} %get-tuple-element.6, s32[128]{0:T(128)S(1)} %get-tuple-element.7, s32[128]{0:T(128)S(1)} %get-tuple-element.8, s32[128]{0:T(128)S(1)} %get-tuple-element.9, s32[128]{0:T(128)S(1)} %get-tuple-element.10, ...), kind=kOutput, calls=%fused_computation | convolution fusion | flops 1611956224 | bytes 6295040 | tf_op jit(solution)/shard_map/dot_general | solution.py:23
  236.6 2.3 convert_element_type.55
  238.9 0.0 copy-done.1
  (9 shorter events, 0.1 us)
Async XLA Ops:
  7.2 0.9 copy-start
  7.2 80.6 %all-gather.2.cloned.1.call-start = ((), (), s32[]{:S(2)}) async-start(), calls=%async_computation | async-start | bytes 2359296 | tf_op jit(solution)/shard_map/all_gather | solution.py:55
  7.9 213.3 %all-reduce.2.cloned.1.call-start = ((), (), s32[]{:S(2)}) async-start(), calls=%async_computation.1 | async-start | bytes 8388608 | tf_op jit(solution)/shard_map/psum | solution.py:53
  23.6 0.7 copy-start.2
  23.6 33.1 %copy-start.3 = (bf16[2048]{0:T(1024)(128)(2,1)S(1)}, bf16[2048]{0:T(1024)(128)(2,1)}, u32[]{:S(2)}) copy-start(bf16[2048]{0:T(1024)(128)(2,1)} %param.8) | copy-start | bytes 12292
  232.7 6.3 %copy-start.1 = (bf16[64,1024]{1,0:T(8,128)(2,1)S(1)}, bf16[64,1024]{1,0:T(8,128)(2,1)}, u32[]{:S(2)}) copy-start(bf16[64,1024]{1,0:T(8,128)(2,1)} %param.5) | copy-start | bytes 393220
Sparse Core Ops, SparseCore 0:
  10.2 52.3 all-gather.1
  66.3 154.8 all-reduce.1
where the time goes:
time: 246 us
  waiting for transfers between devices  134 us (54%)
  blocking collectives  63.3 us (26%)
  matrix products  23.2 us (9%)
  between operations  14.2 us (6%)
  other arithmetic  6.29 us (3%)
  local copies, waits for them, and re-layouts  4.57 us (2%)
    psum x1, waiting for transfers between devices, body(): summed = lax.psum(projected, 'tensor')  133 us
    all_gather x1, blocking collectives, body(): lax.all_gather(norm_bias, 'tensor', axis=0, tiled=True)  32.4 us
    all_gather x1, blocking collectives, body(): lax.all_gather(norm_gain, 'tensor', axis=0, tiled=True)  30.9 us
    dot_general x1, matrix products, body(): jnp.dot(attended, out_weight, preferred_element_type=jnp.float32)  15.5 us
    dot_general x2, matrix products, rotate(): jnp.dot(values.reshape(-1, length), rotation, precision=lax.Precision.HIG...  7.64 us
  transfers between devices with their start and end apart: 2, of which 1 were waited for; matrix products, arithmetic and copies ran while one was open for 6% of the time, Pallas kernels for 0%

commit v1 on v0

--- a/solution.py
+++ b/solution.py
@@ -39,35 +39,39 @@
     return rotate(blocks.reshape(quanta.shape), rotation).astype(jnp.bfloat16)
 
 
-def normalize(stream, centre, spread, gain_part, bias_part):
-    scaled = (stream - centre) * lax.rsqrt(spread + 1e-05)
-    return scaled * gain_part.astype(jnp.float32) + bias_part.astype(jnp.float32)
-
-
 def body(attended, out_weight, residual, norm_gain, norm_bias):
     rotation = hadamard(BLOCK_LEN)
-    full_width = out_weight.shape[1]
-    devices = lax.axis_size("tensor")
-    local_width = full_width // devices
+    n = lax.axis_size("tensor")
+    width = out_weight.shape[1]
     projected = jnp.dot(attended, out_weight, preferred_element_type=jnp.float32)
-    summed = lax.psum(projected, "tensor")
-    stream_in, gain_all, bias_all = (
-        lax.all_gather(residual, "tensor", axis=1, tiled=True),
-        lax.all_gather(norm_gain, "tensor", axis=0, tiled=True),
-        lax.all_gather(norm_bias, "tensor", axis=0, tiled=True),
+    own = lax.psum_scatter(
+        projected.astype(jnp.bfloat16), "tensor", scatter_dimension=1, tiled=True
     )
-    stream = stream_in.astype(jnp.float32) + summed
-    centre = jnp.mean(stream, axis=1, keepdims=True)
-    offsets = stream - centre
-    spread = jnp.mean(offsets * offsets, axis=1, keepdims=True)
-    normal_rows = normalize(stream, centre, spread, gain_all, bias_all)
+    stream = residual.astype(jnp.float32) + own.astype(jnp.float32)
+    total = jnp.sum(stream, axis=1, keepdims=True)
+    local_mean = total / stream.shape[1]
+    local_square = jnp.sum((stream - local_mean) ** 2, axis=1, keepdims=True)
+    stats = jnp.concatenate([local_mean, local_square], axis=1)
+    parts = [stats]
+    for k in range(1, n):
+        parts.append(
+            lax.ppermute(stats, "tensor", [(i, (i + k) % n) for i in range(n)])
+        )
+    means = jnp.stack([p[:, 0] for p in parts])
+    squares = jnp.stack([p[:, 1] for p in parts])
+    centre = jnp.mean(means, axis=0)
+    spread = (
+        jnp.sum(squares, axis=0)
+        + stream.shape[1] * jnp.sum((means - centre) ** 2, axis=0)
+    ) / width
+    offsets = stream - centre[:, None]
+    normal_rows = offsets * lax.rsqrt(spread + 1e-05)[:, None] * norm_gain.astype(
+        jnp.float32
+    ) + norm_bias.astype(jnp.float32)
     quanta, scales = encode(rotate(normal_rows, rotation), BLOCK_LEN)
-    own_slice = lax.dynamic_slice_in_dim(
-        stream, lax.axis_index("tensor") * local_width, local_width, 1
-    )
-    stream_out = own_slice.astype(jnp.bfloat16)
     normed = decode(quanta, scales, rotation)
-    return (stream_out, normed)
+    normed = lax.all_gather(normed, "tensor", axis=1, tiled=True)
+    return (stream.astype(jnp.bfloat16), normed)
 
 
 def solution(mesh):

time: 246 us -> 174 us (0.71)
  blocking collectives: 63.3 us -> 0 us
  waiting for transfers between devices: 134 us -> 124 us
  starting transfers between devices: 0.08 us -> 9.5 us
  matrix products: 23.2 us -> 16.7 us
    psum x1 -> x0, waiting for transfers between devices: 133 us -> none  [body(): summed = lax.psum(projected, 'tensor')]
    reduce_scatter x0 -> x1, waiting for transfers between devices: none -> 70.7 us  [body(): lax.psum_scatter(projected.astype(jnp.bfloat16), 'tensor', scatter_dimens...]
    all_gather x2 -> x0, blocking collectives: 63.3 us -> none  [the longest x1 32.4 us: body(): lax.all_gather(norm_bias, 'tensor', axis=0, tiled=True)]
    all_gather x1, waiting for transfers between devices: 0.02 us -> 46.7 us  [body(): normed = lax.all_gather(normed, 'tensor', axis=1, tiled=True)]
    ppermute x0 -> x7, starting transfers between devices: none -> 9.42 us  [body(): lax.ppermute(stats, 'tensor', [(i, (i + k) % n) for i in range(n)])]
    ppermute x0 -> x7, waiting for transfers between devices: none -> 6.16 us  [body(): lax.ppermute(stats, 'tensor', [(i, (i + k) % n) for i in range(n)])]
    dot_general x2, matrix products: 7.64 us -> 1.57 us  [rotate(): jnp.dot(values.reshape(-1, length), rotation, precision=lax.Precision.HIG...]
  transfers between devices with their start and end apart: 2 -> 9, of which waited for: 1 -> 5; matrix products, arithmetic and copies ran while one was open for 6% -> 0% of each run, Pallas kernels for 0% -> 0%
where the time goes in v1:
time: 174 us; the launch traced here: 173 us
  waiting for transfers between devices  124 us (71%)
  matrix products  16.7 us (10%)
  between operations  14.2 us (8%)
  starting transfers between devices  9.5 us (5%)
  local copies, waits for them, and re-layouts  4.99 us (3%)
  other arithmetic  4.33 us (2%)
    reduce_scatter x1, waiting for transfers between devices, body(): lax.psum_scatter(projected.astype(jnp.bfloat16), 'tensor', scatter_dimens...  70.7 us
    all_gather x1, waiting for transfers between devices, body(): normed = lax.all_gather(normed, 'tensor', axis=1, tiled=True)  46.7 us
    dot_general x1, matrix products, body(): jnp.dot(attended, out_weight, preferred_element_type=jnp.float32)  15.1 us
    ppermute x7, starting transfers between devices, body(): lax.ppermute(stats, 'tensor', [(i, (i + k) % n) for i in range(n)])  9.42 us
    ppermute x7, waiting for transfers between devices, body(): lax.ppermute(stats, 'tensor', [(i, (i + k) % n) for i in range(n)])  6.16 us
    unnamed x10, local copies, waits for them, and re-layouts  3.98 us
  transfers between devices with their start and end apart: 9, of which 5 were waited for; matrix products, arithmetic and copies ran while one was open for 0% of the time, Pallas kernels for 0%

profile of v1, /device:TPU:0, one launch (start us, length us, event | category | flops | bytes accessed | tf_op | source)
XLA Modules:
  0.0 173.3 jit_solution(18176591201196599786)
XLA Ops:
  7.2 0.0 copy-start
  7.2 0.0 copy-start.1
  7.2 0.0 copy-start.2
  7.2 0.0 copy-start.3
  7.2 0.0 reduce-scatter.2.cloned.1.call-start
  7.3 0.8 copy-done
  8.1 15.1 %convolution_convert_fusion = bf16[64,16384]{1,0:T(8,128)(2,1)} fusion(bf16[64,1024]{1,0:T(8,128)(2,1)S(1)} %copy-done, bf16[1024,16384]{1,0:T(8,128)(2,1)} %param.6), kind=kOutput, calls=%fused_computation | convolution fusion | flops 2148532224 | bytes 35782656 | tf_op jit(solution)/shard_map/dot_general | solution.py:46
  23.2 0.0 reduce-scatter.2.cloned.1.call-update
  23.2 0.0 all-gather.2.cloned.1.call-start
  23.3 70.7 %reduce-scatter.2.cloned.1.call-done = bf16[64,2048]{1,0:T(8,128)(2,1)} async-done(((bf16[64,16384]{1,0:T(8,128)(2,1)}), bf16[64,2048]{1,0:T(8,128)(2,1)}) %reduce-scatter.2.cloned.1.call-update) | async-done | bytes 262160 | tf_op jit(solution)/shard_map/reduce_scatter | solution.py:47
  94.0 0.0 copy-done.1
  94.0 1.1 fusion
  95.1 1.2 multiply_reduce_fusion
  96.3 2.1 %collective-permute-start.6 = (f32[64,2]{0,1:T(2,128)S(1)}, f32[64,2]{0,1:T(2,128)S(1)}, u32[]{:S(2)}, u32[]{:S(2)}) collective-permute-start(f32[64,2]{0,1:T(2,128)S(1)} %pad_maximum_fusion), channel_id=1, source_target_pairs={{0,7},{1,0},{2,1},{3,2},{4,3},{5,4},{6,5},{7,6},{8,15},{9,8},{10,9... | collective-permute-start | bytes 1544 | tf_op jit(solution)/shard_map/ppermute | solution.py:58
  98.5 0.0 copy-done.2
  98.5 0.0 copy-done.3
  98.5 1.9 %collective-permute-start.5 = (f32[64,2]{0,1:T(2,128)S(1)}, f32[64,2]{0,1:T(2,128)S(1)}, u32[]{:S(2)}, u32[]{:S(2)}) collective-permute-start(f32[64,2]{0,1:T(2,128)S(1)} %pad_maximum_fusion), channel_id=1, source_target_pairs={{0,6},{1,7},{2,0},{3,1},{4,2},{5,3},{6,4},{7,5},{8,14},{9,15},{10,... | collective-permute-start | bytes 1544 | tf_op jit(solution)/shard_map/ppermute | solution.py:58
  100.4 0.0 collective-permute-start.4
  100.4 2.5 %collective-permute-start.3 = (f32[64,2]{0,1:T(2,128)S(1)}, f32[64,2]{0,1:T(2,128)S(1)}, u32[]{:S(2)}, u32[]{:S(2)}) collective-permute-start(f32[64,2]{0,1:T(2,128)S(1)} %pad_maximum_fusion), channel_id=1, source_target_pairs={{0,4},{1,5},{2,6},{3,7},{4,0},{5,1},{6,2},{7,3},{8,12},{9,13},{10,... | collective-permute-start | bytes 1544 | tf_op jit(solution)/shard_map/ppermute | solution.py:58
  102.9 0.4 collective-permute-start.2
  103.3 0.0 collective-permute-done.6
  103.3 2.4 %collective-permute-start.1 = (f32[64,2]{0,1:T(2,128)S(1)}, f32[64,2]{0,1:T(2,128)S(1)}, u32[]{:S(2)}, u32[]{:S(2)}) collective-permute-start(f32[64,2]{0,1:T(2,128)S(1)} %pad_maximum_fusion), channel_id=1, source_target_pairs={{0,2},{1,3},{2,4},{3,5},{4,6},{5,7},{6,0},{7,1},{8,10},{9,11},{10,... | collective-permute-start | bytes 1544 | tf_op jit(solution)/shard_map/ppermute | solution.py:58
  105.7 0.0 collective-permute-done.5
  105.7 0.1 collective-permute-start
  105.8 0.0 collective-permute-done.4
  105.8 0.0 collective-permute-done.3
  105.8 2.4 %collective-permute-done.2 = f32[64,2]{0,1:T(2,128)S(1)} collective-permute-done((f32[64,2]{0,1:T(2,128)S(1)}, f32[64,2]{0,1:T(2,128)S(1)}, u32[]{:S(2)}, u32[]{:S(2)}) %collective-permute-start.2) | collective-permute-done | bytes 544 | tf_op jit(solution)/shard_map/ppermute | solution.py:58
  108.3 0.4 collective-permute-done.1
  108.7 3.3 %collective-permute-done = f32[64,2]{0,1:T(2,128)S(1)} collective-permute-done((f32[64,2]{0,1:T(2,128)S(1)}, f32[64,2]{0,1:T(2,128)S(1)}, u32[]{:S(2)}, u32[]{:S(2)}) %collective-permute-start) | collective-permute-done | bytes 544 | tf_op jit(solution)/shard_map/ppermute | solution.py:58
  112.1 1.7 add_bitcast_fusion
  113.8 0.1 copy.10
  113.9 0.8 abs_reduce_fusion
  114.7 0.1 copy.8
  114.8 0.1 copy.9
  114.9 0.2 convert_multiply_fusion
  115.1 0.7 convolution_convert_fusion.1
  115.8 0.8 convert_element_type.63
  116.7 0.0 all-gather.2.cloned.1.call-update
  116.7 46.7 %all-gather.2.cloned.1.call-done = bf16[64,16384]{1,0:T(8,128)(2,1)} async-done(((bf16[64,2048]{1,0:T(8,128)(2,1)}), bf16[64,16384]{1,0:T(8,128)(2,1)}) %all-gather.2.cloned.1.call-update) | async-done | bytes 2097168 | tf_op jit(solution)/shard_map/all_gather | solution.py:73
  163.4 3.0 %copy.12 = bf16[64,16384]{1,0:T(8,128)(2,1)} copy(bf16[64,16384]{1,0:T(8,128)(2,1)} %all-gather.2.cloned.1.call-done) | data formatting | bytes 4194304
  (20 shorter events, 0.1 us)
Async XLA Ops:
  7.2 0.9 copy-start
  7.2 86.8 %copy-start.1 = (bf16[64,2048]{1,0:T(8,128)(2,1)S(1)}, bf16[64,2048]{1,0:T(8,128)(2,1)}, u32[]{:S(2)}) copy-start(bf16[64,2048]{1,0:T(8,128)(2,1)} %param.7) | copy-start | bytes 786436
  7.2 91.3 %copy-start.2 = (bf16[2048]{0:T(1024)(128)(2,1)S(1)}, bf16[2048]{0:T(1024)(128)(2,1)}, u32[]{:S(2)}) copy-start(bf16[2048]{0:T(1024)(128)(2,1)} %param.8) | copy-start | bytes 12292
  7.2 91.3 %copy-start.3 = (bf16[2048]{0:T(1024)(128)(2,1)S(1)}, bf16[2048]{0:T(1024)(128)(2,1)}, u32[]{:S(2)}) copy-start(bf16[2048]{0:T(1024)(128)(2,1)} %param.9) | copy-start | bytes 12292
  7.2 86.8 %reduce-scatter.2.cloned.1.call-start = ((), (), s32[]{:S(2)}) async-start(), calls=%async_computation.1 | async-start | bytes 2359296 | tf_op jit(solution)/shard_map/reduce_scatter | solution.py:47
  23.2 140.2 %all-gather.2.cloned.1.call-start = ((), (), s32[]{:S(2)}) async-start(), calls=%async_computation.2 | async-start | bytes 2359296 | tf_op jit(solution)/shard_map/all_gather | solution.py:73
  96.3 7.0 %collective-permute-start.6 = (f32[64,2]{0,1:T(2,128)S(1)}, f32[64,2]{0,1:T(2,128)S(1)}, u32[]{:S(2)}, u32[]{:S(2)}) collective-permute-start(f32[64,2]{0,1:T(2,128)S(1)} %pad_maximum_fusion), channel_id=1, source_target_pairs={{0,7},{1,0},{2,1},{3,2},{4,3},{5,4},{6,5},{7,6},{8,15},{9,8},{10,9... | collective-permute-start | bytes 1544 | tf_op jit(solution)/shard_map/ppermute | solution.py:58
  98.5 7.2 %collective-permute-start.5 = (f32[64,2]{0,1:T(2,128)S(1)}, f32[64,2]{0,1:T(2,128)S(1)}, u32[]{:S(2)}, u32[]{:S(2)}) collective-permute-start(f32[64,2]{0,1:T(2,128)S(1)} %pad_maximum_fusion), channel_id=1, source_target_pairs={{0,6},{1,7},{2,0},{3,1},{4,2},{5,3},{6,4},{7,5},{8,14},{9,15},{10,... | collective-permute-start | bytes 1544 | tf_op jit(solution)/shard_map/ppermute | solution.py:58
  100.4 5.4 %collective-permute-start.4 = (f32[64,2]{0,1:T(2,128)S(1)}, f32[64,2]{0,1:T(2,128)S(1)}, u32[]{:S(2)}, u32[]{:S(2)}) collective-permute-start(f32[64,2]{0,1:T(2,128)S(1)} %pad_maximum_fusion), channel_id=1, source_target_pairs={{0,5},{1,6},{2,7},{3,0},{4,1},{5,2},{6,3},{7,4},{8,13},{9,14},{10,... | collective-permute-start | bytes 1544 | tf_op jit(solution)/shard_map/ppermute | solution.py:58
  100.4 5.4 %collective-permute-start.3 = (f32[64,2]{0,1:T(2,128)S(1)}, f32[64,2]{0,1:T(2,128)S(1)}, u32[]{:S(2)}, u32[]{:S(2)}) collective-permute-start(f32[64,2]{0,1:T(2,128)S(1)} %pad_maximum_fusion), channel_id=1, source_target_pairs={{0,4},{1,5},{2,6},{3,7},{4,0},{5,1},{6,2},{7,3},{8,12},{9,13},{10,... | collective-permute-start | bytes 1544 | tf_op jit(solution)/shard_map/ppermute | solution.py:58
  102.9 5.4 %collective-permute-start.2 = (f32[64,2]{0,1:T(2,128)S(1)}, f32[64,2]{0,1:T(2,128)S(1)}, u32[]{:S(2)}, u32[]{:S(2)}) collective-permute-start(f32[64,2]{0,1:T(2,128)S(1)} %pad_maximum_fusion), channel_id=1, source_target_pairs={{0,3},{1,4},{2,5},{3,6},{4,7},{5,0},{6,1},{7,2},{8,11},{9,12},{10,... | collective-permute-start | bytes 1544 | tf_op jit(solution)/shard_map/ppermute | solution.py:58
  103.3 5.4 %collective-permute-start.1 = (f32[64,2]{0,1:T(2,128)S(1)}, f32[64,2]{0,1:T(2,128)S(1)}, u32[]{:S(2)}, u32[]{:S(2)}) collective-permute-start(f32[64,2]{0,1:T(2,128)S(1)} %pad_maximum_fusion), channel_id=1, source_target_pairs={{0,2},{1,3},{2,4},{3,5},{4,6},{5,7},{6,0},{7,1},{8,10},{9,11},{10,... | collective-permute-start | bytes 1544 | tf_op jit(solution)/shard_map/ppermute | solution.py:58
  105.7 6.3 %collective-permute-start = (f32[64,2]{0,1:T(2,128)S(1)}, f32[64,2]{0,1:T(2,128)S(1)}, u32[]{:S(2)}, u32[]{:S(2)}) collective-permute-start(f32[64,2]{0,1:T(2,128)S(1)} %pad_maximum_fusion), channel_id=1, source_target_pairs={{0,1},{1,2},{2,3},{3,4},{4,5},{5,6},{6,7},{7,0},{8,9},{9,10},{10,1... | collective-permute-start | bytes 1544 | tf_op jit(solution)/shard_map/ppermute | solution.py:58
Sparse Core Ops, SparseCore 0:
  23.3 70.6 reduce-scatter.1
  116.8 46.5 all-gather.1

commit v2 on v1

v2 whole, which is shorter than its diff:
```python
import functools
import math

import jax
import jax.numpy as jnp
from jax import lax
from jax.experimental import pallas as pl
from jax.experimental.pallas import tpu as pltpu
from jax.sharding import PartitionSpec as P

BLOCK_LEN = 128
VMEM_BYTES = 40 * 1024 * 1024


def factors(n):
    inner = 1 << ((n.bit_length() - 1) // 2)
    return n // inner, inner


def tile_width(width):
    for tile in (1024, 512, 256, 128):
        if width % tile == 0:
            return tile
    return width


def signs(length):
    rows = lax.broadcasted_iota(jnp.int32, (length, length), 0)
    columns = lax.broadcasted_iota(jnp.int32, (length, length), 1)
    common = jnp.bitwise_and(rows, columns)
    parity = jnp.zeros((length, length), jnp.int32)
    for bit_index in range(length.bit_length() - 1):
        parity = parity + jnp.bitwise_and(jnp.right_shift(common, bit_index), 1)
    return (1 - 2 * jnp.bitwise_and(parity, 1)).astype(jnp.bfloat16)


def product_kernel(which, rows_ref, weight_ref, out_ref):
    del which
    out_ref[0] = jnp.dot(
        rows_ref[...], weight_ref[...], preferred_element_type=jnp.float32
    ).astype(out_ref.dtype)


def product(attended, weight, inner, nz, nx, halves, half, dtype):
    rows, depth = attended.shape
    part = weight.shape[1] // (nz * nx * halves)
    tile = tile_width(part)
    per = part // tile

    def weight_index(z, j, which):
        return (0, ((z * nx + which[0]) * halves + half) * per + j)

    return pl.pallas_call(
        product_kernel,
        out_shape=jax.ShapeDtypeStruct((nz, rows, part), dtype),
        grid_spec=pltpu.PrefetchScalarGridSpec(
            num_scalar_prefetch=1,
            grid=(nz, per),
            in_specs=[
                pl.BlockSpec((rows, depth), lambda z, j, which: (0, 0)),
                pl.BlockSpec((depth, tile), weight_index),
            ],
            out_specs=pl.BlockSpec((1, rows, tile), lambda z, j, which: (z, 0, j)),
        ),
        compiler_params=pltpu.CompilerParams(vmem_limit_bytes=VMEM_BYTES),
        cost_estimate=pl.CostEstimate(
            flops=2 * rows * depth * part * nz,
            bytes_accessed=2 * depth * part * nz,
            transcendentals=0,
        ),
    )(inner.reshape(1), attended, weight)


def rows_kernel(stream_ref, centre_ref, inverse_ref, gain_ref, bias_ref, out_ref):
    rows, width = stream_ref.shape
    blocks = width // BLOCK_LEN
    table = signs(BLOCK_LEN)
    unit = 1.0 / math.sqrt(BLOCK_LEN)
    gain = gain_ref[...].astype(jnp.float32)
    bias = bias_ref[...].astype(jnp.float32)
    normal = (stream_ref[...] - centre_ref[...]) * inverse_ref[...] * gain + bias
    normal = jnp.concatenate(
        [normal[:, b * BLOCK_LEN : (b + 1) * BLOCK_LEN] for b in range(blocks)], axis=0
    )
    coded = jnp.zeros(normal.shape, jnp.float32)
    rest = normal
    for _ in range(3):
        piece = rest.astype(jnp.bfloat16)
        coded = coded + jnp.dot(piece, table, preferred_element_type=jnp.float32)
        rest = rest - piece.astype(jnp.float32)
    coded = coded * unit
    largest = jnp.max(jnp.abs(coded), axis=1, keepdims=True)
    scales = (largest / 448.0 + 1e-06).astype(jnp.bfloat16).astype(jnp.float32)
    quanta = (coded / scales).astype(jnp.bfloat16)
    back = jnp.dot(quanta, table, preferred_element_type=jnp.float32) * (scales * unit)
    back = back.astype(out_ref.dtype)
    for b in range(blocks):
        out_ref[:, b * BLOCK_LEN : (b + 1) * BLOCK_LEN] = back[b * rows : (b + 1) * rows]


def row_work(stream, centre, inverse, gain, bias):
    rows, width = stream.shape
    return pl.pallas_call(
        rows_kernel,
        out_shape=jax.ShapeDtypeStruct((rows, width), jnp.bfloat16),
        compiler_params=pltpu.CompilerParams(vmem_limit_bytes=VMEM_BYTES),
    )(stream, centre, inverse, gain.reshape(1, width), bias.reshape(1, width))


def place_kernel(which, piece_ref, *refs):
    del which
    refs[-1][...] = piece_ref[0]


def place(whole, pieces, inner, nx, halves, half):
    nz, rows, part = pieces.shape
    earlier = [] if whole is None else [whole]
    return pl.pallas_call(
        place_kernel,
        out_shape=jax.ShapeDtypeStruct((rows, nz * nx * halves * part), pieces.dtype),
        grid_spec=pltpu.PrefetchScalarGridSpec(
            num_scalar_prefetch=1,
            grid=(nz,),
            in_specs=[
                pl.BlockSpec((1, rows, part), lambda z, which: (z, 0, 0)),
            ]
            + [pl.BlockSpec(memory_space=pl.ANY)] * len(earlier),
            out_specs=pl.BlockSpec(
                (rows, part), lambda z, which: (0, (z * nx + which[0]) * halves + half)
            ),
        ),
        input_output_aliases={2: 0} if earlier else {},
        cost_estimate=pl.CostEstimate(
            flops=0, bytes_accessed=4 * nz * rows * part, transcendentals=0
        ),
    )(inner.reshape(1), pieces, *earlier)


def body(attended, out_weight, residual, norm_gain, norm_bias):
    n = lax.axis_size("tensor")
    nz, nx = factors(n)
    width = out_weight.shape[1]
    local = width // n
    halves = 2 if local % (2 * BLOCK_LEN) == 0 else 1
    part = local // halves
    me = lax.axis_index("tensor")
    inner = me % nx
    along_z = [[z * nx + x for z in range(nz)] for x in range(nx)]
    swap = [
        [(z * nx + x, z * nx + (x ^ j)) for z in range(nz) for x in range(nx)]
        for j in range(nx)
    ]

    own = []
    for half in range(halves):
        sent = []
        for j in range(1, nx):
            piece = product(attended, out_weight, inner ^ j, nz, nx, halves, half, jnp.bfloat16)
            sent.append(lax.ppermute(piece, "tensor", swap[j]))
        kept = product(attended, out_weight, inner, nz, nx, halves, half, jnp.float32)
        for piece in sent:
            kept = kept + piece.astype(jnp.float32)
        arrived = lax.all_to_all(
            kept.astype(jnp.bfloat16), "tensor", 0, 0, axis_index_groups=along_z, tiled=True
        )
        base = residual[:, half * part : (half + 1) * part].astype(jnp.float32)
        own.append(base + jnp.sum(arrived.astype(jnp.float32), axis=0))
    stream = jnp.concatenate(own, axis=1)

    mean = jnp.mean(stream, axis=1)
    square = jnp.sum((stream - mean[:, None]) ** 2, axis=1)
    stats = jnp.stack([mean, square])
    stats = lax.all_to_all(
        jnp.broadcast_to(stats[None], (n,) + stats.shape), "tensor", 0, 0, tiled=True
    )
    centre = jnp.mean(stats[:, 0], axis=0)
    spread = (
        jnp.sum(stats[:, 1], axis=0) + local * jnp.sum((stats[:, 0] - centre) ** 2, axis=0)
    ) / width
    inverse = lax.rsqrt(spread + 1e-05)

    normed = row_work(stream, centre[:, None], inverse[:, None], norm_gain, norm_bias)
    whole = None
    for half in range(halves):
        piece = normed[:, half * part : (half + 1) * part]
        line = lax.all_to_all(
            jnp.broadcast_to(piece[None], (nz,) + piece.shape),
            "tensor",
            0,
            0,
            axis_index_groups=along_z,
            tiled=True,
        )
        whole = place(whole, line, inner, nx, halves, half)
        for j in range(1, nx):
            other = lax.ppermute(line, "tensor", swap[j])
            whole = place(whole, other, inner ^ j, nx, halves, half)
    return (stream.astype(jnp.bfloat16), whole)


def solution(mesh):
    placed = (
        P(("groups", "dp"), "tensor"),
        P("tensor", None),
        P(("groups", "dp"), "tensor"),
        P("tensor"),
        P("tensor"),
    )
    return jax.shard_map(
        body,
        mesh=mesh,
        in_specs=placed,
        out_specs=(P(("groups", "dp"), "tensor"), P(("groups", "dp"), None)),
        check_vma=False,
    )
```

time: 174 us -> 118 us (0.68)
  waiting for transfers between devices: 124 us -> 39.7 us
  Pallas kernels: 0 us -> 33.2 us
  matrix products: 16.7 us -> 0 us
  blocking collectives: 0 us -> 14.2 us
  between operations: 14.2 us -> 0.84 us
  starting transfers between devices: 9.5 us -> 20.3 us
    reduce_scatter x1 -> x0, waiting for transfers between devices: 70.7 us -> none  [body(): lax.psum_scatter(projected.astype(jnp.bfloat16), 'tensor', scatter_dimens...]
    all_gather x1 -> x0, waiting for transfers between devices: 46.7 us -> none  [body(): normed = lax.all_gather(normed, 'tensor', axis=1, tiled=True)]
    all_to_all x0 -> x4, waiting for transfers between devices: none -> 37 us  [the longest x2 18.7 us: body(): lax.all_to_all(kept.astype(jnp.bfloat16), 'tensor', 0, 0, axis_index_grou...]
    pallas_call x0 -> x9, Pallas kernels: none -> 33.2 us  [the longest x4 19.8 us: product(): pl.pallas_call(product_kernel, out_shape=jax.ShapeDtypeStruct((nz, rows,...]
    dot_general x3 -> x0, matrix products: 16.7 us -> none  [the longest x1 15.1 us: body(): jnp.dot(attended, out_weight, preferred_element_type=jnp.float32)]
    all_to_all x0 -> x4, starting transfers between devices: none -> 16 us  [the longest x2 8.92 us: body(): lax.all_to_all(kept.astype(jnp.bfloat16), 'tensor', 0, 0, axis_index_grou...]
    all_to_all x0 -> x1, blocking collectives: none -> 14.2 us  [body(): lax.all_to_all(jnp.broadcast_to(piece[None], (nz,) + piece.shape), 'tenso...]
    ppermute x7 -> x4, starting transfers between devices: 9.42 us -> 4.27 us  [the longest x2 3.1 us: body(): sent.append(lax.ppermute(piece, 'tensor', swap[j]))]
  transfers between devices with their start and end apart: 9 -> 8, of which waited for: 5 -> 5; matrix products, arithmetic and copies ran while one was open for 0% -> 2% of each run, Pallas kernels for 0% -> 21%
where the time goes in v2:
time: 118 us; the launch traced here: 117 us
  waiting for transfers between devices  39.7 us (34%)
  Pallas kernels  33.2 us (28%)
  starting transfers between devices  20.3 us (17%)
  blocking collectives  14.2 us (12%)
  local copies, waits for them, and re-layouts  5.04 us (4%)
  other arithmetic  3.93 us (3%)
    pallas_call x4, Pallas kernels, product(): pl.pallas_call(product_kernel, out_shape=jax.ShapeDtypeStruct((nz, rows,...  19.8 us
    all_to_all x2, waiting for transfers between devices, body(): lax.all_to_all(kept.astype(jnp.bfloat16), 'tensor', 0, 0, axis_index_grou...  18.7 us
    all_to_all x1, blocking collectives, body(): lax.all_to_all(jnp.broadcast_to(piece[None], (nz,) + piece.shape), 'tenso...  14.2 us
    pallas_call x4, Pallas kernels, place(): pl.pallas_call(place_kernel, out_shape=jax.ShapeDtypeStruct((rows, nz * n...  12.6 us
    all_to_all x1, waiting for transfers between devices, body(): lax.all_to_all(jnp.broadcast_to(piece[None], (nz,) + piece.shape), 'tenso...  12 us
    all_to_all x2, starting transfers between devices, body(): lax.all_to_all(kept.astype(jnp.bfloat16), 'tensor', 0, 0, axis_index_grou...  8.92 us
    all_to_all x1, waiting for transfers between devices, body(): lax.all_to_all(jnp.broadcast_to(stats[None], (n,) + stats.shape), 'tensor...  6.34 us
    all_to_all x1, starting transfers between devices, body(): lax.all_to_all(jnp.broadcast_to(stats[None], (n,) + stats.shape), 'tensor...  3.66 us
  transfers between devices with their start and end apart: 8, of which 5 were waited for; matrix products, arithmetic and copies ran while one was open for 2% of the time, Pallas kernels for 21%

profile of v2, /device:TPU:0, one launch (start us, length us, event | category | flops | bytes accessed | tf_op | source)
XLA Modules:
  0.0 117.2 jit_solution(13540692695012822240)
XLA Ops:
  0.6 0.0 copy-start
  0.7 0.9 copy-done
  1.5 5.0 %shard_map.71 = bf16[4,64,1024]{2,1,0:T(8,128)(2,1)S(1)} custom-call(s32[1]{0:T(128)} %bitcast.1.which, bf16[64,1024]{1,0:T(8,128)(2,1)S(1)} %copy-done, bf16[1024,16384]{1,0:T(8,128)(2,1)} %weight_ref.7), custom_call_target="tpu_custom_call" | custom-call | flops 536870912 | bytes 8388608 | tf_op jit(solution)/shard_map/pallas_call | solution.py:53
  6.5 0.0 copy-start.1
  6.5 3.0 %collective-permute-start.1 = (bf16[4,64,1024]{2,1,0:T(8,128)(2,1)S(1)}, bf16[4,64,1024]{2,1,0:T(8,128)(2,1)S(1)}, u32[]{:S(2)}, u32[]{:S(2)}) collective-permute-start(bf16[4,64,1024]{2,1,0:T(8,128)(2,1)S(1)} %shard_map.71), channel_id=1, source_target_pairs={{0,1},{1,0},{2,3},{3,2},{4,5},{5,4},{6,7},{7,6},{8,9},{9,8},{10,11... | collective-permute-start | bytes 1572872 | tf_op jit(solution)/shard_map/ppermute | solution.py:159
  9.5 5.0 %shard_map.69 = bf16[4,64,1024]{2,1,0:T(8,128)(2,1)S(1)} custom-call(s32[1]{0:T(128)} %bitcast.1.which, bf16[64,1024]{1,0:T(8,128)(2,1)S(1)} %copy-done, bf16[1024,16384]{1,0:T(8,128)(2,1)} %weight_ref.7), custom_call_target="tpu_custom_call" | custom-call | flops 536870912 | bytes 8388608 | tf_op jit(solution)/shard_map/pallas_call | solution.py:53
  14.5 0.1 collective-permute-start
  14.6 5.0 %shard_map.70 = f32[4,64,1024]{2,1,0:T(8,128)S(1)} custom-call(s32[1]{0:T(128)} %bitcast.which, bf16[64,1024]{1,0:T(8,128)(2,1)S(1)} %copy-done.1, bf16[1024,16384]{1,0:T(8,128)(2,1)} %weight_ref.7), custom_call_target="tpu_custom_call" | custom-call | flops 536870912 | bytes 8388608 | tf_op jit(solution)/shard_map/pallas_call | solution.py:53
  19.6 2.7 %collective-permute-done.1 = bf16[4,64,1024]{2,1,0:T(8,128)(2,1)S(1)} collective-permute-done((bf16[4,64,1024]{2,1,0:T(8,128)(2,1)S(1)}, bf16[4,64,1024]{2,1,0:T(8,128)(2,1)S(1)}, u32[]{:S(2)}, u32[]{:S(2)}) %collective-permute-start.1) | collective-permute-done | bytes 524320 | tf_op jit(solution)/shard_map/ppermute | solution.py:159
  22.3 1.0 add_convert_fusion
  23.2 5.4 %all-to-all-start.1 = ((bf16[4,64,1024]{2,1,0:T(8,128)(2,1)}), bf16[4,64,1024]{2,1,0:T(8,128)(2,1)S(1)}, u32[]{:S(2)}, u32[]{:S(2)}) async-start(bf16[4,64,1024]{2,1,0:T(8,128)(2,1)} %add_convert_fusion), calls=%async_computation.1 | async-start | bytes 1048576 | tf_op jit(solution)/shard_map/all_to_all | solution.py:163
  28.7 5.0 %shard_map.68 = f32[4,64,1024]{2,1,0:T(8,128)S(1)} custom-call(s32[1]{0:T(128)} %bitcast.which, bf16[64,1024]{1,0:T(8,128)(2,1)S(1)} %copy-done.1, bf16[1024,16384]{1,0:T(8,128)(2,1)} %weight_ref.7), custom_call_target="tpu_custom_call" | custom-call | flops 536870912 | bytes 8388608 | tf_op jit(solution)/shard_map/pallas_call | solution.py:53
  33.6 0.0 copy-start.6
  33.7 1.0 add_convert_fusion.1
  34.6 6.5 %all-to-all-done.1 = bf16[4,64,1024]{2,1,0:T(8,128)(2,1)S(1)} async-done(((bf16[4,64,1024]{2,1,0:T(8,128)(2,1)}), bf16[4,64,1024]{2,1,0:T(8,128)(2,1)S(1)}, u32[]{:S(2)}, u32[]{:S(2)}) %all-to-all-start.1) | async-done | bytes 524320 | tf_op jit(solution)/shard_map/all_to_all | solution.py:163
  41.1 3.5 %all-to-all-start = ((bf16[4,64,1024]{2,1,0:T(8,128)(2,1)}), bf16[4,64,1024]{2,1,0:T(8,128)(2,1)S(1)}, u32[]{:S(2)}, u32[]{:S(2)}) async-start(bf16[4,64,1024]{2,1,0:T(8,128)(2,1)} %add_convert_fusion.1), calls=%async_computation | async-start | bytes 1048576 | tf_op jit(solution)/shard_map/all_to_all | solution.py:163
  44.6 0.0 copy-start.7
  44.6 0.0 copy-start.8
  44.6 0.1 convert_reduce_fusion
  44.7 12.2 %all-to-all-done = bf16[4,64,1024]{2,1,0:T(8,128)(2,1)S(1)} async-done(((bf16[4,64,1024]{2,1,0:T(8,128)(2,1)}), bf16[4,64,1024]{2,1,0:T(8,128)(2,1)S(1)}, u32[]{:S(2)}, u32[]{:S(2)}) %all-to-all-start) | async-done | bytes 524320 | tf_op jit(solution)/shard_map/all_to_all | solution.py:163
  56.9 0.1 convert_reduce_fusion.1
  57.0 0.2 fusion.3
  57.1 0.2 multiply_reduce_fusion
  57.4 0.7 reshape.95
  58.1 3.7 %all-to-all-start.2 = ((f32[8,1,128]{2,1,0:T(1,128)}), f32[8,1,128]{2,1,0:T(1,128)S(1)}, u32[]{:S(2)}, u32[]{:S(2)}) async-start(f32[8,1,128]{2,1,0:T(1,128)} %reshape.95), calls=%async_computation.2 | async-start | bytes 8192 | tf_op jit(solution)/shard_map/all_to_all | solution.py:173
  61.8 6.3 %all-to-all-done.2 = f32[8,1,128]{2,1,0:T(1,128)S(1)} async-done(((f32[8,1,128]{2,1,0:T(1,128)}), f32[8,1,128]{2,1,0:T(1,128)S(1)}, u32[]{:S(2)}, u32[]{:S(2)}) %all-to-all-start.2) | async-done | bytes 4128 | tf_op jit(solution)/shard_map/all_to_all | solution.py:173
  68.1 0.5 broadcast.69
  68.6 0.7 reduce.4
  69.3 0.1 reshape.96
  69.5 0.1 copy.17.inverse_ref
  69.6 0.1 copy.16.centre_ref
  69.7 0.7 shard_map.72
  70.4 0.1 broadcast_in_dim.8
  70.5 14.2 %all_to_all.25.piece_ref = bf16[4,64,1024]{2,1,0:T(8,128)(2,1)S(1)} all-to-all(bf16[4,64,1024]{2,1,0:T(8,128)(2,1)S(1)} %broadcast_in_dim.8), channel_id=1, replica_groups={{0,2,4,6},{1,3,5,7},{8,10,12,14},{9,11,13,15},{16,18,20,22},{17,19,21,2..., dimensions={0} | all-to-all | bytes 1048576 | tf_op jit(solution)/shard_map/all_to_all | solution.py:186
  84.7 0.9 broadcast_in_dim.7
  85.7 3.5 %all-to-all-start.3 = ((bf16[4,64,1024]{2,1,0:T(8,128)(2,1)}), bf16[4,64,1024]{2,1,0:T(8,128)(2,1)S(1)}, u32[]{:S(2)}, u32[]{:S(2)}) async-start(bf16[4,64,1024]{2,1,0:T(8,128)(2,1)} %broadcast_in_dim.7), calls=%async_computation.3 | async-start | bytes 1048576 | tf_op jit(solution)/shard_map/all_to_all | solution.py:186
  89.1 0.6 collective-permute-start.3
  89.8 12.0 %all-to-all-done.3.piece_ref = bf16[4,64,1024]{2,1,0:T(8,128)(2,1)S(1)} async-done(((bf16[4,64,1024]{2,1,0:T(8,128)(2,1)}), bf16[4,64,1024]{2,1,0:T(8,128)(2,1)S(1)}, u32[]{:S(2)}, u32[]{:S(2)}) %all-to-all-start.3) | async-done | bytes 524320 | tf_op jit(solution)/shard_map/all_to_all | solution.py:186
  101.7 0.6 collective-permute-start.2
  102.3 0.7 fusion.1
  103.0 3.2 %shard_map.73.refs_0_ = bf16[64,16384]{1,0:T(8,128)(2,1)} custom-call(s32[1]{0:T(128)} %bitcast.which, bf16[4,64,1024]{2,1,0:T(8,128)(2,1)} %copy-done.3), custom_call_target="tpu_custom_call" | custom-call | bytes 1048576 | tf_op jit(solution)/shard_map/pallas_call | solution.py:118
  106.2 0.0 collective-permute-done.3.piece_ref
  106.2 0.8 copy-done.5
  107.0 3.2 %shard_map.74.refs_0_ = bf16[64,16384]{1,0:T(8,128)(2,1)} custom-call(s32[1]{0:T(128)} %bitcast.1.which, bf16[4,64,1024]{2,1,0:T(8,128)(2,1)} %copy-done.5, bf16[64,16384]{1,0:T(8,128)(2,1)} %shard_map.73.refs_0_), custom_call_target="tpu_custom_call", output_to_operand_aliasing={{}: (2, {})} | custom-call | bytes 1048576 | tf_op jit(solution)/shard_map/pallas_call | solution.py:118
  110.1 3.2 %shard_map.75.refs_0_ = bf16[64,16384]{1,0:T(8,128)(2,1)} custom-call(s32[1]{0:T(128)} %bitcast.which, bf16[4,64,1024]{2,1,0:T(8,128)(2,1)} %copy-done.2, bf16[64,16384]{1,0:T(8,128)(2,1)} %shard_map.74.refs_0_), custom_call_target="tpu_custom_call", output_to_operand_aliasing={{}: (2, {})} | custom-call | bytes 1048576 | tf_op jit(solution)/shard_map/pallas_call | solution.py:118
  113.3 0.0 collective-permute-done.2.piece_ref
  113.3 0.8 copy-done.4
  114.1 3.2 %shard_map.76 = bf16[64,16384]{1,0:T(8,128)(2,1)} custom-call(s32[1]{0:T(128)} %bitcast.1.which, bf16[4,64,1024]{2,1,0:T(8,128)(2,1)} %copy-done.4, bf16[64,16384]{1,0:T(8,128)(2,1)} %shard_map.75.refs_0_), custom_call_target="tpu_custom_call", output_to_operand_aliasing={{}: (2, {})} | custom-call | bytes 1048576 | tf_op jit(solution)/shard_map/pallas_call | solution.py:118
  (23 shorter events, 0.2 us)
Async XLA Ops:
  0.6 0.9 copy-start
  6.5 8.1 %copy-start.1 = (bf16[64,1024]{1,0:T(8,128)(2,1)S(1)}, bf16[64,1024]{1,0:T(8,128)(2,1)}, u32[]{:S(2)}) copy-start(bf16[64,1024]{1,0:T(8,128)(2,1)} %rows_ref.7) | copy-start | bytes 393220
  6.5 15.8 %collective-permute-start.1 = (bf16[4,64,1024]{2,1,0:T(8,128)(2,1)S(1)}, bf16[4,64,1024]{2,1,0:T(8,128)(2,1)S(1)}, u32[]{:S(2)}, u32[]{:S(2)}) collective-permute-start(bf16[4,64,1024]{2,1,0:T(8,128)(2,1)S(1)} %shard_map.71), channel_id=1, source_target_pairs={{0,1},{1,0},{2,3},{3,2},{4,5},{5,4},{6,7},{7,6},{8,9},{9,8},{10,11... | collective-permute-start | bytes 1572872 | tf_op jit(solution)/shard_map/ppermute | solution.py:159
  14.5 19.2 %collective-permute-start = (bf16[4,64,1024]{2,1,0:T(8,128)(2,1)S(1)}, bf16[4,64,1024]{2,1,0:T(8,128)(2,1)S(1)}, u32[]{:S(2)}, u32[]{:S(2)}) collective-permute-start(bf16[4,64,1024]{2,1,0:T(8,128)(2,1)S(1)} %shard_map.69), channel_id=1, source_target_pairs={{0,1},{1,0},{2,3},{3,2},{4,5},{5,4},{6,7},{7,6},{8,9},{9,8},{10,11... | collective-permute-start | bytes 1572872 | tf_op jit(solution)/shard_map/ppermute | solution.py:159
  23.2 17.9 %all-to-all-start.1 = ((bf16[4,64,1024]{2,1,0:T(8,128)(2,1)}), bf16[4,64,1024]{2,1,0:T(8,128)(2,1)S(1)}, u32[]{:S(2)}, u32[]{:S(2)}) async-start(bf16[4,64,1024]{2,1,0:T(8,128)(2,1)} %add_convert_fusion), calls=%async_computation.1 | async-start | bytes 1048576 | tf_op jit(solution)/shard_map/all_to_all | solution.py:163
  33.6 23.3 %copy-start.6 = (bf16[64,2048]{1,0:T(8,128)(2,1)S(1)}, bf16[64,2048]{1,0:T(8,128)(2,1)}, u32[]{:S(2)}) copy-start(bf16[64,2048]{1,0:T(8,128)(2,1)} %param.7) | copy-start | bytes 786436
  41.1 15.7 %all-to-all-start = ((bf16[4,64,1024]{2,1,0:T(8,128)(2,1)}), bf16[4,64,1024]{2,1,0:T(8,128)(2,1)S(1)}, u32[]{:S(2)}, u32[]{:S(2)}) async-start(bf16[4,64,1024]{2,1,0:T(8,128)(2,1)} %add_convert_fusion.1), calls=%async_computation | async-start | bytes 1048576 | tf_op jit(solution)/shard_map/all_to_all | solution.py:163
  44.6 17.1 %copy-start.7 = (bf16[2048]{0:T(1024)(128)(2,1)S(1)}, bf16[2048]{0:T(1024)(128)(2,1)}, u32[]{:S(2)}) copy-start(bf16[2048]{0:T(1024)(128)(2,1)} %param.8) | copy-start | bytes 12292
  44.6 17.1 %copy-start.8 = (bf16[2048]{0:T(1024)(128)(2,1)S(1)}, bf16[2048]{0:T(1024)(128)(2,1)}, u32[]{:S(2)}) copy-start(bf16[2048]{0:T(1024)(128)(2,1)} %param.9) | copy-start | bytes 12292
  58.1 10.0 %all-to-all-start.2 = ((f32[8,1,128]{2,1,0:T(1,128)}), f32[8,1,128]{2,1,0:T(1,128)S(1)}, u32[]{:S(2)}, u32[]{:S(2)}) async-start(f32[8,1,128]{2,1,0:T(1,128)} %reshape.95), calls=%async_computation.2 | async-start | bytes 8192 | tf_op jit(solution)/shard_map/all_to_all | solution.py:173
  84.7 18.3 %copy-start.3 = (bf16[4,64,1024]{2,1,0:T(8,128)(2,1)}, bf16[4,64,1024]{2,1,0:T(8,128)(2,1)S(1)}, u32[]{:S(2)}) copy-start(bf16[4,64,1024]{2,1,0:T(8,128)(2,1)S(1)} %all_to_all.25.piece_ref) | copy-start | bytes 1572868
  85.7 16.1 %all-to-all-start.3 = ((bf16[4,64,1024]{2,1,0:T(8,128)(2,1)}), bf16[4,64,1024]{2,1,0:T(8,128)(2,1)S(1)}, u32[]{:S(2)}, u32[]{:S(2)}) async-start(bf16[4,64,1024]{2,1,0:T(8,128)(2,1)} %broadcast_in_dim.7), calls=%async_computation.3 | async-start | bytes 1048576 | tf_op jit(solution)/shard_map/all_to_all | solution.py:186
  89.1 17.0 %collective-permute-start.3 = (bf16[4,64,1024]{2,1,0:T(8,128)(2,1)S(1)}, bf16[4,64,1024]{2,1,0:T(8,128)(2,1)S(1)}, u32[]{:S(2)}, u32[]{:S(2)}) collective-permute-start(bf16[4,64,1024]{2,1,0:T(8,128)(2,1)S(1)} %all_to_all.25.piece_ref), channel_id=1, source_target_pairs={{0,1},{1,0},{2,3},{3,2},{4,5},{5,4},{6,7},{7,6},{8,9},{9,8},{10,11... | collective-permute-start | bytes 1572872 | tf_op jit(solution)/shard_map/ppermute | solution.py:196
  101.7 8.4 %copy-start.2 = (bf16[4,64,1024]{2,1,0:T(8,128)(2,1)}, bf16[4,64,1024]{2,1,0:T(8,128)(2,1)S(1)}, u32[]{:S(2)}) copy-start(bf16[4,64,1024]{2,1,0:T(8,128)(2,1)S(1)} %all-to-all-done.3.piece_ref) | copy-start | bytes 1572868
  101.7 11.6 %collective-permute-start.2 = (bf16[4,64,1024]{2,1,0:T(8,128)(2,1)S(1)}, bf16[4,64,1024]{2,1,0:T(8,128)(2,1)S(1)}, u32[]{:S(2)}, u32[]{:S(2)}) collective-permute-start(bf16[4,64,1024]{2,1,0:T(8,128)(2,1)S(1)} %all-to-all-done.3.piece_ref), channel_id=1, source_target_pairs={{0,1},{1,0},{2,3},{3,2},{4,5},{5,4},{6,7},{7,6},{8,9},{9,8},{10,11... | collective-permute-start | bytes 1572872 | tf_op jit(solution)/shard_map/ppermute | solution.py:196
  106.2 0.8 copy-start.5
  113.3 0.8 copy-start.4

commit v3 on v2

v3 whole, which is shorter than its diff:
```python
import functools
import math

import jax
import jax.numpy as jnp
from jax import lax
from jax.experimental import pallas as pl
from jax.experimental.pallas import tpu as pltpu
from jax.sharding import PartitionSpec as P

BLOCK_LEN = 128
LANES = 128
VMEM_BYTES = 40 * 1024 * 1024


def factors(n):
    inner = 1 << ((n.bit_length() - 1) // 2)
    return n // inner, inner


def tile_width(width, most):
    while width % most:
        most //= 2
    return most


def signs(length):
    rows = lax.broadcasted_iota(jnp.int32, (length, length), 0)
    columns = lax.broadcasted_iota(jnp.int32, (length, length), 1)
    common = jnp.bitwise_and(rows, columns)
    parity = jnp.zeros((length, length), jnp.int32)
    for bit_index in range(length.bit_length() - 1):
        parity = parity + jnp.bitwise_and(jnp.right_shift(common, bit_index), 1)
    return (1 - 2 * jnp.bitwise_and(parity, 1)).astype(jnp.bfloat16)


def product_kernel(which, rows_ref, weight_ref, out_ref):
    del which
    out_ref[...] = jnp.dot(
        rows_ref[...], weight_ref[...], preferred_element_type=jnp.float32
    ).astype(out_ref.dtype)


def product(attended, weight, target, local, dtype):
    rows, depth = attended.shape
    tile = tile_width(local, 512)
    per = local // tile
    return pl.pallas_call(
        product_kernel,
        out_shape=jax.ShapeDtypeStruct((rows, local), dtype),
        grid_spec=pltpu.PrefetchScalarGridSpec(
            num_scalar_prefetch=1,
            grid=(per,),
            in_specs=[
                pl.BlockSpec((rows, depth), lambda j, which: (0, 0)),
                pl.BlockSpec((depth, tile), lambda j, which: (0, which[0] * per + j)),
            ],
            out_specs=pl.BlockSpec((rows, tile), lambda j, which: (0, j)),
        ),
        compiler_params=pltpu.CompilerParams(vmem_limit_bytes=VMEM_BYTES),
        cost_estimate=pl.CostEstimate(
            flops=2 * rows * depth * local,
            bytes_accessed=2 * depth * local,
            transcendentals=0,
        ),
        name="product",
    )(target.reshape(1), attended, weight)


def stream_kernel(count, residual_ref, *refs):
    terms, (half_ref, stats_ref) = refs[:count], refs[count:]
    stream = residual_ref[...].astype(jnp.float32)
    for term in terms:
        stream = stream + term[...].astype(jnp.float32)
    rows, width = stream.shape
    half_ref[...] = stream.astype(half_ref.dtype)
    mean = jnp.sum(stream, axis=1, keepdims=True) / width
    square = jnp.sum((stream - mean) ** 2, axis=1, keepdims=True)
    lane = lax.broadcasted_iota(jnp.int32, (rows, LANES), 1)
    table = jnp.where(lane == 0, mean, jnp.where(lane == 1, square, 0.0))
    if rows < LANES:
        table = jnp.concatenate(
            [table, jnp.zeros((LANES - rows, LANES), jnp.float32)], axis=0
        )
    stats = jnp.transpose(table)[:8]
    for d in range(stats_ref.shape[0]):
        stats_ref[d] = stats


def own_stream(residual, terms, n):
    rows, local = residual.shape
    return pl.pallas_call(
        functools.partial(stream_kernel, len(terms)),
        out_shape=(
            jax.ShapeDtypeStruct((rows, local), jnp.bfloat16),
            jax.ShapeDtypeStruct((n, 8, LANES), jnp.float32),
        ),
        compiler_params=pltpu.CompilerParams(vmem_limit_bytes=VMEM_BYTES),
        cost_estimate=pl.CostEstimate(
            flops=20 * rows * local, bytes_accessed=16 * rows * local, transcendentals=0
        ),
        name="own_stream",
    )(residual, *terms)


def moments_kernel(local, stats_ref, out_ref):
    n = stats_ref.shape[0]
    rows = out_ref.shape[0]
    centre = jnp.zeros((1, LANES), jnp.float32)
    for d in range(n):
        centre = centre + stats_ref[d, 0:1]
    centre = centre / n
    spread = jnp.zeros((1, LANES), jnp.float32)
    for d in range(n):
        away = stats_ref[d, 0:1] - centre
        spread = spread + stats_ref[d, 1:2] + local * (away * away)
    inverse = lax.rsqrt(spread / (n * local) + 1e-05)
    row = lax.broadcasted_iota(jnp.int32, (LANES, LANES), 0)
    table = jnp.where(row == 0, centre, jnp.where(row == 1, inverse, 0.0))
    out_ref[...] = jnp.transpose(table)[:rows]


def moments(stats, rows, local):
    return pl.pallas_call(
        functools.partial(moments_kernel, local),
        out_shape=jax.ShapeDtypeStruct((rows, LANES), jnp.float32),
        name="moments",
    )(stats)


def rows_kernel(source, piece_ref, moments_ref, scaling_ref, *refs):
    out_ref, done_ref, semaphore = refs[-3:]
    rows, width = piece_ref.shape
    blocks = width // BLOCK_LEN
    table = signs(BLOCK_LEN)
    unit = 1.0 / math.sqrt(BLOCK_LEN)
    owner = source[0]
    scaling = scaling_ref[owner].astype(jnp.float32)
    gain, bias = scaling[0:1], scaling[1:2]
    centre = moments_ref[:, 0:1]
    inverse = moments_ref[:, 1:2]
    normal = (piece_ref[...].astype(jnp.float32) - centre) * inverse * gain + bias
    normal = jnp.concatenate(
        [normal[:, b * BLOCK_LEN : (b + 1) * BLOCK_LEN] for b in range(blocks)], axis=0
    )
    coded = jnp.zeros(normal.shape, jnp.float32)
    rest = normal
    for _ in range(3):
        part = rest.astype(jnp.bfloat16)
        coded = coded + jnp.dot(part, table, preferred_element_type=jnp.float32)
        rest = rest - part.astype(jnp.float32)
    coded = coded * unit
    largest = jnp.max(jnp.abs(coded), axis=1, keepdims=True)
    scales = (largest / 448.0 + 1e-06).astype(jnp.bfloat16).astype(jnp.float32)
    quanta = (coded / scales).astype(jnp.bfloat16)
    back = jnp.dot(quanta, table, preferred_element_type=jnp.float32) * (scales * unit)
    back = back.astype(out_ref.dtype)
    for b in range(blocks):
        done_ref[:, b * BLOCK_LEN : (b + 1) * BLOCK_LEN] = back[b * rows : (b + 1) * rows]
    columns = pl.ds(pl.multiple_of(owner * width, LANES), width)
    copy = pltpu.make_async_copy(done_ref, out_ref.at[:, columns], semaphore)
    copy.start()
    copy.wait()


def finish(whole, source, piece, columns, scaling):
    rows, local = piece.shape
    n = scaling.shape[0]
    earlier = [] if whole is None else [whole]
    vmem = pl.BlockSpec(memory_space=pltpu.VMEM)
    return pl.pallas_call(
        rows_kernel,
        out_shape=jax.ShapeDtypeStruct((rows, n * local), jnp.bfloat16),
        grid_spec=pltpu.PrefetchScalarGridSpec(
            num_scalar_prefetch=1,
            grid=(1,),
            in_specs=[
                pl.BlockSpec((rows, local), lambda i, source: (0, 0)),
                pl.BlockSpec((rows, LANES), lambda i, source: (0, 0)),
                pl.BlockSpec((n, 2, local), lambda i, source: (0, 0, 0)),
            ]
            + [pl.BlockSpec(memory_space=pl.ANY)] * len(earlier),
            out_specs=pl.BlockSpec(memory_space=pl.ANY),
            scratch_shapes=[
                pltpu.VMEM((rows, local), jnp.bfloat16),
                pltpu.SemaphoreType.DMA,
            ],
        ),
        input_output_aliases={4: 0} if earlier else {},
        compiler_params=pltpu.CompilerParams(vmem_limit_bytes=VMEM_BYTES),
        cost_estimate=pl.CostEstimate(
            flops=8 * BLOCK_LEN * rows * local,
            bytes_accessed=4 * rows * local,
            transcendentals=0,
        ),
        name="finish",
    )(source.reshape(1), piece, columns, scaling, *earlier)


def body(attended, out_weight, residual, norm_gain, norm_bias):
    n = lax.axis_size("tensor")
    nz, nx = factors(n)
    rows = attended.shape[0]
    local = out_weight.shape[1] // n
    me = lax.axis_index("tensor")
    outer, inner = me // nx, me % nx
    every = [(z, x) for z in range(nz) for x in range(nx)]
    swap = [[(z * nx + x, z * nx + (x ^ j)) for z, x in every] for j in range(nx)]
    jump = [[(z * nx + x, (z ^ k) * nx + x) for z, x in every] for k in range(nz)]
    order = list(range(nz - 1, -1, -1))

    arrived = []
    kept = None
    for k in order:
        sent = []
        for j in range(1, nx):
            target = (outer ^ k) * nx + (inner ^ j)
            sent.append(
                lax.ppermute(
                    product(attended, out_weight, target, local, jnp.bfloat16),
                    "tensor",
                    swap[j],
                )
            )
        kept = product(attended, out_weight, (outer ^ k) * nx + inner, local, jnp.float32)
        if k:
            for piece in sent:
                kept = kept + piece.astype(jnp.float32)
            last = kept.astype(jnp.bfloat16)
            arrived.append(lax.ppermute(last, "tensor", jump[k]))
        else:
            arrived += [kept] + sent

    scaling = jnp.stack([norm_gain, norm_bias])
    scaling, _ = lax.optimization_barrier((scaling, last))
    scaling = lax.all_to_all(
        jnp.broadcast_to(scaling[None], (n,) + scaling.shape), "tensor", 0, 0, tiled=True
    )

    stream_out, stats = own_stream(residual, arrived, n)
    near = [(k, lax.ppermute(stream_out, "tensor", jump[k])) for k in order[:-1]]
    pieces = [(0, stream_out)] + near[::-1]
    stats = lax.all_to_all(stats, "tensor", 0, 0, tiled=True)
    columns = moments(stats, rows, local)

    whole = None
    for k, piece in pieces:
        whole = finish(whole, (outer ^ k) * nx + inner, piece, columns, scaling)
        for j in range(1, nx):
            other = lax.ppermute(piece, "tensor", swap[j])
            whole = finish(whole, (outer ^ k) * nx + (inner ^ j), other, columns, scaling)
    return (stream_out, whole)


def solution(mesh):
    placed = (
        P(("groups", "dp"), "tensor"),
        P("tensor", None),
        P(("groups", "dp"), "tensor"),
        P("tensor"),
        P("tensor"),
    )
    return jax.shard_map(
        body,
        mesh=mesh,
        in_specs=placed,
        out_specs=(P(("groups", "dp"), "tensor"), P(("groups", "dp"), None)),
        check_vma=False,
    )
```

time: 118 us -> 112 us (0.949)
  blocking collectives: 14.2 us -> 0 us
  starting transfers between devices: 20.3 us -> 32 us
  Pallas kernels: 33.2 us -> 42 us
  waiting for transfers between devices: 39.7 us -> 33.1 us
  other arithmetic: 3.93 us -> 0.22 us
  local copies, waits for them, and re-layouts: 5.04 us -> 3.31 us
    all_to_all x4 -> x2, waiting for transfers between devices: 37 us -> 9 us  [the longest x1 5.42 us: body(): lax.all_to_all(jnp.broadcast_to(scaling[None], (n,) + scaling.shape), 'te...]
    ppermute x4 -> x14, waiting for transfers between devices: 2.72 us -> 24.1 us  [the longest x3 12.2 us: body(): arrived.append(lax.ppermute(last, 'tensor', jump[k]))]
    ppermute x4 -> x14, starting transfers between devices: 4.27 us -> 23.6 us  [the longest x3 8.44 us: body(): lax.ppermute(stream_out, 'tensor', jump[k])]
    all_to_all x1 -> x0, blocking collectives: 14.2 us -> none  [body(): lax.all_to_all(jnp.broadcast_to(piece[None], (nz,) + piece.shape), 'tenso...]
    pallas_call x9 -> x18, Pallas kernels: 33.2 us -> 42 us  [the longest x8 28.1 us: product(): pl.pallas_call(product_kernel, out_shape=jax.ShapeDtypeStruct((rows, loca...]
    all_to_all x4 -> x2, starting transfers between devices: 16 us -> 8.36 us  [the longest x1 4.72 us: body(): lax.all_to_all(jnp.broadcast_to(scaling[None], (n,) + scaling.shape), 'te...]
    convert_element_type x3, other arithmetic: 2.64 us -> 0.19 us  [body(): last = kept.astype(jnp.bfloat16)]
    unnamed x20 -> x18, local copies, waits for them, and re-layouts: 3.29 us -> 2.63 us
  transfers between devices with their start and end apart: 8 -> 16, of which waited for: 5 -> 5; matrix products, arithmetic and copies ran while one was open for 2% -> 1% of each run, Pallas kernels for 21% -> 32%
where the time goes in v3:
time: 112 us; the launch traced here: 111 us
  Pallas kernels  42 us (38%)
  waiting for transfers between devices  33.1 us (30%)
  starting transfers between devices  32 us (29%)
  local copies, waits for them, and re-layouts  3.31 us (3%)
    pallas_call x8, Pallas kernels, product(): pl.pallas_call(product_kernel, out_shape=jax.ShapeDtypeStruct((rows, loca...  28.1 us
    ppermute x3, waiting for transfers between devices, body(): arrived.append(lax.ppermute(last, 'tensor', jump[k]))  12.2 us
    ppermute x3, waiting for transfers between devices, body(): lax.ppermute(stream_out, 'tensor', jump[k])  11.8 us
    pallas_call x8, Pallas kernels, finish(): pl.pallas_call(rows_kernel, out_shape=jax.ShapeDtypeStruct((rows, n * loc...  11.4 us
    ppermute x3, starting transfers between devices, body(): lax.ppermute(stream_out, 'tensor', jump[k])  8.44 us
    all_to_all x1, waiting for transfers between devices, body(): lax.all_to_all(jnp.broadcast_to(scaling[None], (n,) + scaling.shape), 'te...  5.42 us
    ppermute x4, starting transfers between devices, body(): lax.ppermute(product(attended, out_weight, target, local, jnp.bfloat16),...  5.27 us
    ppermute x4, starting transfers between devices, body(): other = lax.ppermute(piece, 'tensor', swap[j])  5.07 us
  transfers between devices with their start and end apart: 16, of which 5 were waited for; matrix products, arithmetic and copies ran while one was open for 1% of the time, Pallas kernels for 32%

profile of v3, /device:TPU:0, one launch (start us, length us, event | category | flops | bytes accessed | tf_op | source)
XLA Modules:
  0.0 111.5 jit_solution(1350032666351962933)
XLA Ops:
  0.7 0.9 copy-done
  1.6 3.5 %product.11 = bf16[64,2048]{1,0:T(8,128)(2,1)S(1)} custom-call(s32[1]{0:T(128)} %bitcast.3.which.source, bf16[64,1024]{1,0:T(8,128)(2,1)S(1)} %copy-done, bf16[1024,16384]{1,0:T(8,128)(2,1)} %weight_ref.15), custom_call_target="tpu_custom_call" | custom-call | flops 268435456 | bytes 4194304 | tf_op jit(solution)/shard_map/product/pallas_call | solution.py:48
  5.1 3.0 %collective-permute-start.2 = (bf16[64,2048]{1,0:T(8,128)(2,1)S(1)}, bf16[64,2048]{1,0:T(8,128)(2,1)S(1)}, u32[]{:S(2)}, u32[]{:S(2)}) collective-permute-start(bf16[64,2048]{1,0:T(8,128)(2,1)S(1)} %product.11), channel_id=1, source_target_pairs={{0,1},{1,0},{2,3},{3,2},{4,5},{5,4},{6,7},{7,6},{8,9},{9,8},{10,11... | collective-permute-start | bytes 786440 | tf_op jit(solution)/shard_map/ppermute | solution.py:219
  8.1 3.5 %product.13 = bf16[64,2048]{1,0:T(8,128)(2,1)S(1)} custom-call(s32[1]{0:T(128)} %bitcast.5.which.source, bf16[64,1024]{1,0:T(8,128)(2,1)S(1)} %copy-done.1, bf16[1024,16384]{1,0:T(8,128)(2,1)} %weight_ref.15), custom_call_target="tpu_custom_call" | custom-call | flops 268435456 | bytes 4194304 | tf_op jit(solution)/shard_map/product/pallas_call | solution.py:48
  11.6 0.1 collective-permute-start.4
  11.7 3.5 %product.9 = bf16[64,2048]{1,0:T(8,128)(2,1)S(1)} custom-call(s32[1]{0:T(128)} %bitcast.1.which.source, bf16[64,1024]{1,0:T(8,128)(2,1)S(1)} %copy-done.1, bf16[1024,16384]{1,0:T(8,128)(2,1)} %weight_ref.15), custom_call_target="tpu_custom_call" | custom-call | flops 268435456 | bytes 4194304 | tf_op jit(solution)/shard_map/product/pallas_call | solution.py:48
  15.2 2.0 %collective-permute-start = (bf16[64,2048]{1,0:T(8,128)(2,1)S(1)}, bf16[64,2048]{1,0:T(8,128)(2,1)S(1)}, u32[]{:S(2)}, u32[]{:S(2)}) collective-permute-start(bf16[64,2048]{1,0:T(8,128)(2,1)S(1)} %product.9), channel_id=1, source_target_pairs={{0,1},{1,0},{2,3},{3,2},{4,5},{5,4},{6,7},{7,6},{8,9},{9,8},{10,11... | collective-permute-start | bytes 786440 | tf_op jit(solution)/shard_map/ppermute | solution.py:219
  17.3 3.5 %product.15 = bf16[64,2048]{1,0:T(8,128)(2,1)S(1)} custom-call(s32[1]{0:T(128)} %bitcast.7.which.source, bf16[64,1024]{1,0:T(8,128)(2,1)S(1)} %copy-done.1, bf16[1024,16384]{1,0:T(8,128)(2,1)} %weight_ref.15), custom_call_target="tpu_custom_call" | custom-call | flops 268435456 | bytes 4194304 | tf_op jit(solution)/shard_map/product/pallas_call | solution.py:48
  20.8 0.1 collective-permute-start.6
  20.9 3.5 %product.10 = f32[64,2048]{1,0:T(8,128)S(1)} custom-call(s32[1]{0:T(128)} %bitcast.2.which.source, bf16[64,1024]{1,0:T(8,128)(2,1)S(1)} %copy-done.1, bf16[1024,16384]{1,0:T(8,128)(2,1)} %weight_ref.15), custom_call_target="tpu_custom_call" | custom-call | flops 268435456 | bytes 4194304 | tf_op jit(solution)/shard_map/product/pallas_call | solution.py:48
  24.4 3.5 %product.12 = f32[64,2048]{1,0:T(8,128)S(1)} custom-call(s32[1]{0:T(128)} %bitcast.4.which.source, bf16[64,1024]{1,0:T(8,128)(2,1)S(1)} %copy-done.1, bf16[1024,16384]{1,0:T(8,128)(2,1)} %weight_ref.15), custom_call_target="tpu_custom_call" | custom-call | flops 268435456 | bytes 4194304 | tf_op jit(solution)/shard_map/product/pallas_call | solution.py:48
  27.9 3.5 %product.8 = f32[64,2048]{1,0:T(8,128)S(1)} custom-call(s32[1]{0:T(128)} %bitcast.which.source, bf16[64,1024]{1,0:T(8,128)(2,1)S(1)} %copy-done.1, bf16[1024,16384]{1,0:T(8,128)(2,1)} %weight_ref.15), custom_call_target="tpu_custom_call" | custom-call | flops 268435456 | bytes 4194304 | tf_op jit(solution)/shard_map/product/pallas_call | solution.py:48
  31.4 0.1 add_convert_fusion.1
  31.5 3.1 %collective-permute-start.3 = (bf16[64,2048]{1,0:T(8,128)(2,1)S(1)}, bf16[64,2048]{1,0:T(8,128)(2,1)S(1)}, u32[]{:S(2)}, u32[]{:S(2)}) collective-permute-start(bf16[64,2048]{1,0:T(8,128)(2,1)S(1)} %add_convert_fusion.1), channel_id=1, source_target_pairs={{0,4},{1,5},{2,6},{3,7},{4,0},{5,1},{6,2},{7,3},{8,12},{9,13},{10,... | collective-permute-start | bytes 786440 | tf_op jit(solution)/shard_map/ppermute | solution.py:230
  34.6 0.1 add_convert_fusion
  34.7 1.6 %collective-permute-start.5 = (bf16[64,2048]{1,0:T(8,128)(2,1)S(1)}, bf16[64,2048]{1,0:T(8,128)(2,1)S(1)}, u32[]{:S(2)}, u32[]{:S(2)}) collective-permute-start(bf16[64,2048]{1,0:T(8,128)(2,1)S(1)} %add_convert_fusion), channel_id=1, source_target_pairs={{0,2},{1,3},{2,0},{3,1},{4,6},{5,7},{6,4},{7,5},{8,10},{9,11},{10,... | collective-permute-start | bytes 786440 | tf_op jit(solution)/shard_map/ppermute | solution.py:230
  36.3 0.1 add_convert_fusion.2
  36.4 0.1 collective-permute-start.1
  36.5 0.0 copy-start.4
  36.5 0.0 copy-start.7
  36.5 3.5 %product.14.refs_3_ = f32[64,2048]{1,0:T(8,128)S(1)} custom-call(s32[1]{0:T(128)} %bitcast.6.which.source, bf16[64,1024]{1,0:T(8,128)(2,1)S(1)} %copy-done.1, bf16[1024,16384]{1,0:T(8,128)(2,1)} %weight_ref.15), custom_call_target="tpu_custom_call" | custom-call | flops 268435456 | bytes 4194304 | tf_op jit(solution)/shard_map/product/pallas_call | solution.py:48
  40.1 12.2 %collective-permute-done.3.refs_1_ = bf16[64,2048]{1,0:T(8,128)(2,1)S(1)} collective-permute-done((bf16[64,2048]{1,0:T(8,128)(2,1)S(1)}, bf16[64,2048]{1,0:T(8,128)(2,1)S(1)}, u32[]{:S(2)}, u32[]{:S(2)}) %collective-permute-start.3) | collective-permute-done | bytes 262176 | tf_op jit(solution)/shard_map/ppermute | solution.py:230
  52.3 1.1 own_stream.1
  53.4 5.1 %collective-permute-start.11 = (bf16[64,2048]{1,0:T(8,128)(2,1)}, bf16[64,2048]{1,0:T(8,128)(2,1)S(1)}, u32[]{:S(2)}, u32[]{:S(2)}) collective-permute-start(bf16[64,2048]{1,0:T(8,128)(2,1)} %get-tuple-element.3.piece_ref), channel_id=1, source_target_pairs={{0,2},{1,3},{2,0},{3,1},{4,6},{5,7},{6,4},{7,5},{8,10},{9,11},{10,... | collective-permute-start | bytes 786440 | tf_op jit(solution)/shard_map/ppermute | solution.py:241
  58.4 1.9 %collective-permute-start.9 = (bf16[64,2048]{1,0:T(8,128)(2,1)}, bf16[64,2048]{1,0:T(8,128)(2,1)S(1)}, u32[]{:S(2)}, u32[]{:S(2)}) collective-permute-start(bf16[64,2048]{1,0:T(8,128)(2,1)} %get-tuple-element.3.piece_ref), channel_id=1, source_target_pairs={{0,4},{1,5},{2,6},{3,7},{4,0},{5,1},{6,2},{7,3},{8,12},{9,13},{10,... | collective-permute-start | bytes 786440 | tf_op jit(solution)/shard_map/ppermute | solution.py:241
  60.4 1.5 %collective-permute-start.7 = (bf16[64,2048]{1,0:T(8,128)(2,1)}, bf16[64,2048]{1,0:T(8,128)(2,1)S(1)}, u32[]{:S(2)}, u32[]{:S(2)}) collective-permute-start(bf16[64,2048]{1,0:T(8,128)(2,1)} %get-tuple-element.3.piece_ref), channel_id=1, source_target_pairs={{0,6},{1,7},{2,4},{3,5},{4,2},{5,3},{6,0},{7,1},{8,14},{9,15},{10,... | collective-permute-start | bytes 786440 | tf_op jit(solution)/shard_map/ppermute | solution.py:241
  61.9 1.6 %collective-permute-start.13 = (bf16[64,2048]{1,0:T(8,128)(2,1)}, bf16[64,2048]{1,0:T(8,128)(2,1)S(1)}, u32[]{:S(2)}, u32[]{:S(2)}) collective-permute-start(bf16[64,2048]{1,0:T(8,128)(2,1)} %get-tuple-element.3.piece_ref), channel_id=1, source_target_pairs={{0,1},{1,0},{2,3},{3,2},{4,5},{5,4},{6,7},{7,6},{8,9},{9,8},{10,11... | collective-permute-start | bytes 786440 | tf_op jit(solution)/shard_map/ppermute | solution.py:250
  63.4 3.6 %all-to-all-start = ((f32[8,8,128]{2,1,0:T(8,128)}), f32[8,8,128]{2,1,0:T(8,128)S(1)}, u32[]{:S(2)}, u32[]{:S(2)}) async-start(f32[8,8,128]{2,1,0:T(8,128)} %get-tuple-element.6), calls=%async_computation | async-start | bytes 65536 | tf_op jit(solution)/shard_map/all_to_all | solution.py:243
  67.0 3.6 %collective-permute-done.11.piece_ref = bf16[64,2048]{1,0:T(8,128)(2,1)S(1)} collective-permute-done((bf16[64,2048]{1,0:T(8,128)(2,1)}, bf16[64,2048]{1,0:T(8,128)(2,1)S(1)}, u32[]{:S(2)}, u32[]{:S(2)}) %collective-permute-start.11) | collective-permute-done | bytes 262176 | tf_op jit(solution)/shard_map/ppermute | solution.py:241
  70.6 1.5 %collective-permute-start.12 = (bf16[64,2048]{1,0:T(8,128)(2,1)S(1)}, bf16[64,2048]{1,0:T(8,128)(2,1)S(1)}, u32[]{:S(2)}, u32[]{:S(2)}) collective-permute-start(bf16[64,2048]{1,0:T(8,128)(2,1)S(1)} %collective-permute-done.11.piece_ref), channel_id=1, source_target_pairs={{0,1},{1,0},{2,3},{3,2},{4,5},{5,4},{6,7},{7,6},{8,9},{9,8},{10,11... | collective-permute-start | bytes 786440 | tf_op jit(solution)/shard_map/ppermute | solution.py:250
  72.1 8.2 %collective-permute-done.9.piece_ref = bf16[64,2048]{1,0:T(8,128)(2,1)S(1)} collective-permute-done((bf16[64,2048]{1,0:T(8,128)(2,1)}, bf16[64,2048]{1,0:T(8,128)(2,1)S(1)}, u32[]{:S(2)}, u32[]{:S(2)}) %collective-permute-start.9) | collective-permute-done | bytes 262176 | tf_op jit(solution)/shard_map/ppermute | solution.py:241
  80.3 1.5 %collective-permute-start.10 = (bf16[64,2048]{1,0:T(8,128)(2,1)S(1)}, bf16[64,2048]{1,0:T(8,128)(2,1)S(1)}, u32[]{:S(2)}, u32[]{:S(2)}) collective-permute-start(bf16[64,2048]{1,0:T(8,128)(2,1)S(1)} %collective-permute-done.9.piece_ref), channel_id=1, source_target_pairs={{0,1},{1,0},{2,3},{3,2},{4,5},{5,4},{6,7},{7,6},{8,9},{9,8},{10,11... | collective-permute-start | bytes 786440 | tf_op jit(solution)/shard_map/ppermute | solution.py:250
  81.8 0.5 collective-permute-start.8
  82.4 3.6 %all-to-all-done.stats_ref = f32[8,8,128]{2,1,0:T(8,128)S(1)} async-done(((f32[8,8,128]{2,1,0:T(8,128)}), f32[8,8,128]{2,1,0:T(8,128)S(1)}, u32[]{:S(2)}, u32[]{:S(2)}) %all-to-all-start) | async-done | bytes 32800 | tf_op jit(solution)/shard_map/all_to_all | solution.py:243
  86.0 0.7 broadcast_in_dim.2
  86.7 4.7 %all-to-all-start.1 = ((bf16[8,2,2048]{2,1,0:T(2,128)(2,1)}), bf16[8,2,2048]{2,1,0:T(2,128)(2,1)S(1)}, u32[]{:S(2)}, u32[]{:S(2)}) async-start(bf16[8,2,2048]{2,1,0:T(2,128)(2,1)} %broadcast_in_dim.2), calls=%async_computation.1 | async-start | bytes 131072 | tf_op jit(solution)/shard_map/all_to_all | solution.py:236
  91.4 1.5 %moments.1.moments_ref = f32[64,128]{1,0:T(8,128)} custom-call(f32[8,8,128]{2,1,0:T(8,128)} %copy-done.6), custom_call_target="tpu_custom_call" | custom-call | tf_op jit(solution)/shard_map/moments/pallas_call | solution.py:124
  92.9 5.4 %all-to-all-done.1.scaling_ref = bf16[8,2,2048]{2,1,0:T(2,128)(2,1)S(1)} async-done(((bf16[8,2,2048]{2,1,0:T(2,128)(2,1)}), bf16[8,2,2048]{2,1,0:T(2,128)(2,1)S(1)}, u32[]{:S(2)}, u32[]{:S(2)}) %all-to-all-start.1) | async-done | bytes 65568 | tf_op jit(solution)/shard_map/all_to_all | solution.py:236
  98.3 0.8 copy-done.2
  99.0 0.9 copy-done.5
  100.0 1.4 %finish.8.refs_0_ = bf16[64,16384]{1,0:T(8,128)(2,1)} custom-call(s32[1]{0:T(128)} %bitcast.6.which.source, bf16[64,2048]{1,0:T(8,128)(2,1)S(1)} %copy-done.5, f32[64,128]{1,0:T(8,128)S(1)} %copy-done.2, bf16[8,2,2048]{2,1,0:T(2,128)(2,1)S(1)} %all-to-all-done.1.scaling_ref), custom_call_target="tpu_custom_call" | custom-call | flops 134217728 | bytes 524288 | tf_op jit(solution)/shard_map/finish/pallas_call | solution.py:171
  101.4 1.4 %finish.9.refs_0_ = bf16[64,16384]{1,0:T(8,128)(2,1)} custom-call(s32[1]{0:T(128)} %bitcast.7.which.source, bf16[64,2048]{1,0:T(8,128)(2,1)S(1)} %collective-permute-done.13.piece_ref, f32[64,128]{1,0:T(8,128)S(1)} %copy-done.3, bf16[8,2,2048]{2,1,0:T(2,128)(2,1)S(1)} %all-to-all-done.1.scaling_ref, ...), custom_call_target="tpu_custom_call", output_to_operand_aliasing={{}: (4, {})} | custom-call | flops 134217728 | bytes 524288 | tf_op jit(solution)/shard_map/finish/pallas_call | solution.py:171
  102.9 1.4 %finish.10.refs_0_ = bf16[64,16384]{1,0:T(8,128)(2,1)} custom-call(s32[1]{0:T(128)} %bitcast.4.which.source, bf16[64,2048]{1,0:T(8,128)(2,1)S(1)} %collective-permute-done.11.piece_ref, f32[64,128]{1,0:T(8,128)S(1)} %copy-done.3, bf16[8,2,2048]{2,1,0:T(2,128)(2,1)S(1)} %all-to-all-done.1.scaling_ref, ...), custom_call_target="tpu_custom_call", output_to_operand_aliasing={{}: (4, {})} | custom-call | flops 134217728 | bytes 524288 | tf_op jit(solution)/shard_map/finish/pallas_call | solution.py:171
  104.3 1.4 %finish.11.refs_0_ = bf16[64,16384]{1,0:T(8,128)(2,1)} custom-call(s32[1]{0:T(128)} %bitcast.5.which.source, bf16[64,2048]{1,0:T(8,128)(2,1)S(1)} %collective-permute-done.12.piece_ref, f32[64,128]{1,0:T(8,128)S(1)} %copy-done.3, bf16[8,2,2048]{2,1,0:T(2,128)(2,1)S(1)} %all-to-all-done.1.scaling_ref, ...), custom_call_target="tpu_custom_call", output_to_operand_aliasing={{}: (4, {})} | custom-call | flops 134217728 | bytes 524288 | tf_op jit(solution)/shard_map/finish/pallas_call | solution.py:171
  105.8 1.4 %finish.12.refs_0_ = bf16[64,16384]{1,0:T(8,128)(2,1)} custom-call(s32[1]{0:T(128)} %bitcast.2.which.source, bf16[64,2048]{1,0:T(8,128)(2,1)S(1)} %collective-permute-done.9.piece_ref, f32[64,128]{1,0:T(8,128)S(1)} %copy-done.3, bf16[8,2,2048]{2,1,0:T(2,128)(2,1)S(1)} %all-to-all-done.1.scaling_ref, ...), custom_call_target="tpu_custom_call", output_to_operand_aliasing={{}: (4, {})} | custom-call | flops 134217728 | bytes 524288 | tf_op jit(solution)/shard_map/finish/pallas_call | solution.py:171
  107.2 1.4 %finish.13.refs_0_ = bf16[64,16384]{1,0:T(8,128)(2,1)} custom-call(s32[1]{0:T(128)} %bitcast.3.which.source, bf16[64,2048]{1,0:T(8,128)(2,1)S(1)} %collective-permute-done.10.piece_ref, f32[64,128]{1,0:T(8,128)S(1)} %copy-done.3, bf16[8,2,2048]{2,1,0:T(2,128)(2,1)S(1)} %all-to-all-done.1.scaling_ref, ...), custom_call_target="tpu_custom_call", output_to_operand_aliasing={{}: (4, {})} | custom-call | flops 134217728 | bytes 524288 | tf_op jit(solution)/shard_map/finish/pallas_call | solution.py:171
  108.6 1.4 %finish.14.refs_0_ = bf16[64,16384]{1,0:T(8,128)(2,1)} custom-call(s32[1]{0:T(128)} %bitcast.which.source, bf16[64,2048]{1,0:T(8,128)(2,1)S(1)} %collective-permute-done.7.piece_ref, f32[64,128]{1,0:T(8,128)S(1)} %copy-done.3, bf16[8,2,2048]{2,1,0:T(2,128)(2,1)S(1)} %all-to-all-done.1.scaling_ref, ...), custom_call_target="tpu_custom_call", output_to_operand_aliasing={{}: (4, {})} | custom-call | flops 134217728 | bytes 524288 | tf_op jit(solution)/shard_map/finish/pallas_call | solution.py:171
  110.1 1.4 %finish.15 = bf16[64,16384]{1,0:T(8,128)(2,1)} custom-call(s32[1]{0:T(128)} %bitcast.1.which.source, bf16[64,2048]{1,0:T(8,128)(2,1)S(1)} %collective-permute-done.8.piece_ref, f32[64,128]{1,0:T(8,128)S(1)} %copy-done.3, bf16[8,2,2048]{2,1,0:T(2,128)(2,1)S(1)} %all-to-all-done.1.scaling_ref, ...), custom_call_target="tpu_custom_call", output_to_operand_aliasing={{}: (4, {})} | custom-call | flops 134217728 | bytes 524288 | tf_op jit(solution)/shard_map/finish/pallas_call | solution.py:171
  (27 shorter events, 0.1 us)
Async XLA Ops:
  0.7 0.9 copy-start
  1.6 6.5 %copy-start.1 = (bf16[64,1024]{1,0:T(8,128)(2,1)S(1)}, bf16[64,1024]{1,0:T(8,128)(2,1)}, u32[]{:S(2)}) copy-start(bf16[64,1024]{1,0:T(8,128)(2,1)} %rows_ref.15) | copy-start | bytes 393220
  5.1 26.3 %collective-permute-start.2 = (bf16[64,2048]{1,0:T(8,128)(2,1)S(1)}, bf16[64,2048]{1,0:T(8,128)(2,1)S(1)}, u32[]{:S(2)}, u32[]{:S(2)}) collective-permute-start(bf16[64,2048]{1,0:T(8,128)(2,1)S(1)} %product.11), channel_id=1, source_target_pairs={{0,1},{1,0},{2,3},{3,2},{4,5},{5,4},{6,7},{7,6},{8,9},{9,8},{10,11... | collective-permute-start | bytes 786440 | tf_op jit(solution)/shard_map/ppermute | solution.py:219
  11.6 23.0 %collective-permute-start.4 = (bf16[64,2048]{1,0:T(8,128)(2,1)S(1)}, bf16[64,2048]{1,0:T(8,128)(2,1)S(1)}, u32[]{:S(2)}, u32[]{:S(2)}) collective-permute-start(bf16[64,2048]{1,0:T(8,128)(2,1)S(1)} %product.13), channel_id=1, source_target_pairs={{0,1},{1,0},{2,3},{3,2},{4,5},{5,4},{6,7},{7,6},{8,9},{9,8},{10,11... | collective-permute-start | bytes 786440 | tf_op jit(solution)/shard_map/ppermute | solution.py:219
  15.2 21.1 %collective-permute-start = (bf16[64,2048]{1,0:T(8,128)(2,1)S(1)}, bf16[64,2048]{1,0:T(8,128)(2,1)S(1)}, u32[]{:S(2)}, u32[]{:S(2)}) collective-permute-start(bf16[64,2048]{1,0:T(8,128)(2,1)S(1)} %product.9), channel_id=1, source_target_pairs={{0,1},{1,0},{2,3},{3,2},{4,5},{5,4},{6,7},{7,6},{8,9},{9,8},{10,11... | collective-permute-start | bytes 786440 | tf_op jit(solution)/shard_map/ppermute | solution.py:219
  20.8 19.3 %collective-permute-start.6 = (bf16[64,2048]{1,0:T(8,128)(2,1)S(1)}, bf16[64,2048]{1,0:T(8,128)(2,1)S(1)}, u32[]{:S(2)}, u32[]{:S(2)}) collective-permute-start(bf16[64,2048]{1,0:T(8,128)(2,1)S(1)} %product.15), channel_id=1, source_target_pairs={{0,1},{1,0},{2,3},{3,2},{4,5},{5,4},{6,7},{7,6},{8,9},{9,8},{10,11... | collective-permute-start | bytes 786440 | tf_op jit(solution)/shard_map/ppermute | solution.py:219
  31.5 20.8 %collective-permute-start.3 = (bf16[64,2048]{1,0:T(8,128)(2,1)S(1)}, bf16[64,2048]{1,0:T(8,128)(2,1)S(1)}, u32[]{:S(2)}, u32[]{:S(2)}) collective-permute-start(bf16[64,2048]{1,0:T(8,128)(2,1)S(1)} %add_convert_fusion.1), channel_id=1, source_target_pairs={{0,4},{1,5},{2,6},{3,7},{4,0},{5,1},{6,2},{7,3},{8,12},{9,13},{10,... | collective-permute-start | bytes 786440 | tf_op jit(solution)/shard_map/ppermute | solution.py:230
  34.7 17.6 %collective-permute-start.5 = (bf16[64,2048]{1,0:T(8,128)(2,1)S(1)}, bf16[64,2048]{1,0:T(8,128)(2,1)S(1)}, u32[]{:S(2)}, u32[]{:S(2)}) collective-permute-start(bf16[64,2048]{1,0:T(8,128)(2,1)S(1)} %add_convert_fusion), channel_id=1, source_target_pairs={{0,2},{1,3},{2,0},{3,1},{4,6},{5,7},{6,4},{7,5},{8,10},{9,11},{10,... | collective-permute-start | bytes 786440 | tf_op jit(solution)/shard_map/ppermute | solution.py:230
  36.4 15.9 %collective-permute-start.1 = (bf16[64,2048]{1,0:T(8,128)(2,1)S(1)}, bf16[64,2048]{1,0:T(8,128)(2,1)S(1)}, u32[]{:S(2)}, u32[]{:S(2)}) collective-permute-start(bf16[64,2048]{1,0:T(8,128)(2,1)S(1)} %add_convert_fusion.2), channel_id=1, source_target_pairs={{0,6},{1,7},{2,4},{3,5},{4,2},{5,3},{6,0},{7,1},{8,14},{9,15},{10,... | collective-permute-start | bytes 786440 | tf_op jit(solution)/shard_map/ppermute | solution.py:230
  36.5 15.8 %copy-start.4 = (bf16[64,2048]{1,0:T(8,128)(2,1)S(1)}, bf16[64,2048]{1,0:T(8,128)(2,1)}, u32[]{:S(2)}) copy-start(bf16[64,2048]{1,0:T(8,128)(2,1)} %residual_ref.1) | copy-start | bytes 786436
  36.5 25.3 %copy-start.7 = (bf16[2048]{0:T(1024)(128)(2,1)S(1)}, bf16[2048]{0:T(1024)(128)(2,1)}, u32[]{:S(2)}) copy-start(bf16[2048]{0:T(1024)(128)(2,1)} %param.9) | copy-start | bytes 12292
  36.5 25.3 %copy-start.8 = (bf16[2048]{0:T(1024)(128)(2,1)S(1)}, bf16[2048]{0:T(1024)(128)(2,1)}, u32[]{:S(2)}) copy-start(bf16[2048]{0:T(1024)(128)(2,1)} %param.8) | copy-start | bytes 12292
  53.4 17.2 %collective-permute-start.11 = (bf16[64,2048]{1,0:T(8,128)(2,1)}, bf16[64,2048]{1,0:T(8,128)(2,1)S(1)}, u32[]{:S(2)}, u32[]{:S(2)}) collective-permute-start(bf16[64,2048]{1,0:T(8,128)(2,1)} %get-tuple-element.3.piece_ref), channel_id=1, source_target_pairs={{0,2},{1,3},{2,0},{3,1},{4,6},{5,7},{6,4},{7,5},{8,10},{9,11},{10,... | collective-permute-start | bytes 786440 | tf_op jit(solution)/shard_map/ppermute | solution.py:241
  58.4 21.9 %collective-permute-start.9 = (bf16[64,2048]{1,0:T(8,128)(2,1)}, bf16[64,2048]{1,0:T(8,128)(2,1)S(1)}, u32[]{:S(2)}, u32[]{:S(2)}) collective-permute-start(bf16[64,2048]{1,0:T(8,128)(2,1)} %get-tuple-element.3.piece_ref), channel_id=1, source_target_pairs={{0,4},{1,5},{2,6},{3,7},{4,0},{5,1},{6,2},{7,3},{8,12},{9,13},{10,... | collective-permute-start | bytes 786440 | tf_op jit(solution)/shard_map/ppermute | solution.py:241
  60.4 21.5 %collective-permute-start.7 = (bf16[64,2048]{1,0:T(8,128)(2,1)}, bf16[64,2048]{1,0:T(8,128)(2,1)S(1)}, u32[]{:S(2)}, u32[]{:S(2)}) collective-permute-start(bf16[64,2048]{1,0:T(8,128)(2,1)} %get-tuple-element.3.piece_ref), channel_id=1, source_target_pairs={{0,6},{1,7},{2,4},{3,5},{4,2},{5,3},{6,0},{7,1},{8,14},{9,15},{10,... | collective-permute-start | bytes 786440 | tf_op jit(solution)/shard_map/ppermute | solution.py:241
  61.9 39.6 %collective-permute-start.13 = (bf16[64,2048]{1,0:T(8,128)(2,1)}, bf16[64,2048]{1,0:T(8,128)(2,1)S(1)}, u32[]{:S(2)}, u32[]{:S(2)}) collective-permute-start(bf16[64,2048]{1,0:T(8,128)(2,1)} %get-tuple-element.3.piece_ref), channel_id=1, source_target_pairs={{0,1},{1,0},{2,3},{3,2},{4,5},{5,4},{6,7},{7,6},{8,9},{9,8},{10,11... | collective-permute-start | bytes 786440 | tf_op jit(solution)/shard_map/ppermute | solution.py:250
  63.4 22.6 %all-to-all-start = ((f32[8,8,128]{2,1,0:T(8,128)}), f32[8,8,128]{2,1,0:T(8,128)S(1)}, u32[]{:S(2)}, u32[]{:S(2)}) async-start(f32[8,8,128]{2,1,0:T(8,128)} %get-tuple-element.6), calls=%async_computation | async-start | bytes 65536 | tf_op jit(solution)/shard_map/all_to_all | solution.py:243
  70.6 33.7 %collective-permute-start.12 = (bf16[64,2048]{1,0:T(8,128)(2,1)S(1)}, bf16[64,2048]{1,0:T(8,128)(2,1)S(1)}, u32[]{:S(2)}, u32[]{:S(2)}) collective-permute-start(bf16[64,2048]{1,0:T(8,128)(2,1)S(1)} %collective-permute-done.11.piece_ref), channel_id=1, source_target_pairs={{0,1},{1,0},{2,3},{3,2},{4,5},{5,4},{6,7},{7,6},{8,9},{9,8},{10,11... | collective-permute-start | bytes 786440 | tf_op jit(solution)/shard_map/ppermute | solution.py:250
  80.3 26.8 %collective-permute-start.10 = (bf16[64,2048]{1,0:T(8,128)(2,1)S(1)}, bf16[64,2048]{1,0:T(8,128)(2,1)S(1)}, u32[]{:S(2)}, u32[]{:S(2)}) collective-permute-start(bf16[64,2048]{1,0:T(8,128)(2,1)S(1)} %collective-permute-done.9.piece_ref), channel_id=1, source_target_pairs={{0,1},{1,0},{2,3},{3,2},{4,5},{5,4},{6,7},{7,6},{8,9},{9,8},{10,11... | collective-permute-start | bytes 786440 | tf_op jit(solution)/shard_map/ppermute | solution.py:250
  81.8 28.2 %collective-permute-start.8 = (bf16[64,2048]{1,0:T(8,128)(2,1)S(1)}, bf16[64,2048]{1,0:T(8,128)(2,1)S(1)}, u32[]{:S(2)}, u32[]{:S(2)}) collective-permute-start(bf16[64,2048]{1,0:T(8,128)(2,1)S(1)} %collective-permute-done.7.piece_ref), channel_id=1, source_target_pairs={{0,1},{1,0},{2,3},{3,2},{4,5},{5,4},{6,7},{7,6},{8,9},{9,8},{10,11... | collective-permute-start | bytes 786440 | tf_op jit(solution)/shard_map/ppermute | solution.py:250
  86.0 5.4 %copy-start.6 = (f32[8,8,128]{2,1,0:T(8,128)}, f32[8,8,128]{2,1,0:T(8,128)S(1)}, u32[]{:S(2)}) copy-start(f32[8,8,128]{2,1,0:T(8,128)S(1)} %all-to-all-done.stats_ref) | copy-start | bytes 98308
  86.7 11.6 %all-to-all-start.1 = ((bf16[8,2,2048]{2,1,0:T(2,128)(2,1)}), bf16[8,2,2048]{2,1,0:T(2,128)(2,1)S(1)}, u32[]{:S(2)}, u32[]{:S(2)}) async-start(bf16[8,2,2048]{2,1,0:T(2,128)(2,1)} %broadcast_in_dim.2), calls=%async_computation.1 | async-start | bytes 131072 | tf_op jit(solution)/shard_map/all_to_all | solution.py:236
  98.3 0.8 copy-start.2
  99.0 0.9 copy-start.5
  100.0 1.4 %copy-start.3 = (f32[64,128]{1,0:T(8,128)S(1)}, f32[64,128]{1,0:T(8,128)}, u32[]{:S(2)}) copy-start(f32[64,128]{1,0:T(8,128)} %moments.1.moments_ref) | copy-start | bytes 98308

commit v4 on v3

v4 whole, which is shorter than its diff:
```python
import functools
import math

import jax
import jax.numpy as jnp
from jax import lax
from jax.experimental import pallas as pl
from jax.experimental.pallas import tpu as pltpu
from jax.sharding import PartitionSpec as P

BLOCK_LEN = 128
LANES = 128
VMEM_BYTES = 40 * 1024 * 1024


def factors(n):
    inner = 1 << ((n.bit_length() - 1) // 2)
    return n // inner, inner


def tile_width(width, most):
    while width % most:
        most //= 2
    return most


def signs(length):
    rows = lax.broadcasted_iota(jnp.int32, (length, length), 0)
    columns = lax.broadcasted_iota(jnp.int32, (length, length), 1)
    common = jnp.bitwise_and(rows, columns)
    parity = jnp.zeros((length, length), jnp.int32)
    for bit_index in range(length.bit_length() - 1):
        parity = parity + jnp.bitwise_and(jnp.right_shift(common, bit_index), 1)
    return (1 - 2 * jnp.bitwise_and(parity, 1)).astype(jnp.bfloat16)


def product_kernel(targets, splits, local, tile, rows_ref, weight_ref, *refs):
    count = len(targets)
    scratch, semaphores = refs[-2:]
    outs = refs[-2 - count : -2]
    nx, per = splits[1], local // tile
    me = lax.axis_index("tensor")
    outer, inner = me // nx, lax.rem(me, nx)
    copies = []
    for t, (k, j) in enumerate(targets):
        owner = jnp.bitwise_xor(outer, k) * nx + jnp.bitwise_xor(inner, j)
        for i in range(per):
            start = pl.multiple_of(owner * local + i * tile, LANES)
            copy = pltpu.make_async_copy(
                weight_ref.at[:, pl.ds(start, tile)],
                scratch.at[t * per + i],
                semaphores.at[t * per + i],
            )
            copy.start()
            copies.append(copy)
    for t in range(count):
        for i in range(per):
            copies[t * per + i].wait()
            outs[t][:, i * tile : (i + 1) * tile] = jnp.dot(
                rows_ref[...], scratch[t * per + i], preferred_element_type=jnp.float32
            ).astype(outs[t].dtype)


def products(attended, weight, targets, splits, local, after):
    rows, depth = attended.shape
    tile = tile_width(local, 512)
    slots = len(targets) * (local // tile)
    vmem = pl.BlockSpec(memory_space=pltpu.VMEM)
    return pl.pallas_call(
        functools.partial(product_kernel, targets, splits, local, tile),
        out_shape=[
            jax.ShapeDtypeStruct((rows, local), jnp.bfloat16 if j else jnp.float32)
            for _, j in targets
        ],
        in_specs=[vmem] + [pl.BlockSpec(memory_space=pl.ANY)] * (1 + len(after)),
        out_specs=[vmem] * len(targets),
        scratch_shapes=[
            pltpu.VMEM((slots, depth, tile), jnp.bfloat16),
            pltpu.SemaphoreType.DMA((slots,)),
        ],
        compiler_params=pltpu.CompilerParams(vmem_limit_bytes=VMEM_BYTES),
        cost_estimate=pl.CostEstimate(
            flops=2 * rows * depth * local * len(targets),
            bytes_accessed=2 * depth * local * len(targets),
            transcendentals=0,
        ),
        name="products",
    )(attended, weight, *after)


def in_three(values):
    parts = []
    for _ in range(3):
        part = values.astype(jnp.bfloat16)
        parts.append(part.astype(jnp.float32))
        values = values - parts[-1]
    return parts


def stream_kernel(count, residual_ref, gain_ref, bias_ref, *refs):
    terms, (half_ref, shared_ref) = refs[:count], refs[count:]
    stream = residual_ref[...].astype(jnp.float32)
    for term in terms:
        stream = stream + term[...].astype(jnp.float32)
    rows, width = stream.shape
    half_ref[...] = stream.astype(half_ref.dtype)
    mean = jnp.sum(stream, axis=1, keepdims=True) / width
    square = jnp.sum((stream - mean) ** 2, axis=1, keepdims=True)
    lane = lax.broadcasted_iota(jnp.int32, (rows, LANES), 1)
    table = jnp.zeros((rows, LANES), jnp.float32)
    for place, part in enumerate(in_three(mean) + in_three(square)):
        table = jnp.where(lane == place, part, table)
    if rows < LANES:
        table = jnp.concatenate(
            [table, jnp.zeros((LANES - rows, LANES), jnp.float32)], axis=0
        )
    stats = jnp.transpose(table)
    fill = shared_ref.shape[1] - 2 * gain_ref.shape[0]
    shared = jnp.concatenate(
        [stats[:fill], gain_ref[...].astype(jnp.float32), bias_ref[...].astype(jnp.float32)],
        axis=0,
    ).astype(jnp.bfloat16)
    for d in range(shared_ref.shape[0]):
        shared_ref[d] = shared


def own_stream(residual, gain, bias, terms, n):
    rows, local = residual.shape
    blocks = local // LANES
    height = (8 + 2 * blocks + 15) // 16 * 16
    return pl.pallas_call(
        functools.partial(stream_kernel, len(terms)),
        out_shape=(
            jax.ShapeDtypeStruct((rows, local), jnp.bfloat16),
            jax.ShapeDtypeStruct((n, height, LANES), jnp.bfloat16),
        ),
        compiler_params=pltpu.CompilerParams(vmem_limit_bytes=VMEM_BYTES),
        cost_estimate=pl.CostEstimate(
            flops=20 * rows * local, bytes_accessed=16 * rows * local, transcendentals=0
        ),
        name="own_stream",
    )(residual, gain.reshape(blocks, LANES), bias.reshape(blocks, LANES), *terms)


def moments_kernel(local, shared_ref, out_ref):
    n = shared_ref.shape[0]
    rows = out_ref.shape[0]
    means, spread = [], jnp.zeros((1, LANES), jnp.float32)
    for d in range(n):
        stats = shared_ref[d, 0:8].astype(jnp.float32)
        means.append(stats[0:1] + stats[1:2] + stats[2:3])
        spread = spread + (stats[3:4] + stats[4:5] + stats[5:6])
    centre = sum(means) / n
    for mean in means:
        spread = spread + local * ((mean - centre) * (mean - centre))
    inverse = lax.rsqrt(spread / (n * local) + 1e-05)
    row = lax.broadcasted_iota(jnp.int32, (LANES, LANES), 0)
    table = jnp.where(row == 0, centre, jnp.where(row == 1, inverse, 0.0))
    out_ref[...] = jnp.transpose(table)[:rows]


def moments(shared, rows, local):
    return pl.pallas_call(
        functools.partial(moments_kernel, local),
        out_shape=jax.ShapeDtypeStruct((rows, LANES), jnp.float32),
        name="moments",
    )(shared)


def rows_kernel(place, splits, piece_ref, moments_ref, shared_ref, *refs):
    out_ref, done_ref, semaphore = refs[-3:]
    rows, width = piece_ref.shape
    blocks = width // BLOCK_LEN
    table = signs(BLOCK_LEN)
    unit = 1.0 / math.sqrt(BLOCK_LEN)
    me = lax.axis_index("tensor")
    outer, inner = me // splits[1], lax.rem(me, splits[1])
    owner = jnp.bitwise_xor(outer, place[0]) * splits[1] + jnp.bitwise_xor(inner, place[1])
    shared = shared_ref[owner].astype(jnp.float32)
    scaling = shared[shared.shape[0] - 2 * blocks :]
    centre = moments_ref[:, 0:1]
    inverse = moments_ref[:, 1:2]
    normal = []
    for b in range(blocks):
        block = piece_ref[:, b * BLOCK_LEN : (b + 1) * BLOCK_LEN].astype(jnp.float32)
        block = (block - centre) * inverse
        normal.append(block * scaling[b : b + 1] + scaling[blocks + b : blocks + b + 1])
    normal = jnp.concatenate(normal, axis=0)
    first = normal.astype(jnp.bfloat16)
    second = (normal - first.astype(jnp.float32)).astype(jnp.bfloat16)
    coded = jnp.dot(first, table, preferred_element_type=jnp.float32)
    coded = coded + jnp.dot(second, table, preferred_element_type=jnp.float32)
    coded = coded * unit
    largest = jnp.max(jnp.abs(coded), axis=1, keepdims=True)
    scales = (largest / 448.0 + 1e-06).astype(jnp.bfloat16).astype(jnp.float32)
    quanta = (coded * (1.0 / scales)).astype(jnp.bfloat16)
    back = jnp.dot(quanta, table, preferred_element_type=jnp.float32) * (scales * unit)
    back = back.astype(out_ref.dtype)
    for b in range(blocks):
        done_ref[:, b * BLOCK_LEN : (b + 1) * BLOCK_LEN] = back[b * rows : (b + 1) * rows]
    columns = pl.ds(pl.multiple_of(owner * width, LANES), width)
    copy = pltpu.make_async_copy(done_ref, out_ref.at[:, columns], semaphore)
    copy.start()
    copy.wait()


def finish(whole, place, splits, piece, columns, shared):
    rows, local = piece.shape
    n = shared.shape[0]
    earlier = [] if whole is None else [whole]
    vmem = pl.BlockSpec(memory_space=pltpu.VMEM)
    return pl.pallas_call(
        functools.partial(rows_kernel, place, splits),
        out_shape=jax.ShapeDtypeStruct((rows, n * local), jnp.bfloat16),
        in_specs=[vmem] * 3 + [pl.BlockSpec(memory_space=pl.ANY)] * len(earlier),
        out_specs=pl.BlockSpec(memory_space=pl.ANY),
        scratch_shapes=[
            pltpu.VMEM((rows, local), jnp.bfloat16),
            pltpu.SemaphoreType.DMA,
        ],
        input_output_aliases={3: 0} if earlier else {},
        compiler_params=pltpu.CompilerParams(vmem_limit_bytes=VMEM_BYTES),
        cost_estimate=pl.CostEstimate(
            flops=8 * BLOCK_LEN * rows * local,
            bytes_accessed=4 * rows * local,
            transcendentals=0,
        ),
        name="finish",
    )(piece, columns, shared, *earlier)


def body(attended, out_weight, residual, norm_gain, norm_bias):
    n = lax.axis_size("tensor")
    nz, nx = splits = factors(n)
    rows = attended.shape[0]
    local = out_weight.shape[1] // n
    every = [(z, x) for z in range(nz) for x in range(nx)]
    swap = [[(z * nx + x, z * nx + (x ^ j)) for z, x in every] for j in range(nx)]
    jump = [[(z * nx + x, (z ^ k) * nx + x) for z, x in every] for k in range(nz)]
    order = list(range(nz - 1, -1, -1))

    arrived, after = [], []
    sent, before = None, None
    for k in order + [None]:
        targets = [] if k is None else [(k, j) for j in range(1, nx)]
        targets += [] if before is None else [(before, 0)]
        terms = products(attended, out_weight, targets, splits, local, after)
        after = [terms[-1]]
        leaving = [] if k is None else [lax.ppermute(t, "tensor", swap[j + 1]) for j, t in enumerate(terms[: nx - 1])]
        if before:
            kept = terms[-1]
            for piece in sent:
                kept = kept + piece.astype(jnp.float32)
            kept = kept.astype(jnp.bfloat16)
            after = [kept]
            arrived.append(lax.ppermute(kept, "tensor", jump[before]))
        elif before == 0:
            arrived += [terms[-1]] + sent
        sent, before = leaving, k

    stream_out, shared = own_stream(residual, norm_gain, norm_bias, arrived, n)
    near = {k: lax.ppermute(stream_out, "tensor", jump[k]) for k in order[:-1]}
    near[0] = stream_out
    shared = lax.all_to_all(shared, "tensor", 0, 0, tiled=True)
    columns = moments(shared, rows, local)

    whole = None
    for k in [0, 1] + order[:-2]:
        whole = finish(whole, (k, 0), splits, near[k], columns, shared)
        for j in range(1, nx):
            other = lax.ppermute(near[k], "tensor", swap[j])
            whole = finish(whole, (k, j), splits, other, columns, shared)
    return (stream_out, whole)


def solution(mesh):
    placed = (
        P(("groups", "dp"), "tensor"),
        P("tensor", None),
        P(("groups", "dp"), "tensor"),
        P("tensor"),
        P("tensor"),
    )
    return jax.shard_map(
        body,
        mesh=mesh,
        in_specs=placed,
        out_specs=(P(("groups", "dp"), "tensor"), P(("groups", "dp"), None)),
        check_vma=False,
    )
```

time: 112 us -> 93.1 us (0.83)
  starting transfers between devices: 32 us -> 19.8 us
  Pallas kernels: 42 us -> 30.5 us
  blocking collectives: 0 us -> 10.2 us
  waiting for transfers between devices: 33.1 us -> 27.7 us
    pallas_call x16 -> x13, Pallas kernels: 39.4 us -> 27.8 us  [the longest x5 16.6 us: products(): pl.pallas_call(functools.partial(product_kernel, targets, splits, local,...]
    all_to_all x0 -> x1, blocking collectives: none -> 10.2 us  [body(): shared = lax.all_to_all(shared, 'tensor', 0, 0, tiled=True)]
    all_to_all x2 -> x0, waiting for transfers between devices: 9 us -> none  [the longest x1 5.42 us: body(): lax.all_to_all(jnp.broadcast_to(scaling[None], (n,) + scaling.shape), 'te...]
    all_to_all x2 -> x0, starting transfers between devices: 8.36 us -> none  [the longest x1 4.72 us: body(): lax.all_to_all(jnp.broadcast_to(scaling[None], (n,) + scaling.shape), 'te...]
    ppermute x14, starting transfers between devices: 23.6 us -> 19.8 us  [the longest x4 6.77 us: body(): other = lax.ppermute(near[k], 'tensor', swap[j])]
    ppermute x14, waiting for transfers between devices: 24.1 us -> 27.7 us  [the longest x3 14.6 us: body(): near = {k: lax.ppermute(stream_out, 'tensor', jump[k]) for k in order[:-1]}]
  transfers between devices with their start and end apart: 16 -> 14, of which waited for: 5 -> 8; matrix products, arithmetic and copies ran while one was open for 1% -> 0% of each run, Pallas kernels for 32% -> 28%
where the time goes in v4:
time: 93.1 us; the launch traced here: 92.8 us
  Pallas kernels  30.5 us (33%)
  waiting for transfers between devices  27.7 us (30%)
  starting transfers between devices  19.8 us (21%)
  blocking collectives  10.2 us (11%)
  local copies, waits for them, and re-layouts  3.52 us (4%)
    pallas_call x5, Pallas kernels, products(): pl.pallas_call(functools.partial(product_kernel, targets, splits, local,...  16.6 us
    ppermute x3, waiting for transfers between devices, body(): near = {k: lax.ppermute(stream_out, 'tensor', jump[k]) for k in order[:-1]}  14.6 us
    pallas_call x8, Pallas kernels, finish(): pl.pallas_call(functools.partial(rows_kernel, place, splits), out_shape=j...  11.3 us
    all_to_all x1, blocking collectives, body(): shared = lax.all_to_all(shared, 'tensor', 0, 0, tiled=True)  10.2 us
    ppermute x4, starting transfers between devices, body(): other = lax.ppermute(near[k], 'tensor', swap[j])  6.77 us
    ppermute x3, waiting for transfers between devices, body(): arrived.append(lax.ppermute(kept, 'tensor', jump[before]))  6.74 us
    ppermute x4, waiting for transfers between devices, body(): lax.ppermute(t, 'tensor', swap[j + 1])  6.41 us
    ppermute x4, starting transfers between devices, body(): lax.ppermute(t, 'tensor', swap[j + 1])  5.46 us
  transfers between devices with their start and end apart: 14, of which 8 were waited for; matrix products, arithmetic and copies ran while one was open for 0% of the time, Pallas kernels for 28%

profile of v4, /device:TPU:0, one launch (start us, length us, event | category | flops | bytes accessed | tf_op | source)
XLA Modules:
  0.0 92.8 jit_solution(772559260769995793)
XLA Ops:
  0.6 0.9 copy-done.2
  1.5 2.5 %products.5.refs_0_ = bf16[64,2048]{1,0:T(8,128)(2,1)S(1)} custom-call(bf16[64,1024]{1,0:T(8,128)(2,1)S(1)} %copy-done.2, bf16[1024,16384]{1,0:T(8,128)(2,1)} %weight_ref.9), custom_call_target="tpu_custom_call" | custom-call | flops 268435456 | bytes 4194304 | tf_op jit(solution)/shard_map/products/pallas_call | solution.py:69
  4.1 3.0 %collective-permute-start = (bf16[64,2048]{1,0:T(8,128)(2,1)S(1)}, bf16[64,2048]{1,0:T(8,128)(2,1)S(1)}, u32[]{:S(2)}, u32[]{:S(2)}) collective-permute-start(bf16[64,2048]{1,0:T(8,128)(2,1)S(1)} %products.5.refs_0_), channel_id=1, source_target_pairs={{0,1},{1,0},{2,3},{3,2},{4,5},{5,4},{6,7},{7,6},{8,9},{9,8},{10,11... | collective-permute-start | bytes 786440 | tf_op jit(solution)/shard_map/ppermute | solution.py:249
  7.1 3.8 %products.6 = (bf16[64,2048]{1,0:T(8,128)(2,1)S(1)}, f32[64,2048]{1,0:T(8,128)S(1)}) custom-call(bf16[64,1024]{1,0:T(8,128)(2,1)S(1)} %copy-done.2, bf16[1024,16384]{1,0:T(8,128)(2,1)} %weight_ref.9, bf16[64,2048]{1,0:T(8,128)(2,1)S(1)} %products.5.refs_0_), custom_call_target="tpu_custom_call" | custom-call | flops 536870912 | bytes 8388608 | tf_op jit(solution)/shard_map/products/pallas_call | solution.py:69
  10.9 0.1 collective-permute-start.2
  11.0 2.8 %collective-permute-done = bf16[64,2048]{1,0:T(8,128)(2,1)S(1)} collective-permute-done((bf16[64,2048]{1,0:T(8,128)(2,1)S(1)}, bf16[64,2048]{1,0:T(8,128)(2,1)S(1)}, u32[]{:S(2)}, u32[]{:S(2)}) %collective-permute-start) | collective-permute-done | bytes 262176 | tf_op jit(solution)/shard_map/ppermute | solution.py:249
  13.8 3.9 %collective-permute-start.1 = (bf16[64,2048]{1,0:T(8,128)(2,1)S(1)}, bf16[64,2048]{1,0:T(8,128)(2,1)S(1)}, u32[]{:S(2)}, u32[]{:S(2)}) collective-permute-start(bf16[64,2048]{1,0:T(8,128)(2,1)S(1)} %add_convert_fusion.2.refs_0_), channel_id=1, source_target_pairs={{0,6},{1,7},{2,4},{3,5},{4,2},{5,3},{6,0},{7,1},{8,14},{9,15},{10,... | collective-permute-start | bytes 786440 | tf_op jit(solution)/shard_map/ppermute | solution.py:256
  17.8 3.8 %products.7 = (bf16[64,2048]{1,0:T(8,128)(2,1)S(1)}, f32[64,2048]{1,0:T(8,128)S(1)}) custom-call(bf16[64,1024]{1,0:T(8,128)(2,1)S(1)} %copy-done.2, bf16[1024,16384]{1,0:T(8,128)(2,1)} %weight_ref.9, bf16[64,2048]{1,0:T(8,128)(2,1)S(1)} %add_convert_fusion.2.refs_0_), custom_call_target="tpu_custom_call" | custom-call | flops 536870912 | bytes 8388608 | tf_op jit(solution)/shard_map/products/pallas_call | solution.py:69
  21.6 2.3 %collective-permute-start.4 = (bf16[64,2048]{1,0:T(8,128)(2,1)S(1)}, bf16[64,2048]{1,0:T(8,128)(2,1)S(1)}, u32[]{:S(2)}, u32[]{:S(2)}) collective-permute-start(bf16[64,2048]{1,0:T(8,128)(2,1)S(1)} %get-tuple-element.14), channel_id=1, source_target_pairs={{0,1},{1,0},{2,3},{3,2},{4,5},{5,4},{6,7},{7,6},{8,9},{9,8},{10,11... | collective-permute-start | bytes 786440 | tf_op jit(solution)/shard_map/ppermute | solution.py:249
  23.9 0.0 collective-permute-done.2
  23.9 0.1 collective-permute-start.3
  24.0 3.8 %products.8 = (bf16[64,2048]{1,0:T(8,128)(2,1)S(1)}, f32[64,2048]{1,0:T(8,128)S(1)}) custom-call(bf16[64,1024]{1,0:T(8,128)(2,1)S(1)} %copy-done.2, bf16[1024,16384]{1,0:T(8,128)(2,1)} %weight_ref.9, bf16[64,2048]{1,0:T(8,128)(2,1)S(1)} %add_convert_fusion.1.refs_0_), custom_call_target="tpu_custom_call" | custom-call | flops 536870912 | bytes 8388608 | tf_op jit(solution)/shard_map/products/pallas_call | solution.py:69
  27.9 0.1 collective-permute-start.6
  28.0 1.4 %collective-permute-done.4 = bf16[64,2048]{1,0:T(8,128)(2,1)S(1)} collective-permute-done((bf16[64,2048]{1,0:T(8,128)(2,1)S(1)}, bf16[64,2048]{1,0:T(8,128)(2,1)S(1)}, u32[]{:S(2)}, u32[]{:S(2)}) %collective-permute-start.4) | collective-permute-done | bytes 262176 | tf_op jit(solution)/shard_map/ppermute | solution.py:249
  29.4 0.0 copy-start.5
  29.5 0.0 copy-start.7
  29.5 0.0 copy-start.8
  29.5 0.1 collective-permute-start.5
  29.6 2.5 %products.9.refs_3_ = f32[64,2048]{1,0:T(8,128)S(1)} custom-call(bf16[64,1024]{1,0:T(8,128)(2,1)S(1)} %copy-done.2, bf16[1024,16384]{1,0:T(8,128)(2,1)} %weight_ref.9, bf16[64,2048]{1,0:T(8,128)(2,1)S(1)} %add_convert_fusion.refs_0_), custom_call_target="tpu_custom_call" | custom-call | flops 268435456 | bytes 4194304 | tf_op jit(solution)/shard_map/products/pallas_call | solution.py:69
  32.1 2.2 %collective-permute-done.6.refs_4_ = bf16[64,2048]{1,0:T(8,128)(2,1)S(1)} collective-permute-done((bf16[64,2048]{1,0:T(8,128)(2,1)S(1)}, bf16[64,2048]{1,0:T(8,128)(2,1)S(1)}, u32[]{:S(2)}, u32[]{:S(2)}) %collective-permute-start.6) | collective-permute-done | bytes 262176 | tf_op jit(solution)/shard_map/ppermute | solution.py:249
  34.3 4.6 %collective-permute-done.3.refs_1_ = bf16[64,2048]{1,0:T(8,128)(2,1)S(1)} collective-permute-done((bf16[64,2048]{1,0:T(8,128)(2,1)S(1)}, bf16[64,2048]{1,0:T(8,128)(2,1)S(1)}, u32[]{:S(2)}, u32[]{:S(2)}) %collective-permute-start.3) | collective-permute-done | bytes 262176 | tf_op jit(solution)/shard_map/ppermute | solution.py:256
  38.9 0.0 collective-permute-done.1.refs_0_
  38.9 2.2 %collective-permute-done.5.refs_2_ = bf16[64,2048]{1,0:T(8,128)(2,1)S(1)} collective-permute-done((bf16[64,2048]{1,0:T(8,128)(2,1)S(1)}, bf16[64,2048]{1,0:T(8,128)(2,1)S(1)}, u32[]{:S(2)}, u32[]{:S(2)}) %collective-permute-start.5) | collective-permute-done | bytes 262176 | tf_op jit(solution)/shard_map/ppermute | solution.py:256
  41.1 1.0 %own_stream.1 = (bf16[64,2048]{1,0:T(8,128)(2,1)}, bf16[8,48,128]{2,1,0:T(8,128)(2,1)S(1)}) custom-call(bf16[64,2048]{1,0:T(8,128)(2,1)S(1)} %copy-done.5, bf16[16,128]{1,0:T(8,128)(2,1)S(1)} %bitcast.2, bf16[16,128]{1,0:T(8,128)(2,1)S(1)} %bitcast.3, bf16[64,2048]{1,0:T(8,128)(2,1)S(1)} %collective-permute-done.1.refs_0_, ...), custom_call_target="tpu_custom_call" | custom-call | flops 2621440 | bytes 2097152 | tf_op jit(solution)/shard_map/own_stream/pallas_call | solution.py:131
  42.1 0.0 collective-permute-start.11
  42.1 1.2 %collective-permute-start.9 = (bf16[64,2048]{1,0:T(8,128)(2,1)}, bf16[64,2048]{1,0:T(8,128)(2,1)S(1)}, u32[]{:S(2)}, u32[]{:S(2)}) collective-permute-start(bf16[64,2048]{1,0:T(8,128)(2,1)} %get-tuple-element.8.piece_ref), channel_id=1, source_target_pairs={{0,6},{1,7},{2,4},{3,5},{4,2},{5,3},{6,0},{7,1},{8,14},{9,15},{10,... | collective-permute-start | bytes 786440 | tf_op jit(solution)/shard_map/ppermute | solution.py:262
  43.3 2.3 %collective-permute-start.7 = (bf16[64,2048]{1,0:T(8,128)(2,1)}, bf16[64,2048]{1,0:T(8,128)(2,1)S(1)}, u32[]{:S(2)}, u32[]{:S(2)}) collective-permute-start(bf16[64,2048]{1,0:T(8,128)(2,1)} %get-tuple-element.8.piece_ref), channel_id=1, source_target_pairs={{0,4},{1,5},{2,6},{3,7},{4,0},{5,1},{6,2},{7,3},{8,12},{9,13},{10,... | collective-permute-start | bytes 786440 | tf_op jit(solution)/shard_map/ppermute | solution.py:262
  45.6 2.0 %collective-permute-start.13 = (bf16[64,2048]{1,0:T(8,128)(2,1)}, bf16[64,2048]{1,0:T(8,128)(2,1)S(1)}, u32[]{:S(2)}, u32[]{:S(2)}) collective-permute-start(bf16[64,2048]{1,0:T(8,128)(2,1)} %get-tuple-element.8.piece_ref), channel_id=1, source_target_pairs={{0,1},{1,0},{2,3},{3,2},{4,5},{5,4},{6,7},{7,6},{8,9},{9,8},{10,11... | collective-permute-start | bytes 786440 | tf_op jit(solution)/shard_map/ppermute | solution.py:271
  47.6 3.3 %collective-permute-done.11.piece_ref = bf16[64,2048]{1,0:T(8,128)(2,1)S(1)} collective-permute-done((bf16[64,2048]{1,0:T(8,128)(2,1)}, bf16[64,2048]{1,0:T(8,128)(2,1)S(1)}, u32[]{:S(2)}, u32[]{:S(2)}) %collective-permute-start.11) | collective-permute-done | bytes 262176 | tf_op jit(solution)/shard_map/ppermute | solution.py:262
  50.8 1.7 %collective-permute-start.12 = (bf16[64,2048]{1,0:T(8,128)(2,1)S(1)}, bf16[64,2048]{1,0:T(8,128)(2,1)S(1)}, u32[]{:S(2)}, u32[]{:S(2)}) collective-permute-start(bf16[64,2048]{1,0:T(8,128)(2,1)S(1)} %collective-permute-done.11.piece_ref), channel_id=1, source_target_pairs={{0,1},{1,0},{2,3},{3,2},{4,5},{5,4},{6,7},{7,6},{8,9},{9,8},{10,11... | collective-permute-start | bytes 786440 | tf_op jit(solution)/shard_map/ppermute | solution.py:271
  52.6 2.9 %collective-permute-done.9.piece_ref = bf16[64,2048]{1,0:T(8,128)(2,1)S(1)} collective-permute-done((bf16[64,2048]{1,0:T(8,128)(2,1)}, bf16[64,2048]{1,0:T(8,128)(2,1)S(1)}, u32[]{:S(2)}, u32[]{:S(2)}) %collective-permute-start.9) | collective-permute-done | bytes 262176 | tf_op jit(solution)/shard_map/ppermute | solution.py:262
  55.5 1.5 %collective-permute-start.10 = (bf16[64,2048]{1,0:T(8,128)(2,1)S(1)}, bf16[64,2048]{1,0:T(8,128)(2,1)S(1)}, u32[]{:S(2)}, u32[]{:S(2)}) collective-permute-start(bf16[64,2048]{1,0:T(8,128)(2,1)S(1)} %collective-permute-done.9.piece_ref), channel_id=1, source_target_pairs={{0,1},{1,0},{2,3},{3,2},{4,5},{5,4},{6,7},{7,6},{8,9},{9,8},{10,11... | collective-permute-start | bytes 786440 | tf_op jit(solution)/shard_map/ppermute | solution.py:271
  57.0 8.4 %collective-permute-done.7.piece_ref = bf16[64,2048]{1,0:T(8,128)(2,1)S(1)} collective-permute-done((bf16[64,2048]{1,0:T(8,128)(2,1)}, bf16[64,2048]{1,0:T(8,128)(2,1)S(1)}, u32[]{:S(2)}, u32[]{:S(2)}) %collective-permute-start.7) | collective-permute-done | bytes 262176 | tf_op jit(solution)/shard_map/ppermute | solution.py:262
  65.4 1.5 %collective-permute-start.8 = (bf16[64,2048]{1,0:T(8,128)(2,1)S(1)}, bf16[64,2048]{1,0:T(8,128)(2,1)S(1)}, u32[]{:S(2)}, u32[]{:S(2)}) collective-permute-start(bf16[64,2048]{1,0:T(8,128)(2,1)S(1)} %collective-permute-done.7.piece_ref), channel_id=1, source_target_pairs={{0,1},{1,0},{2,3},{3,2},{4,5},{5,4},{6,7},{7,6},{8,9},{9,8},{10,11... | collective-permute-start | bytes 786440 | tf_op jit(solution)/shard_map/ppermute | solution.py:271
  66.9 10.2 %all_to_all.5.shared_ref = bf16[8,48,128]{2,1,0:T(8,128)(2,1)} all-to-all(bf16[8,48,128]{2,1,0:T(8,128)(2,1)S(1)} %get-tuple-element.17), channel_id=1, replica_groups=mesh['groups'=2,'dp'=2,'tensor'=8] {'tensor'}, dimensions={0} | all-to-all | bytes 196608 | tf_op jit(solution)/shard_map/all_to_all | solution.py:264
  77.1 1.7 %moments.1.moments_ref = f32[64,128]{1,0:T(8,128)} custom-call(bf16[8,48,128]{2,1,0:T(8,128)(2,1)} %all_to_all.5.shared_ref), custom_call_target="tpu_custom_call" | custom-call | tf_op jit(solution)/shard_map/moments/pallas_call | solution.py:163
  78.8 0.9 copy-done
  79.7 0.8 copy-done.3
  80.5 0.9 %copy-done.6 = bf16[64,2048]{1,0:T(8,128)(2,1)S(1)} copy-done((bf16[64,2048]{1,0:T(8,128)(2,1)S(1)}, bf16[64,2048]{1,0:T(8,128)(2,1)}, u32[]{:S(2)}) %copy-start.6) | copy-done | bytes 262168
  81.4 1.4 %finish.8.refs_0_ = bf16[64,16384]{1,0:T(8,128)(2,1)} custom-call(bf16[64,2048]{1,0:T(8,128)(2,1)S(1)} %copy-done.6, f32[64,128]{1,0:T(8,128)S(1)} %copy-done.3, bf16[8,48,128]{2,1,0:T(8,128)(2,1)S(1)} %copy-done), custom_call_target="tpu_custom_call" | custom-call | flops 134217728 | bytes 524288 | tf_op jit(solution)/shard_map/finish/pallas_call | solution.py:212
  82.8 0.0 collective-permute-done.13.piece_ref
  82.9 1.4 %finish.9.refs_0_ = bf16[64,16384]{1,0:T(8,128)(2,1)} custom-call(bf16[64,2048]{1,0:T(8,128)(2,1)S(1)} %collective-permute-done.13.piece_ref, f32[64,128]{1,0:T(8,128)S(1)} %copy-done.4, bf16[8,48,128]{2,1,0:T(8,128)(2,1)S(1)} %copy-done.1, bf16[64,16384]{1,0:T(8,128)(2,1)} %finish.8.refs_0_), custom_call_target="tpu_custom_call", output_to_operand_aliasing={{}: (3, {})} | custom-call | flops 134217728 | bytes 524288 | tf_op jit(solution)/shard_map/finish/pallas_call | solution.py:212
  84.3 1.4 %finish.10.refs_0_ = bf16[64,16384]{1,0:T(8,128)(2,1)} custom-call(bf16[64,2048]{1,0:T(8,128)(2,1)S(1)} %collective-permute-done.11.piece_ref, f32[64,128]{1,0:T(8,128)S(1)} %copy-done.4, bf16[8,48,128]{2,1,0:T(8,128)(2,1)S(1)} %copy-done.1, bf16[64,16384]{1,0:T(8,128)(2,1)} %finish.9.refs_0_), custom_call_target="tpu_custom_call", output_to_operand_aliasing={{}: (3, {})} | custom-call | flops 134217728 | bytes 524288 | tf_op jit(solution)/shard_map/finish/pallas_call | solution.py:212
  85.7 1.4 %finish.11.refs_0_ = bf16[64,16384]{1,0:T(8,128)(2,1)} custom-call(bf16[64,2048]{1,0:T(8,128)(2,1)S(1)} %collective-permute-done.12.piece_ref, f32[64,128]{1,0:T(8,128)S(1)} %copy-done.4, bf16[8,48,128]{2,1,0:T(8,128)(2,1)S(1)} %copy-done.1, bf16[64,16384]{1,0:T(8,128)(2,1)} %finish.10.refs_0_), custom_call_target="tpu_custom_call", output_to_operand_aliasing={{}: (3, {})} | custom-call | flops 134217728 | bytes 524288 | tf_op jit(solution)/shard_map/finish/pallas_call | solution.py:212
  87.1 1.4 %finish.12.refs_0_ = bf16[64,16384]{1,0:T(8,128)(2,1)} custom-call(bf16[64,2048]{1,0:T(8,128)(2,1)S(1)} %collective-permute-done.9.piece_ref, f32[64,128]{1,0:T(8,128)S(1)} %copy-done.4, bf16[8,48,128]{2,1,0:T(8,128)(2,1)S(1)} %copy-done.1, bf16[64,16384]{1,0:T(8,128)(2,1)} %finish.11.refs_0_), custom_call_target="tpu_custom_call", output_to_operand_aliasing={{}: (3, {})} | custom-call | flops 134217728 | bytes 524288 | tf_op jit(solution)/shard_map/finish/pallas_call | solution.py:212
  88.5 1.4 %finish.13.refs_0_ = bf16[64,16384]{1,0:T(8,128)(2,1)} custom-call(bf16[64,2048]{1,0:T(8,128)(2,1)S(1)} %collective-permute-done.10.piece_ref, f32[64,128]{1,0:T(8,128)S(1)} %copy-done.4, bf16[8,48,128]{2,1,0:T(8,128)(2,1)S(1)} %copy-done.1, bf16[64,16384]{1,0:T(8,128)(2,1)} %finish.12.refs_0_), custom_call_target="tpu_custom_call", output_to_operand_aliasing={{}: (3, {})} | custom-call | flops 134217728 | bytes 524288 | tf_op jit(solution)/shard_map/finish/pallas_call | solution.py:212
  90.0 1.4 %finish.14.refs_0_ = bf16[64,16384]{1,0:T(8,128)(2,1)} custom-call(bf16[64,2048]{1,0:T(8,128)(2,1)S(1)} %collective-permute-done.7.piece_ref, f32[64,128]{1,0:T(8,128)S(1)} %copy-done.4, bf16[8,48,128]{2,1,0:T(8,128)(2,1)S(1)} %copy-done.1, bf16[64,16384]{1,0:T(8,128)(2,1)} %finish.13.refs_0_), custom_call_target="tpu_custom_call", output_to_operand_aliasing={{}: (3, {})} | custom-call | flops 134217728 | bytes 524288 | tf_op jit(solution)/shard_map/finish/pallas_call | solution.py:212
  91.4 1.4 %finish.15 = bf16[64,16384]{1,0:T(8,128)(2,1)} custom-call(bf16[64,2048]{1,0:T(8,128)(2,1)S(1)} %collective-permute-done.8.piece_ref, f32[64,128]{1,0:T(8,128)S(1)} %copy-done.4, bf16[8,48,128]{2,1,0:T(8,128)(2,1)S(1)} %copy-done.1, bf16[64,16384]{1,0:T(8,128)(2,1)} %finish.14.refs_0_), custom_call_target="tpu_custom_call", output_to_operand_aliasing={{}: (3, {})} | custom-call | flops 134217728 | bytes 524288 | tf_op jit(solution)/shard_map/finish/pallas_call | solution.py:212
  (17 shorter events, 0.2 us)
Async XLA Ops:
  0.6 0.9 copy-start.2
  4.1 9.7 %collective-permute-start = (bf16[64,2048]{1,0:T(8,128)(2,1)S(1)}, bf16[64,2048]{1,0:T(8,128)(2,1)S(1)}, u32[]{:S(2)}, u32[]{:S(2)}) collective-permute-start(bf16[64,2048]{1,0:T(8,128)(2,1)S(1)} %products.5.refs_0_), channel_id=1, source_target_pairs={{0,1},{1,0},{2,3},{3,2},{4,5},{5,4},{6,7},{7,6},{8,9},{9,8},{10,11... | collective-permute-start | bytes 786440 | tf_op jit(solution)/shard_map/ppermute | solution.py:249
  10.9 13.0 %collective-permute-start.2 = (bf16[64,2048]{1,0:T(8,128)(2,1)S(1)}, bf16[64,2048]{1,0:T(8,128)(2,1)S(1)}, u32[]{:S(2)}, u32[]{:S(2)}) collective-permute-start(bf16[64,2048]{1,0:T(8,128)(2,1)S(1)} %get-tuple-element.12), channel_id=1, source_target_pairs={{0,1},{1,0},{2,3},{3,2},{4,5},{5,4},{6,7},{7,6},{8,9},{9,8},{10,11... | collective-permute-start | bytes 786440 | tf_op jit(solution)/shard_map/ppermute | solution.py:249
  13.8 25.1 %collective-permute-start.1 = (bf16[64,2048]{1,0:T(8,128)(2,1)S(1)}, bf16[64,2048]{1,0:T(8,128)(2,1)S(1)}, u32[]{:S(2)}, u32[]{:S(2)}) collective-permute-start(bf16[64,2048]{1,0:T(8,128)(2,1)S(1)} %add_convert_fusion.2.refs_0_), channel_id=1, source_target_pairs={{0,6},{1,7},{2,4},{3,5},{4,2},{5,3},{6,0},{7,1},{8,14},{9,15},{10,... | collective-permute-start | bytes 786440 | tf_op jit(solution)/shard_map/ppermute | solution.py:256
  21.6 7.8 %collective-permute-start.4 = (bf16[64,2048]{1,0:T(8,128)(2,1)S(1)}, bf16[64,2048]{1,0:T(8,128)(2,1)S(1)}, u32[]{:S(2)}, u32[]{:S(2)}) collective-permute-start(bf16[64,2048]{1,0:T(8,128)(2,1)S(1)} %get-tuple-element.14), channel_id=1, source_target_pairs={{0,1},{1,0},{2,3},{3,2},{4,5},{5,4},{6,7},{7,6},{8,9},{9,8},{10,11... | collective-permute-start | bytes 786440 | tf_op jit(solution)/shard_map/ppermute | solution.py:249
  23.9 15.0 %collective-permute-start.3 = (bf16[64,2048]{1,0:T(8,128)(2,1)S(1)}, bf16[64,2048]{1,0:T(8,128)(2,1)S(1)}, u32[]{:S(2)}, u32[]{:S(2)}) collective-permute-start(bf16[64,2048]{1,0:T(8,128)(2,1)S(1)} %add_convert_fusion.1.refs_0_), channel_id=1, source_target_pairs={{0,4},{1,5},{2,6},{3,7},{4,0},{5,1},{6,2},{7,3},{8,12},{9,13},{10,... | collective-permute-start | bytes 786440 | tf_op jit(solution)/shard_map/ppermute | solution.py:256
  27.9 6.4 %collective-permute-start.6 = (bf16[64,2048]{1,0:T(8,128)(2,1)S(1)}, bf16[64,2048]{1,0:T(8,128)(2,1)S(1)}, u32[]{:S(2)}, u32[]{:S(2)}) collective-permute-start(bf16[64,2048]{1,0:T(8,128)(2,1)S(1)} %get-tuple-element.15), channel_id=1, source_target_pairs={{0,1},{1,0},{2,3},{3,2},{4,5},{5,4},{6,7},{7,6},{8,9},{9,8},{10,11... | collective-permute-start | bytes 786440 | tf_op jit(solution)/shard_map/ppermute | solution.py:249
  29.4 11.6 %copy-start.5 = (bf16[64,2048]{1,0:T(8,128)(2,1)S(1)}, bf16[64,2048]{1,0:T(8,128)(2,1)}, u32[]{:S(2)}) copy-start(bf16[64,2048]{1,0:T(8,128)(2,1)} %residual_ref.1) | copy-start | bytes 786436
  29.5 11.6 %copy-start.7 = (bf16[2048]{0:T(1024)(128)(2,1)S(1)}, bf16[2048]{0:T(1024)(128)(2,1)}, u32[]{:S(2)}) copy-start(bf16[2048]{0:T(1024)(128)(2,1)} %param.8) | copy-start | bytes 12292
  29.5 11.6 %copy-start.8 = (bf16[2048]{0:T(1024)(128)(2,1)S(1)}, bf16[2048]{0:T(1024)(128)(2,1)}, u32[]{:S(2)}) copy-start(bf16[2048]{0:T(1024)(128)(2,1)} %param.9) | copy-start | bytes 12292
  29.5 11.6 %collective-permute-start.5 = (bf16[64,2048]{1,0:T(8,128)(2,1)S(1)}, bf16[64,2048]{1,0:T(8,128)(2,1)S(1)}, u32[]{:S(2)}, u32[]{:S(2)}) collective-permute-start(bf16[64,2048]{1,0:T(8,128)(2,1)S(1)} %add_convert_fusion.refs_0_), channel_id=1, source_target_pairs={{0,2},{1,3},{2,0},{3,1},{4,6},{5,7},{6,4},{7,5},{8,10},{9,11},{10,... | collective-permute-start | bytes 786440 | tf_op jit(solution)/shard_map/ppermute | solution.py:256
  42.1 8.7 %collective-permute-start.11 = (bf16[64,2048]{1,0:T(8,128)(2,1)}, bf16[64,2048]{1,0:T(8,128)(2,1)S(1)}, u32[]{:S(2)}, u32[]{:S(2)}) collective-permute-start(bf16[64,2048]{1,0:T(8,128)(2,1)} %get-tuple-element.8.piece_ref), channel_id=1, source_target_pairs={{0,2},{1,3},{2,0},{3,1},{4,6},{5,7},{6,4},{7,5},{8,10},{9,11},{10,... | collective-permute-start | bytes 786440 | tf_op jit(solution)/shard_map/ppermute | solution.py:262
  42.1 13.4 %collective-permute-start.9 = (bf16[64,2048]{1,0:T(8,128)(2,1)}, bf16[64,2048]{1,0:T(8,128)(2,1)S(1)}, u32[]{:S(2)}, u32[]{:S(2)}) collective-permute-start(bf16[64,2048]{1,0:T(8,128)(2,1)} %get-tuple-element.8.piece_ref), channel_id=1, source_target_pairs={{0,6},{1,7},{2,4},{3,5},{4,2},{5,3},{6,0},{7,1},{8,14},{9,15},{10,... | collective-permute-start | bytes 786440 | tf_op jit(solution)/shard_map/ppermute | solution.py:262
  43.3 22.2 %collective-permute-start.7 = (bf16[64,2048]{1,0:T(8,128)(2,1)}, bf16[64,2048]{1,0:T(8,128)(2,1)S(1)}, u32[]{:S(2)}, u32[]{:S(2)}) collective-permute-start(bf16[64,2048]{1,0:T(8,128)(2,1)} %get-tuple-element.8.piece_ref), channel_id=1, source_target_pairs={{0,4},{1,5},{2,6},{3,7},{4,0},{5,1},{6,2},{7,3},{8,12},{9,13},{10,... | collective-permute-start | bytes 786440 | tf_op jit(solution)/shard_map/ppermute | solution.py:262
  45.6 37.2 %collective-permute-start.13 = (bf16[64,2048]{1,0:T(8,128)(2,1)}, bf16[64,2048]{1,0:T(8,128)(2,1)S(1)}, u32[]{:S(2)}, u32[]{:S(2)}) collective-permute-start(bf16[64,2048]{1,0:T(8,128)(2,1)} %get-tuple-element.8.piece_ref), channel_id=1, source_target_pairs={{0,1},{1,0},{2,3},{3,2},{4,5},{5,4},{6,7},{7,6},{8,9},{9,8},{10,11... | collective-permute-start | bytes 786440 | tf_op jit(solution)/shard_map/ppermute | solution.py:271
  50.8 34.8 %collective-permute-start.12 = (bf16[64,2048]{1,0:T(8,128)(2,1)S(1)}, bf16[64,2048]{1,0:T(8,128)(2,1)S(1)}, u32[]{:S(2)}, u32[]{:S(2)}) collective-permute-start(bf16[64,2048]{1,0:T(8,128)(2,1)S(1)} %collective-permute-done.11.piece_ref), channel_id=1, source_target_pairs={{0,1},{1,0},{2,3},{3,2},{4,5},{5,4},{6,7},{7,6},{8,9},{9,8},{10,11... | collective-permute-start | bytes 786440 | tf_op jit(solution)/shard_map/ppermute | solution.py:271
  55.5 33.0 %collective-permute-start.10 = (bf16[64,2048]{1,0:T(8,128)(2,1)S(1)}, bf16[64,2048]{1,0:T(8,128)(2,1)S(1)}, u32[]{:S(2)}, u32[]{:S(2)}) collective-permute-start(bf16[64,2048]{1,0:T(8,128)(2,1)S(1)} %collective-permute-done.9.piece_ref), channel_id=1, source_target_pairs={{0,1},{1,0},{2,3},{3,2},{4,5},{5,4},{6,7},{7,6},{8,9},{9,8},{10,11... | collective-permute-start | bytes 786440 | tf_op jit(solution)/shard_map/ppermute | solution.py:271
  65.4 25.9 %collective-permute-start.8 = (bf16[64,2048]{1,0:T(8,128)(2,1)S(1)}, bf16[64,2048]{1,0:T(8,128)(2,1)S(1)}, u32[]{:S(2)}, u32[]{:S(2)}) collective-permute-start(bf16[64,2048]{1,0:T(8,128)(2,1)S(1)} %collective-permute-done.7.piece_ref), channel_id=1, source_target_pairs={{0,1},{1,0},{2,3},{3,2},{4,5},{5,4},{6,7},{7,6},{8,9},{9,8},{10,11... | collective-permute-start | bytes 786440 | tf_op jit(solution)/shard_map/ppermute | solution.py:271
  77.1 5.7 %copy-start.1 = (bf16[8,48,128]{2,1,0:T(8,128)(2,1)S(1)}, bf16[8,48,128]{2,1,0:T(8,128)(2,1)}, u32[]{:S(2)}) copy-start(bf16[8,48,128]{2,1,0:T(8,128)(2,1)} %all_to_all.5.shared_ref) | copy-start | bytes 294916
  78.8 0.9 copy-start
  79.7 0.8 copy-start.3
  80.5 0.9 %copy-start.6 = (bf16[64,2048]{1,0:T(8,128)(2,1)S(1)}, bf16[64,2048]{1,0:T(8,128)(2,1)}, u32[]{:S(2)}) copy-start(bf16[64,2048]{1,0:T(8,128)(2,1)} %get-tuple-element.8.piece_ref) | copy-start | bytes 786436
  81.4 1.4 %copy-start.4 = (f32[64,128]{1,0:T(8,128)S(1)}, f32[64,128]{1,0:T(8,128)}, u32[]{:S(2)}) copy-start(f32[64,128]{1,0:T(8,128)} %moments.1.moments_ref) | copy-start | bytes 98308

commit v5 on v4

--- a/solution.py
+++ b/solution.py
@@ -36,11 +36,13 @@
 
 def product_kernel(targets, splits, local, tile, rows_ref, weight_ref, *refs):
     count = len(targets)
-    scratch, semaphores = refs[-2:]
-    outs = refs[-2 - count : -2]
+    held, scratch, semaphores = refs[-3:]
+    outs = refs[-3 - count : -3]
     nx, per = splits[1], local // tile
     me = lax.axis_index("tensor")
     outer, inner = me // nx, lax.rem(me, nx)
+    first = pltpu.make_async_copy(rows_ref, held, semaphores.at[count * per])
+    first.start()
     copies = []
     for t, (k, j) in enumerate(targets):
         owner = jnp.bitwise_xor(outer, k) * nx + jnp.bitwise_xor(inner, j)
@@ -53,11 +55,12 @@
             )
             copy.start()
             copies.append(copy)
+    first.wait()
     for t in range(count):
         for i in range(per):
             copies[t * per + i].wait()
             outs[t][:, i * tile : (i + 1) * tile] = jnp.dot(
-                rows_ref[...], scratch[t * per + i], preferred_element_type=jnp.float32
+                held[...], scratch[t * per + i], preferred_element_type=jnp.float32
             ).astype(outs[t].dtype)
 
 
@@ -72,11 +75,13 @@
             jax.ShapeDtypeStruct((rows, local), jnp.bfloat16 if j else jnp.float32)
             for _, j in targets
         ],
-        in_specs=[vmem] + [pl.BlockSpec(memory_space=pl.ANY)] * (1 + len(after)),
+        in_specs=[pl.BlockSpec(memory_space=pltpu.HBM)] * 2
+        + [pl.BlockSpec(memory_space=pl.ANY)] * len(after),
         out_specs=[vmem] * len(targets),
         scratch_shapes=[
+            pltpu.VMEM((rows, depth), jnp.bfloat16),
             pltpu.VMEM((slots, depth, tile), jnp.bfloat16),
-            pltpu.SemaphoreType.DMA((slots,)),
+            pltpu.SemaphoreType.DMA((slots + 1,)),
         ],
         compiler_params=pltpu.CompilerParams(vmem_limit_bytes=VMEM_BYTES),
         cost_estimate=pl.CostEstimate(
@@ -142,7 +147,8 @@
     )(residual, gain.reshape(blocks, LANES), bias.reshape(blocks, LANES), *terms)
 
 
-def moments_kernel(local, shared_ref, out_ref):
+def moments_kernel(local, passed, shared_ref, *refs):
+    out_ref = refs[passed]
     n = shared_ref.shape[0]
     rows = out_ref.shape[0]
     means, spread = [], jnp.zeros((1, LANES), jnp.float32)
@@ -159,25 +165,24 @@
     out_ref[...] = jnp.transpose(table)[:rows]
 
 
-def moments(shared, rows, local):
-    return pl.pallas_call(
-        functools.partial(moments_kernel, local),
-        out_shape=jax.ShapeDtypeStruct((rows, LANES), jnp.float32),
+def moments(shared, passed, rows, local):
+    vmem = pl.BlockSpec(memory_space=pltpu.VMEM)
+    anywhere = [pl.BlockSpec(memory_space=pl.ANY)] * len(passed)
+    columns, *passed = pl.pallas_call(
+        functools.partial(moments_kernel, local, len(passed)),
+        out_shape=[jax.ShapeDtypeStruct((rows, LANES), jnp.float32)]
+        + [jax.ShapeDtypeStruct(p.shape, p.dtype) for p in passed],
+        in_specs=[vmem] + anywhere,
+        out_specs=[vmem] + anywhere,
+        input_output_aliases={1 + i: 1 + i for i in range(len(passed))},
         name="moments",
-    )(shared)
-
-
-def rows_kernel(place, splits, piece_ref, moments_ref, shared_ref, *refs):
-    out_ref, done_ref, semaphore = refs[-3:]
-    rows, width = piece_ref.shape
-    blocks = width // BLOCK_LEN
-    table = signs(BLOCK_LEN)
+    )(shared, *passed)
+    return columns, passed
+
+
+def coded_rows(piece_ref, moments_ref, scaling, table):
+    blocks = piece_ref.shape[1] // BLOCK_LEN
     unit = 1.0 / math.sqrt(BLOCK_LEN)
-    me = lax.axis_index("tensor")
-    outer, inner = me // splits[1], lax.rem(me, splits[1])
-    owner = jnp.bitwise_xor(outer, place[0]) * splits[1] + jnp.bitwise_xor(inner, place[1])
-    shared = shared_ref[owner].astype(jnp.float32)
-    scaling = shared[shared.shape[0] - 2 * blocks :]
     centre = moments_ref[:, 0:1]
     inverse = moments_ref[:, 1:2]
     normal = []
@@ -195,38 +200,64 @@
     scales = (largest / 448.0 + 1e-06).astype(jnp.bfloat16).astype(jnp.float32)
     quanta = (coded * (1.0 / scales)).astype(jnp.bfloat16)
     back = jnp.dot(quanta, table, preferred_element_type=jnp.float32) * (scales * unit)
-    back = back.astype(out_ref.dtype)
-    for b in range(blocks):
-        done_ref[:, b * BLOCK_LEN : (b + 1) * BLOCK_LEN] = back[b * rows : (b + 1) * rows]
-    columns = pl.ds(pl.multiple_of(owner * width, LANES), width)
-    copy = pltpu.make_async_copy(done_ref, out_ref.at[:, columns], semaphore)
-    copy.start()
-    copy.wait()
-
-
-def finish(whole, place, splits, piece, columns, shared):
-    rows, local = piece.shape
+    return back.astype(jnp.bfloat16)
+
+
+def finish_kernel(places, splits, moments_ref, shared_ref, *refs):
+    count = len(places)
+    pieces = refs[:count]
+    out_ref, done_ref, semaphores = refs[-3:]
+    rows, width = pieces[0].shape
+    blocks = width // BLOCK_LEN
+    table = signs(BLOCK_LEN)
+    me = lax.axis_index("tensor")
+    outer, inner = me // splits[1], lax.rem(me, splits[1])
+    copies = []
+    for p, (k, j) in enumerate(places):
+        owner = jnp.bitwise_xor(outer, k) * splits[1] + jnp.bitwise_xor(inner, j)
+        shared = shared_ref[owner].astype(jnp.float32)
+        back = coded_rows(
+            pieces[p], moments_ref, shared[shared.shape[0] - 2 * blocks :], table
+        )
+        for b in range(blocks):
+            done_ref[p, :, b * BLOCK_LEN : (b + 1) * BLOCK_LEN] = back[
+                b * rows : (b + 1) * rows
+            ]
+        columns = pl.ds(pl.multiple_of(owner * width, LANES), width)
+        copy = pltpu.make_async_copy(
+            done_ref.at[p], out_ref.at[:, columns], semaphores.at[p]
+        )
+        copy.start()
+        copies.append(copy)
+    for copy in copies:
+        copy.wait()
+
+
+def finish(whole, places, splits, pieces, columns, shared):
+    rows, local = pieces[0].shape
+    count = len(pieces)
     n = shared.shape[0]
     earlier = [] if whole is None else [whole]
     vmem = pl.BlockSpec(memory_space=pltpu.VMEM)
     return pl.pallas_call(
-        functools.partial(rows_kernel, place, splits),
+        functools.partial(finish_kernel, places, splits),
         out_shape=jax.ShapeDtypeStruct((rows, n * local), jnp.bfloat16),
-        in_specs=[vmem] * 3 + [pl.BlockSpec(memory_space=pl.ANY)] * len(earlier),
+        in_specs=[vmem] * (2 + count)
+        + [pl.BlockSpec(memory_space=pl.ANY)] * len(earlier),
         out_specs=pl.BlockSpec(memory_space=pl.ANY),
         scratch_shapes=[
-            pltpu.VMEM((rows, local), jnp.bfloat16),
-            pltpu.SemaphoreType.DMA,
+            pltpu.VMEM((count, rows, local), jnp.bfloat16),
+            pltpu.SemaphoreType.DMA((count,)),
         ],
-        input_output_aliases={3: 0} if earlier else {},
+        input_output_aliases={2 + count: 0} if earlier else {},
         compiler_params=pltpu.CompilerParams(vmem_limit_bytes=VMEM_BYTES),
         cost_estimate=pl.CostEstimate(
-            flops=8 * BLOCK_LEN * rows * local,
-            bytes_accessed=4 * rows * local,
+            flops=8 * BLOCK_LEN * rows * local * count,
+            bytes_accessed=4 * rows * local * count,
             transcendentals=0,
         ),
         name="finish",
-    )(piece, columns, shared, *earlier)
+    )(columns, shared, *pieces, *earlier)
 
 
 def body(attended, out_weight, residual, norm_gain, norm_bias):
@@ -237,39 +268,62 @@
     every = [(z, x) for z in range(nz) for x in range(nx)]
     swap = [[(z * nx + x, z * nx + (x ^ j)) for z, x in every] for j in range(nx)]
     jump = [[(z * nx + x, (z ^ k) * nx + x) for z, x in every] for k in range(nz)]
+
+    away = [[(k, j) for j in range(1, nx)] for k in range(nz)]
+    here = [[(k, 0)] for k in range(nz)]
     order = list(range(nz - 1, -1, -1))
-
-    arrived, after = [], []
-    sent, before = None, None
-    for k in order + [None]:
-        targets = [] if k is None else [(k, j) for j in range(1, nx)]
-        targets += [] if before is None else [(before, 0)]
-        terms = products(attended, out_weight, targets, splits, local, after)
-        after = [terms[-1]]
-        leaving = [] if k is None else [lax.ppermute(t, "tensor", swap[j + 1]) for j, t in enumerate(terms[: nx - 1])]
-        if before:
-            kept = terms[-1]
-            for piece in sent:
-                kept = kept + piece.astype(jnp.float32)
-            kept = kept.astype(jnp.bfloat16)
-            after = [kept]
-            arrived.append(lax.ppermute(kept, "tensor", jump[before]))
-        elif before == 0:
-            arrived += [terms[-1]] + sent
-        sent, before = leaving, k
-
-    stream_out, shared = own_stream(residual, norm_gain, norm_bias, arrived, n)
-    near = {k: lax.ppermute(stream_out, "tensor", jump[k]) for k in order[:-1]}
-    near[0] = stream_out
+    calls = [away[order[0]], away[order[1]] + away[order[2]] + here[order[0]]]
+    for i in range(2, nz - 1):
+        calls.append(away[order[i + 1]] + here[order[i - 1]])
+    calls[-1] = calls[-1] + here[1]
+    calls.append(here[0])
+    joins = [[]] + [[k] for k in order[:-1]] + [[]]
+    joins[-3:] = [joins[-3] + joins[-2], []]
+    terms = {k: [] for k in range(nz)}
+    after = []
+    for targets, joined in zip(calls, joins):
+        results = products(attended, out_weight, targets, splits, local, after)
+        after = [results[-1]]
+        for (k, j), result in zip(targets, results):
+            terms[k].append(lax.ppermute(result, "tensor", swap[j]) if j else result)
+        for k in joined:
+            bit = k & -k
+            total = terms[k][0].astype(jnp.float32)
+            for term in terms[k][1:]:
+                total = total + term.astype(jnp.float32)
+            total = total.astype(jnp.bfloat16)
+            after = [total]
+            terms[k ^ bit].append(lax.ppermute(total, "tensor", jump[bit]))
+
+    stream_out, shared = own_stream(residual, norm_gain, norm_bias, terms[0], n)
     shared = lax.all_to_all(shared, "tensor", 0, 0, tiled=True)
-    columns = moments(shared, rows, local)
+    have = {0: stream_out}
+    top = nz // 2
+    have[top] = lax.ppermute(stream_out, "tensor", jump[top])
+    have[1] = lax.ppermute(stream_out, "tensor", jump[1])
+    early = away[0] + away[1]
+    crossed = {(k, j): lax.ppermute(have[k], "tensor", swap[j]) for k, j in early}
+    columns, passed = moments(
+        shared, [have[top]] + [crossed[p] for p in early], rows, local
+    )
+    have[top] = passed[0]
+    crossed.update(zip(early, passed[1:]))
+    for k in sorted(range(2, nz), key=lambda k: (-(k & -k), k)):
+        if k != top:
+            have[k] = lax.ppermute(have[k ^ (k & -k)], "tensor", jump[k & -k])
 
     whole = None
-    for k in [0, 1] + order[:-2]:
-        whole = finish(whole, (k, 0), splits, near[k], columns, shared)
-        for j in range(1, nx):
-            other = lax.ppermute(near[k], "tensor", swap[j])
-            whole = finish(whole, (k, j), splits, other, columns, shared)
+    for k in range(nz):
+        places = here[k] + away[k]
+        pieces = [have[k]] + [
+            crossed.get(p) if p in crossed else lax.ppermute(have[k], "tensor", swap[p[1]])
+            for p in away[k]
+        ]
+        if k < nz - 1:
+            whole = finish(whole, places, splits, pieces, columns, shared)
+        else:
+            for place, piece in zip(places, pieces):
+                whole = finish(whole, [place], splits, [piece], columns, shared)
     return (stream_out, whole)
 
 

time: 93.1 us -> 87.7 us (0.942)
  waiting for transfers between devices: 27.7 us -> 22.5 us
  Pallas kernels: 30.5 us -> 27.2 us
  local copies, waits for them, and re-layouts: 3.52 us -> 5.95 us
    ppermute x14, waiting for transfers between devices: 27.7 us -> 22.5 us  [the longest x3 7.68 us: body(): terms[k ^ bit].append(lax.ppermute(total, 'tensor', jump[bit]))]
    pallas_call x9 -> x6, Pallas kernels: 12.9 us -> 10.4 us  [the longest x5 8.73 us: finish(): pl.pallas_call(functools.partial(finish_kernel, places, splits), out_shap...]
    unnamed x18 -> x30, local copies, waits for them, and re-layouts: 3.52 us -> 5.95 us
    pallas_call x5 -> x4, Pallas kernels: 16.6 us -> 15.8 us  [products(): pl.pallas_call(functools.partial(product_kernel, targets, splits, local,...]
  transfers between devices with their start and end apart: 14 -> 14, of which waited for: 8 -> 5; matrix products, arithmetic and copies ran while one was open for 0% -> 0% of each run, Pallas kernels for 28% -> 23%
where the time goes in v5:
time: 87.7 us; the launch traced here: 87.4 us
  Pallas kernels  27.2 us (31%)
  waiting for transfers between devices  22.5 us (26%)
  starting transfers between devices  19.7 us (22%)
  blocking collectives  11.1 us (13%)
  local copies, waits for them, and re-layouts  5.95 us (7%)
    pallas_call x4, Pallas kernels, products(): pl.pallas_call(functools.partial(product_kernel, targets, splits, local,...  15.8 us
    all_to_all x1, blocking collectives, body(): shared = lax.all_to_all(shared, 'tensor', 0, 0, tiled=True)  11.1 us
    pallas_call x5, Pallas kernels, finish(): pl.pallas_call(functools.partial(finish_kernel, places, splits), out_shap...  8.73 us
    ppermute x3, waiting for transfers between devices, body(): terms[k ^ bit].append(lax.ppermute(total, 'tensor', jump[bit]))  7.68 us
    unnamed x30, local copies, waits for them, and re-layouts  5.95 us
    ppermute x3, starting transfers between devices, body(): terms[k ^ bit].append(lax.ppermute(total, 'tensor', jump[bit]))  5.94 us
    ppermute x4, starting transfers between devices, body(): terms[k].append(lax.ppermute(result, 'tensor', swap[j]) if j else result)  5.68 us
    ppermute x1, waiting for transfers between devices, body(): have[k] = lax.ppermute(have[k ^ k & -k], 'tensor', jump[k & -k])  5.32 us
  transfers between devices with their start and end apart: 14, of which 5 were waited for; matrix products, arithmetic and copies ran while one was open for 0% of the time, Pallas kernels for 23%

profile of v5, /device:TPU:0, one launch (start us, length us, event | category | flops | bytes accessed | tf_op | source)
XLA Modules:
  0.0 87.4 jit_solution(12258541227360745046)
XLA Ops:
  0.6 0.9 %copy-done.2 = bf16[64,1024]{1,0:T(8,128)(2,1)S(1)} copy-done((bf16[64,1024]{1,0:T(8,128)(2,1)S(1)}, bf16[64,1024]{1,0:T(8,128)(2,1)}, u32[]{:S(2)}) %copy-start.2) | copy-done | bytes 131096
  1.5 2.7 %products.4.refs_0_ = bf16[64,2048]{1,0:T(8,128)(2,1)S(1)} custom-call(bf16[64,1024]{1,0:T(8,128)(2,1)S(1)} %copy-done.2, bf16[1024,16384]{1,0:T(8,128)(2,1)} %weight_ref.7), custom_call_target="tpu_custom_call" | custom-call | flops 268435456 | bytes 4194304 | tf_op jit(solution)/shard_map/products/pallas_call | solution.py:72
  4.2 3.0 %collective-permute-start = (bf16[64,2048]{1,0:T(8,128)(2,1)S(1)}, bf16[64,2048]{1,0:T(8,128)(2,1)S(1)}, u32[]{:S(2)}, u32[]{:S(2)}) collective-permute-start(bf16[64,2048]{1,0:T(8,128)(2,1)S(1)} %products.4.refs_0_), channel_id=1, source_target_pairs={{0,1},{1,0},{2,3},{3,2},{4,5},{5,4},{6,7},{7,6},{8,9},{9,8},{10,11... | collective-permute-start | bytes 786440 | tf_op jit(solution)/shard_map/ppermute | solution.py:288
  7.2 5.2 %products.5 = (bf16[64,2048]{1,0:T(8,128)(2,1)S(1)}, bf16[64,2048]{1,0:T(8,128)(2,1)S(1)}, f32[64,2048]{1,0:T(8,128)S(1)}) custom-call(bf16[64,1024]{1,0:T(8,128)(2,1)S(1)} %copy-done.2, bf16[1024,16384]{1,0:T(8,128)(2,1)} %weight_ref.7, bf16[64,2048]{1,0:T(8,128)(2,1)S(1)} %products.4.refs_0_), custom_call_target="tpu_custom_call" | custom-call | flops 805306368 | bytes 12582912 | tf_op jit(solution)/shard_map/products/pallas_call | solution.py:72
  12.5 0.1 collective-permute-start.2
  12.6 2.0 %collective-permute-start.5 = (bf16[64,2048]{1,0:T(8,128)(2,1)S(1)}, bf16[64,2048]{1,0:T(8,128)(2,1)S(1)}, u32[]{:S(2)}, u32[]{:S(2)}) collective-permute-start(bf16[64,2048]{1,0:T(8,128)(2,1)S(1)} %get-tuple-element.18), channel_id=1, source_target_pairs={{0,1},{1,0},{2,3},{3,2},{4,5},{5,4},{6,7},{7,6},{8,9},{9,8},{10,11... | collective-permute-start | bytes 786440 | tf_op jit(solution)/shard_map/ppermute | solution.py:288
  14.6 0.0 collective-permute-done
  14.6 1.6 %collective-permute-start.3 = (bf16[64,2048]{1,0:T(8,128)(2,1)S(1)}, bf16[64,2048]{1,0:T(8,128)(2,1)S(1)}, u32[]{:S(2)}, u32[]{:S(2)}) collective-permute-start(bf16[64,2048]{1,0:T(8,128)(2,1)S(1)} %add_convert_fusion.2.refs_0_), channel_id=1, source_target_pairs={{0,2},{1,3},{2,0},{3,1},{4,6},{5,7},{6,4},{7,5},{8,10},{9,11},{10,... | collective-permute-start | bytes 786440 | tf_op jit(solution)/shard_map/ppermute | solution.py:296
  16.3 5.2 %products.6 = (bf16[64,2048]{1,0:T(8,128)(2,1)S(1)}, f32[64,2048]{1,0:T(8,128)S(1)}, f32[64,2048]{1,0:T(8,128)S(1)}) custom-call(bf16[64,1024]{1,0:T(8,128)(2,1)S(1)} %copy-done.2, bf16[1024,16384]{1,0:T(8,128)(2,1)} %weight_ref.7, bf16[64,2048]{1,0:T(8,128)(2,1)S(1)} %add_convert_fusion.2.refs_0_), custom_call_target="tpu_custom_call" | custom-call | flops 805306368 | bytes 12582912 | tf_op jit(solution)/shard_map/products/pallas_call | solution.py:72
  21.5 4.4 %collective-permute-done.5 = bf16[64,2048]{1,0:T(8,128)(2,1)S(1)} collective-permute-done((bf16[64,2048]{1,0:T(8,128)(2,1)S(1)}, bf16[64,2048]{1,0:T(8,128)(2,1)S(1)}, u32[]{:S(2)}, u32[]{:S(2)}) %collective-permute-start.5) | collective-permute-done | bytes 262176 | tf_op jit(solution)/shard_map/ppermute | solution.py:288
  26.0 1.6 %collective-permute-start.6 = (bf16[64,2048]{1,0:T(8,128)(2,1)S(1)}, bf16[64,2048]{1,0:T(8,128)(2,1)S(1)}, u32[]{:S(2)}, u32[]{:S(2)}) collective-permute-start(bf16[64,2048]{1,0:T(8,128)(2,1)S(1)} %add_convert_fusion.refs_0_), channel_id=1, source_target_pairs={{0,2},{1,3},{2,0},{3,1},{4,6},{5,7},{6,4},{7,5},{8,10},{9,11},{10,... | collective-permute-start | bytes 786440 | tf_op jit(solution)/shard_map/ppermute | solution.py:296
  27.6 0.6 collective-permute-start.1
  28.2 0.0 collective-permute-done.2
  28.2 0.1 add_convert_fusion.1
  28.3 0.0 copy-start.11
  28.3 0.0 copy-start.13
  28.3 0.0 copy-start.14
  28.3 2.7 %collective-permute-start.4 = (bf16[64,2048]{1,0:T(8,128)(2,1)S(1)}, bf16[64,2048]{1,0:T(8,128)(2,1)S(1)}, u32[]{:S(2)}, u32[]{:S(2)}) collective-permute-start(bf16[64,2048]{1,0:T(8,128)(2,1)S(1)} %add_convert_fusion.1), channel_id=1, source_target_pairs={{0,4},{1,5},{2,6},{3,7},{4,0},{5,1},{6,2},{7,3},{8,12},{9,13},{10,... | collective-permute-start | bytes 786440 | tf_op jit(solution)/shard_map/ppermute | solution.py:296
  31.0 2.7 %products.7.refs_3_ = f32[64,2048]{1,0:T(8,128)S(1)} custom-call(bf16[64,1024]{1,0:T(8,128)(2,1)S(1)} %copy-done.2, bf16[1024,16384]{1,0:T(8,128)(2,1)} %weight_ref.7, bf16[64,2048]{1,0:T(8,128)(2,1)S(1)} %add_convert_fusion.refs_0_), custom_call_target="tpu_custom_call" | custom-call | flops 268435456 | bytes 4194304 | tf_op jit(solution)/shard_map/products/pallas_call | solution.py:72
  33.7 4.1 %collective-permute-done.6.refs_2_ = bf16[64,2048]{1,0:T(8,128)(2,1)S(1)} collective-permute-done((bf16[64,2048]{1,0:T(8,128)(2,1)S(1)}, bf16[64,2048]{1,0:T(8,128)(2,1)S(1)}, u32[]{:S(2)}, u32[]{:S(2)}) %collective-permute-start.6) | collective-permute-done | bytes 262176 | tf_op jit(solution)/shard_map/ppermute | solution.py:296
  37.8 0.0 collective-permute-done.1.refs_0_
  37.8 3.5 %collective-permute-done.4.refs_1_ = bf16[64,2048]{1,0:T(8,128)(2,1)S(1)} collective-permute-done((bf16[64,2048]{1,0:T(8,128)(2,1)S(1)}, bf16[64,2048]{1,0:T(8,128)(2,1)S(1)}, u32[]{:S(2)}, u32[]{:S(2)}) %collective-permute-start.4) | collective-permute-done | bytes 262176 | tf_op jit(solution)/shard_map/ppermute | solution.py:296
  41.4 1.0 %own_stream.1 = (bf16[64,2048]{1,0:T(8,128)(2,1)}, bf16[8,48,128]{2,1,0:T(8,128)(2,1)S(1)}) custom-call(bf16[64,2048]{1,0:T(8,128)(2,1)S(1)} %copy-done.11, bf16[16,128]{1,0:T(8,128)(2,1)S(1)} %bitcast.2, bf16[16,128]{1,0:T(8,128)(2,1)S(1)} %bitcast.3, bf16[64,2048]{1,0:T(8,128)(2,1)S(1)} %collective-permute-done.1.refs_0_, ...), custom_call_target="tpu_custom_call" | custom-call | flops 2621440 | bytes 2097152 | tf_op jit(solution)/shard_map/own_stream/pallas_call | solution.py:136
  42.4 3.1 %collective-permute-start.7 = (bf16[64,2048]{1,0:T(8,128)(2,1)}, bf16[64,2048]{1,0:T(8,128)(2,1)S(1)}, u32[]{:S(2)}, u32[]{:S(2)}) collective-permute-start(bf16[64,2048]{1,0:T(8,128)(2,1)} %get-tuple-element.12.refs_0_), channel_id=1, source_target_pairs={{0,4},{1,5},{2,6},{3,7},{4,0},{5,1},{6,2},{7,3},{8,12},{9,13},{10,... | collective-permute-start | bytes 786440 | tf_op jit(solution)/shard_map/ppermute | solution.py:302
  45.5 1.3 %collective-permute-start.8 = (bf16[64,2048]{1,0:T(8,128)(2,1)}, bf16[64,2048]{1,0:T(8,128)(2,1)S(1)}, u32[]{:S(2)}, u32[]{:S(2)}) collective-permute-start(bf16[64,2048]{1,0:T(8,128)(2,1)} %get-tuple-element.12.refs_0_), channel_id=1, source_target_pairs={{0,1},{1,0},{2,3},{3,2},{4,5},{5,4},{6,7},{7,6},{8,9},{9,8},{10,11... | collective-permute-start | bytes 786440 | tf_op jit(solution)/shard_map/ppermute | solution.py:305
  46.7 5.0 %collective-permute-done.9.refs_0_ = bf16[64,2048]{1,0:T(8,128)(2,1)S(1)} collective-permute-done((bf16[64,2048]{1,0:T(8,128)(2,1)}, bf16[64,2048]{1,0:T(8,128)(2,1)S(1)}, u32[]{:S(2)}, u32[]{:S(2)}) %collective-permute-start.9) | collective-permute-done | bytes 262176 | tf_op jit(solution)/shard_map/ppermute | solution.py:303
  51.8 2.1 %collective-permute-start.10 = (bf16[64,2048]{1,0:T(8,128)(2,1)S(1)}, bf16[64,2048]{1,0:T(8,128)(2,1)S(1)}, u32[]{:S(2)}, u32[]{:S(2)}) collective-permute-start(bf16[64,2048]{1,0:T(8,128)(2,1)S(1)} %collective-permute-done.9.refs_0_), channel_id=1, source_target_pairs={{0,1},{1,0},{2,3},{3,2},{4,5},{5,4},{6,7},{7,6},{8,9},{9,8},{10,11... | collective-permute-start | bytes 786440 | tf_op jit(solution)/shard_map/ppermute | solution.py:305
  53.9 11.1 %all_to_all.5.shared_ref = bf16[8,48,128]{2,1,0:T(8,128)(2,1)} all-to-all(bf16[8,48,128]{2,1,0:T(8,128)(2,1)S(1)} %get-tuple-element.21), channel_id=1, replica_groups=mesh['groups'=2,'dp'=2,'tensor'=8] {'tensor'}, dimensions={0} | all-to-all | bytes 196608 | tf_op jit(solution)/shard_map/all_to_all | solution.py:299
  65.0 0.0 collective-permute-done.7.refs_0_
  65.0 0.0 collective-permute-done.8.refs_1_
  65.0 0.0 copy-start.7
  65.0 0.7 copy-done.3
  65.7 0.1 copy-done.7
  65.8 0.7 copy-done.5
  66.5 1.6 %moments.1 = (f32[64,128]{1,0:T(8,128)}, bf16[64,2048]{1,0:T(8,128)(2,1)}, bf16[64,2048]{1,0:T(8,128)(2,1)}, bf16[64,2048]{1,0:T(8,128)(2,1)}) custom-call(bf16[8,48,128]{2,1,0:T(8,128)(2,1)} %all_to_all.5.shared_ref, bf16[64,2048]{1,0:T(8,128)(2,1)} %copy-done.3, ...), custom_call_target="tpu_custom_call", output_to_operand_aliasing={{1}: (1, {}), {2}: (2, {}), {3}: (3, {})} | custom-call | tf_op jit(solution)/shard_map/moments/pallas_call | solution.py:171
  68.1 0.0 collective-permute-start.11
  68.1 1.2 %collective-permute-start.13 = (bf16[64,2048]{1,0:T(8,128)(2,1)}, bf16[64,2048]{1,0:T(8,128)(2,1)S(1)}, u32[]{:S(2)}, u32[]{:S(2)}) collective-permute-start(bf16[64,2048]{1,0:T(8,128)(2,1)} %get-tuple-element.23.refs_0_), channel_id=1, source_target_pairs={{0,1},{1,0},{2,3},{3,2},{4,5},{5,4},{6,7},{7,6},{8,9},{9,8},{10,11... | collective-permute-start | bytes 786440 | tf_op jit(solution)/shard_map/ppermute | solution.py:319
  69.3 5.3 %collective-permute-done.11.refs_0_ = bf16[64,2048]{1,0:T(8,128)(2,1)S(1)} collective-permute-done((bf16[64,2048]{1,0:T(8,128)(2,1)}, bf16[64,2048]{1,0:T(8,128)(2,1)S(1)}, u32[]{:S(2)}, u32[]{:S(2)}) %collective-permute-start.11) | collective-permute-done | bytes 262176 | tf_op jit(solution)/shard_map/ppermute | solution.py:313
  74.7 0.3 collective-permute-start.12
  75.0 0.9 %copy-done = bf16[8,48,128]{2,1,0:T(8,128)(2,1)S(1)} copy-done((bf16[8,48,128]{2,1,0:T(8,128)(2,1)S(1)}, bf16[8,48,128]{2,1,0:T(8,128)(2,1)}, u32[]{:S(2)}) %copy-start) | copy-done | bytes 98328
  75.9 0.9 %copy-done.8 = bf16[64,2048]{1,0:T(8,128)(2,1)S(1)} copy-done((bf16[64,2048]{1,0:T(8,128)(2,1)S(1)}, bf16[64,2048]{1,0:T(8,128)(2,1)}, u32[]{:S(2)}) %copy-start.8) | copy-done | bytes 262168
  76.8 0.8 copy-done.9
  77.6 0.9 %copy-done.12 = bf16[64,2048]{1,0:T(8,128)(2,1)S(1)} copy-done((bf16[64,2048]{1,0:T(8,128)(2,1)S(1)}, bf16[64,2048]{1,0:T(8,128)(2,1)}, u32[]{:S(2)}) %copy-start.12) | copy-done | bytes 262168
  78.5 2.0 %finish.5.refs_2_ = bf16[64,16384]{1,0:T(8,128)(2,1)} custom-call(f32[64,128]{1,0:T(8,128)S(1)} %copy-done.9, bf16[8,48,128]{2,1,0:T(8,128)(2,1)S(1)} %copy-done, bf16[64,2048]{1,0:T(8,128)(2,1)S(1)} %copy-done.12, bf16[64,2048]{1,0:T(8,128)(2,1)S(1)} %copy-done.8), custom_call_target="tpu_custom_call" | custom-call | flops 268435456 | bytes 1048576 | tf_op jit(solution)/shard_map/finish/pallas_call | solution.py:242
  80.5 2.0 %finish.6.refs_2_ = bf16[64,16384]{1,0:T(8,128)(2,1)} custom-call(f32[64,128]{1,0:T(8,128)S(1)} %copy-done.10, bf16[8,48,128]{2,1,0:T(8,128)(2,1)S(1)} %copy-done.1, bf16[64,2048]{1,0:T(8,128)(2,1)S(1)} %collective-permute-done.9.refs_0_, bf16[64,2048]{1,0:T(8,128)(2,1)S(1)} %copy-done.6, ...), custom_call_target="tpu_custom_call", output_to_operand_aliasing={{}: (4, {})} | custom-call | flops 268435456 | bytes 1048576 | tf_op jit(solution)/shard_map/finish/pallas_call | solution.py:242
  82.5 2.0 %finish.7.refs_1_ = bf16[64,16384]{1,0:T(8,128)(2,1)} custom-call(f32[64,128]{1,0:T(8,128)S(1)} %copy-done.10, bf16[8,48,128]{2,1,0:T(8,128)(2,1)S(1)} %copy-done.1, bf16[64,2048]{1,0:T(8,128)(2,1)S(1)} %copy-done.4, bf16[64,2048]{1,0:T(8,128)(2,1)S(1)} %collective-permute-done.13.refs_1_, ...), custom_call_target="tpu_custom_call", output_to_operand_aliasing={{}: (4, {})} | custom-call | flops 268435456 | bytes 1048576 | tf_op jit(solution)/shard_map/finish/pallas_call | solution.py:242
  84.5 1.4 %finish.8.refs_1_ = bf16[64,16384]{1,0:T(8,128)(2,1)} custom-call(f32[64,128]{1,0:T(8,128)S(1)} %copy-done.10, bf16[8,48,128]{2,1,0:T(8,128)(2,1)S(1)} %copy-done.1, bf16[64,2048]{1,0:T(8,128)(2,1)S(1)} %collective-permute-done.11.refs_0_, bf16[64,16384]{1,0:T(8,128)(2,1)} %finish.7.refs_1_), custom_call_target="tpu_custom_call", output_to_operand_aliasing={{}: (3, {})} | custom-call | flops 134217728 | bytes 524288 | tf_op jit(solution)/shard_map/finish/pallas_call | solution.py:242
  86.0 1.4 %finish.9 = bf16[64,16384]{1,0:T(8,128)(2,1)} custom-call(f32[64,128]{1,0:T(8,128)S(1)} %copy-done.10, bf16[8,48,128]{2,1,0:T(8,128)(2,1)S(1)} %copy-done.1, bf16[64,2048]{1,0:T(8,128)(2,1)S(1)} %collective-permute-done.12.refs_0_, bf16[64,16384]{1,0:T(8,128)(2,1)} %finish.8.refs_1_), custom_call_target="tpu_custom_call", output_to_operand_aliasing={{}: (3, {})} | custom-call | flops 134217728 | bytes 524288 | tf_op jit(solution)/shard_map/finish/pallas_call | solution.py:242
  (25 shorter events, 0.1 us)
Async XLA Ops:
  0.6 0.9 %copy-start.2 = (bf16[64,1024]{1,0:T(8,128)(2,1)S(1)}, bf16[64,1024]{1,0:T(8,128)(2,1)}, u32[]{:S(2)}) copy-start(bf16[64,1024]{1,0:T(8,128)(2,1)} %rows_ref.7) | copy-start | bytes 393220
  4.2 10.3 %collective-permute-start = (bf16[64,2048]{1,0:T(8,128)(2,1)S(1)}, bf16[64,2048]{1,0:T(8,128)(2,1)S(1)}, u32[]{:S(2)}, u32[]{:S(2)}) collective-permute-start(bf16[64,2048]{1,0:T(8,128)(2,1)S(1)} %products.4.refs_0_), channel_id=1, source_target_pairs={{0,1},{1,0},{2,3},{3,2},{4,5},{5,4},{6,7},{7,6},{8,9},{9,8},{10,11... | collective-permute-start | bytes 786440 | tf_op jit(solution)/shard_map/ppermute | solution.py:288
  12.5 15.7 %collective-permute-start.2 = (bf16[64,2048]{1,0:T(8,128)(2,1)S(1)}, bf16[64,2048]{1,0:T(8,128)(2,1)S(1)}, u32[]{:S(2)}, u32[]{:S(2)}) collective-permute-start(bf16[64,2048]{1,0:T(8,128)(2,1)S(1)} %get-tuple-element.16), channel_id=1, source_target_pairs={{0,1},{1,0},{2,3},{3,2},{4,5},{5,4},{6,7},{7,6},{8,9},{9,8},{10,11... | collective-permute-start | bytes 786440 | tf_op jit(solution)/shard_map/ppermute | solution.py:288
  12.6 13.3 %collective-permute-start.5 = (bf16[64,2048]{1,0:T(8,128)(2,1)S(1)}, bf16[64,2048]{1,0:T(8,128)(2,1)S(1)}, u32[]{:S(2)}, u32[]{:S(2)}) collective-permute-start(bf16[64,2048]{1,0:T(8,128)(2,1)S(1)} %get-tuple-element.18), channel_id=1, source_target_pairs={{0,1},{1,0},{2,3},{3,2},{4,5},{5,4},{6,7},{7,6},{8,9},{9,8},{10,11... | collective-permute-start | bytes 786440 | tf_op jit(solution)/shard_map/ppermute | solution.py:288
  14.6 13.6 %collective-permute-start.3 = (bf16[64,2048]{1,0:T(8,128)(2,1)S(1)}, bf16[64,2048]{1,0:T(8,128)(2,1)S(1)}, u32[]{:S(2)}, u32[]{:S(2)}) collective-permute-start(bf16[64,2048]{1,0:T(8,128)(2,1)S(1)} %add_convert_fusion.2.refs_0_), channel_id=1, source_target_pairs={{0,2},{1,3},{2,0},{3,1},{4,6},{5,7},{6,4},{7,5},{8,10},{9,11},{10,... | collective-permute-start | bytes 786440 | tf_op jit(solution)/shard_map/ppermute | solution.py:296
  26.0 11.8 %collective-permute-start.6 = (bf16[64,2048]{1,0:T(8,128)(2,1)S(1)}, bf16[64,2048]{1,0:T(8,128)(2,1)S(1)}, u32[]{:S(2)}, u32[]{:S(2)}) collective-permute-start(bf16[64,2048]{1,0:T(8,128)(2,1)S(1)} %add_convert_fusion.refs_0_), channel_id=1, source_target_pairs={{0,2},{1,3},{2,0},{3,1},{4,6},{5,7},{6,4},{7,5},{8,10},{9,11},{10,... | collective-permute-start | bytes 786440 | tf_op jit(solution)/shard_map/ppermute | solution.py:296
  27.6 10.2 %collective-permute-start.1 = (bf16[64,2048]{1,0:T(8,128)(2,1)S(1)}, bf16[64,2048]{1,0:T(8,128)(2,1)S(1)}, u32[]{:S(2)}, u32[]{:S(2)}) collective-permute-start(bf16[64,2048]{1,0:T(8,128)(2,1)S(1)} %get-tuple-element.15), channel_id=1, source_target_pairs={{0,1},{1,0},{2,3},{3,2},{4,5},{5,4},{6,7},{7,6},{8,9},{9,8},{10,11... | collective-permute-start | bytes 786440 | tf_op jit(solution)/shard_map/ppermute | solution.py:288
  28.3 13.1 %copy-start.11 = (bf16[64,2048]{1,0:T(8,128)(2,1)S(1)}, bf16[64,2048]{1,0:T(8,128)(2,1)}, u32[]{:S(2)}) copy-start(bf16[64,2048]{1,0:T(8,128)(2,1)} %residual_ref.1) | copy-start | bytes 786436
  28.3 13.0 %copy-start.13 = (bf16[2048]{0:T(1024)(128)(2,1)S(1)}, bf16[2048]{0:T(1024)(128)(2,1)}, u32[]{:S(2)}) copy-start(bf16[2048]{0:T(1024)(128)(2,1)} %param.8) | copy-start | bytes 12292
  28.3 13.0 %copy-start.14 = (bf16[2048]{0:T(1024)(128)(2,1)S(1)}, bf16[2048]{0:T(1024)(128)(2,1)}, u32[]{:S(2)}) copy-start(bf16[2048]{0:T(1024)(128)(2,1)} %param.9) | copy-start | bytes 12292
  28.3 13.0 %collective-permute-start.4 = (bf16[64,2048]{1,0:T(8,128)(2,1)S(1)}, bf16[64,2048]{1,0:T(8,128)(2,1)S(1)}, u32[]{:S(2)}, u32[]{:S(2)}) collective-permute-start(bf16[64,2048]{1,0:T(8,128)(2,1)S(1)} %add_convert_fusion.1), channel_id=1, source_target_pairs={{0,4},{1,5},{2,6},{3,7},{4,0},{5,1},{6,2},{7,3},{8,12},{9,13},{10,... | collective-permute-start | bytes 786440 | tf_op jit(solution)/shard_map/ppermute | solution.py:296
  42.4 9.4 %collective-permute-start.9 = (bf16[64,2048]{1,0:T(8,128)(2,1)}, bf16[64,2048]{1,0:T(8,128)(2,1)S(1)}, u32[]{:S(2)}, u32[]{:S(2)}) collective-permute-start(bf16[64,2048]{1,0:T(8,128)(2,1)} %get-tuple-element.12.refs_0_), channel_id=1, source_target_pairs={{0,2},{1,3},{2,0},{3,1},{4,6},{5,7},{6,4},{7,5},{8,10},{9,11},{10,... | collective-permute-start | bytes 786440 | tf_op jit(solution)/shard_map/ppermute | solution.py:303
  42.4 22.6 %collective-permute-start.7 = (bf16[64,2048]{1,0:T(8,128)(2,1)}, bf16[64,2048]{1,0:T(8,128)(2,1)S(1)}, u32[]{:S(2)}, u32[]{:S(2)}) collective-permute-start(bf16[64,2048]{1,0:T(8,128)(2,1)} %get-tuple-element.12.refs_0_), channel_id=1, source_target_pairs={{0,4},{1,5},{2,6},{3,7},{4,0},{5,1},{6,2},{7,3},{8,12},{9,13},{10,... | collective-permute-start | bytes 786440 | tf_op jit(solution)/shard_map/ppermute | solution.py:302
  45.5 19.5 %collective-permute-start.8 = (bf16[64,2048]{1,0:T(8,128)(2,1)}, bf16[64,2048]{1,0:T(8,128)(2,1)S(1)}, u32[]{:S(2)}, u32[]{:S(2)}) collective-permute-start(bf16[64,2048]{1,0:T(8,128)(2,1)} %get-tuple-element.12.refs_0_), channel_id=1, source_target_pairs={{0,1},{1,0},{2,3},{3,2},{4,5},{5,4},{6,7},{7,6},{8,9},{9,8},{10,11... | collective-permute-start | bytes 786440 | tf_op jit(solution)/shard_map/ppermute | solution.py:305
  51.8 13.2 %collective-permute-start.10 = (bf16[64,2048]{1,0:T(8,128)(2,1)S(1)}, bf16[64,2048]{1,0:T(8,128)(2,1)S(1)}, u32[]{:S(2)}, u32[]{:S(2)}) collective-permute-start(bf16[64,2048]{1,0:T(8,128)(2,1)S(1)} %collective-permute-done.9.refs_0_), channel_id=1, source_target_pairs={{0,1},{1,0},{2,3},{3,2},{4,5},{5,4},{6,7},{7,6},{8,9},{9,8},{10,11... | collective-permute-start | bytes 786440 | tf_op jit(solution)/shard_map/ppermute | solution.py:305
  65.0 15.5 %copy-start.1 = (bf16[8,48,128]{2,1,0:T(8,128)(2,1)S(1)}, bf16[8,48,128]{2,1,0:T(8,128)(2,1)}, u32[]{:S(2)}) copy-start(bf16[8,48,128]{2,1,0:T(8,128)(2,1)} %all_to_all.5.shared_ref) | copy-start | bytes 294916
  65.0 0.7 copy-start.3
  65.0 0.8 copy-start.7
  65.8 0.7 copy-start.5
  68.1 6.6 %collective-permute-start.11 = (bf16[64,2048]{1,0:T(8,128)(2,1)}, bf16[64,2048]{1,0:T(8,128)(2,1)S(1)}, u32[]{:S(2)}, u32[]{:S(2)}) collective-permute-start(bf16[64,2048]{1,0:T(8,128)(2,1)} %get-tuple-element.23.refs_0_), channel_id=1, source_target_pairs={{0,2},{1,3},{2,0},{3,1},{4,6},{5,7},{6,4},{7,5},{8,10},{9,11},{10,... | collective-permute-start | bytes 786440 | tf_op jit(solution)/shard_map/ppermute | solution.py:313
  68.1 14.4 %collective-permute-start.13 = (bf16[64,2048]{1,0:T(8,128)(2,1)}, bf16[64,2048]{1,0:T(8,128)(2,1)S(1)}, u32[]{:S(2)}, u32[]{:S(2)}) collective-permute-start(bf16[64,2048]{1,0:T(8,128)(2,1)} %get-tuple-element.23.refs_0_), channel_id=1, source_target_pairs={{0,1},{1,0},{2,3},{3,2},{4,5},{5,4},{6,7},{7,6},{8,9},{9,8},{10,11... | collective-permute-start | bytes 786440 | tf_op jit(solution)/shard_map/ppermute | solution.py:319
  74.7 11.3 %collective-permute-start.12 = (bf16[64,2048]{1,0:T(8,128)(2,1)S(1)}, bf16[64,2048]{1,0:T(8,128)(2,1)S(1)}, u32[]{:S(2)}, u32[]{:S(2)}) collective-permute-start(bf16[64,2048]{1,0:T(8,128)(2,1)S(1)} %collective-permute-done.11.refs_0_), channel_id=1, source_target_pairs={{0,1},{1,0},{2,3},{3,2},{4,5},{5,4},{6,7},{7,6},{8,9},{9,8},{10,11... | collective-permute-start | bytes 786440 | tf_op jit(solution)/shard_map/ppermute | solution.py:319
  75.0 0.9 %copy-start = (bf16[8,48,128]{2,1,0:T(8,128)(2,1)S(1)}, bf16[8,48,128]{2,1,0:T(8,128)(2,1)}, u32[]{:S(2)}) copy-start(bf16[8,48,128]{2,1,0:T(8,128)(2,1)} %all_to_all.5.shared_ref) | copy-start | bytes 294916
  75.9 0.9 %copy-start.8 = (bf16[64,2048]{1,0:T(8,128)(2,1)S(1)}, bf16[64,2048]{1,0:T(8,128)(2,1)}, u32[]{:S(2)}) copy-start(bf16[64,2048]{1,0:T(8,128)(2,1)} %get-tuple-element.25.refs_1_) | copy-start | bytes 786436
  76.8 0.8 copy-start.9
  77.6 0.9 %copy-start.12 = (bf16[64,2048]{1,0:T(8,128)(2,1)S(1)}, bf16[64,2048]{1,0:T(8,128)(2,1)}, u32[]{:S(2)}) copy-start(bf16[64,2048]{1,0:T(8,128)(2,1)} %get-tuple-element.12.refs_0_) | copy-start | bytes 786436
  78.5 2.0 %copy-start.6 = (bf16[64,2048]{1,0:T(8,128)(2,1)S(1)}, bf16[64,2048]{1,0:T(8,128)(2,1)}, u32[]{:S(2)}) copy-start(bf16[64,2048]{1,0:T(8,128)(2,1)} %get-tuple-element.24.refs_1_) | copy-start | bytes 786436
  78.5 2.0 %copy-start.10 = (f32[64,128]{1,0:T(8,128)S(1)}, f32[64,128]{1,0:T(8,128)}, u32[]{:S(2)}) copy-start(f32[64,128]{1,0:T(8,128)} %get-tuple-element.22.moments_ref) | copy-start | bytes 98308
  80.5 2.0 %copy-start.4 = (bf16[64,2048]{1,0:T(8,128)(2,1)S(1)}, bf16[64,2048]{1,0:T(8,128)(2,1)}, u32[]{:S(2)}) copy-start(bf16[64,2048]{1,0:T(8,128)(2,1)} %get-tuple-element.23.refs_0_) | copy-start | bytes 786436

commit v6 on v5

--- a/solution.py
+++ b/solution.py
@@ -10,7 +10,7 @@
 
 BLOCK_LEN = 128
 LANES = 128
-VMEM_BYTES = 40 * 1024 * 1024
+MIB = 1024 * 1024
 
 
 def factors(n):
@@ -83,7 +83,9 @@
             pltpu.VMEM((slots, depth, tile), jnp.bfloat16),
             pltpu.SemaphoreType.DMA((slots + 1,)),
         ],
-        compiler_params=pltpu.CompilerParams(vmem_limit_bytes=VMEM_BYTES),
+        compiler_params=pltpu.CompilerParams(
+            vmem_limit_bytes=40 * MIB
+        ),
         cost_estimate=pl.CostEstimate(
             flops=2 * rows * depth * local * len(targets),
             bytes_accessed=2 * depth * local * len(targets),
@@ -103,12 +105,14 @@
 
 
 def stream_kernel(count, residual_ref, gain_ref, bias_ref, *refs):
-    terms, (half_ref, shared_ref) = refs[:count], refs[count:]
+    terms, (half_ref, sent_ref) = refs[:count], refs[count:]
     stream = residual_ref[...].astype(jnp.float32)
     for term in terms:
         stream = stream + term[...].astype(jnp.float32)
     rows, width = stream.shape
-    half_ref[...] = stream.astype(half_ref.dtype)
+    half = stream.astype(half_ref.dtype)
+    half_ref[...] = half
+    sent_ref[:, :width] = half
     mean = jnp.sum(stream, axis=1, keepdims=True) / width
     square = jnp.sum((stream - mean) ** 2, axis=1, keepdims=True)
     lane = lax.broadcasted_iota(jnp.int32, (rows, LANES), 1)
@@ -119,27 +123,23 @@
         table = jnp.concatenate(
             [table, jnp.zeros((LANES - rows, LANES), jnp.float32)], axis=0
         )
-    stats = jnp.transpose(table)
-    fill = shared_ref.shape[1] - 2 * gain_ref.shape[0]
-    shared = jnp.concatenate(
-        [stats[:fill], gain_ref[...].astype(jnp.float32), bias_ref[...].astype(jnp.float32)],
+    stats = jnp.transpose(table)[: rows - 2 * gain_ref.shape[0]]
+    sent_ref[:, width:] = jnp.concatenate(
+        [stats, gain_ref[...].astype(jnp.float32), bias_ref[...].astype(jnp.float32)],
         axis=0,
-    ).astype(jnp.bfloat16)
-    for d in range(shared_ref.shape[0]):
-        shared_ref[d] = shared
-
-
-def own_stream(residual, gain, bias, terms, n):
+    ).astype(sent_ref.dtype)
+
+
+def own_stream(residual, gain, bias, terms):
     rows, local = residual.shape
     blocks = local // LANES
-    height = (8 + 2 * blocks + 15) // 16 * 16
     return pl.pallas_call(
         functools.partial(stream_kernel, len(terms)),
         out_shape=(
             jax.ShapeDtypeStruct((rows, local), jnp.bfloat16),
-            jax.ShapeDtypeStruct((n, height, LANES), jnp.bfloat16),
-        ),
-        compiler_params=pltpu.CompilerParams(vmem_limit_bytes=VMEM_BYTES),
+            jax.ShapeDtypeStruct((rows, local + LANES), jnp.bfloat16),
+        ),
+        compiler_params=pltpu.CompilerParams(vmem_limit_bytes=8 * MIB),
         cost_estimate=pl.CostEstimate(
             flops=20 * rows * local, bytes_accessed=16 * rows * local, transcendentals=0
         ),
@@ -147,47 +147,50 @@
     )(residual, gain.reshape(blocks, LANES), bias.reshape(blocks, LANES), *terms)
 
 
-def moments_kernel(local, passed, shared_ref, *refs):
-    out_ref = refs[passed]
-    n = shared_ref.shape[0]
-    rows = out_ref.shape[0]
+def nothing_kernel(*refs):
+    del refs
+
+
+def first_of_all(piece, *after):
+    anywhere = pl.BlockSpec(memory_space=pl.ANY)
+    return pl.pallas_call(
+        nothing_kernel,
+        out_shape=jax.ShapeDtypeStruct(piece.shape, piece.dtype),
+        in_specs=[anywhere] * (1 + len(after)),
+        out_specs=anywhere,
+        input_output_aliases={0: 0},
+        compiler_params=pltpu.CompilerParams(vmem_limit_bytes=MIB),
+        cost_estimate=pl.CostEstimate(
+            flops=10**10, bytes_accessed=10**8, transcendentals=0
+        ),
+        name="first_of_all",
+    )(piece, *after)
+
+
+def moments(pieces, local):
+    rows = pieces[0].shape[0]
     means, spread = [], jnp.zeros((1, LANES), jnp.float32)
-    for d in range(n):
-        stats = shared_ref[d, 0:8].astype(jnp.float32)
+    for piece in pieces:
+        stats = piece[0:8, local:].astype(jnp.float32)
         means.append(stats[0:1] + stats[1:2] + stats[2:3])
         spread = spread + (stats[3:4] + stats[4:5] + stats[5:6])
-    centre = sum(means) / n
+    centre = sum(means) / len(means)
     for mean in means:
         spread = spread + local * ((mean - centre) * (mean - centre))
-    inverse = lax.rsqrt(spread / (n * local) + 1e-05)
+    inverse = lax.rsqrt(spread / (len(means) * local) + 1e-05)
     row = lax.broadcasted_iota(jnp.int32, (LANES, LANES), 0)
     table = jnp.where(row == 0, centre, jnp.where(row == 1, inverse, 0.0))
-    out_ref[...] = jnp.transpose(table)[:rows]
-
-
-def moments(shared, passed, rows, local):
-    vmem = pl.BlockSpec(memory_space=pltpu.VMEM)
-    anywhere = [pl.BlockSpec(memory_space=pl.ANY)] * len(passed)
-    columns, *passed = pl.pallas_call(
-        functools.partial(moments_kernel, local, len(passed)),
-        out_shape=[jax.ShapeDtypeStruct((rows, LANES), jnp.float32)]
-        + [jax.ShapeDtypeStruct(p.shape, p.dtype) for p in passed],
-        in_specs=[vmem] + anywhere,
-        out_specs=[vmem] + anywhere,
-        input_output_aliases={1 + i: 1 + i for i in range(len(passed))},
-        name="moments",
-    )(shared, *passed)
-    return columns, passed
-
-
-def coded_rows(piece_ref, moments_ref, scaling, table):
-    blocks = piece_ref.shape[1] // BLOCK_LEN
+    table = jnp.transpose(table)[:rows]
+    return table[:, 0:1], table[:, 1:2]
+
+
+def coded_rows(piece, local, centre, inverse, table):
+    rows, blocks = piece.shape[0], local // BLOCK_LEN
     unit = 1.0 / math.sqrt(BLOCK_LEN)
-    centre = moments_ref[:, 0:1]
-    inverse = moments_ref[:, 1:2]
+    scaling = piece[rows - 2 * blocks :, local:].astype(jnp.float32)
     normal = []
     for b in range(blocks):
-        block = piece_ref[:, b * BLOCK_LEN : (b + 1) * BLOCK_LEN].astype(jnp.float32)
+        block = piece[:, b * BLOCK_LEN : (b + 1) * BLOCK_LEN].astype(jnp.float32)
         block = (block - centre) * inverse
         normal.append(block * scaling[b : b + 1] + scaling[blocks + b : blocks + b + 1])
     normal = jnp.concatenate(normal, axis=0)
@@ -203,26 +206,23 @@
     return back.astype(jnp.bfloat16)
 
 
-def finish_kernel(places, splits, moments_ref, shared_ref, *refs):
+def finish_kernel(places, splits, *refs):
     count = len(places)
-    pieces = refs[:count]
-    out_ref, done_ref, semaphores = refs[-3:]
-    rows, width = pieces[0].shape
-    blocks = width // BLOCK_LEN
+    pieces, (out_ref, done_ref, semaphores) = refs[:count], refs[count:]
+    rows = pieces[0].shape[0]
+    width = done_ref.shape[2]
     table = signs(BLOCK_LEN)
+    centre, inverse = moments(pieces, width)
     me = lax.axis_index("tensor")
     outer, inner = me // splits[1], lax.rem(me, splits[1])
     copies = []
     for p, (k, j) in enumerate(places):
-        owner = jnp.bitwise_xor(outer, k) * splits[1] + jnp.bitwise_xor(inner, j)
-        shared = shared_ref[owner].astype(jnp.float32)
-        back = coded_rows(
-            pieces[p], moments_ref, shared[shared.shape[0] - 2 * blocks :], table
-        )
-        for b in range(blocks):
+        back = coded_rows(pieces[p], width, centre, inverse, table)
+        for b in range(width // BLOCK_LEN):
             done_ref[p, :, b * BLOCK_LEN : (b + 1) * BLOCK_LEN] = back[
                 b * rows : (b + 1) * rows
             ]
+        owner = jnp.bitwise_xor(outer, k) * splits[1] + jnp.bitwise_xor(inner, j)
         columns = pl.ds(pl.multiple_of(owner * width, LANES), width)
         copy = pltpu.make_async_copy(
             done_ref.at[p], out_ref.at[:, columns], semaphores.at[p]
@@ -233,31 +233,27 @@
         copy.wait()
 
 
-def finish(whole, places, splits, pieces, columns, shared):
-    rows, local = pieces[0].shape
+def finish(places, splits, pieces, local):
+    rows = pieces[0].shape[0]
     count = len(pieces)
-    n = shared.shape[0]
-    earlier = [] if whole is None else [whole]
     vmem = pl.BlockSpec(memory_space=pltpu.VMEM)
     return pl.pallas_call(
         functools.partial(finish_kernel, places, splits),
-        out_shape=jax.ShapeDtypeStruct((rows, n * local), jnp.bfloat16),
-        in_specs=[vmem] * (2 + count)
-        + [pl.BlockSpec(memory_space=pl.ANY)] * len(earlier),
+        out_shape=jax.ShapeDtypeStruct((rows, count * local), jnp.bfloat16),
+        in_specs=[vmem] * count,
         out_specs=pl.BlockSpec(memory_space=pl.ANY),
         scratch_shapes=[
             pltpu.VMEM((count, rows, local), jnp.bfloat16),
             pltpu.SemaphoreType.DMA((count,)),
         ],
-        input_output_aliases={2 + count: 0} if earlier else {},
-        compiler_params=pltpu.CompilerParams(vmem_limit_bytes=VMEM_BYTES),
+        compiler_params=pltpu.CompilerParams(vmem_limit_bytes=16 * MIB),
         cost_estimate=pl.CostEstimate(
             flops=8 * BLOCK_LEN * rows * local * count,
             bytes_accessed=4 * rows * local * count,
             transcendentals=0,
         ),
         name="finish",
-    )(columns, shared, *pieces, *earlier)
+    )(*pieces)
 
 
 def body(attended, out_weight, residual, norm_gain, norm_bias):
@@ -293,38 +289,29 @@
                 total = total + term.astype(jnp.float32)
             total = total.astype(jnp.bfloat16)
             after = [total]
-            terms[k ^ bit].append(lax.ppermute(total, "tensor", jump[bit]))
-
-    stream_out, shared = own_stream(residual, norm_gain, norm_bias, terms[0], n)
-    shared = lax.all_to_all(shared, "tensor", 0, 0, tiled=True)
-    have = {0: stream_out}
+            joined_to = lax.ppermute(total, "tensor", jump[bit])
+            if k == nz // 2:
+                joined_to = first_of_all(joined_to)
+            terms[k ^ bit].append(joined_to)
+
+    stream_out, sent = own_stream(residual, norm_gain, norm_bias, terms[0])
+    have = {0: sent}
+    crossed = {}
     top = nz // 2
-    have[top] = lax.ppermute(stream_out, "tensor", jump[top])
-    have[1] = lax.ppermute(stream_out, "tensor", jump[1])
-    early = away[0] + away[1]
-    crossed = {(k, j): lax.ppermute(have[k], "tensor", swap[j]) for k, j in early}
-    columns, passed = moments(
-        shared, [have[top]] + [crossed[p] for p in early], rows, local
-    )
-    have[top] = passed[0]
-    crossed.update(zip(early, passed[1:]))
-    for k in sorted(range(2, nz), key=lambda k: (-(k & -k), k)):
+    have[top] = lax.ppermute(sent, "tensor", jump[top])
+    have[1] = lax.ppermute(sent, "tensor", jump[1])
+    for p in away[0] + away[1]:
+        crossed[p] = lax.ppermute(have[p[0]], "tensor", swap[p[1]])
+    have[top] = first_of_all(have[top], *crossed.values())
+    for k in sorted(range(2, nz), key=lambda k: (k & (k - 1), k)):
         if k != top:
             have[k] = lax.ppermute(have[k ^ (k & -k)], "tensor", jump[k & -k])
-
-    whole = None
-    for k in range(nz):
-        places = here[k] + away[k]
-        pieces = [have[k]] + [
-            crossed.get(p) if p in crossed else lax.ppermute(have[k], "tensor", swap[p[1]])
-            for p in away[k]
-        ]
-        if k < nz - 1:
-            whole = finish(whole, places, splits, pieces, columns, shared)
-        else:
-            for place, piece in zip(places, pieces):
-                whole = finish(whole, [place], splits, [piece], columns, shared)
-    return (stream_out, whole)
+    places = [place for k in range(nz) for place in here[k] + away[k]]
+    for p in places:
+        if p[1] and p not in crossed:
+            crossed[p] = lax.ppermute(have[p[0]], "tensor", swap[p[1]])
+    pieces = [crossed[p] if p[1] else have[p[0]] for p in places]
+    return (stream_out, finish(places, splits, pieces, local))
 
 
 def solution(mesh):

time: 87.7 us -> 76.4 us (0.87)
  waiting for transfers between devices: 22.5 us -> 34.8 us
  blocking collectives: 11.1 us -> 0 us
  Pallas kernels: 27.2 us -> 22.1 us
  local copies, waits for them, and re-layouts: 5.95 us -> 0.92 us
  starting transfers between devices: 19.7 us -> 17.5 us
    ppermute x9, waiting for transfers between devices: 12.7 us -> 26.5 us  [the longest x4 10.2 us: body(): crossed[p] = lax.ppermute(have[p[0]], 'tensor', swap[p[1]])]
    all_to_all x1 -> x0, blocking collectives: 11.1 us -> none  [body(): shared = lax.all_to_all(shared, 'tensor', 0, 0, tiled=True)]
    unnamed x30 -> x8, local copies, waits for them, and re-layouts: 5.95 us -> 0.92 us
    pallas_call x5 -> x1, Pallas kernels: 8.73 us -> 5.3 us  [finish(): pl.pallas_call(functools.partial(finish_kernel, places, splits), out_shap...]
    ppermute x9, starting transfers between devices: 14 us -> 12.3 us  [the longest x3 6.18 us: body(): joined_to = lax.ppermute(total, 'tensor', jump[bit])]
    ppermute x4, waiting for transfers between devices: 4.42 us -> 2.77 us  [body(): terms[k].append(lax.ppermute(result, 'tensor', swap[j]) if j else result)]
    pallas_call x1 -> x2, Pallas kernels: 1.63 us -> 0.01 us  [first_of_all(): pl.pallas_call(nothing_kernel, out_shape=jax.ShapeDtypeStruct(piece.shape...]
  transfers between devices with their start and end apart: 14 -> 14, of which waited for: 5 -> 10; matrix products, arithmetic and copies ran while one was open for 0% -> 0% of each run, Pallas kernels for 23% -> 17%
where the time goes in v6:
time: 76.4 us; the launch traced here: 76.3 us
  waiting for transfers between devices  34.8 us (46%)
  Pallas kernels  22.1 us (29%)
  starting transfers between devices  17.5 us (23%)
  local copies, waits for them, and re-layouts  0.92 us (1%)
    pallas_call x4, Pallas kernels, products(): pl.pallas_call(functools.partial(product_kernel, targets, splits, local,...  15.8 us
    ppermute x4, waiting for transfers between devices, body(): crossed[p] = lax.ppermute(have[p[0]], 'tensor', swap[p[1]])  10.2 us
    ppermute x1, waiting for transfers between devices, body(): have[1] = lax.ppermute(sent, 'tensor', jump[1])  7.91 us
    ppermute x3, waiting for transfers between devices, body(): joined_to = lax.ppermute(total, 'tensor', jump[bit])  6.78 us
    ppermute x3, starting transfers between devices, body(): joined_to = lax.ppermute(total, 'tensor', jump[bit])  6.18 us
    ppermute x1, waiting for transfers between devices, body(): have[k] = lax.ppermute(have[k ^ k & -k], 'tensor', jump[k & -k])  5.58 us
    pallas_call x1, Pallas kernels, finish(): pl.pallas_call(functools.partial(finish_kernel, places, splits), out_shap...  5.3 us
    ppermute x4, starting transfers between devices, body(): terms[k].append(lax.ppermute(result, 'tensor', swap[j]) if j else result)  5.22 us
  transfers between devices with their start and end apart: 14, of which 10 were waited for; matrix products, arithmetic and copies ran while one was open for 0% of the time, Pallas kernels for 17%

profile of v6, /device:TPU:0, one launch (start us, length us, event | category | flops | bytes accessed | tf_op | source)
XLA Modules:
  0.0 76.3 jit_solution(3358559182217898529)
XLA Ops:
  0.6 0.0 copy-start
  0.6 0.9 %copy-done = bf16[64,1024]{1,0:T(8,128)(2,1)S(1)} copy-done((bf16[64,1024]{1,0:T(8,128)(2,1)S(1)}, bf16[64,1024]{1,0:T(8,128)(2,1)}, u32[]{:S(2)}) %copy-start) | copy-done | bytes 131096
  1.5 2.7 %products.4.refs_0_ = bf16[64,2048]{1,0:T(8,128)(2,1)S(1)} custom-call(bf16[64,1024]{1,0:T(8,128)(2,1)S(1)} %copy-done, bf16[1024,16384]{1,0:T(8,128)(2,1)} %weight_ref.7), custom_call_target="tpu_custom_call" | custom-call | flops 268435456 | bytes 4194304 | tf_op jit(solution)/shard_map/products/pallas_call | solution.py:72
  4.2 3.0 %collective-permute-start = (bf16[64,2048]{1,0:T(8,128)(2,1)S(1)}, bf16[64,2048]{1,0:T(8,128)(2,1)S(1)}, u32[]{:S(2)}, u32[]{:S(2)}) collective-permute-start(bf16[64,2048]{1,0:T(8,128)(2,1)S(1)} %products.4.refs_0_), channel_id=1, source_target_pairs={{0,1},{1,0},{2,3},{3,2},{4,5},{5,4},{6,7},{7,6},{8,9},{9,8},{10,11... | collective-permute-start | bytes 786440 | tf_op jit(solution)/shard_map/ppermute | solution.py:284
  7.2 5.2 %products.5 = (bf16[64,2048]{1,0:T(8,128)(2,1)S(1)}, bf16[64,2048]{1,0:T(8,128)(2,1)S(1)}, f32[64,2048]{1,0:T(8,128)S(1)}) custom-call(bf16[64,1024]{1,0:T(8,128)(2,1)S(1)} %copy-done, bf16[1024,16384]{1,0:T(8,128)(2,1)} %weight_ref.7, bf16[64,2048]{1,0:T(8,128)(2,1)S(1)} %products.4.refs_0_), custom_call_target="tpu_custom_call" | custom-call | flops 805306368 | bytes 12582912 | tf_op jit(solution)/shard_map/products/pallas_call | solution.py:72
  12.5 0.1 collective-permute-start.2
  12.6 0.9 %collective-permute-done = bf16[64,2048]{1,0:T(8,128)(2,1)S(1)} collective-permute-done((bf16[64,2048]{1,0:T(8,128)(2,1)S(1)}, bf16[64,2048]{1,0:T(8,128)(2,1)S(1)}, u32[]{:S(2)}, u32[]{:S(2)}) %collective-permute-start) | collective-permute-done | bytes 262176 | tf_op jit(solution)/shard_map/ppermute | solution.py:284
  13.6 1.9 %collective-permute-start.3 = (bf16[64,2048]{1,0:T(8,128)(2,1)S(1)}, bf16[64,2048]{1,0:T(8,128)(2,1)S(1)}, u32[]{:S(2)}, u32[]{:S(2)}) collective-permute-start(bf16[64,2048]{1,0:T(8,128)(2,1)S(1)} %add_convert_fusion.2.refs_0_), channel_id=1, source_target_pairs={{0,2},{1,3},{2,0},{3,1},{4,6},{5,7},{6,4},{7,5},{8,10},{9,11},{10,... | collective-permute-start | bytes 786440 | tf_op jit(solution)/shard_map/ppermute | solution.py:292
  15.5 1.5 %collective-permute-start.5 = (bf16[64,2048]{1,0:T(8,128)(2,1)S(1)}, bf16[64,2048]{1,0:T(8,128)(2,1)S(1)}, u32[]{:S(2)}, u32[]{:S(2)}) collective-permute-start(bf16[64,2048]{1,0:T(8,128)(2,1)S(1)} %get-tuple-element.14), channel_id=1, source_target_pairs={{0,1},{1,0},{2,3},{3,2},{4,5},{5,4},{6,7},{7,6},{8,9},{9,8},{10,11... | collective-permute-start | bytes 786440 | tf_op jit(solution)/shard_map/ppermute | solution.py:284
  17.0 5.2 %products.6 = (bf16[64,2048]{1,0:T(8,128)(2,1)S(1)}, f32[64,2048]{1,0:T(8,128)S(1)}, f32[64,2048]{1,0:T(8,128)S(1)}) custom-call(bf16[64,1024]{1,0:T(8,128)(2,1)S(1)} %copy-done, bf16[1024,16384]{1,0:T(8,128)(2,1)} %weight_ref.7, bf16[64,2048]{1,0:T(8,128)(2,1)S(1)} %add_convert_fusion.2.refs_0_), custom_call_target="tpu_custom_call" | custom-call | flops 805306368 | bytes 12582912 | tf_op jit(solution)/shard_map/products/pallas_call | solution.py:72
  22.2 0.6 collective-permute-start.1
  22.8 0.0 collective-permute-done.2
  22.8 0.0 collective-permute-done.3
  22.8 0.1 add_convert_fusion.1
  22.9 2.7 %collective-permute-start.4 = (bf16[64,2048]{1,0:T(8,128)(2,1)S(1)}, bf16[64,2048]{1,0:T(8,128)(2,1)S(1)}, u32[]{:S(2)}, u32[]{:S(2)}) collective-permute-start(bf16[64,2048]{1,0:T(8,128)(2,1)S(1)} %add_convert_fusion.1), channel_id=1, source_target_pairs={{0,4},{1,5},{2,6},{3,7},{4,0},{5,1},{6,2},{7,3},{8,12},{9,13},{10,... | collective-permute-start | bytes 786440 | tf_op jit(solution)/shard_map/ppermute | solution.py:292
  25.6 1.8 %collective-permute-done.5 = bf16[64,2048]{1,0:T(8,128)(2,1)S(1)} collective-permute-done((bf16[64,2048]{1,0:T(8,128)(2,1)S(1)}, bf16[64,2048]{1,0:T(8,128)(2,1)S(1)}, u32[]{:S(2)}, u32[]{:S(2)}) %collective-permute-start.5) | collective-permute-done | bytes 262176 | tf_op jit(solution)/shard_map/ppermute | solution.py:284
  27.4 0.0 copy-start.1
  27.4 0.0 copy-start.2
  27.5 0.0 copy-start.3
  27.5 1.6 %collective-permute-start.6 = (bf16[64,2048]{1,0:T(8,128)(2,1)S(1)}, bf16[64,2048]{1,0:T(8,128)(2,1)S(1)}, u32[]{:S(2)}, u32[]{:S(2)}) collective-permute-start(bf16[64,2048]{1,0:T(8,128)(2,1)S(1)} %add_convert_fusion.refs_0_), channel_id=1, source_target_pairs={{0,2},{1,3},{2,0},{3,1},{4,6},{5,7},{6,4},{7,5},{8,10},{9,11},{10,... | collective-permute-start | bytes 786440 | tf_op jit(solution)/shard_map/ppermute | solution.py:292
  29.1 2.7 %products.7.refs_3_ = f32[64,2048]{1,0:T(8,128)S(1)} custom-call(bf16[64,1024]{1,0:T(8,128)(2,1)S(1)} %copy-done, bf16[1024,16384]{1,0:T(8,128)(2,1)} %weight_ref.7, bf16[64,2048]{1,0:T(8,128)(2,1)S(1)} %add_convert_fusion.refs_0_), custom_call_target="tpu_custom_call" | custom-call | flops 268435456 | bytes 4194304 | tf_op jit(solution)/shard_map/products/pallas_call | solution.py:72
  31.8 4.1 %collective-permute-done.4.refs_0_ = bf16[64,2048]{1,0:T(8,128)(2,1)S(1)} collective-permute-done((bf16[64,2048]{1,0:T(8,128)(2,1)S(1)}, bf16[64,2048]{1,0:T(8,128)(2,1)S(1)}, u32[]{:S(2)}, u32[]{:S(2)}) %collective-permute-start.4) | collective-permute-done | bytes 262176 | tf_op jit(solution)/shard_map/ppermute | solution.py:292
  35.9 0.0 collective-permute-done.1.refs_0_
  35.9 2.7 %collective-permute-done.6.refs_2_ = bf16[64,2048]{1,0:T(8,128)(2,1)S(1)} collective-permute-done((bf16[64,2048]{1,0:T(8,128)(2,1)S(1)}, bf16[64,2048]{1,0:T(8,128)(2,1)S(1)}, u32[]{:S(2)}, u32[]{:S(2)}) %collective-permute-start.6) | collective-permute-done | bytes 262176 | tf_op jit(solution)/shard_map/ppermute | solution.py:292
  38.6 0.0 copy-done.1
  38.6 0.0 copy-done.2
  38.6 0.0 copy-done.3
  38.6 1.0 %own_stream.1 = (bf16[64,2048]{1,0:T(8,128)(2,1)}, bf16[64,2176]{1,0:T(8,128)(2,1)S(1)}) custom-call(bf16[64,2048]{1,0:T(8,128)(2,1)S(1)} %copy-done.1, bf16[16,128]{1,0:T(8,128)(2,1)S(1)} %bitcast.2, bf16[16,128]{1,0:T(8,128)(2,1)S(1)} %bitcast.3, bf16[64,2048]{1,0:T(8,128)(2,1)S(1)} %collective-permute-done.1.refs_0_, ...), custom_call_target="tpu_custom_call" | custom-call | flops 2621440 | bytes 2097152 | tf_op jit(solution)/shard_map/own_stream/pallas_call | solution.py:136
  39.6 0.0 collective-permute-start.8
  39.6 3.0 %collective-permute-start.10 = (bf16[64,2176]{1,0:T(8,128)(2,1)S(1)}, bf16[64,2176]{1,0:T(8,128)(2,1)S(1)}, u32[]{:S(2)}, u32[]{:S(2)}) collective-permute-start(bf16[64,2176]{1,0:T(8,128)(2,1)S(1)} %get-tuple-element.17.refs_0_), channel_id=1, source_target_pairs={{0,4},{1,5},{2,6},{3,7},{4,0},{5,1},{6,2},{7,3},{8,12},{9,13},{10,... | collective-permute-start | bytes 835592 | tf_op jit(solution)/shard_map/ppermute | solution.py:301
  42.6 0.6 collective-permute-start.7
  43.2 7.9 %collective-permute-done.8.refs_2_ = bf16[64,2176]{1,0:T(8,128)(2,1)S(1)} collective-permute-done((bf16[64,2176]{1,0:T(8,128)(2,1)S(1)}, bf16[64,2176]{1,0:T(8,128)(2,1)S(1)}, u32[]{:S(2)}, u32[]{:S(2)}) %collective-permute-start.8) | collective-permute-done | bytes 278560 | tf_op jit(solution)/shard_map/ppermute | solution.py:302
  51.1 0.5 collective-permute-start.9
  51.7 1.6 %collective-permute-done.10.refs_0_ = bf16[64,2176]{1,0:T(8,128)(2,1)S(1)} collective-permute-done((bf16[64,2176]{1,0:T(8,128)(2,1)S(1)}, bf16[64,2176]{1,0:T(8,128)(2,1)S(1)}, u32[]{:S(2)}, u32[]{:S(2)}) %collective-permute-start.10) | collective-permute-done | bytes 278560 | tf_op jit(solution)/shard_map/ppermute | solution.py:301
  53.3 0.0 collective-permute-done.7.refs_1_
  53.3 4.6 %collective-permute-done.9.refs_2_.refs_3_ = bf16[64,2176]{1,0:T(8,128)(2,1)S(1)} collective-permute-done((bf16[64,2176]{1,0:T(8,128)(2,1)S(1)}, bf16[64,2176]{1,0:T(8,128)(2,1)S(1)}, u32[]{:S(2)}, u32[]{:S(2)}) %collective-permute-start.9) | collective-permute-done | bytes 278560 | tf_op jit(solution)/shard_map/ppermute | solution.py:304
  57.9 0.0 collective-permute-start.12
  57.9 1.0 %collective-permute-start.11 = (bf16[64,2176]{1,0:T(8,128)(2,1)S(1)}, bf16[64,2176]{1,0:T(8,128)(2,1)S(1)}, u32[]{:S(2)}, u32[]{:S(2)}) collective-permute-start(bf16[64,2176]{1,0:T(8,128)(2,1)S(1)} %first_of_all.3.refs_4_), channel_id=1, source_target_pairs={{0,1},{1,0},{2,3},{3,2},{4,5},{5,4},{6,7},{7,6},{8,9},{9,8},{10,11... | collective-permute-start | bytes 835592 | tf_op jit(solution)/shard_map/ppermute | solution.py:312
  58.9 5.6 %collective-permute-done.12.refs_6_ = bf16[64,2176]{1,0:T(8,128)(2,1)S(1)} collective-permute-done((bf16[64,2176]{1,0:T(8,128)(2,1)S(1)}, bf16[64,2176]{1,0:T(8,128)(2,1)S(1)}, u32[]{:S(2)}, u32[]{:S(2)}) %collective-permute-start.12) | collective-permute-done | bytes 278560 | tf_op jit(solution)/shard_map/ppermute | solution.py:308
  64.4 1.0 %collective-permute-start.13 = (bf16[64,2176]{1,0:T(8,128)(2,1)S(1)}, bf16[64,2176]{1,0:T(8,128)(2,1)S(1)}, u32[]{:S(2)}, u32[]{:S(2)}) collective-permute-start(bf16[64,2176]{1,0:T(8,128)(2,1)S(1)} %collective-permute-done.12.refs_6_), channel_id=1, source_target_pairs={{0,1},{1,0},{2,3},{3,2},{4,5},{5,4},{6,7},{7,6},{8,9},{9,8},{10,11... | collective-permute-start | bytes 835592 | tf_op jit(solution)/shard_map/ppermute | solution.py:312
  65.4 0.6 collective-permute-done.11.refs_5_
  66.0 5.0 %collective-permute-done.13.refs_7_ = bf16[64,2176]{1,0:T(8,128)(2,1)S(1)} collective-permute-done((bf16[64,2176]{1,0:T(8,128)(2,1)S(1)}, bf16[64,2176]{1,0:T(8,128)(2,1)S(1)}, u32[]{:S(2)}, u32[]{:S(2)}) %collective-permute-start.13) | collective-permute-done | bytes 278560 | tf_op jit(solution)/shard_map/ppermute | solution.py:312
  71.0 5.3 %finish.1 = bf16[64,16384]{1,0:T(8,128)(2,1)} custom-call(bf16[64,2176]{1,0:T(8,128)(2,1)S(1)} %get-tuple-element.17.refs_0_, bf16[64,2176]{1,0:T(8,128)(2,1)S(1)} %collective-permute-done.7.refs_1_, bf16[64,2176]{1,0:T(8,128)(2,1)S(1)} %collective-permute-done.8.refs_2_, bf16[64,2176]{1,0:T(8,128)(2,1)S(1)} %collective-permute-done.9.refs_2_.refs_3_, ...), custom_call_target="tpu_custom_call" | custom-call | flops 1073741824 | bytes 4194304 | tf_op jit(solution)/shard_map/finish/pallas_call | solution.py:240
  (4 shorter events, 0.1 us)
Async XLA Ops:
  0.6 0.9 %copy-start = (bf16[64,1024]{1,0:T(8,128)(2,1)S(1)}, bf16[64,1024]{1,0:T(8,128)(2,1)}, u32[]{:S(2)}) copy-start(bf16[64,1024]{1,0:T(8,128)(2,1)} %rows_ref.7) | copy-start | bytes 393220
  4.2 9.3 %collective-permute-start = (bf16[64,2048]{1,0:T(8,128)(2,1)S(1)}, bf16[64,2048]{1,0:T(8,128)(2,1)S(1)}, u32[]{:S(2)}, u32[]{:S(2)}) collective-permute-start(bf16[64,2048]{1,0:T(8,128)(2,1)S(1)} %products.4.refs_0_), channel_id=1, source_target_pairs={{0,1},{1,0},{2,3},{3,2},{4,5},{5,4},{6,7},{7,6},{8,9},{9,8},{10,11... | collective-permute-start | bytes 786440 | tf_op jit(solution)/shard_map/ppermute | solution.py:284
  12.5 10.3 %collective-permute-start.2 = (bf16[64,2048]{1,0:T(8,128)(2,1)S(1)}, bf16[64,2048]{1,0:T(8,128)(2,1)S(1)}, u32[]{:S(2)}, u32[]{:S(2)}) collective-permute-start(bf16[64,2048]{1,0:T(8,128)(2,1)S(1)} %get-tuple-element.12), channel_id=1, source_target_pairs={{0,1},{1,0},{2,3},{3,2},{4,5},{5,4},{6,7},{7,6},{8,9},{9,8},{10,11... | collective-permute-start | bytes 786440 | tf_op jit(solution)/shard_map/ppermute | solution.py:284
  13.6 9.2 %collective-permute-start.3 = (bf16[64,2048]{1,0:T(8,128)(2,1)S(1)}, bf16[64,2048]{1,0:T(8,128)(2,1)S(1)}, u32[]{:S(2)}, u32[]{:S(2)}) collective-permute-start(bf16[64,2048]{1,0:T(8,128)(2,1)S(1)} %add_convert_fusion.2.refs_0_), channel_id=1, source_target_pairs={{0,2},{1,3},{2,0},{3,1},{4,6},{5,7},{6,4},{7,5},{8,10},{9,11},{10,... | collective-permute-start | bytes 786440 | tf_op jit(solution)/shard_map/ppermute | solution.py:292
  15.5 11.9 %collective-permute-start.5 = (bf16[64,2048]{1,0:T(8,128)(2,1)S(1)}, bf16[64,2048]{1,0:T(8,128)(2,1)S(1)}, u32[]{:S(2)}, u32[]{:S(2)}) collective-permute-start(bf16[64,2048]{1,0:T(8,128)(2,1)S(1)} %get-tuple-element.14), channel_id=1, source_target_pairs={{0,1},{1,0},{2,3},{3,2},{4,5},{5,4},{6,7},{7,6},{8,9},{9,8},{10,11... | collective-permute-start | bytes 786440 | tf_op jit(solution)/shard_map/ppermute | solution.py:284
  22.2 13.7 %collective-permute-start.1 = (bf16[64,2048]{1,0:T(8,128)(2,1)S(1)}, bf16[64,2048]{1,0:T(8,128)(2,1)S(1)}, u32[]{:S(2)}, u32[]{:S(2)}) collective-permute-start(bf16[64,2048]{1,0:T(8,128)(2,1)S(1)} %get-tuple-element.11), channel_id=1, source_target_pairs={{0,1},{1,0},{2,3},{3,2},{4,5},{5,4},{6,7},{7,6},{8,9},{9,8},{10,11... | collective-permute-start | bytes 786440 | tf_op jit(solution)/shard_map/ppermute | solution.py:284
  22.9 13.0 %collective-permute-start.4 = (bf16[64,2048]{1,0:T(8,128)(2,1)S(1)}, bf16[64,2048]{1,0:T(8,128)(2,1)S(1)}, u32[]{:S(2)}, u32[]{:S(2)}) collective-permute-start(bf16[64,2048]{1,0:T(8,128)(2,1)S(1)} %add_convert_fusion.1), channel_id=1, source_target_pairs={{0,4},{1,5},{2,6},{3,7},{4,0},{5,1},{6,2},{7,3},{8,12},{9,13},{10,... | collective-permute-start | bytes 786440 | tf_op jit(solution)/shard_map/ppermute | solution.py:292
  27.4 11.1 %copy-start.1 = (bf16[64,2048]{1,0:T(8,128)(2,1)S(1)}, bf16[64,2048]{1,0:T(8,128)(2,1)}, u32[]{:S(2)}) copy-start(bf16[64,2048]{1,0:T(8,128)(2,1)} %residual_ref.1) | copy-start | bytes 786436
  27.4 11.1 %copy-start.2 = (bf16[2048]{0:T(1024)(128)(2,1)S(1)}, bf16[2048]{0:T(1024)(128)(2,1)}, u32[]{:S(2)}) copy-start(bf16[2048]{0:T(1024)(128)(2,1)} %param.8) | copy-start | bytes 12292
  27.5 11.1 %copy-start.3 = (bf16[2048]{0:T(1024)(128)(2,1)S(1)}, bf16[2048]{0:T(1024)(128)(2,1)}, u32[]{:S(2)}) copy-start(bf16[2048]{0:T(1024)(128)(2,1)} %param.9) | copy-start | bytes 12292
  27.5 11.1 %collective-permute-start.6 = (bf16[64,2048]{1,0:T(8,128)(2,1)S(1)}, bf16[64,2048]{1,0:T(8,128)(2,1)S(1)}, u32[]{:S(2)}, u32[]{:S(2)}) collective-permute-start(bf16[64,2048]{1,0:T(8,128)(2,1)S(1)} %add_convert_fusion.refs_0_), channel_id=1, source_target_pairs={{0,2},{1,3},{2,0},{3,1},{4,6},{5,7},{6,4},{7,5},{8,10},{9,11},{10,... | collective-permute-start | bytes 786440 | tf_op jit(solution)/shard_map/ppermute | solution.py:292
  39.6 11.6 %collective-permute-start.8 = (bf16[64,2176]{1,0:T(8,128)(2,1)S(1)}, bf16[64,2176]{1,0:T(8,128)(2,1)S(1)}, u32[]{:S(2)}, u32[]{:S(2)}) collective-permute-start(bf16[64,2176]{1,0:T(8,128)(2,1)S(1)} %get-tuple-element.17.refs_0_), channel_id=1, source_target_pairs={{0,2},{1,3},{2,0},{3,1},{4,6},{5,7},{6,4},{7,5},{8,10},{9,11},{10,... | collective-permute-start | bytes 835592 | tf_op jit(solution)/shard_map/ppermute | solution.py:302
  39.6 13.7 %collective-permute-start.10 = (bf16[64,2176]{1,0:T(8,128)(2,1)S(1)}, bf16[64,2176]{1,0:T(8,128)(2,1)S(1)}, u32[]{:S(2)}, u32[]{:S(2)}) collective-permute-start(bf16[64,2176]{1,0:T(8,128)(2,1)S(1)} %get-tuple-element.17.refs_0_), channel_id=1, source_target_pairs={{0,4},{1,5},{2,6},{3,7},{4,0},{5,1},{6,2},{7,3},{8,12},{9,13},{10,... | collective-permute-start | bytes 835592 | tf_op jit(solution)/shard_map/ppermute | solution.py:301
  42.6 10.7 %collective-permute-start.7 = (bf16[64,2176]{1,0:T(8,128)(2,1)S(1)}, bf16[64,2176]{1,0:T(8,128)(2,1)S(1)}, u32[]{:S(2)}, u32[]{:S(2)}) collective-permute-start(bf16[64,2176]{1,0:T(8,128)(2,1)S(1)} %get-tuple-element.17.refs_0_), channel_id=1, source_target_pairs={{0,1},{1,0},{2,3},{3,2},{4,5},{5,4},{6,7},{7,6},{8,9},{9,8},{10,11... | collective-permute-start | bytes 835592 | tf_op jit(solution)/shard_map/ppermute | solution.py:304
  51.1 6.8 %collective-permute-start.9 = (bf16[64,2176]{1,0:T(8,128)(2,1)S(1)}, bf16[64,2176]{1,0:T(8,128)(2,1)S(1)}, u32[]{:S(2)}, u32[]{:S(2)}) collective-permute-start(bf16[64,2176]{1,0:T(8,128)(2,1)S(1)} %collective-permute-done.8.refs_2_), channel_id=1, source_target_pairs={{0,1},{1,0},{2,3},{3,2},{4,5},{5,4},{6,7},{7,6},{8,9},{9,8},{10,11... | collective-permute-start | bytes 835592 | tf_op jit(solution)/shard_map/ppermute | solution.py:304
  57.9 6.5 %collective-permute-start.12 = (bf16[64,2176]{1,0:T(8,128)(2,1)S(1)}, bf16[64,2176]{1,0:T(8,128)(2,1)S(1)}, u32[]{:S(2)}, u32[]{:S(2)}) collective-permute-start(bf16[64,2176]{1,0:T(8,128)(2,1)S(1)} %first_of_all.3.refs_4_), channel_id=1, source_target_pairs={{0,2},{1,3},{2,0},{3,1},{4,6},{5,7},{6,4},{7,5},{8,10},{9,11},{10,... | collective-permute-start | bytes 835592 | tf_op jit(solution)/shard_map/ppermute | solution.py:308
  57.9 8.1 %collective-permute-start.11 = (bf16[64,2176]{1,0:T(8,128)(2,1)S(1)}, bf16[64,2176]{1,0:T(8,128)(2,1)S(1)}, u32[]{:S(2)}, u32[]{:S(2)}) collective-permute-start(bf16[64,2176]{1,0:T(8,128)(2,1)S(1)} %first_of_all.3.refs_4_), channel_id=1, source_target_pairs={{0,1},{1,0},{2,3},{3,2},{4,5},{5,4},{6,7},{7,6},{8,9},{9,8},{10,11... | collective-permute-start | bytes 835592 | tf_op jit(solution)/shard_map/ppermute | solution.py:312
  64.4 6.5 %collective-permute-start.13 = (bf16[64,2176]{1,0:T(8,128)(2,1)S(1)}, bf16[64,2176]{1,0:T(8,128)(2,1)S(1)}, u32[]{:S(2)}, u32[]{:S(2)}) collective-permute-start(bf16[64,2176]{1,0:T(8,128)(2,1)S(1)} %collective-permute-done.12.refs_6_), channel_id=1, source_target_pairs={{0,1},{1,0},{2,3},{3,2},{4,5},{5,4},{6,7},{7,6},{8,9},{9,8},{10,11... | collective-permute-start | bytes 835592 | tf_op jit(solution)/shard_map/ppermute | solution.py:312

commit v7 on v6

--- a/solution.py
+++ b/solution.py
@@ -105,7 +105,7 @@
 
 
 def stream_kernel(count, residual_ref, gain_ref, bias_ref, *refs):
-    terms, (half_ref, sent_ref) = refs[:count], refs[count:]
+    terms, (half_ref, sent_ref, stats_ref) = refs[:count], refs[count:]
     stream = residual_ref[...].astype(jnp.float32)
     for term in terms:
         stream = stream + term[...].astype(jnp.float32)
@@ -123,7 +123,9 @@
         table = jnp.concatenate(
             [table, jnp.zeros((LANES - rows, LANES), jnp.float32)], axis=0
         )
-    stats = jnp.transpose(table)[: rows - 2 * gain_ref.shape[0]]
+    stats = jnp.transpose(table)
+    stats_ref[...] = stats[: stats_ref.shape[0]].astype(stats_ref.dtype)
+    stats = stats[: rows - 2 * gain_ref.shape[0]]
     sent_ref[:, width:] = jnp.concatenate(
         [stats, gain_ref[...].astype(jnp.float32), bias_ref[...].astype(jnp.float32)],
         axis=0,
@@ -138,6 +140,7 @@
         out_shape=(
             jax.ShapeDtypeStruct((rows, local), jnp.bfloat16),
             jax.ShapeDtypeStruct((rows, local + LANES), jnp.bfloat16),
+            jax.ShapeDtypeStruct((16, LANES), jnp.bfloat16),
         ),
         compiler_params=pltpu.CompilerParams(vmem_limit_bytes=8 * MIB),
         cost_estimate=pl.CostEstimate(
@@ -151,7 +154,7 @@
     del refs
 
 
-def first_of_all(piece, *after):
+def unchanged(piece, *after, cost=10**10):
     anywhere = pl.BlockSpec(memory_space=pl.ANY)
     return pl.pallas_call(
         nothing_kernel,
@@ -161,27 +164,46 @@
         input_output_aliases={0: 0},
         compiler_params=pltpu.CompilerParams(vmem_limit_bytes=MIB),
         cost_estimate=pl.CostEstimate(
-            flops=10**10, bytes_accessed=10**8, transcendentals=0
-        ),
-        name="first_of_all",
+            flops=cost, bytes_accessed=cost // 100, transcendentals=0
+        ),
+        name="unchanged",
     )(piece, *after)
 
 
-def moments(pieces, local):
-    rows = pieces[0].shape[0]
-    means, spread = [], jnp.zeros((1, LANES), jnp.float32)
-    for piece in pieces:
-        stats = piece[0:8, local:].astype(jnp.float32)
+def moments(tables, counts):
+    whole = sum(counts)
+    means, squares = [], jnp.zeros((1, LANES), jnp.float32)
+    for table in tables:
+        stats = table.astype(jnp.float32)
         means.append(stats[0:1] + stats[1:2] + stats[2:3])
-        spread = spread + (stats[3:4] + stats[4:5] + stats[5:6])
-    centre = sum(means) / len(means)
-    for mean in means:
-        spread = spread + local * ((mean - centre) * (mean - centre))
-    inverse = lax.rsqrt(spread / (len(means) * local) + 1e-05)
-    row = lax.broadcasted_iota(jnp.int32, (LANES, LANES), 0)
-    table = jnp.where(row == 0, centre, jnp.where(row == 1, inverse, 0.0))
-    table = jnp.transpose(table)[:rows]
-    return table[:, 0:1], table[:, 1:2]
+        squares = squares + (stats[3:4] + stats[4:5] + stats[5:6])
+    centre = sum(mean * (count / whole) for mean, count in zip(means, counts))
+    for mean, count in zip(means, counts):
+        squares = squares + count * ((mean - centre) * (mean - centre))
+    return centre, squares
+
+
+def merge_kernel(sent_ref, *refs):
+    out_ref = refs[-1]
+    rows = out_ref.shape[0]
+    local = out_ref.shape[1] - LANES
+    tables = [sent_ref[0:8, local:]] + [ref[0:8] for ref in refs[:-1]]
+    centre, squares = moments(tables, [local] * len(tables))
+    row = lax.broadcasted_iota(jnp.int32, (rows, LANES), 0)
+    table = sent_ref[:, local:].astype(jnp.float32)
+    for place, part in enumerate(in_three(centre) + in_three(squares)):
+        table = jnp.where(row == place, part, table)
+    out_ref[:, :local] = sent_ref[:, :local]
+    out_ref[:, local:] = table.astype(out_ref.dtype)
+
+
+def merge(sent, others):
+    return pl.pallas_call(
+        merge_kernel,
+        out_shape=jax.ShapeDtypeStruct(sent.shape, sent.dtype),
+        compiler_params=pltpu.CompilerParams(vmem_limit_bytes=4 * MIB),
+        name="merge",
+    )(sent, *others)
 
 
 def coded_rows(piece, local, centre, inverse, table):
@@ -206,26 +228,35 @@
     return back.astype(jnp.bfloat16)
 
 
-def finish_kernel(places, splits, *refs):
-    count = len(places)
-    pieces, (out_ref, done_ref, semaphores) = refs[:count], refs[count:]
+def finish_kernel(places, splits, counts, total, *refs):
+    pieces, refs = refs[: len(places)], refs[len(places) :]
     rows = pieces[0].shape[0]
-    width = done_ref.shape[2]
+    width = pieces[0].shape[1] - LANES
+    if counts:
+        tables, (out_ref, columns_ref) = refs[: len(counts)], refs[-4:-2]
+        centre, squares = moments([t[0:8, width:] for t in tables], counts)
+        inverse = lax.rsqrt(squares / total + 1e-05)
+        row = lax.broadcasted_iota(jnp.int32, (LANES, LANES), 0)
+        table = jnp.where(row == 0, centre, jnp.where(row == 1, inverse, 0.0))
+        columns = jnp.transpose(table)[:rows]
+        columns_ref[...] = columns
+    else:
+        columns, out_ref = refs[0][...], refs[-3]
+    done_ref, semaphores = refs[-2:]
     table = signs(BLOCK_LEN)
-    centre, inverse = moments(pieces, width)
     me = lax.axis_index("tensor")
     outer, inner = me // splits[1], lax.rem(me, splits[1])
     copies = []
     for p, (k, j) in enumerate(places):
-        back = coded_rows(pieces[p], width, centre, inverse, table)
+        back = coded_rows(pieces[p], width, columns[:, 0:1], columns[:, 1:2], table)
         for b in range(width // BLOCK_LEN):
             done_ref[p, :, b * BLOCK_LEN : (b + 1) * BLOCK_LEN] = back[
                 b * rows : (b + 1) * rows
             ]
         owner = jnp.bitwise_xor(outer, k) * splits[1] + jnp.bitwise_xor(inner, j)
-        columns = pl.ds(pl.multiple_of(owner * width, LANES), width)
+        place = pl.ds(pl.multiple_of(owner * width, LANES), width)
         copy = pltpu.make_async_copy(
-            done_ref.at[p], out_ref.at[:, columns], semaphores.at[p]
+            done_ref.at[p], out_ref.at[:, place], semaphores.at[p]
         )
         copy.start()
         copies.append(copy)
@@ -233,19 +264,26 @@
         copy.wait()
 
 
-def finish(places, splits, pieces, local):
-    rows = pieces[0].shape[0]
+def finish(places, splits, pieces, tables, counts, earlier, total):
+    rows, local = pieces[0].shape[0], pieces[0].shape[1] - LANES
     count = len(pieces)
     vmem = pl.BlockSpec(memory_space=pltpu.VMEM)
-    return pl.pallas_call(
-        functools.partial(finish_kernel, places, splits),
-        out_shape=jax.ShapeDtypeStruct((rows, count * local), jnp.bfloat16),
-        in_specs=[vmem] * count,
-        out_specs=pl.BlockSpec(memory_space=pl.ANY),
+    anywhere = pl.BlockSpec(memory_space=pl.ANY)
+    given = tables + earlier[::-1]
+    out_shape = [jax.ShapeDtypeStruct((rows, total), jnp.bfloat16)]
+    if not earlier:
+        out_shape.append(jax.ShapeDtypeStruct((rows, LANES), jnp.float32))
+    return pl.pallas_call(
+        functools.partial(finish_kernel, places, splits, counts, total),
+        out_shape=out_shape,
+        in_specs=[vmem] * (count + len(given) - len(earlier) // 2)
+        + [anywhere] * (len(earlier) // 2),
+        out_specs=[anywhere, vmem][: len(out_shape)],
         scratch_shapes=[
             pltpu.VMEM((count, rows, local), jnp.bfloat16),
             pltpu.SemaphoreType.DMA((count,)),
         ],
+        input_output_aliases={count + len(given) - 1: 0} if earlier else {},
         compiler_params=pltpu.CompilerParams(vmem_limit_bytes=16 * MIB),
         cost_estimate=pl.CostEstimate(
             flops=8 * BLOCK_LEN * rows * local * count,
@@ -253,7 +291,7 @@
             transcendentals=0,
         ),
         name="finish",
-    )(*pieces)
+    )(*pieces, *given)
 
 
 def body(attended, out_weight, residual, norm_gain, norm_bias):
@@ -276,12 +314,19 @@
     joins = [[]] + [[k] for k in order[:-1]] + [[]]
     joins[-3:] = [joins[-3] + joins[-2], []]
     terms = {k: [] for k in range(nz)}
-    after = []
+    after, held, released = [], [], []
     for targets, joined in zip(calls, joins):
-        results = products(attended, out_weight, targets, splits, local, after)
+        results = products(
+            attended, out_weight, targets, splits, local, after + released
+        )
         after = [results[-1]]
         for (k, j), result in zip(targets, results):
-            terms[k].append(lax.ppermute(result, "tensor", swap[j]) if j else result)
+            if j and k:
+                result = lax.ppermute(result, "tensor", swap[j])
+            if j and not k:
+                held.append((result, swap[j]))
+            else:
+                terms[k].append(result)
         for k in joined:
             bit = k & -k
             total = terms[k][0].astype(jnp.float32)
@@ -289,29 +334,42 @@
                 total = total + term.astype(jnp.float32)
             total = total.astype(jnp.bfloat16)
             after = [total]
+            if k == 2:
+                for piece, pairs in held:
+                    piece = unchanged(piece, total, cost=0)
+                    released.append(piece)
+                    piece = lax.ppermute(piece, "tensor", pairs)
+                    terms[0].append(piece)
             joined_to = lax.ppermute(total, "tensor", jump[bit])
             if k == nz // 2:
-                joined_to = first_of_all(joined_to)
+                joined_to = unchanged(joined_to)
             terms[k ^ bit].append(joined_to)
 
-    stream_out, sent = own_stream(residual, norm_gain, norm_bias, terms[0])
-    have = {0: sent}
+    stream_out, sent, stats = own_stream(residual, norm_gain, norm_bias, terms[0])
+    others = [lax.ppermute(stats, "tensor", swap[j]) for j in range(1, nx)]
+    merged = merge(sent, others)
+    have = {0: merged, 1: lax.ppermute(sent, "tensor", jump[1])}
     crossed = {}
     top = nz // 2
-    have[top] = lax.ppermute(sent, "tensor", jump[top])
-    have[1] = lax.ppermute(sent, "tensor", jump[1])
-    for p in away[0] + away[1]:
-        crossed[p] = lax.ppermute(have[p[0]], "tensor", swap[p[1]])
-    have[top] = first_of_all(have[top], *crossed.values())
+    have[top] = lax.ppermute(merged, "tensor", jump[top])
+    for k, j in away[0] + away[1]:
+        crossed[k, j] = lax.ppermute(have[k] if k else sent, "tensor", swap[j])
+    have[top] = unchanged(have[top], *crossed.values())
     for k in sorted(range(2, nz), key=lambda k: (k & (k - 1), k)):
         if k != top:
             have[k] = lax.ppermute(have[k ^ (k & -k)], "tensor", jump[k & -k])
     places = [place for k in range(nz) for place in here[k] + away[k]]
-    for p in places:
-        if p[1] and p not in crossed:
-            crossed[p] = lax.ppermute(have[p[0]], "tensor", swap[p[1]])
-    pieces = [crossed[p] if p[1] else have[p[0]] for p in places]
-    return (stream_out, finish(places, splits, pieces, local))
+    for k, j in places:
+        if j and k > 1:
+            crossed[k, j] = lax.ppermute(have[k], "tensor", swap[j])
+    pieces = {(k, j): crossed[k, j] if j else have[k] for k, j in places}
+    alone = here[1] + away[1]
+    tables = [have[k] for k in range(nz) if k != 1] + [pieces[p] for p in alone]
+    counts = [nx * local] * (nz - 1) + [local] * len(alone)
+    first, last = places[: 1 - nx], places[1 - nx :]
+    result = finish(first, splits, [pieces[p] for p in first], tables, counts, [], n * local)
+    result = finish(last, splits, [pieces[p] for p in last], [], [], list(result), n * local)
+    return (stream_out, result[0])
 
 
 def solution(mesh):

time: 76.4 us -> 71.2 us (0.932)
  waiting for transfers between devices: 34.8 us -> 25.5 us
  starting transfers between devices: 17.5 us -> 20.7 us
  Pallas kernels: 22.1 us -> 23 us
    ppermute x10 -> x11, waiting for transfers between devices: 22.5 us -> 12.9 us  [the longest x1 7.08 us: body(): have[top] = lax.ppermute(merged, 'tensor', jump[top])]
    ppermute x10 -> x11, starting transfers between devices: 11.4 us -> 14.6 us  [the longest x3 4.62 us: body(): result = lax.ppermute(result, 'tensor', swap[j])]
    pallas_call x3 -> x6, Pallas kernels: 5.3 us -> 6.15 us  [the longest x2 6.1 us: finish(): pl.pallas_call(functools.partial(finish_kernel, places, splits, counts, t...]
  transfers between devices with their start and end apart: 14 -> 15, of which waited for: 10 -> 9; matrix products, arithmetic and copies ran while one was open for 0% -> 0% of each run, Pallas kernels for 17% -> 25%
where the time goes in v7:
time: 71.2 us; the launch traced here: 71 us
  waiting for transfers between devices  25.5 us (36%)
  Pallas kernels  23 us (32%)
  starting transfers between devices  20.7 us (29%)
  local copies, waits for them, and re-layouts  0.92 us (1%)
  between operations  0.76 us (1%)
    pallas_call x4, Pallas kernels, products(): pl.pallas_call(functools.partial(product_kernel, targets, splits, local,...  15.8 us
    ppermute x3, waiting for transfers between devices, body(): joined_to = lax.ppermute(total, 'tensor', jump[bit])  7.29 us
    ppermute x1, waiting for transfers between devices, body(): have[top] = lax.ppermute(merged, 'tensor', jump[top])  7.08 us
    ppermute x3, starting transfers between devices, body(): joined_to = lax.ppermute(total, 'tensor', jump[bit])  6.19 us
    pallas_call x2, Pallas kernels, finish(): pl.pallas_call(functools.partial(finish_kernel, places, splits, counts, t...  6.1 us
    ppermute x1, waiting for transfers between devices, body(): have[k] = lax.ppermute(have[k ^ k & -k], 'tensor', jump[k & -k])  5.24 us
    ppermute x3, starting transfers between devices, body(): result = lax.ppermute(result, 'tensor', swap[j])  4.62 us
    ppermute x1, starting transfers between devices, body(): have[top] = lax.ppermute(merged, 'tensor', jump[top])  3.41 us
  transfers between devices with their start and end apart: 15, of which 9 were waited for; matrix products, arithmetic and copies ran while one was open for 0% of the time, Pallas kernels for 25%

profile of v7, /device:TPU:0, one launch (start us, length us, event | category | flops | bytes accessed | tf_op | source)
XLA Modules:
  0.0 71.0 jit_solution(4832379074377725221)
XLA Ops:
  0.6 0.0 copy-start
  0.6 0.9 %copy-done = bf16[64,1024]{1,0:T(8,128)(2,1)S(1)} copy-done((bf16[64,1024]{1,0:T(8,128)(2,1)S(1)}, bf16[64,1024]{1,0:T(8,128)(2,1)}, u32[]{:S(2)}) %copy-start) | copy-done | bytes 131096
  1.5 2.7 %products.4.refs_0_ = bf16[64,2048]{1,0:T(8,128)(2,1)S(1)} custom-call(bf16[64,1024]{1,0:T(8,128)(2,1)S(1)} %copy-done, bf16[1024,16384]{1,0:T(8,128)(2,1)} %weight_ref.7), custom_call_target="tpu_custom_call" | custom-call | flops 268435456 | bytes 4194304 | tf_op jit(solution)/shard_map/products/pallas_call | solution.py:72
  4.2 3.0 %collective-permute-start = (bf16[64,2048]{1,0:T(8,128)(2,1)S(1)}, bf16[64,2048]{1,0:T(8,128)(2,1)S(1)}, u32[]{:S(2)}, u32[]{:S(2)}) collective-permute-start(bf16[64,2048]{1,0:T(8,128)(2,1)S(1)} %products.4.refs_0_), channel_id=1, source_target_pairs={{0,1},{1,0},{2,3},{3,2},{4,5},{5,4},{6,7},{7,6},{8,9},{9,8},{10,11... | collective-permute-start | bytes 786440 | tf_op jit(solution)/shard_map/ppermute | solution.py:325
  7.2 5.2 %products.5 = (bf16[64,2048]{1,0:T(8,128)(2,1)S(1)}, bf16[64,2048]{1,0:T(8,128)(2,1)S(1)}, f32[64,2048]{1,0:T(8,128)S(1)}) custom-call(bf16[64,1024]{1,0:T(8,128)(2,1)S(1)} %copy-done, bf16[1024,16384]{1,0:T(8,128)(2,1)} %weight_ref.7, bf16[64,2048]{1,0:T(8,128)(2,1)S(1)} %products.4.refs_0_), custom_call_target="tpu_custom_call" | custom-call | flops 805306368 | bytes 12582912 | tf_op jit(solution)/shard_map/products/pallas_call | solution.py:72
  12.5 0.1 collective-permute-start.1
  12.6 0.9 %collective-permute-done = bf16[64,2048]{1,0:T(8,128)(2,1)S(1)} collective-permute-done((bf16[64,2048]{1,0:T(8,128)(2,1)S(1)}, bf16[64,2048]{1,0:T(8,128)(2,1)S(1)}, u32[]{:S(2)}, u32[]{:S(2)}) %collective-permute-start) | collective-permute-done | bytes 262176 | tf_op jit(solution)/shard_map/ppermute | solution.py:325
  13.6 1.9 %collective-permute-start.2 = (bf16[64,2048]{1,0:T(8,128)(2,1)S(1)}, bf16[64,2048]{1,0:T(8,128)(2,1)S(1)}, u32[]{:S(2)}, u32[]{:S(2)}) collective-permute-start(bf16[64,2048]{1,0:T(8,128)(2,1)S(1)} %add_convert_fusion.2.refs_0_), channel_id=1, source_target_pairs={{0,2},{1,3},{2,0},{3,1},{4,6},{5,7},{6,4},{7,5},{8,10},{9,11},{10,... | collective-permute-start | bytes 786440 | tf_op jit(solution)/shard_map/ppermute | solution.py:343
  15.5 1.5 %collective-permute-start.5 = (bf16[64,2048]{1,0:T(8,128)(2,1)S(1)}, bf16[64,2048]{1,0:T(8,128)(2,1)S(1)}, u32[]{:S(2)}, u32[]{:S(2)}) collective-permute-start(bf16[64,2048]{1,0:T(8,128)(2,1)S(1)} %get-tuple-element.17), channel_id=1, source_target_pairs={{0,1},{1,0},{2,3},{3,2},{4,5},{5,4},{6,7},{7,6},{8,9},{9,8},{10,11... | collective-permute-start | bytes 786440 | tf_op jit(solution)/shard_map/ppermute | solution.py:325
  17.0 5.2 %products.6 = (bf16[64,2048]{1,0:T(8,128)(2,1)S(1)}, f32[64,2048]{1,0:T(8,128)S(1)}, f32[64,2048]{1,0:T(8,128)S(1)}) custom-call(bf16[64,1024]{1,0:T(8,128)(2,1)S(1)} %copy-done, bf16[1024,16384]{1,0:T(8,128)(2,1)} %weight_ref.7, bf16[64,2048]{1,0:T(8,128)(2,1)S(1)} %add_convert_fusion.2.refs_0_), custom_call_target="tpu_custom_call" | custom-call | flops 805306368 | bytes 12582912 | tf_op jit(solution)/shard_map/products/pallas_call | solution.py:72
  22.2 0.0 collective-permute-done.1
  22.2 0.0 collective-permute-done.2
  22.2 0.1 add_convert_fusion.1.refs_1_
  22.3 2.7 %collective-permute-start.4 = (bf16[64,2048]{1,0:T(8,128)(2,1)S(1)}, bf16[64,2048]{1,0:T(8,128)(2,1)S(1)}, u32[]{:S(2)}, u32[]{:S(2)}) collective-permute-start(bf16[64,2048]{1,0:T(8,128)(2,1)S(1)} %add_convert_fusion.1.refs_1_), channel_id=1, source_target_pairs={{0,4},{1,5},{2,6},{3,7},{4,0},{5,1},{6,2},{7,3},{8,12},{9,13},{10,... | collective-permute-start | bytes 786440 | tf_op jit(solution)/shard_map/ppermute | solution.py:343
  25.0 0.9 %collective-permute-done.5 = bf16[64,2048]{1,0:T(8,128)(2,1)S(1)} collective-permute-done((bf16[64,2048]{1,0:T(8,128)(2,1)S(1)}, bf16[64,2048]{1,0:T(8,128)(2,1)S(1)}, u32[]{:S(2)}, u32[]{:S(2)}) %collective-permute-start.5) | collective-permute-done | bytes 262176 | tf_op jit(solution)/shard_map/ppermute | solution.py:325
  26.0 1.6 %collective-permute-start.6 = (bf16[64,2048]{1,0:T(8,128)(2,1)S(1)}, bf16[64,2048]{1,0:T(8,128)(2,1)S(1)}, u32[]{:S(2)}, u32[]{:S(2)}) collective-permute-start(bf16[64,2048]{1,0:T(8,128)(2,1)S(1)} %add_convert_fusion.refs_0_), channel_id=1, source_target_pairs={{0,2},{1,3},{2,0},{3,1},{4,6},{5,7},{6,4},{7,5},{8,10},{9,11},{10,... | collective-permute-start | bytes 786440 | tf_op jit(solution)/shard_map/ppermute | solution.py:343
  27.6 0.6 collective-permute-start.3
  28.2 2.7 %products.7.refs_3_ = f32[64,2048]{1,0:T(8,128)S(1)} custom-call(bf16[64,1024]{1,0:T(8,128)(2,1)S(1)} %copy-done, bf16[1024,16384]{1,0:T(8,128)(2,1)} %weight_ref.7, bf16[64,2048]{1,0:T(8,128)(2,1)S(1)} %add_convert_fusion.refs_0_, bf16[64,2048]{1,0:T(8,128)(2,1)S(1)} %unchanged.3.refs_1_), custom_call_target="tpu_custom_call" | custom-call | flops 268435456 | bytes 4194304 | tf_op jit(solution)/shard_map/products/pallas_call | solution.py:72
  30.9 0.0 copy-start.1
  30.9 0.0 copy-start.2
  30.9 0.0 copy-start.3
  30.9 4.6 %collective-permute-done.4.refs_0_ = bf16[64,2048]{1,0:T(8,128)(2,1)S(1)} collective-permute-done((bf16[64,2048]{1,0:T(8,128)(2,1)S(1)}, bf16[64,2048]{1,0:T(8,128)(2,1)S(1)}, u32[]{:S(2)}, u32[]{:S(2)}) %collective-permute-start.4) | collective-permute-done | bytes 262176 | tf_op jit(solution)/shard_map/ppermute | solution.py:343
  35.5 2.7 %collective-permute-done.6.refs_2_ = bf16[64,2048]{1,0:T(8,128)(2,1)S(1)} collective-permute-done((bf16[64,2048]{1,0:T(8,128)(2,1)S(1)}, bf16[64,2048]{1,0:T(8,128)(2,1)S(1)}, u32[]{:S(2)}, u32[]{:S(2)}) %collective-permute-start.6) | collective-permute-done | bytes 262176 | tf_op jit(solution)/shard_map/ppermute | solution.py:343
  38.2 0.0 collective-permute-done.3.refs_0_
  38.2 0.0 copy-done.1
  38.2 0.0 copy-done.2
  38.2 0.0 copy-done.3
  38.2 1.0 %own_stream.1 = (bf16[64,2048]{1,0:T(8,128)(2,1)}, bf16[64,2176]{1,0:T(8,128)(2,1)S(1)}, bf16[16,128]{1,0:T(8,128)(2,1)S(1)}) custom-call(bf16[64,2048]{1,0:T(8,128)(2,1)S(1)} %copy-done.1, bf16[16,128]{1,0:T(8,128)(2,1)S(1)} %bitcast.2, bf16[16,128]{1,0:T(8,128)(2,1)S(1)} %bitcast.3, bf16[64,2048]{1,0:T(8,128)(2,1)S(1)} %collective-permute-done.3.refs_0_, ...), custom_call_target="tpu_custom_call" | custom-call | flops 2621440 | bytes 2097152 | tf_op jit(solution)/shard_map/own_stream/pallas_call | solution.py:138
  39.2 0.0 collective-permute-start.10
  39.2 0.9 %collective-permute-start.7 = (bf16[16,128]{1,0:T(8,128)(2,1)S(1)}, bf16[16,128]{1,0:T(8,128)(2,1)S(1)}, u32[]{:S(2)}, u32[]{:S(2)}) collective-permute-start(bf16[16,128]{1,0:T(8,128)(2,1)S(1)} %get-tuple-element.21), channel_id=1, source_target_pairs={{0,1},{1,0},{2,3},{3,2},{4,5},{5,4},{6,7},{7,6},{8,9},{9,8},{10,11... | collective-permute-start | bytes 12296 | tf_op jit(solution)/shard_map/ppermute | solution.py:349
  40.1 1.1 %collective-permute-start.9 = (bf16[64,2176]{1,0:T(8,128)(2,1)S(1)}, bf16[64,2176]{1,0:T(8,128)(2,1)S(1)}, u32[]{:S(2)}, u32[]{:S(2)}) collective-permute-start(bf16[64,2176]{1,0:T(8,128)(2,1)S(1)} %get-tuple-element.20.sent_ref), channel_id=1, source_target_pairs={{0,1},{1,0},{2,3},{3,2},{4,5},{5,4},{6,7},{7,6},{8,9},{9,8},{10,11... | collective-permute-start | bytes 835592 | tf_op jit(solution)/shard_map/ppermute | solution.py:356
  41.2 1.7 %collective-permute-done.7.refs_0_ = bf16[16,128]{1,0:T(8,128)(2,1)S(1)} collective-permute-done((bf16[16,128]{1,0:T(8,128)(2,1)S(1)}, bf16[16,128]{1,0:T(8,128)(2,1)S(1)}, u32[]{:S(2)}, u32[]{:S(2)}) %collective-permute-start.7) | collective-permute-done | bytes 4128 | tf_op jit(solution)/shard_map/ppermute | solution.py:349
  43.0 3.4 %collective-permute-start.8 = (bf16[64,2176]{1,0:T(8,128)(2,1)S(1)}, bf16[64,2176]{1,0:T(8,128)(2,1)S(1)}, u32[]{:S(2)}, u32[]{:S(2)}) collective-permute-start(bf16[64,2176]{1,0:T(8,128)(2,1)S(1)} %merge.1.refs_0_.refs_7_), channel_id=1, source_target_pairs={{0,4},{1,5},{2,6},{3,7},{4,0},{5,1},{6,2},{7,3},{8,12},{9,13},{10,... | collective-permute-start | bytes 835592 | tf_op jit(solution)/shard_map/ppermute | solution.py:354
  46.4 1.7 %collective-permute-done.10.refs_2_.refs_10_ = bf16[64,2176]{1,0:T(8,128)(2,1)S(1)} collective-permute-done((bf16[64,2176]{1,0:T(8,128)(2,1)S(1)}, bf16[64,2176]{1,0:T(8,128)(2,1)S(1)}, u32[]{:S(2)}, u32[]{:S(2)}) %collective-permute-start.10) | collective-permute-done | bytes 278560 | tf_op jit(solution)/shard_map/ppermute | solution.py:351
  48.1 1.4 %collective-permute-start.11 = (bf16[64,2176]{1,0:T(8,128)(2,1)S(1)}, bf16[64,2176]{1,0:T(8,128)(2,1)S(1)}, u32[]{:S(2)}, u32[]{:S(2)}) collective-permute-start(bf16[64,2176]{1,0:T(8,128)(2,1)S(1)} %collective-permute-done.10.refs_2_.refs_10_), channel_id=1, source_target_pairs={{0,1},{1,0},{2,3},{3,2},{4,5},{5,4},{6,7},{7,6},{8,9},{9,8},{10,11... | collective-permute-start | bytes 835592 | tf_op jit(solution)/shard_map/ppermute | solution.py:356
  49.5 0.0 collective-permute-done.9.refs_1_
  49.5 7.1 %collective-permute-done.8.refs_0_ = bf16[64,2176]{1,0:T(8,128)(2,1)S(1)} collective-permute-done((bf16[64,2176]{1,0:T(8,128)(2,1)S(1)}, bf16[64,2176]{1,0:T(8,128)(2,1)S(1)}, u32[]{:S(2)}, u32[]{:S(2)}) %collective-permute-start.8) | collective-permute-done | bytes 278560 | tf_op jit(solution)/shard_map/ppermute | solution.py:354
  56.5 0.0 collective-permute-done.11.refs_2_.refs_3_.refs_11_
  56.5 0.0 collective-permute-start.12
  56.5 1.3 %collective-permute-start.14 = (bf16[64,2176]{1,0:T(8,128)(2,1)S(1)}, bf16[64,2176]{1,0:T(8,128)(2,1)S(1)}, u32[]{:S(2)}, u32[]{:S(2)}) collective-permute-start(bf16[64,2176]{1,0:T(8,128)(2,1)S(1)} %unchanged.5.refs_4_.refs_8_), channel_id=1, source_target_pairs={{0,1},{1,0},{2,3},{3,2},{4,5},{5,4},{6,7},{7,6},{8,9},{9,8},{10,11... | collective-permute-start | bytes 835592 | tf_op jit(solution)/shard_map/ppermute | solution.py:364
  57.8 5.2 %collective-permute-done.12.refs_6_.refs_9_ = bf16[64,2176]{1,0:T(8,128)(2,1)S(1)} collective-permute-done((bf16[64,2176]{1,0:T(8,128)(2,1)S(1)}, bf16[64,2176]{1,0:T(8,128)(2,1)S(1)}, u32[]{:S(2)}, u32[]{:S(2)}) %collective-permute-start.12) | collective-permute-done | bytes 278560 | tf_op jit(solution)/shard_map/ppermute | solution.py:360
  63.1 1.2 %collective-permute-start.13 = (bf16[64,2176]{1,0:T(8,128)(2,1)S(1)}, bf16[64,2176]{1,0:T(8,128)(2,1)S(1)}, u32[]{:S(2)}, u32[]{:S(2)}) collective-permute-start(bf16[64,2176]{1,0:T(8,128)(2,1)S(1)} %collective-permute-done.12.refs_6_.refs_9_), channel_id=1, source_target_pairs={{0,1},{1,0},{2,3},{3,2},{4,5},{5,4},{6,7},{7,6},{8,9},{9,8},{10,11... | collective-permute-start | bytes 835592 | tf_op jit(solution)/shard_map/ppermute | solution.py:364
  64.3 0.0 collective-permute-done.14.refs_5_
  64.3 4.7 %finish.2 = (bf16[64,16384]{1,0:T(8,128)(2,1)}, f32[64,128]{1,0:T(8,128)S(1)}) custom-call(bf16[64,2176]{1,0:T(8,128)(2,1)S(1)} %merge.1.refs_0_.refs_7_, bf16[64,2176]{1,0:T(8,128)(2,1)S(1)} %collective-permute-done.9.refs_1_, bf16[64,2176]{1,0:T(8,128)(2,1)S(1)} %collective-permute-done.10.refs_2_.refs_10_, ...), custom_call_target="tpu_custom_call" | custom-call | flops 939524096 | bytes 3670016 | tf_op jit(solution)/shard_map/finish/pallas_call | solution.py:276
  69.0 0.6 collective-permute-done.13.refs_0_
  69.6 1.4 %finish.3 = bf16[64,16384]{1,0:T(8,128)(2,1)} custom-call(bf16[64,2176]{1,0:T(8,128)(2,1)S(1)} %collective-permute-done.13.refs_0_, f32[64,128]{1,0:T(8,128)S(1)} %get-tuple-element.22.refs_1_, bf16[64,16384]{1,0:T(8,128)(2,1)} %get-tuple-element.23.refs_2_), custom_call_target="tpu_custom_call", output_to_operand_aliasing={{}: (2, {})} | custom-call | flops 134217728 | bytes 524288 | tf_op jit(solution)/shard_map/finish/pallas_call | solution.py:276
  (6 shorter events, 0.1 us)
Async XLA Ops:
  0.6 0.9 %copy-start = (bf16[64,1024]{1,0:T(8,128)(2,1)S(1)}, bf16[64,1024]{1,0:T(8,128)(2,1)}, u32[]{:S(2)}) copy-start(bf16[64,1024]{1,0:T(8,128)(2,1)} %rows_ref.7) | copy-start | bytes 393220
  4.2 9.3 %collective-permute-start = (bf16[64,2048]{1,0:T(8,128)(2,1)S(1)}, bf16[64,2048]{1,0:T(8,128)(2,1)S(1)}, u32[]{:S(2)}, u32[]{:S(2)}) collective-permute-start(bf16[64,2048]{1,0:T(8,128)(2,1)S(1)} %products.4.refs_0_), channel_id=1, source_target_pairs={{0,1},{1,0},{2,3},{3,2},{4,5},{5,4},{6,7},{7,6},{8,9},{9,8},{10,11... | collective-permute-start | bytes 786440 | tf_op jit(solution)/shard_map/ppermute | solution.py:325
  12.5 9.7 %collective-permute-start.1 = (bf16[64,2048]{1,0:T(8,128)(2,1)S(1)}, bf16[64,2048]{1,0:T(8,128)(2,1)S(1)}, u32[]{:S(2)}, u32[]{:S(2)}) collective-permute-start(bf16[64,2048]{1,0:T(8,128)(2,1)S(1)} %get-tuple-element.15), channel_id=1, source_target_pairs={{0,1},{1,0},{2,3},{3,2},{4,5},{5,4},{6,7},{7,6},{8,9},{9,8},{10,11... | collective-permute-start | bytes 786440 | tf_op jit(solution)/shard_map/ppermute | solution.py:325
  13.6 8.6 %collective-permute-start.2 = (bf16[64,2048]{1,0:T(8,128)(2,1)S(1)}, bf16[64,2048]{1,0:T(8,128)(2,1)S(1)}, u32[]{:S(2)}, u32[]{:S(2)}) collective-permute-start(bf16[64,2048]{1,0:T(8,128)(2,1)S(1)} %add_convert_fusion.2.refs_0_), channel_id=1, source_target_pairs={{0,2},{1,3},{2,0},{3,1},{4,6},{5,7},{6,4},{7,5},{8,10},{9,11},{10,... | collective-permute-start | bytes 786440 | tf_op jit(solution)/shard_map/ppermute | solution.py:343
  15.5 10.4 %collective-permute-start.5 = (bf16[64,2048]{1,0:T(8,128)(2,1)S(1)}, bf16[64,2048]{1,0:T(8,128)(2,1)S(1)}, u32[]{:S(2)}, u32[]{:S(2)}) collective-permute-start(bf16[64,2048]{1,0:T(8,128)(2,1)S(1)} %get-tuple-element.17), channel_id=1, source_target_pairs={{0,1},{1,0},{2,3},{3,2},{4,5},{5,4},{6,7},{7,6},{8,9},{9,8},{10,11... | collective-permute-start | bytes 786440 | tf_op jit(solution)/shard_map/ppermute | solution.py:325
  22.3 13.2 %collective-permute-start.4 = (bf16[64,2048]{1,0:T(8,128)(2,1)S(1)}, bf16[64,2048]{1,0:T(8,128)(2,1)S(1)}, u32[]{:S(2)}, u32[]{:S(2)}) collective-permute-start(bf16[64,2048]{1,0:T(8,128)(2,1)S(1)} %add_convert_fusion.1.refs_1_), channel_id=1, source_target_pairs={{0,4},{1,5},{2,6},{3,7},{4,0},{5,1},{6,2},{7,3},{8,12},{9,13},{10,... | collective-permute-start | bytes 786440 | tf_op jit(solution)/shard_map/ppermute | solution.py:343
  26.0 12.2 %collective-permute-start.6 = (bf16[64,2048]{1,0:T(8,128)(2,1)S(1)}, bf16[64,2048]{1,0:T(8,128)(2,1)S(1)}, u32[]{:S(2)}, u32[]{:S(2)}) collective-permute-start(bf16[64,2048]{1,0:T(8,128)(2,1)S(1)} %add_convert_fusion.refs_0_), channel_id=1, source_target_pairs={{0,2},{1,3},{2,0},{3,1},{4,6},{5,7},{6,4},{7,5},{8,10},{9,11},{10,... | collective-permute-start | bytes 786440 | tf_op jit(solution)/shard_map/ppermute | solution.py:343
  27.6 10.6 %collective-permute-start.3 = (bf16[64,2048]{1,0:T(8,128)(2,1)S(1)}, bf16[64,2048]{1,0:T(8,128)(2,1)S(1)}, u32[]{:S(2)}, u32[]{:S(2)}) collective-permute-start(bf16[64,2048]{1,0:T(8,128)(2,1)S(1)} %unchanged.3.refs_1_), channel_id=1, source_target_pairs={{0,1},{1,0},{2,3},{3,2},{4,5},{5,4},{6,7},{7,6},{8,9},{9,8},{10,11... | collective-permute-start | bytes 786440 | tf_op jit(solution)/shard_map/ppermute | solution.py:341
  30.9 7.3 %copy-start.1 = (bf16[64,2048]{1,0:T(8,128)(2,1)S(1)}, bf16[64,2048]{1,0:T(8,128)(2,1)}, u32[]{:S(2)}) copy-start(bf16[64,2048]{1,0:T(8,128)(2,1)} %residual_ref.1) | copy-start | bytes 786436
  30.9 7.3 %copy-start.2 = (bf16[2048]{0:T(1024)(128)(2,1)S(1)}, bf16[2048]{0:T(1024)(128)(2,1)}, u32[]{:S(2)}) copy-start(bf16[2048]{0:T(1024)(128)(2,1)} %param.8) | copy-start | bytes 12292
  30.9 7.3 %copy-start.3 = (bf16[2048]{0:T(1024)(128)(2,1)S(1)}, bf16[2048]{0:T(1024)(128)(2,1)}, u32[]{:S(2)}) copy-start(bf16[2048]{0:T(1024)(128)(2,1)} %param.9) | copy-start | bytes 12292
  39.2 8.9 %collective-permute-start.10 = (bf16[64,2176]{1,0:T(8,128)(2,1)S(1)}, bf16[64,2176]{1,0:T(8,128)(2,1)S(1)}, u32[]{:S(2)}, u32[]{:S(2)}) collective-permute-start(bf16[64,2176]{1,0:T(8,128)(2,1)S(1)} %get-tuple-element.20.sent_ref), channel_id=1, source_target_pairs={{0,2},{1,3},{2,0},{3,1},{4,6},{5,7},{6,4},{7,5},{8,10},{9,11},{10,... | collective-permute-start | bytes 835592 | tf_op jit(solution)/shard_map/ppermute | solution.py:351
  39.2 3.7 %collective-permute-start.7 = (bf16[16,128]{1,0:T(8,128)(2,1)S(1)}, bf16[16,128]{1,0:T(8,128)(2,1)S(1)}, u32[]{:S(2)}, u32[]{:S(2)}) collective-permute-start(bf16[16,128]{1,0:T(8,128)(2,1)S(1)} %get-tuple-element.21), channel_id=1, source_target_pairs={{0,1},{1,0},{2,3},{3,2},{4,5},{5,4},{6,7},{7,6},{8,9},{9,8},{10,11... | collective-permute-start | bytes 12296 | tf_op jit(solution)/shard_map/ppermute | solution.py:349
  40.1 9.4 %collective-permute-start.9 = (bf16[64,2176]{1,0:T(8,128)(2,1)S(1)}, bf16[64,2176]{1,0:T(8,128)(2,1)S(1)}, u32[]{:S(2)}, u32[]{:S(2)}) collective-permute-start(bf16[64,2176]{1,0:T(8,128)(2,1)S(1)} %get-tuple-element.20.sent_ref), channel_id=1, source_target_pairs={{0,1},{1,0},{2,3},{3,2},{4,5},{5,4},{6,7},{7,6},{8,9},{9,8},{10,11... | collective-permute-start | bytes 835592 | tf_op jit(solution)/shard_map/ppermute | solution.py:356
  43.0 13.6 %collective-permute-start.8 = (bf16[64,2176]{1,0:T(8,128)(2,1)S(1)}, bf16[64,2176]{1,0:T(8,128)(2,1)S(1)}, u32[]{:S(2)}, u32[]{:S(2)}) collective-permute-start(bf16[64,2176]{1,0:T(8,128)(2,1)S(1)} %merge.1.refs_0_.refs_7_), channel_id=1, source_target_pairs={{0,4},{1,5},{2,6},{3,7},{4,0},{5,1},{6,2},{7,3},{8,12},{9,13},{10,... | collective-permute-start | bytes 835592 | tf_op jit(solution)/shard_map/ppermute | solution.py:354
  48.1 8.4 %collective-permute-start.11 = (bf16[64,2176]{1,0:T(8,128)(2,1)S(1)}, bf16[64,2176]{1,0:T(8,128)(2,1)S(1)}, u32[]{:S(2)}, u32[]{:S(2)}) collective-permute-start(bf16[64,2176]{1,0:T(8,128)(2,1)S(1)} %collective-permute-done.10.refs_2_.refs_10_), channel_id=1, source_target_pairs={{0,1},{1,0},{2,3},{3,2},{4,5},{5,4},{6,7},{7,6},{8,9},{9,8},{10,11... | collective-permute-start | bytes 835592 | tf_op jit(solution)/shard_map/ppermute | solution.py:356
  56.5 6.5 %collective-permute-start.12 = (bf16[64,2176]{1,0:T(8,128)(2,1)S(1)}, bf16[64,2176]{1,0:T(8,128)(2,1)S(1)}, u32[]{:S(2)}, u32[]{:S(2)}) collective-permute-start(bf16[64,2176]{1,0:T(8,128)(2,1)S(1)} %unchanged.5.refs_4_.refs_8_), channel_id=1, source_target_pairs={{0,2},{1,3},{2,0},{3,1},{4,6},{5,7},{6,4},{7,5},{8,10},{9,11},{10,... | collective-permute-start | bytes 835592 | tf_op jit(solution)/shard_map/ppermute | solution.py:360
  56.5 7.8 %collective-permute-start.14 = (bf16[64,2176]{1,0:T(8,128)(2,1)S(1)}, bf16[64,2176]{1,0:T(8,128)(2,1)S(1)}, u32[]{:S(2)}, u32[]{:S(2)}) collective-permute-start(bf16[64,2176]{1,0:T(8,128)(2,1)S(1)} %unchanged.5.refs_4_.refs_8_), channel_id=1, source_target_pairs={{0,1},{1,0},{2,3},{3,2},{4,5},{5,4},{6,7},{7,6},{8,9},{9,8},{10,11... | collective-permute-start | bytes 835592 | tf_op jit(solution)/shard_map/ppermute | solution.py:364
  63.1 6.5 %collective-permute-start.13 = (bf16[64,2176]{1,0:T(8,128)(2,1)S(1)}, bf16[64,2176]{1,0:T(8,128)(2,1)S(1)}, u32[]{:S(2)}, u32[]{:S(2)}) collective-permute-start(bf16[64,2176]{1,0:T(8,128)(2,1)S(1)} %collective-permute-done.12.refs_6_.refs_9_), channel_id=1, source_target_pairs={{0,1},{1,0},{2,3},{3,2},{4,5},{5,4},{6,7},{7,6},{8,9},{9,8},{10,11... | collective-permute-start | bytes 835592 | tf_op jit(solution)/shard_map/ppermute | solution.py:364

commit v8 on v7

--- a/solution.py
+++ b/solution.py
@@ -183,27 +183,52 @@
     return centre, squares
 
 
-def merge_kernel(sent_ref, *refs):
+def merge_kernel(local, *refs):
     out_ref = refs[-1]
-    rows = out_ref.shape[0]
-    local = out_ref.shape[1] - LANES
-    tables = [sent_ref[0:8, local:]] + [ref[0:8] for ref in refs[:-1]]
-    centre, squares = moments(tables, [local] * len(tables))
-    row = lax.broadcasted_iota(jnp.int32, (rows, LANES), 0)
-    table = sent_ref[:, local:].astype(jnp.float32)
+    centre, squares = moments([ref[0:8] for ref in refs[:-1]], [local] * len(refs[:-1]))
+    row = lax.broadcasted_iota(jnp.int32, out_ref.shape, 0)
+    table = jnp.zeros(out_ref.shape, jnp.float32)
     for place, part in enumerate(in_three(centre) + in_three(squares)):
         table = jnp.where(row == place, part, table)
-    out_ref[:, :local] = sent_ref[:, :local]
-    out_ref[:, local:] = table.astype(out_ref.dtype)
-
-
-def merge(sent, others):
-    return pl.pallas_call(
-        merge_kernel,
-        out_shape=jax.ShapeDtypeStruct(sent.shape, sent.dtype),
+    out_ref[...] = table.astype(out_ref.dtype)
+
+
+def merge(tables, local):
+    return pl.pallas_call(
+        functools.partial(merge_kernel, local),
+        out_shape=jax.ShapeDtypeStruct(tables[0].shape, tables[0].dtype),
+        compiler_params=pltpu.CompilerParams(vmem_limit_bytes=2 * MIB),
+        cost_estimate=pl.CostEstimate(
+            flops=10**9, bytes_accessed=10**7, transcendentals=0
+        ),
+        name="merge",
+    )(*tables)
+
+
+def replace_kernel(piece_ref, table_ref, *refs):
+    out_ref = refs[-1]
+    local, height = piece_ref.shape[1] - LANES, table_ref.shape[0]
+    out_ref[:, :local] = piece_ref[:, :local]
+    out_ref[:, local:] = piece_ref[:, local:]
+    row = lax.broadcasted_iota(jnp.int32, table_ref.shape, 0)
+    table = jnp.where(
+        row < 6,
+        table_ref[...].astype(jnp.float32),
+        piece_ref[:height, local:].astype(jnp.float32),
+    )
+    out_ref[:height, local:] = table.astype(out_ref.dtype)
+
+
+def replace(piece, table, after):
+    vmem = pl.BlockSpec(memory_space=pltpu.VMEM)
+    return pl.pallas_call(
+        replace_kernel,
+        out_shape=jax.ShapeDtypeStruct(piece.shape, piece.dtype),
+        in_specs=[vmem, vmem] + [pl.BlockSpec(memory_space=pl.ANY)] * len(after),
+        out_specs=vmem,
         compiler_params=pltpu.CompilerParams(vmem_limit_bytes=4 * MIB),
-        name="merge",
-    )(sent, *others)
+        name="replace",
+    )(piece, table, *after)
 
 
 def coded_rows(piece, local, centre, inverse, table):
@@ -234,7 +259,9 @@
     width = pieces[0].shape[1] - LANES
     if counts:
         tables, (out_ref, columns_ref) = refs[: len(counts)], refs[-4:-2]
-        centre, squares = moments([t[0:8, width:] for t in tables], counts)
+        centre, squares = moments(
+            [t[0:8, t.shape[1] - LANES :] for t in tables], counts
+        )
         inverse = lax.rsqrt(squares / total + 1e-05)
         row = lax.broadcasted_iota(jnp.int32, (LANES, LANES), 0)
         table = jnp.where(row == 0, centre, jnp.where(row == 1, inverse, 0.0))
@@ -346,25 +373,34 @@
             terms[k ^ bit].append(joined_to)
 
     stream_out, sent, stats = own_stream(residual, norm_gain, norm_bias, terms[0])
+    have = {0: sent, 1: lax.ppermute(sent, "tensor", jump[1])}
+    top = nz // 2
+    far = lax.ppermute(sent, "tensor", jump[top])
     others = [lax.ppermute(stats, "tensor", swap[j]) for j in range(1, nx)]
-    merged = merge(sent, others)
-    have = {0: merged, 1: lax.ppermute(sent, "tensor", jump[1])}
+    merged = merge([stats] + others, local)
+    have[1] = unchanged(have[1], merged, cost=0)
     crossed = {}
-    top = nz // 2
-    have[top] = lax.ppermute(merged, "tensor", jump[top])
     for k, j in away[0] + away[1]:
-        crossed[k, j] = lax.ppermute(have[k] if k else sent, "tensor", swap[j])
-    have[top] = unchanged(have[top], *crossed.values())
+        crossed[k, j] = lax.ppermute(have[k], "tensor", swap[j])
+    have[top] = replace(
+        far,
+        lax.ppermute(merged, "tensor", jump[top]),
+        [have[1]] + [crossed[p] for p in away[0]],
+    )
+    whole = replace(sent, merged, []) if top > 2 else sent
     for k in sorted(range(2, nz), key=lambda k: (k & (k - 1), k)):
         if k != top:
-            have[k] = lax.ppermute(have[k ^ (k & -k)], "tensor", jump[k & -k])
+            rest = k & (k - 1)
+            have[k] = lax.ppermute(have[rest] if rest else whole, "tensor", jump[k & -k])
+    for p in away[1]:
+        crossed[p] = unchanged(unchanged(crossed[p]))
     places = [place for k in range(nz) for place in here[k] + away[k]]
     for k, j in places:
         if j and k > 1:
             crossed[k, j] = lax.ppermute(have[k], "tensor", swap[j])
     pieces = {(k, j): crossed[k, j] if j else have[k] for k, j in places}
     alone = here[1] + away[1]
-    tables = [have[k] for k in range(nz) if k != 1] + [pieces[p] for p in alone]
+    tables = [merged] + [have[k] for k in range(2, nz)] + [pieces[p] for p in alone]
     counts = [nx * local] * (nz - 1) + [local] * len(alone)
     first, last = places[: 1 - nx], places[1 - nx :]
     result = finish(first, splits, [pieces[p] for p in first], tables, counts, [], n * local)

time: 71.2 us -> 71.7 us (level)
  waiting for transfers between devices: 25.5 us -> 26.6 us
    ppermute x5 -> x4, starting transfers between devices: 5.91 us -> 3.37 us  [the longest x1 3.35 us: body(): far = lax.ppermute(sent, 'tensor', jump[top])]
    ppermute x2 -> x4, starting transfers between devices: 2.56 us -> 4.5 us  [body(): crossed[k, j] = lax.ppermute(have[k], 'tensor', swap[j])]
    ppermute x1, waiting for transfers between devices: 1.69 us -> 0.01 us  [body(): others = [lax.ppermute(stats, 'tensor', swap[j]) for j in range(1, nx)]]
    ppermute x2 -> x4, waiting for transfers between devices: 0.59 us -> 2.22 us  [body(): crossed[k, j] = lax.ppermute(have[k], 'tensor', swap[j])]
    ppermute x5 -> x4, waiting for transfers between devices: 14 us -> 15.2 us  [the longest x1 5.41 us: body(): have = {0: sent, 1: lax.ppermute(sent, 'tensor', jump[1])}]
  transfers between devices with their start and end apart: 15 -> 16, of which waited for: 9 -> 9; matrix products, arithmetic and copies ran while one was open for 0% -> 0% of each run, Pallas kernels for 25% -> 25%
where the time goes in v8:
time: 71.7 us; the launch traced here: 71.6 us
  waiting for transfers between devices  26.6 us (37%)
  Pallas kernels  23 us (32%)
  starting transfers between devices  20.2 us (28%)
  local copies, waits for them, and re-layouts  0.92 us (1%)
  between operations  0.77 us (1%)
    pallas_call x4, Pallas kernels, products(): pl.pallas_call(functools.partial(product_kernel, targets, splits, local,...  15.8 us
    ppermute x3, waiting for transfers between devices, body(): joined_to = lax.ppermute(total, 'tensor', jump[bit])  7.29 us
    ppermute x3, starting transfers between devices, body(): joined_to = lax.ppermute(total, 'tensor', jump[bit])  6.19 us
    pallas_call x2, Pallas kernels, finish(): pl.pallas_call(functools.partial(finish_kernel, places, splits, counts, t...  6.13 us
    ppermute x1, waiting for transfers between devices, body(): have = {0: sent, 1: lax.ppermute(sent, 'tensor', jump[1])}  5.41 us
    ppermute x1, waiting for transfers between devices, body(): lax.ppermute(have[rest] if rest else whole, 'tensor', jump[k & -k])  5.26 us
    ppermute x3, starting transfers between devices, body(): result = lax.ppermute(result, 'tensor', swap[j])  4.62 us
    ppermute x4, starting transfers between devices, body(): crossed[k, j] = lax.ppermute(have[k], 'tensor', swap[j])  4.5 us
  transfers between devices with their start and end apart: 16, of which 9 were waited for; matrix products, arithmetic and copies ran while one was open for 0% of the time, Pallas kernels for 25%

profile of v8, /device:TPU:0, one launch (start us, length us, event | category | flops | bytes accessed | tf_op | source)
XLA Modules:
  0.0 71.6 jit_solution(12704302317629989322)
XLA Ops:
  0.6 0.0 copy-start
  0.6 0.9 %copy-done = bf16[64,1024]{1,0:T(8,128)(2,1)S(1)} copy-done((bf16[64,1024]{1,0:T(8,128)(2,1)S(1)}, bf16[64,1024]{1,0:T(8,128)(2,1)}, u32[]{:S(2)}) %copy-start) | copy-done | bytes 131096
  1.5 2.7 %products.4.refs_0_ = bf16[64,2048]{1,0:T(8,128)(2,1)S(1)} custom-call(bf16[64,1024]{1,0:T(8,128)(2,1)S(1)} %copy-done, bf16[1024,16384]{1,0:T(8,128)(2,1)} %weight_ref.7), custom_call_target="tpu_custom_call" | custom-call | flops 268435456 | bytes 4194304 | tf_op jit(solution)/shard_map/products/pallas_call | solution.py:72
  4.2 3.0 %collective-permute-start = (bf16[64,2048]{1,0:T(8,128)(2,1)S(1)}, bf16[64,2048]{1,0:T(8,128)(2,1)S(1)}, u32[]{:S(2)}, u32[]{:S(2)}) collective-permute-start(bf16[64,2048]{1,0:T(8,128)(2,1)S(1)} %products.4.refs_0_), channel_id=1, source_target_pairs={{0,1},{1,0},{2,3},{3,2},{4,5},{5,4},{6,7},{7,6},{8,9},{9,8},{10,11... | collective-permute-start | bytes 786440 | tf_op jit(solution)/shard_map/ppermute | solution.py:352
  7.2 5.2 %products.5 = (bf16[64,2048]{1,0:T(8,128)(2,1)S(1)}, bf16[64,2048]{1,0:T(8,128)(2,1)S(1)}, f32[64,2048]{1,0:T(8,128)S(1)}) custom-call(bf16[64,1024]{1,0:T(8,128)(2,1)S(1)} %copy-done, bf16[1024,16384]{1,0:T(8,128)(2,1)} %weight_ref.7, bf16[64,2048]{1,0:T(8,128)(2,1)S(1)} %products.4.refs_0_), custom_call_target="tpu_custom_call" | custom-call | flops 805306368 | bytes 12582912 | tf_op jit(solution)/shard_map/products/pallas_call | solution.py:72
  12.5 0.1 collective-permute-start.1
  12.6 0.9 %collective-permute-done = bf16[64,2048]{1,0:T(8,128)(2,1)S(1)} collective-permute-done((bf16[64,2048]{1,0:T(8,128)(2,1)S(1)}, bf16[64,2048]{1,0:T(8,128)(2,1)S(1)}, u32[]{:S(2)}, u32[]{:S(2)}) %collective-permute-start) | collective-permute-done | bytes 262176 | tf_op jit(solution)/shard_map/ppermute | solution.py:352
  13.6 1.9 %collective-permute-start.2 = (bf16[64,2048]{1,0:T(8,128)(2,1)S(1)}, bf16[64,2048]{1,0:T(8,128)(2,1)S(1)}, u32[]{:S(2)}, u32[]{:S(2)}) collective-permute-start(bf16[64,2048]{1,0:T(8,128)(2,1)S(1)} %add_convert_fusion.2.refs_0_), channel_id=1, source_target_pairs={{0,2},{1,3},{2,0},{3,1},{4,6},{5,7},{6,4},{7,5},{8,10},{9,11},{10,... | collective-permute-start | bytes 786440 | tf_op jit(solution)/shard_map/ppermute | solution.py:370
  15.5 1.5 %collective-permute-start.5 = (bf16[64,2048]{1,0:T(8,128)(2,1)S(1)}, bf16[64,2048]{1,0:T(8,128)(2,1)S(1)}, u32[]{:S(2)}, u32[]{:S(2)}) collective-permute-start(bf16[64,2048]{1,0:T(8,128)(2,1)S(1)} %get-tuple-element.17), channel_id=1, source_target_pairs={{0,1},{1,0},{2,3},{3,2},{4,5},{5,4},{6,7},{7,6},{8,9},{9,8},{10,11... | collective-permute-start | bytes 786440 | tf_op jit(solution)/shard_map/ppermute | solution.py:352
  17.0 5.2 %products.6 = (bf16[64,2048]{1,0:T(8,128)(2,1)S(1)}, f32[64,2048]{1,0:T(8,128)S(1)}, f32[64,2048]{1,0:T(8,128)S(1)}) custom-call(bf16[64,1024]{1,0:T(8,128)(2,1)S(1)} %copy-done, bf16[1024,16384]{1,0:T(8,128)(2,1)} %weight_ref.7, bf16[64,2048]{1,0:T(8,128)(2,1)S(1)} %add_convert_fusion.2.refs_0_), custom_call_target="tpu_custom_call" | custom-call | flops 805306368 | bytes 12582912 | tf_op jit(solution)/shard_map/products/pallas_call | solution.py:72
  22.2 0.0 collective-permute-done.1
  22.2 0.0 collective-permute-done.2
  22.2 0.1 add_convert_fusion.1.refs_1_
  22.3 2.7 %collective-permute-start.4 = (bf16[64,2048]{1,0:T(8,128)(2,1)S(1)}, bf16[64,2048]{1,0:T(8,128)(2,1)S(1)}, u32[]{:S(2)}, u32[]{:S(2)}) collective-permute-start(bf16[64,2048]{1,0:T(8,128)(2,1)S(1)} %add_convert_fusion.1.refs_1_), channel_id=1, source_target_pairs={{0,4},{1,5},{2,6},{3,7},{4,0},{5,1},{6,2},{7,3},{8,12},{9,13},{10,... | collective-permute-start | bytes 786440 | tf_op jit(solution)/shard_map/ppermute | solution.py:370
  25.0 0.9 %collective-permute-done.5 = bf16[64,2048]{1,0:T(8,128)(2,1)S(1)} collective-permute-done((bf16[64,2048]{1,0:T(8,128)(2,1)S(1)}, bf16[64,2048]{1,0:T(8,128)(2,1)S(1)}, u32[]{:S(2)}, u32[]{:S(2)}) %collective-permute-start.5) | collective-permute-done | bytes 262176 | tf_op jit(solution)/shard_map/ppermute | solution.py:352
  26.0 1.6 %collective-permute-start.6 = (bf16[64,2048]{1,0:T(8,128)(2,1)S(1)}, bf16[64,2048]{1,0:T(8,128)(2,1)S(1)}, u32[]{:S(2)}, u32[]{:S(2)}) collective-permute-start(bf16[64,2048]{1,0:T(8,128)(2,1)S(1)} %add_convert_fusion.refs_0_), channel_id=1, source_target_pairs={{0,2},{1,3},{2,0},{3,1},{4,6},{5,7},{6,4},{7,5},{8,10},{9,11},{10,... | collective-permute-start | bytes 786440 | tf_op jit(solution)/shard_map/ppermute | solution.py:370
  27.6 0.6 collective-permute-start.3
  28.2 2.7 %products.7.refs_3_ = f32[64,2048]{1,0:T(8,128)S(1)} custom-call(bf16[64,1024]{1,0:T(8,128)(2,1)S(1)} %copy-done, bf16[1024,16384]{1,0:T(8,128)(2,1)} %weight_ref.7, bf16[64,2048]{1,0:T(8,128)(2,1)S(1)} %add_convert_fusion.refs_0_, bf16[64,2048]{1,0:T(8,128)(2,1)S(1)} %unchanged.5.refs_1_), custom_call_target="tpu_custom_call" | custom-call | flops 268435456 | bytes 4194304 | tf_op jit(solution)/shard_map/products/pallas_call | solution.py:72
  30.9 0.0 copy-start.1
  30.9 0.0 copy-start.2
  30.9 0.0 copy-start.3
  30.9 4.6 %collective-permute-done.4.refs_0_ = bf16[64,2048]{1,0:T(8,128)(2,1)S(1)} collective-permute-done((bf16[64,2048]{1,0:T(8,128)(2,1)S(1)}, bf16[64,2048]{1,0:T(8,128)(2,1)S(1)}, u32[]{:S(2)}, u32[]{:S(2)}) %collective-permute-start.4) | collective-permute-done | bytes 262176 | tf_op jit(solution)/shard_map/ppermute | solution.py:370
  35.5 2.7 %collective-permute-done.6.refs_2_ = bf16[64,2048]{1,0:T(8,128)(2,1)S(1)} collective-permute-done((bf16[64,2048]{1,0:T(8,128)(2,1)S(1)}, bf16[64,2048]{1,0:T(8,128)(2,1)S(1)}, u32[]{:S(2)}, u32[]{:S(2)}) %collective-permute-start.6) | collective-permute-done | bytes 262176 | tf_op jit(solution)/shard_map/ppermute | solution.py:370
  38.2 0.0 collective-permute-done.3.refs_0_
  38.2 0.0 copy-done.1
  38.2 0.0 copy-done.2
  38.2 0.0 copy-done.3
  38.2 1.0 %own_stream.1 = (bf16[64,2048]{1,0:T(8,128)(2,1)}, bf16[64,2176]{1,0:T(8,128)(2,1)S(1)}, bf16[16,128]{1,0:T(8,128)(2,1)S(1)}) custom-call(bf16[64,2048]{1,0:T(8,128)(2,1)S(1)} %copy-done.1, bf16[16,128]{1,0:T(8,128)(2,1)S(1)} %bitcast.2, bf16[16,128]{1,0:T(8,128)(2,1)S(1)} %bitcast.3, bf16[64,2048]{1,0:T(8,128)(2,1)S(1)} %collective-permute-done.3.refs_0_, ...), custom_call_target="tpu_custom_call" | custom-call | flops 2621440 | bytes 2097152 | tf_op jit(solution)/shard_map/own_stream/pallas_call | solution.py:138
  39.2 0.0 collective-permute-start.10
  39.2 0.9 %collective-permute-start.8 = (bf16[16,128]{1,0:T(8,128)(2,1)S(1)}, bf16[16,128]{1,0:T(8,128)(2,1)S(1)}, u32[]{:S(2)}, u32[]{:S(2)}) collective-permute-start(bf16[16,128]{1,0:T(8,128)(2,1)S(1)} %get-tuple-element.21.refs_0_), channel_id=1, source_target_pairs={{0,1},{1,0},{2,3},{3,2},{4,5},{5,4},{6,7},{7,6},{8,9},{9,8},{10,11... | collective-permute-start | bytes 12296 | tf_op jit(solution)/shard_map/ppermute | solution.py:379
  40.1 1.1 %collective-permute-start.11 = (bf16[64,2176]{1,0:T(8,128)(2,1)S(1)}, bf16[64,2176]{1,0:T(8,128)(2,1)S(1)}, u32[]{:S(2)}, u32[]{:S(2)}) collective-permute-start(bf16[64,2176]{1,0:T(8,128)(2,1)S(1)} %get-tuple-element.20.refs_0_), channel_id=1, source_target_pairs={{0,1},{1,0},{2,3},{3,2},{4,5},{5,4},{6,7},{7,6},{8,9},{9,8},{10,11... | collective-permute-start | bytes 835592 | tf_op jit(solution)/shard_map/ppermute | solution.py:384
  41.2 3.4 %collective-permute-start.7 = (bf16[64,2176]{1,0:T(8,128)(2,1)S(1)}, bf16[64,2176]{1,0:T(8,128)(2,1)S(1)}, u32[]{:S(2)}, u32[]{:S(2)}) collective-permute-start(bf16[64,2176]{1,0:T(8,128)(2,1)S(1)} %get-tuple-element.20.refs_0_), channel_id=1, source_target_pairs={{0,4},{1,5},{2,6},{3,7},{4,0},{5,1},{6,2},{7,3},{8,12},{9,13},{10,... | collective-permute-start | bytes 835592 | tf_op jit(solution)/shard_map/ppermute | solution.py:378
  44.6 0.0 collective-permute-done.8.refs_1_
  44.6 5.4 %collective-permute-done.10.refs_0_ = bf16[64,2176]{1,0:T(8,128)(2,1)S(1)} collective-permute-done((bf16[64,2176]{1,0:T(8,128)(2,1)S(1)}, bf16[64,2176]{1,0:T(8,128)(2,1)S(1)}, u32[]{:S(2)}, u32[]{:S(2)}) %collective-permute-start.10) | collective-permute-done | bytes 278560 | tf_op jit(solution)/shard_map/ppermute | solution.py:376
  50.0 1.3 %collective-permute-start.14 = (bf16[64,2176]{1,0:T(8,128)(2,1)S(1)}, bf16[64,2176]{1,0:T(8,128)(2,1)S(1)}, u32[]{:S(2)}, u32[]{:S(2)}) collective-permute-start(bf16[64,2176]{1,0:T(8,128)(2,1)S(1)} %unchanged.7.refs_0_.refs_2_.refs_10_), channel_id=1, source_target_pairs={{0,1},{1,0},{2,3},{3,2},{4,5},{5,4},{6,7},{7,6},{8,9},{9,8},{10,11... | collective-permute-start | bytes 835592 | tf_op jit(solution)/shard_map/ppermute | solution.py:384
  51.3 0.0 collective-permute-start.9
  51.3 4.5 %collective-permute-done.9.table_ref = bf16[16,128]{1,0:T(8,128)(2,1)S(1)} collective-permute-done((bf16[16,128]{1,0:T(8,128)(2,1)S(1)}, bf16[16,128]{1,0:T(8,128)(2,1)S(1)}, u32[]{:S(2)}, u32[]{:S(2)}) %collective-permute-start.9) | collective-permute-done | bytes 4128 | tf_op jit(solution)/shard_map/ppermute | solution.py:387
  55.8 0.0 collective-permute-done.11.refs_1_
  55.8 0.0 collective-permute-done.7.piece_ref
  55.9 1.2 %collective-permute-start.15 = (bf16[64,2176]{1,0:T(8,128)(2,1)S(1)}, bf16[64,2176]{1,0:T(8,128)(2,1)S(1)}, u32[]{:S(2)}, u32[]{:S(2)}) collective-permute-start(bf16[64,2176]{1,0:T(8,128)(2,1)S(1)} %replace.1.refs_4_.refs_8_), channel_id=1, source_target_pairs={{0,1},{1,0},{2,3},{3,2},{4,5},{5,4},{6,7},{7,6},{8,9},{9,8},{10,11... | collective-permute-start | bytes 835592 | tf_op jit(solution)/shard_map/ppermute | solution.py:400
  57.1 0.0 collective-permute-start.12
  57.1 1.3 %collective-permute-done.14.refs_0_ = bf16[64,2176]{1,0:T(8,128)(2,1)S(1)} collective-permute-done((bf16[64,2176]{1,0:T(8,128)(2,1)S(1)}, bf16[64,2176]{1,0:T(8,128)(2,1)S(1)}, u32[]{:S(2)}, u32[]{:S(2)}) %collective-permute-start.14) | collective-permute-done | bytes 278560 | tf_op jit(solution)/shard_map/ppermute | solution.py:384
  58.3 5.3 %collective-permute-done.12.refs_6_.refs_9_ = bf16[64,2176]{1,0:T(8,128)(2,1)S(1)} collective-permute-done((bf16[64,2176]{1,0:T(8,128)(2,1)S(1)}, bf16[64,2176]{1,0:T(8,128)(2,1)S(1)}, u32[]{:S(2)}, u32[]{:S(2)}) %collective-permute-start.12) | collective-permute-done | bytes 278560 | tf_op jit(solution)/shard_map/ppermute | solution.py:394
  63.6 0.9 %collective-permute-start.13 = (bf16[64,2176]{1,0:T(8,128)(2,1)S(1)}, bf16[64,2176]{1,0:T(8,128)(2,1)S(1)}, u32[]{:S(2)}, u32[]{:S(2)}) collective-permute-start(bf16[64,2176]{1,0:T(8,128)(2,1)S(1)} %collective-permute-done.12.refs_6_.refs_9_), channel_id=1, source_target_pairs={{0,1},{1,0},{2,3},{3,2},{4,5},{5,4},{6,7},{7,6},{8,9},{9,8},{10,11... | collective-permute-start | bytes 835592 | tf_op jit(solution)/shard_map/ppermute | solution.py:400
  64.5 0.0 collective-permute-done.15.refs_5_
  64.5 4.7 %finish.2 = (bf16[64,16384]{1,0:T(8,128)(2,1)}, f32[64,128]{1,0:T(8,128)S(1)}) custom-call(bf16[64,2176]{1,0:T(8,128)(2,1)S(1)} %get-tuple-element.20.refs_0_, bf16[64,2176]{1,0:T(8,128)(2,1)S(1)} %collective-permute-done.11.refs_1_, bf16[64,2176]{1,0:T(8,128)(2,1)S(1)} %unchanged.7.refs_0_.refs_2_.refs_10_, bf16[64,2176]{1,0:T(8,128)(2,1)S(1)} %unchanged.9.refs_3_.refs_11_, ...), custom_call_target="tpu_custom_call" | custom-call | flops 939524096 | bytes 3670016 | tf_op jit(solution)/shard_map/finish/pallas_call | solution.py:303
  69.2 0.9 %collective-permute-done.13.refs_0_ = bf16[64,2176]{1,0:T(8,128)(2,1)S(1)} collective-permute-done((bf16[64,2176]{1,0:T(8,128)(2,1)S(1)}, bf16[64,2176]{1,0:T(8,128)(2,1)S(1)}, u32[]{:S(2)}, u32[]{:S(2)}) %collective-permute-start.13) | collective-permute-done | bytes 278560 | tf_op jit(solution)/shard_map/ppermute | solution.py:400
  70.2 1.4 %finish.3 = bf16[64,16384]{1,0:T(8,128)(2,1)} custom-call(bf16[64,2176]{1,0:T(8,128)(2,1)S(1)} %collective-permute-done.13.refs_0_, f32[64,128]{1,0:T(8,128)S(1)} %get-tuple-element.22.refs_1_, bf16[64,16384]{1,0:T(8,128)(2,1)} %get-tuple-element.23.refs_2_), custom_call_target="tpu_custom_call", output_to_operand_aliasing={{}: (2, {})} | custom-call | flops 134217728 | bytes 524288 | tf_op jit(solution)/shard_map/finish/pallas_call | solution.py:303
  (9 shorter events, 0.1 us)
Async XLA Ops:
  0.6 0.9 %copy-start = (bf16[64,1024]{1,0:T(8,128)(2,1)S(1)}, bf16[64,1024]{1,0:T(8,128)(2,1)}, u32[]{:S(2)}) copy-start(bf16[64,1024]{1,0:T(8,128)(2,1)} %rows_ref.7) | copy-start | bytes 393220
  4.2 9.3 %collective-permute-start = (bf16[64,2048]{1,0:T(8,128)(2,1)S(1)}, bf16[64,2048]{1,0:T(8,128)(2,1)S(1)}, u32[]{:S(2)}, u32[]{:S(2)}) collective-permute-start(bf16[64,2048]{1,0:T(8,128)(2,1)S(1)} %products.4.refs_0_), channel_id=1, source_target_pairs={{0,1},{1,0},{2,3},{3,2},{4,5},{5,4},{6,7},{7,6},{8,9},{9,8},{10,11... | collective-permute-start | bytes 786440 | tf_op jit(solution)/shard_map/ppermute | solution.py:352
  12.5 9.7 %collective-permute-start.1 = (bf16[64,2048]{1,0:T(8,128)(2,1)S(1)}, bf16[64,2048]{1,0:T(8,128)(2,1)S(1)}, u32[]{:S(2)}, u32[]{:S(2)}) collective-permute-start(bf16[64,2048]{1,0:T(8,128)(2,1)S(1)} %get-tuple-element.15), channel_id=1, source_target_pairs={{0,1},{1,0},{2,3},{3,2},{4,5},{5,4},{6,7},{7,6},{8,9},{9,8},{10,11... | collective-permute-start | bytes 786440 | tf_op jit(solution)/shard_map/ppermute | solution.py:352
  13.6 8.6 %collective-permute-start.2 = (bf16[64,2048]{1,0:T(8,128)(2,1)S(1)}, bf16[64,2048]{1,0:T(8,128)(2,1)S(1)}, u32[]{:S(2)}, u32[]{:S(2)}) collective-permute-start(bf16[64,2048]{1,0:T(8,128)(2,1)S(1)} %add_convert_fusion.2.refs_0_), channel_id=1, source_target_pairs={{0,2},{1,3},{2,0},{3,1},{4,6},{5,7},{6,4},{7,5},{8,10},{9,11},{10,... | collective-permute-start | bytes 786440 | tf_op jit(solution)/shard_map/ppermute | solution.py:370
  15.5 10.4 %collective-permute-start.5 = (bf16[64,2048]{1,0:T(8,128)(2,1)S(1)}, bf16[64,2048]{1,0:T(8,128)(2,1)S(1)}, u32[]{:S(2)}, u32[]{:S(2)}) collective-permute-start(bf16[64,2048]{1,0:T(8,128)(2,1)S(1)} %get-tuple-element.17), channel_id=1, source_target_pairs={{0,1},{1,0},{2,3},{3,2},{4,5},{5,4},{6,7},{7,6},{8,9},{9,8},{10,11... | collective-permute-start | bytes 786440 | tf_op jit(solution)/shard_map/ppermute | solution.py:352
  22.3 13.2 %collective-permute-start.4 = (bf16[64,2048]{1,0:T(8,128)(2,1)S(1)}, bf16[64,2048]{1,0:T(8,128)(2,1)S(1)}, u32[]{:S(2)}, u32[]{:S(2)}) collective-permute-start(bf16[64,2048]{1,0:T(8,128)(2,1)S(1)} %add_convert_fusion.1.refs_1_), channel_id=1, source_target_pairs={{0,4},{1,5},{2,6},{3,7},{4,0},{5,1},{6,2},{7,3},{8,12},{9,13},{10,... | collective-permute-start | bytes 786440 | tf_op jit(solution)/shard_map/ppermute | solution.py:370
  26.0 12.2 %collective-permute-start.6 = (bf16[64,2048]{1,0:T(8,128)(2,1)S(1)}, bf16[64,2048]{1,0:T(8,128)(2,1)S(1)}, u32[]{:S(2)}, u32[]{:S(2)}) collective-permute-start(bf16[64,2048]{1,0:T(8,128)(2,1)S(1)} %add_convert_fusion.refs_0_), channel_id=1, source_target_pairs={{0,2},{1,3},{2,0},{3,1},{4,6},{5,7},{6,4},{7,5},{8,10},{9,11},{10,... | collective-permute-start | bytes 786440 | tf_op jit(solution)/shard_map/ppermute | solution.py:370
  27.6 10.6 %collective-permute-start.3 = (bf16[64,2048]{1,0:T(8,128)(2,1)S(1)}, bf16[64,2048]{1,0:T(8,128)(2,1)S(1)}, u32[]{:S(2)}, u32[]{:S(2)}) collective-permute-start(bf16[64,2048]{1,0:T(8,128)(2,1)S(1)} %unchanged.5.refs_1_), channel_id=1, source_target_pairs={{0,1},{1,0},{2,3},{3,2},{4,5},{5,4},{6,7},{7,6},{8,9},{9,8},{10,11... | collective-permute-start | bytes 786440 | tf_op jit(solution)/shard_map/ppermute | solution.py:368
  30.9 7.3 %copy-start.1 = (bf16[64,2048]{1,0:T(8,128)(2,1)S(1)}, bf16[64,2048]{1,0:T(8,128)(2,1)}, u32[]{:S(2)}) copy-start(bf16[64,2048]{1,0:T(8,128)(2,1)} %residual_ref.1) | copy-start | bytes 786436
  30.9 7.3 %copy-start.2 = (bf16[2048]{0:T(1024)(128)(2,1)S(1)}, bf16[2048]{0:T(1024)(128)(2,1)}, u32[]{:S(2)}) copy-start(bf16[2048]{0:T(1024)(128)(2,1)} %param.8) | copy-start | bytes 12292
  30.9 7.3 %copy-start.3 = (bf16[2048]{0:T(1024)(128)(2,1)S(1)}, bf16[2048]{0:T(1024)(128)(2,1)}, u32[]{:S(2)}) copy-start(bf16[2048]{0:T(1024)(128)(2,1)} %param.9) | copy-start | bytes 12292
  39.2 10.8 %collective-permute-start.10 = (bf16[64,2176]{1,0:T(8,128)(2,1)S(1)}, bf16[64,2176]{1,0:T(8,128)(2,1)S(1)}, u32[]{:S(2)}, u32[]{:S(2)}) collective-permute-start(bf16[64,2176]{1,0:T(8,128)(2,1)S(1)} %get-tuple-element.20.refs_0_), channel_id=1, source_target_pairs={{0,2},{1,3},{2,0},{3,1},{4,6},{5,7},{6,4},{7,5},{8,10},{9,11},{10,... | collective-permute-start | bytes 835592 | tf_op jit(solution)/shard_map/ppermute | solution.py:376
  39.2 5.4 %collective-permute-start.8 = (bf16[16,128]{1,0:T(8,128)(2,1)S(1)}, bf16[16,128]{1,0:T(8,128)(2,1)S(1)}, u32[]{:S(2)}, u32[]{:S(2)}) collective-permute-start(bf16[16,128]{1,0:T(8,128)(2,1)S(1)} %get-tuple-element.21.refs_0_), channel_id=1, source_target_pairs={{0,1},{1,0},{2,3},{3,2},{4,5},{5,4},{6,7},{7,6},{8,9},{9,8},{10,11... | collective-permute-start | bytes 12296 | tf_op jit(solution)/shard_map/ppermute | solution.py:379
  40.1 15.7 %collective-permute-start.11 = (bf16[64,2176]{1,0:T(8,128)(2,1)S(1)}, bf16[64,2176]{1,0:T(8,128)(2,1)S(1)}, u32[]{:S(2)}, u32[]{:S(2)}) collective-permute-start(bf16[64,2176]{1,0:T(8,128)(2,1)S(1)} %get-tuple-element.20.refs_0_), channel_id=1, source_target_pairs={{0,1},{1,0},{2,3},{3,2},{4,5},{5,4},{6,7},{7,6},{8,9},{9,8},{10,11... | collective-permute-start | bytes 835592 | tf_op jit(solution)/shard_map/ppermute | solution.py:384
  41.2 14.6 %collective-permute-start.7 = (bf16[64,2176]{1,0:T(8,128)(2,1)S(1)}, bf16[64,2176]{1,0:T(8,128)(2,1)S(1)}, u32[]{:S(2)}, u32[]{:S(2)}) collective-permute-start(bf16[64,2176]{1,0:T(8,128)(2,1)S(1)} %get-tuple-element.20.refs_0_), channel_id=1, source_target_pairs={{0,4},{1,5},{2,6},{3,7},{4,0},{5,1},{6,2},{7,3},{8,12},{9,13},{10,... | collective-permute-start | bytes 835592 | tf_op jit(solution)/shard_map/ppermute | solution.py:378
  50.0 8.3 %collective-permute-start.14 = (bf16[64,2176]{1,0:T(8,128)(2,1)S(1)}, bf16[64,2176]{1,0:T(8,128)(2,1)S(1)}, u32[]{:S(2)}, u32[]{:S(2)}) collective-permute-start(bf16[64,2176]{1,0:T(8,128)(2,1)S(1)} %unchanged.7.refs_0_.refs_2_.refs_10_), channel_id=1, source_target_pairs={{0,1},{1,0},{2,3},{3,2},{4,5},{5,4},{6,7},{7,6},{8,9},{9,8},{10,11... | collective-permute-start | bytes 835592 | tf_op jit(solution)/shard_map/ppermute | solution.py:384
  51.3 4.5 %collective-permute-start.9 = (bf16[16,128]{1,0:T(8,128)(2,1)S(1)}, bf16[16,128]{1,0:T(8,128)(2,1)S(1)}, u32[]{:S(2)}, u32[]{:S(2)}) collective-permute-start(bf16[16,128]{1,0:T(8,128)(2,1)S(1)} %merge.1.refs_1_.refs_7_), channel_id=1, source_target_pairs={{0,4},{1,5},{2,6},{3,7},{4,0},{5,1},{6,2},{7,3},{8,12},{9,13},{10,... | collective-permute-start | bytes 12296 | tf_op jit(solution)/shard_map/ppermute | solution.py:387
  55.9 8.6 %collective-permute-start.15 = (bf16[64,2176]{1,0:T(8,128)(2,1)S(1)}, bf16[64,2176]{1,0:T(8,128)(2,1)S(1)}, u32[]{:S(2)}, u32[]{:S(2)}) collective-permute-start(bf16[64,2176]{1,0:T(8,128)(2,1)S(1)} %replace.1.refs_4_.refs_8_), channel_id=1, source_target_pairs={{0,1},{1,0},{2,3},{3,2},{4,5},{5,4},{6,7},{7,6},{8,9},{9,8},{10,11... | collective-permute-start | bytes 835592 | tf_op jit(solution)/shard_map/ppermute | solution.py:400
  57.1 6.5 %collective-permute-start.12 = (bf16[64,2176]{1,0:T(8,128)(2,1)S(1)}, bf16[64,2176]{1,0:T(8,128)(2,1)S(1)}, u32[]{:S(2)}, u32[]{:S(2)}) collective-permute-start(bf16[64,2176]{1,0:T(8,128)(2,1)S(1)} %replace.1.refs_4_.refs_8_), channel_id=1, source_target_pairs={{0,2},{1,3},{2,0},{3,1},{4,6},{5,7},{6,4},{7,5},{8,10},{9,11},{10,... | collective-permute-start | bytes 835592 | tf_op jit(solution)/shard_map/ppermute | solution.py:394
  63.6 6.5 %collective-permute-start.13 = (bf16[64,2176]{1,0:T(8,128)(2,1)S(1)}, bf16[64,2176]{1,0:T(8,128)(2,1)S(1)}, u32[]{:S(2)}, u32[]{:S(2)}) collective-permute-start(bf16[64,2176]{1,0:T(8,128)(2,1)S(1)} %collective-permute-done.12.refs_6_.refs_9_), channel_id=1, source_target_pairs={{0,1},{1,0},{2,3},{3,2},{4,5},{5,4},{6,7},{7,6},{8,9},{9,8},{10,11... | collective-permute-start | bytes 835592 | tf_op jit(solution)/shard_map/ppermute | solution.py:400

commit v9 on v7

--- a/solution.py
+++ b/solution.py
@@ -37,7 +37,9 @@
 def product_kernel(targets, splits, local, tile, rows_ref, weight_ref, *refs):
     count = len(targets)
     held, scratch, semaphores = refs[-3:]
-    outs = refs[-3 - count : -3]
+    token = refs[-4]
+    outs = refs[-4 - count : -4]
+    token[...] = jnp.zeros_like(token)
     nx, per = splits[1], local // tile
     me = lax.axis_index("tensor")
     outer, inner = me // nx, lax.rem(me, nx)
@@ -74,17 +76,18 @@
         out_shape=[
             jax.ShapeDtypeStruct((rows, local), jnp.bfloat16 if j else jnp.float32)
             for _, j in targets
-        ],
+        ]
+        + [jax.ShapeDtypeStruct((8, LANES), jnp.float32)],
         in_specs=[pl.BlockSpec(memory_space=pltpu.HBM)] * 2
         + [pl.BlockSpec(memory_space=pl.ANY)] * len(after),
-        out_specs=[vmem] * len(targets),
+        out_specs=[vmem] * (len(targets) + 1),
         scratch_shapes=[
             pltpu.VMEM((rows, depth), jnp.bfloat16),
             pltpu.VMEM((slots, depth, tile), jnp.bfloat16),
             pltpu.SemaphoreType.DMA((slots + 1,)),
         ],
         compiler_params=pltpu.CompilerParams(
-            vmem_limit_bytes=40 * MIB
+            vmem_limit_bytes=(40 if after else 60) * MIB
         ),
         cost_estimate=pl.CostEstimate(
             flops=2 * rows * depth * local * len(targets),
@@ -105,7 +108,7 @@
 
 
 def stream_kernel(count, residual_ref, gain_ref, bias_ref, *refs):
-    terms, (half_ref, sent_ref, stats_ref) = refs[:count], refs[count:]
+    terms, (half_ref, sent_ref, stats_ref, *head) = refs[:count], refs[count:]
     stream = residual_ref[...].astype(jnp.float32)
     for term in terms:
         stream = stream + term[...].astype(jnp.float32)
@@ -113,6 +116,8 @@
     half = stream.astype(half_ref.dtype)
     half_ref[...] = half
     sent_ref[:, :width] = half
+    for ref in head:
+        ref[...] = half[:, : ref.shape[1]]
     mean = jnp.sum(stream, axis=1, keepdims=True) / width
     square = jnp.sum((stream - mean) ** 2, axis=1, keepdims=True)
     lane = lax.broadcasted_iota(jnp.int32, (rows, LANES), 1)
@@ -132,7 +137,7 @@
     ).astype(sent_ref.dtype)
 
 
-def own_stream(residual, gain, bias, terms):
+def own_stream(residual, gain, bias, terms, first):
     rows, local = residual.shape
     blocks = local // LANES
     return pl.pallas_call(
@@ -141,7 +146,8 @@
             jax.ShapeDtypeStruct((rows, local), jnp.bfloat16),
             jax.ShapeDtypeStruct((rows, local + LANES), jnp.bfloat16),
             jax.ShapeDtypeStruct((16, LANES), jnp.bfloat16),
-        ),
+        )
+        + (jax.ShapeDtypeStruct((rows, first), jnp.bfloat16),) * bool(first),
         compiler_params=pltpu.CompilerParams(vmem_limit_bytes=8 * MIB),
         cost_estimate=pl.CostEstimate(
             flops=20 * rows * local, bytes_accessed=16 * rows * local, transcendentals=0
@@ -183,36 +189,37 @@
     return centre, squares
 
 
-def merge_kernel(sent_ref, *refs):
+def merge_kernel(first, sent_ref, *refs):
     out_ref = refs[-1]
     rows = out_ref.shape[0]
-    local = out_ref.shape[1] - LANES
+    local = sent_ref.shape[1] - LANES
     tables = [sent_ref[0:8, local:]] + [ref[0:8] for ref in refs[:-1]]
     centre, squares = moments(tables, [local] * len(tables))
     row = lax.broadcasted_iota(jnp.int32, (rows, LANES), 0)
     table = sent_ref[:, local:].astype(jnp.float32)
     for place, part in enumerate(in_three(centre) + in_three(squares)):
         table = jnp.where(row == place, part, table)
-    out_ref[:, :local] = sent_ref[:, :local]
-    out_ref[:, local:] = table.astype(out_ref.dtype)
-
-
-def merge(sent, others):
+    out_ref[:, : local - first] = sent_ref[:, first:local]
+    out_ref[:, local - first :] = table.astype(out_ref.dtype)
+
+
+def merge(sent, others, first):
     return pl.pallas_call(
-        merge_kernel,
-        out_shape=jax.ShapeDtypeStruct(sent.shape, sent.dtype),
+        functools.partial(merge_kernel, first),
+        out_shape=jax.ShapeDtypeStruct((sent.shape[0], sent.shape[1] - first), sent.dtype),
         compiler_params=pltpu.CompilerParams(vmem_limit_bytes=4 * MIB),
         name="merge",
     )(sent, *others)
 
 
-def coded_rows(piece, local, centre, inverse, table):
-    rows, blocks = piece.shape[0], local // BLOCK_LEN
+def coded_rows(parts, local, centre, inverse, table):
+    rows, blocks = parts[0].shape[0], local // BLOCK_LEN
     unit = 1.0 / math.sqrt(BLOCK_LEN)
-    scaling = piece[rows - 2 * blocks :, local:].astype(jnp.float32)
+    columns = [part[:, c : c + LANES] for part in parts for c in range(0, part.shape[1], LANES)]
+    scaling = columns[-1][rows - 2 * blocks :].astype(jnp.float32)
     normal = []
     for b in range(blocks):
-        block = piece[:, b * BLOCK_LEN : (b + 1) * BLOCK_LEN].astype(jnp.float32)
+        block = columns[b].astype(jnp.float32)
         block = (block - centre) * inverse
         normal.append(block * scaling[b : b + 1] + scaling[blocks + b : blocks + b + 1])
     normal = jnp.concatenate(normal, axis=0)
@@ -228,13 +235,17 @@
     return back.astype(jnp.bfloat16)
 
 
-def finish_kernel(places, splits, counts, total, *refs):
-    pieces, refs = refs[: len(places)], refs[len(places) :]
-    rows = pieces[0].shape[0]
-    width = pieces[0].shape[1] - LANES
+def finish_kernel(places, splits, lengths, counts, total, *refs):
+    pieces = []
+    for length in lengths:
+        pieces.append(refs[:length])
+        refs = refs[length:]
+    rows, width = refs[-2].shape[1:]
     if counts:
         tables, (out_ref, columns_ref) = refs[: len(counts)], refs[-4:-2]
-        centre, squares = moments([t[0:8, width:] for t in tables], counts)
+        centre, squares = moments(
+            [t[0:8, t.shape[1] - LANES :] for t in tables], counts
+        )
         inverse = lax.rsqrt(squares / total + 1e-05)
         row = lax.broadcasted_iota(jnp.int32, (LANES, LANES), 0)
         table = jnp.where(row == 0, centre, jnp.where(row == 1, inverse, 0.0))
@@ -264,26 +275,28 @@
         copy.wait()
 
 
-def finish(places, splits, pieces, tables, counts, earlier, total):
-    rows, local = pieces[0].shape[0], pieces[0].shape[1] - LANES
+def finish(places, splits, pieces, local, tables, counts, earlier, total):
+    rows = pieces[0][0].shape[0]
     count = len(pieces)
+    lengths = [len(parts) for parts in pieces]
+    pieces = [part for parts in pieces for part in parts]
     vmem = pl.BlockSpec(memory_space=pltpu.VMEM)
     anywhere = pl.BlockSpec(memory_space=pl.ANY)
-    given = tables + earlier[::-1]
+    given = pieces + tables + earlier[::-1]
     out_shape = [jax.ShapeDtypeStruct((rows, total), jnp.bfloat16)]
     if not earlier:
         out_shape.append(jax.ShapeDtypeStruct((rows, LANES), jnp.float32))
     return pl.pallas_call(
-        functools.partial(finish_kernel, places, splits, counts, total),
+        functools.partial(finish_kernel, places, splits, lengths, counts, total),
         out_shape=out_shape,
-        in_specs=[vmem] * (count + len(given) - len(earlier) // 2)
+        in_specs=[vmem] * (len(given) - len(earlier) // 2)
         + [anywhere] * (len(earlier) // 2),
         out_specs=[anywhere, vmem][: len(out_shape)],
         scratch_shapes=[
             pltpu.VMEM((count, rows, local), jnp.bfloat16),
             pltpu.SemaphoreType.DMA((count,)),
         ],
-        input_output_aliases={count + len(given) - 1: 0} if earlier else {},
+        input_output_aliases={len(given) - 1: 0} if earlier else {},
         compiler_params=pltpu.CompilerParams(vmem_limit_bytes=16 * MIB),
         cost_estimate=pl.CostEstimate(
             flops=8 * BLOCK_LEN * rows * local * count,
@@ -291,7 +304,7 @@
             transcendentals=0,
         ),
         name="finish",
-    )(*pieces, *given)
+    )(*given)
 
 
 def body(attended, out_weight, residual, norm_gain, norm_bias):
@@ -316,10 +329,10 @@
     terms = {k: [] for k in range(nz)}
     after, held, released = [], [], []
     for targets, joined in zip(calls, joins):
-        results = products(
+        *results, token = products(
             attended, out_weight, targets, splits, local, after + released
         )
-        after = [results[-1]]
+        after = [token]
         for (k, j), result in zip(targets, results):
             if j and k:
                 result = lax.ppermute(result, "tensor", swap[j])
@@ -345,30 +358,47 @@
                 joined_to = unchanged(joined_to)
             terms[k ^ bit].append(joined_to)
 
-    stream_out, sent, stats = own_stream(residual, norm_gain, norm_bias, terms[0])
+    first = local // 2 if local % (2 * LANES) == 0 else 0
+    stream_out, sent, stats, *head = own_stream(
+        residual, norm_gain, norm_bias, terms[0], first
+    )
     others = [lax.ppermute(stats, "tensor", swap[j]) for j in range(1, nx)]
-    merged = merge(sent, others)
-    have = {0: merged, 1: lax.ppermute(sent, "tensor", jump[1])}
+    base = head + [merge(sent, others, first)]
+    top = nz // 2
+    near = unchanged(lax.ppermute(sent, "tensor", jump[1]), base[-1], cost=0)
+    have = {0: [sent], 1: [near]}
     crossed = {}
-    top = nz // 2
-    have[top] = lax.ppermute(merged, "tensor", jump[top])
     for k, j in away[0] + away[1]:
-        crossed[k, j] = lax.ppermute(have[k] if k else sent, "tensor", swap[j])
-    have[top] = unchanged(have[top], *crossed.values())
+        crossed[k, j] = [lax.ppermute(have[k][0], "tensor", swap[j])]
+    far = [lax.ppermute(part, "tensor", jump[top]) for part in base]
+    far[:-1] = [unchanged(part, near) for part in far[:-1]]
+    far[-1] = unchanged(far[-1], *far[:-1], *[crossed[p][0] for p in away[0] + away[1]])
+    have[top] = far
     for k in sorted(range(2, nz), key=lambda k: (k & (k - 1), k)):
         if k != top:
-            have[k] = lax.ppermute(have[k ^ (k & -k)], "tensor", jump[k & -k])
+            rest = k & (k - 1)
+            have[k] = [
+                lax.ppermute(part, "tensor", jump[k & -k])
+                for part in (have[rest] if rest else base)
+            ]
     places = [place for k in range(nz) for place in here[k] + away[k]]
     for k, j in places:
         if j and k > 1:
-            crossed[k, j] = lax.ppermute(have[k], "tensor", swap[j])
+            parts = [lax.ppermute(part, "tensor", swap[j]) for part in have[k]]
+            if k in (top, nz - 1):
+                parts[:-1] = [unchanged(part) for part in parts[:-1]]
+            crossed[k, j] = parts
     pieces = {(k, j): crossed[k, j] if j else have[k] for k, j in places}
     alone = here[1] + away[1]
-    tables = [have[k] for k in range(nz) if k != 1] + [pieces[p] for p in alone]
+    tables = [base[-1]] + [have[k][-1] for k in range(2, nz)] + [pieces[p][0] for p in alone]
     counts = [nx * local] * (nz - 1) + [local] * len(alone)
-    first, last = places[: 1 - nx], places[1 - nx :]
-    result = finish(first, splits, [pieces[p] for p in first], tables, counts, [], n * local)
-    result = finish(last, splits, [pieces[p] for p in last], [], [], list(result), n * local)
+    early, last = places[: 1 - nx], places[1 - nx :]
+    result = finish(
+        early, splits, [pieces[p] for p in early], local, tables, counts, [], n * local
+    )
+    result = finish(
+        last, splits, [pieces[p] for p in last], local, [], [], list(result), n * local
+    )
     return (stream_out, result[0])
 
 

time: 71.2 us -> 74.8 us (1.051)
  Pallas kernels: 23 us -> 24.6 us
  waiting for transfers between devices: 25.5 us -> 26.8 us
  starting transfers between devices: 20.7 us -> 21.5 us
    ppermute x7 -> x11, waiting for transfers between devices: 14.6 us -> 16.7 us  [the longest x2 5.73 us: body(): lax.ppermute(part, 'tensor', jump[k & -k])]
    pallas_call x4, Pallas kernels: 15.8 us -> 17.4 us  [products(): pl.pallas_call(functools.partial(product_kernel, targets, splits, local,...]
    ppermute x7 -> x11, starting transfers between devices: 8.47 us -> 9.05 us  [the longest x2 3.48 us: body(): far = [lax.ppermute(part, 'tensor', jump[top]) for part in base]]
  transfers between devices with their start and end apart: 15 -> 19, of which waited for: 9 -> 11; matrix products, arithmetic and copies ran while one was open for 0% -> 0% of each run, Pallas kernels for 25% -> 25%
where the time goes in v9:
time: 74.8 us; the launch traced here: 74.6 us
  waiting for transfers between devices  26.8 us (36%)
  Pallas kernels  24.6 us (33%)
  starting transfers between devices  21.5 us (29%)
  between operations  0.78 us (1%)
    pallas_call x4, Pallas kernels, products(): pl.pallas_call(functools.partial(product_kernel, targets, splits, local,...  17.4 us
    ppermute x3, waiting for transfers between devices, body(): joined_to = lax.ppermute(total, 'tensor', jump[bit])  6.96 us
    ppermute x3, starting transfers between devices, body(): joined_to = lax.ppermute(total, 'tensor', jump[bit])  6.28 us
    pallas_call x2, Pallas kernels, finish(): pl.pallas_call(functools.partial(finish_kernel, places, splits, lengths,...  6.11 us
    ppermute x2, waiting for transfers between devices, body(): lax.ppermute(part, 'tensor', jump[k & -k])  5.73 us
    ppermute x4, waiting for transfers between devices, body(): parts = [lax.ppermute(part, 'tensor', swap[j]) for part in have[k]]  5.52 us
    ppermute x3, starting transfers between devices, body(): result = lax.ppermute(result, 'tensor', swap[j])  4.58 us
    ppermute x1, waiting for transfers between devices, body(): near = unchanged(lax.ppermute(sent, 'tensor', jump[1]), base[-1], cost=0)  3.85 us
  transfers between devices with their start and end apart: 19, of which 11 were waited for; matrix products, arithmetic and copies ran while one was open for 0% of the time, Pallas kernels for 25%

profile of v9, /device:TPU:0, one launch (start us, length us, event | category | flops | bytes accessed | tf_op | source)
XLA Modules:
  0.0 74.6 jit_solution(6632656187406011088)
XLA Ops:
  0.6 3.3 %products.4 = (bf16[64,2048]{1,0:T(8,128)(2,1)}, f32[8,128]{1,0:T(8,128)}) custom-call(bf16[64,1024]{1,0:T(8,128)(2,1)} %rows_ref.7, bf16[1024,16384]{1,0:T(8,128)(2,1)} %weight_ref.7), custom_call_target="tpu_custom_call" | custom-call | flops 268435456 | bytes 4194304 | tf_op jit(solution)/shard_map/products/pallas_call | solution.py:74
  4.0 3.0 %collective-permute-start = (bf16[64,2048]{1,0:T(8,128)(2,1)}, bf16[64,2048]{1,0:T(8,128)(2,1)S(1)}, u32[]{:S(2)}, u32[]{:S(2)}) collective-permute-start(bf16[64,2048]{1,0:T(8,128)(2,1)} %get-tuple-element.17), channel_id=1, source_target_pairs={{0,1},{1,0},{2,3},{3,2},{4,5},{5,4},{6,7},{7,6},{8,9},{9,8},{10,11... | collective-permute-start | bytes 786440 | tf_op jit(solution)/shard_map/ppermute | solution.py:338
  7.0 0.7 copy-done.4
  7.7 5.6 %products.5 = (bf16[64,2048]{1,0:T(8,128)(2,1)S(1)}, bf16[64,2048]{1,0:T(8,128)(2,1)S(1)}, f32[64,2048]{1,0:T(8,128)S(1)}, f32[8,128]{1,0:T(8,128)}) custom-call(bf16[64,1024]{1,0:T(8,128)(2,1)S(1)} %copy-done, bf16[1024,16384]{1,0:T(8,128)(2,1)} %weight_ref.7, f32[8,128]{1,0:T(8,128)S(1)} %copy-done.4), custom_call_target="tpu_custom_call" | custom-call | flops 805306368 | bytes 12582912 | tf_op jit(solution)/shard_map/products/pallas_call | solution.py:74
  13.2 0.1 collective-permute-start.1
  13.3 0.2 collective-permute-done
  13.5 0.1 add_convert_fusion.2.refs_0_
  13.6 2.0 %collective-permute-start.2 = (bf16[64,2048]{1,0:T(8,128)(2,1)S(1)}, bf16[64,2048]{1,0:T(8,128)(2,1)S(1)}, u32[]{:S(2)}, u32[]{:S(2)}) collective-permute-start(bf16[64,2048]{1,0:T(8,128)(2,1)S(1)} %add_convert_fusion.2.refs_0_), channel_id=1, source_target_pairs={{0,2},{1,3},{2,0},{3,1},{4,6},{5,7},{6,4},{7,5},{8,10},{9,11},{10,... | collective-permute-start | bytes 786440 | tf_op jit(solution)/shard_map/ppermute | solution.py:356
  15.6 1.5 %collective-permute-start.5 = (bf16[64,2048]{1,0:T(8,128)(2,1)S(1)}, bf16[64,2048]{1,0:T(8,128)(2,1)S(1)}, u32[]{:S(2)}, u32[]{:S(2)}) collective-permute-start(bf16[64,2048]{1,0:T(8,128)(2,1)S(1)} %get-tuple-element.23), channel_id=1, source_target_pairs={{0,1},{1,0},{2,3},{3,2},{4,5},{5,4},{6,7},{7,6},{8,9},{9,8},{10,11... | collective-permute-start | bytes 786440 | tf_op jit(solution)/shard_map/ppermute | solution.py:338
  17.0 5.6 %products.6 = (bf16[64,2048]{1,0:T(8,128)(2,1)S(1)}, f32[64,2048]{1,0:T(8,128)S(1)}, f32[64,2048]{1,0:T(8,128)S(1)}, f32[8,128]{1,0:T(8,128)}) custom-call(bf16[64,1024]{1,0:T(8,128)(2,1)S(1)} %copy-done, bf16[1024,16384]{1,0:T(8,128)(2,1)} %weight_ref.7, bf16[64,2048]{1,0:T(8,128)(2,1)S(1)} %add_convert_fusion.2.refs_0_), custom_call_target="tpu_custom_call" | custom-call | flops 805306368 | bytes 12582912 | tf_op jit(solution)/shard_map/products/pallas_call | solution.py:74
  22.6 0.0 collective-permute-done.1
  22.6 0.0 collective-permute-done.2
  22.6 0.1 add_convert_fusion.1.refs_1_
  22.7 2.7 %collective-permute-start.4 = (bf16[64,2048]{1,0:T(8,128)(2,1)S(1)}, bf16[64,2048]{1,0:T(8,128)(2,1)S(1)}, u32[]{:S(2)}, u32[]{:S(2)}) collective-permute-start(bf16[64,2048]{1,0:T(8,128)(2,1)S(1)} %add_convert_fusion.1.refs_1_), channel_id=1, source_target_pairs={{0,4},{1,5},{2,6},{3,7},{4,0},{5,1},{6,2},{7,3},{8,12},{9,13},{10,... | collective-permute-start | bytes 786440 | tf_op jit(solution)/shard_map/ppermute | solution.py:356
  25.4 1.3 %collective-permute-done.5 = bf16[64,2048]{1,0:T(8,128)(2,1)S(1)} collective-permute-done((bf16[64,2048]{1,0:T(8,128)(2,1)S(1)}, bf16[64,2048]{1,0:T(8,128)(2,1)S(1)}, u32[]{:S(2)}, u32[]{:S(2)}) %collective-permute-start.5) | collective-permute-done | bytes 262176 | tf_op jit(solution)/shard_map/ppermute | solution.py:338
  26.7 0.1 add_convert_fusion.refs_0_
  26.8 1.6 %collective-permute-start.6 = (bf16[64,2048]{1,0:T(8,128)(2,1)S(1)}, bf16[64,2048]{1,0:T(8,128)(2,1)S(1)}, u32[]{:S(2)}, u32[]{:S(2)}) collective-permute-start(bf16[64,2048]{1,0:T(8,128)(2,1)S(1)} %add_convert_fusion.refs_0_), channel_id=1, source_target_pairs={{0,2},{1,3},{2,0},{3,1},{4,6},{5,7},{6,4},{7,5},{8,10},{9,11},{10,... | collective-permute-start | bytes 786440 | tf_op jit(solution)/shard_map/ppermute | solution.py:356
  28.4 0.5 collective-permute-start.3
  28.9 3.0 %products.7 = (f32[64,2048]{1,0:T(8,128)S(1)}, f32[8,128]{1,0:T(8,128)}) custom-call(bf16[64,1024]{1,0:T(8,128)(2,1)S(1)} %copy-done, bf16[1024,16384]{1,0:T(8,128)(2,1)} %weight_ref.7, bf16[64,2048]{1,0:T(8,128)(2,1)S(1)} %add_convert_fusion.refs_0_, bf16[64,2048]{1,0:T(8,128)(2,1)S(1)} %unchanged.7.refs_1_), custom_call_target="tpu_custom_call" | custom-call | flops 268435456 | bytes 4194304 | tf_op jit(solution)/shard_map/products/pallas_call | solution.py:74
  31.9 0.0 copy-start.1
  31.9 0.0 copy-start.2
  32.0 0.0 copy-start.3
  32.0 4.3 %collective-permute-done.4.refs_0_ = bf16[64,2048]{1,0:T(8,128)(2,1)S(1)} collective-permute-done((bf16[64,2048]{1,0:T(8,128)(2,1)S(1)}, bf16[64,2048]{1,0:T(8,128)(2,1)S(1)}, u32[]{:S(2)}, u32[]{:S(2)}) %collective-permute-start.4) | collective-permute-done | bytes 262176 | tf_op jit(solution)/shard_map/ppermute | solution.py:356
  36.2 2.7 %collective-permute-done.6.refs_2_ = bf16[64,2048]{1,0:T(8,128)(2,1)S(1)} collective-permute-done((bf16[64,2048]{1,0:T(8,128)(2,1)S(1)}, bf16[64,2048]{1,0:T(8,128)(2,1)S(1)}, u32[]{:S(2)}, u32[]{:S(2)}) %collective-permute-start.6) | collective-permute-done | bytes 262176 | tf_op jit(solution)/shard_map/ppermute | solution.py:356
  38.9 0.0 collective-permute-done.3.refs_0_
  39.0 1.0 %own_stream.1 = (bf16[64,2048]{1,0:T(8,128)(2,1)}, bf16[64,2176]{1,0:T(8,128)(2,1)S(1)}, bf16[16,128]{1,0:T(8,128)(2,1)S(1)}, bf16[64,1024]{1,0:T(8,128)(2,1)S(1)}) custom-call(bf16[64,2048]{1,0:T(8,128)(2,1)S(1)} %copy-done.1, bf16[16,128]{1,0:T(8,128)(2,1)S(1)} %bitcast.2, bf16[16,128]{1,0:T(8,128)(2,1)S(1)} %bitcast.3, ...), custom_call_target="tpu_custom_call" | custom-call | flops 2621440 | bytes 2097152 | tf_op jit(solution)/shard_map/own_stream/pallas_call | solution.py:143
  40.0 0.0 collective-permute-start.8
  40.0 3.4 %collective-permute-start.7 = (bf16[64,1024]{1,0:T(8,128)(2,1)S(1)}, bf16[64,1024]{1,0:T(8,128)(2,1)S(1)}, u32[]{:S(2)}, u32[]{:S(2)}) collective-permute-start(bf16[64,1024]{1,0:T(8,128)(2,1)S(1)} %get-tuple-element.27), channel_id=1, source_target_pairs={{0,4},{1,5},{2,6},{3,7},{4,0},{5,1},{6,2},{7,3},{8,12},{9,13},{10,... | collective-permute-start | bytes 393224 | tf_op jit(solution)/shard_map/ppermute | solution.py:373
  43.4 1.1 %collective-permute-start.9 = (bf16[16,128]{1,0:T(8,128)(2,1)S(1)}, bf16[16,128]{1,0:T(8,128)(2,1)S(1)}, u32[]{:S(2)}, u32[]{:S(2)}) collective-permute-start(bf16[16,128]{1,0:T(8,128)(2,1)S(1)} %get-tuple-element.29), channel_id=1, source_target_pairs={{0,1},{1,0},{2,3},{3,2},{4,5},{5,4},{6,7},{7,6},{8,9},{9,8},{10,11... | collective-permute-start | bytes 12296 | tf_op jit(solution)/shard_map/ppermute | solution.py:365
  44.5 0.9 %collective-permute-start.13 = (bf16[64,2176]{1,0:T(8,128)(2,1)S(1)}, bf16[64,2176]{1,0:T(8,128)(2,1)S(1)}, u32[]{:S(2)}, u32[]{:S(2)}) collective-permute-start(bf16[64,2176]{1,0:T(8,128)(2,1)S(1)} %get-tuple-element.28.sent_ref.refs_0_), channel_id=1, source_target_pairs={{0,1},{1,0},{2,3},{3,2},{4,5},{5,4},{6,7},{7,6},{8,9},{9,8},{10,11... | collective-permute-start | bytes 835592 | tf_op jit(solution)/shard_map/ppermute | solution.py:372
  45.4 1.7 %collective-permute-done.9.refs_0_ = bf16[16,128]{1,0:T(8,128)(2,1)S(1)} collective-permute-done((bf16[16,128]{1,0:T(8,128)(2,1)S(1)}, bf16[16,128]{1,0:T(8,128)(2,1)S(1)}, u32[]{:S(2)}, u32[]{:S(2)}) %collective-permute-start.9) | collective-permute-done | bytes 4128 | tf_op jit(solution)/shard_map/ppermute | solution.py:365
  47.1 0.1 collective-permute-start.12
  47.2 3.8 %collective-permute-done.8.refs_0_ = bf16[64,2176]{1,0:T(8,128)(2,1)S(1)} collective-permute-done((bf16[64,2176]{1,0:T(8,128)(2,1)S(1)}, bf16[64,2176]{1,0:T(8,128)(2,1)S(1)}, u32[]{:S(2)}, u32[]{:S(2)}) %collective-permute-start.8) | collective-permute-done | bytes 278560 | tf_op jit(solution)/shard_map/ppermute | solution.py:368
  51.0 0.0 collective-permute-start.14
  51.1 2.3 %collective-permute-start.10 = (bf16[64,1024]{1,0:T(8,128)(2,1)S(1)}, bf16[64,1024]{1,0:T(8,128)(2,1)S(1)}, u32[]{:S(2)}, u32[]{:S(2)}) collective-permute-start(bf16[64,1024]{1,0:T(8,128)(2,1)S(1)} %unchanged.10.refs_1_.refs_4_), channel_id=1, source_target_pairs={{0,2},{1,3},{2,0},{3,1},{4,6},{5,7},{6,4},{7,5},{8,10},{9,11},{10,... | collective-permute-start | bytes 393224 | tf_op jit(solution)/shard_map/ppermute | solution.py:381
  53.4 1.1 %collective-permute-start.17 = (bf16[64,1024]{1,0:T(8,128)(2,1)S(1)}, bf16[64,1024]{1,0:T(8,128)(2,1)S(1)}, u32[]{:S(2)}, u32[]{:S(2)}) collective-permute-start(bf16[64,1024]{1,0:T(8,128)(2,1)S(1)} %unchanged.10.refs_1_.refs_4_), channel_id=1, source_target_pairs={{0,1},{1,0},{2,3},{3,2},{4,5},{5,4},{6,7},{7,6},{8,9},{9,8},{10,11... | collective-permute-start | bytes 393224 | tf_op jit(solution)/shard_map/ppermute | solution.py:387
  54.5 3.5 %collective-permute-done.10.refs_8_ = bf16[64,1024]{1,0:T(8,128)(2,1)S(1)} collective-permute-done((bf16[64,1024]{1,0:T(8,128)(2,1)S(1)}, bf16[64,1024]{1,0:T(8,128)(2,1)S(1)}, u32[]{:S(2)}, u32[]{:S(2)}) %collective-permute-start.10) | collective-permute-done | bytes 131104 | tf_op jit(solution)/shard_map/ppermute | solution.py:381
  58.0 1.0 %collective-permute-start.11 = (bf16[64,1024]{1,0:T(8,128)(2,1)S(1)}, bf16[64,1024]{1,0:T(8,128)(2,1)S(1)}, u32[]{:S(2)}, u32[]{:S(2)}) collective-permute-start(bf16[64,1024]{1,0:T(8,128)(2,1)S(1)} %collective-permute-done.10.refs_8_), channel_id=1, source_target_pairs={{0,1},{1,0},{2,3},{3,2},{4,5},{5,4},{6,7},{7,6},{8,9},{9,8},{10,11... | collective-permute-start | bytes 393224 | tf_op jit(solution)/shard_map/ppermute | solution.py:387
  59.0 1.6 %collective-permute-done.14.refs_3_.refs_14_ = bf16[64,2176]{1,0:T(8,128)(2,1)S(1)} collective-permute-done((bf16[64,2176]{1,0:T(8,128)(2,1)S(1)}, bf16[64,2176]{1,0:T(8,128)(2,1)S(1)}, u32[]{:S(2)}, u32[]{:S(2)}) %collective-permute-start.14) | collective-permute-done | bytes 278560 | tf_op jit(solution)/shard_map/ppermute | solution.py:372
  60.6 0.0 collective-permute-start.15
  60.6 2.8 %collective-permute-done.17.refs_0_ = bf16[64,1024]{1,0:T(8,128)(2,1)S(1)} collective-permute-done((bf16[64,1024]{1,0:T(8,128)(2,1)S(1)}, bf16[64,1024]{1,0:T(8,128)(2,1)S(1)}, u32[]{:S(2)}, u32[]{:S(2)}) %collective-permute-start.17) | collective-permute-done | bytes 131104 | tf_op jit(solution)/shard_map/ppermute | solution.py:387
  63.4 0.1 collective-permute-start.18
  63.5 2.2 %collective-permute-done.15.refs_9_.refs_12_ = bf16[64,1152]{1,0:T(8,128)(2,1)S(1)} collective-permute-done((bf16[64,1152]{1,0:T(8,128)(2,1)S(1)}, bf16[64,1152]{1,0:T(8,128)(2,1)S(1)}, u32[]{:S(2)}, u32[]{:S(2)}) %collective-permute-start.15) | collective-permute-done | bytes 147488 | tf_op jit(solution)/shard_map/ppermute | solution.py:381
  65.7 0.1 collective-permute-start.16
  65.8 2.7 %collective-permute-done.18.refs_7_ = bf16[64,1152]{1,0:T(8,128)(2,1)S(1)} collective-permute-done((bf16[64,1152]{1,0:T(8,128)(2,1)S(1)}, bf16[64,1152]{1,0:T(8,128)(2,1)S(1)}, u32[]{:S(2)}, u32[]{:S(2)}) %collective-permute-start.18) | collective-permute-done | bytes 147488 | tf_op jit(solution)/shard_map/ppermute | solution.py:387
  68.5 4.7 %finish.2 = (bf16[64,16384]{1,0:T(8,128)(2,1)}, f32[64,128]{1,0:T(8,128)S(1)}) custom-call(bf16[64,2176]{1,0:T(8,128)(2,1)S(1)} %get-tuple-element.28.sent_ref.refs_0_, bf16[64,2176]{1,0:T(8,128)(2,1)S(1)} %collective-permute-done.13.refs_2_.refs_1_, bf16[64,2176]{1,0:T(8,128)(2,1)S(1)} %unchanged.9.refs_1_.refs_2_.refs_13_, ...), custom_call_target="tpu_custom_call" | custom-call | flops 939524096 | bytes 3670016 | tf_op jit(solution)/shard_map/finish/pallas_call | solution.py:289
  73.2 0.0 collective-permute-done.16.refs_1_
  73.2 1.4 %finish.3 = bf16[64,16384]{1,0:T(8,128)(2,1)} custom-call(bf16[64,1024]{1,0:T(8,128)(2,1)S(1)} %unchanged.11.refs_0_, bf16[64,1152]{1,0:T(8,128)(2,1)S(1)} %collective-permute-done.16.refs_1_, f32[64,128]{1,0:T(8,128)S(1)} %get-tuple-element.30.refs_2_, bf16[64,16384]{1,0:T(8,128)(2,1)} %get-tuple-element.31.refs_3_), custom_call_target="tpu_custom_call", output_to_operand_aliasing={{}: (3, {})} | custom-call | flops 134217728 | bytes 524288 | tf_op jit(solution)/shard_map/finish/pallas_call | solution.py:289
  (18 shorter events, 0.1 us)
Async XLA Ops:
  0.6 6.4 %copy-start = (bf16[64,1024]{1,0:T(8,128)(2,1)S(1)}, bf16[64,1024]{1,0:T(8,128)(2,1)}, u32[]{:S(2)}) copy-start(bf16[64,1024]{1,0:T(8,128)(2,1)} %rows_ref.7) | copy-start | bytes 393220
  4.0 9.5 %collective-permute-start = (bf16[64,2048]{1,0:T(8,128)(2,1)}, bf16[64,2048]{1,0:T(8,128)(2,1)S(1)}, u32[]{:S(2)}, u32[]{:S(2)}) collective-permute-start(bf16[64,2048]{1,0:T(8,128)(2,1)} %get-tuple-element.17), channel_id=1, source_target_pairs={{0,1},{1,0},{2,3},{3,2},{4,5},{5,4},{6,7},{7,6},{8,9},{9,8},{10,11... | collective-permute-start | bytes 786440 | tf_op jit(solution)/shard_map/ppermute | solution.py:338
  7.0 0.7 copy-start.4
  13.2 9.4 %collective-permute-start.1 = (bf16[64,2048]{1,0:T(8,128)(2,1)S(1)}, bf16[64,2048]{1,0:T(8,128)(2,1)S(1)}, u32[]{:S(2)}, u32[]{:S(2)}) collective-permute-start(bf16[64,2048]{1,0:T(8,128)(2,1)S(1)} %get-tuple-element.21), channel_id=1, source_target_pairs={{0,1},{1,0},{2,3},{3,2},{4,5},{5,4},{6,7},{7,6},{8,9},{9,8},{10,11... | collective-permute-start | bytes 786440 | tf_op jit(solution)/shard_map/ppermute | solution.py:338
  13.6 9.0 %collective-permute-start.2 = (bf16[64,2048]{1,0:T(8,128)(2,1)S(1)}, bf16[64,2048]{1,0:T(8,128)(2,1)S(1)}, u32[]{:S(2)}, u32[]{:S(2)}) collective-permute-start(bf16[64,2048]{1,0:T(8,128)(2,1)S(1)} %add_convert_fusion.2.refs_0_), channel_id=1, source_target_pairs={{0,2},{1,3},{2,0},{3,1},{4,6},{5,7},{6,4},{7,5},{8,10},{9,11},{10,... | collective-permute-start | bytes 786440 | tf_op jit(solution)/shard_map/ppermute | solution.py:356
  15.6 11.1 %collective-permute-start.5 = (bf16[64,2048]{1,0:T(8,128)(2,1)S(1)}, bf16[64,2048]{1,0:T(8,128)(2,1)S(1)}, u32[]{:S(2)}, u32[]{:S(2)}) collective-permute-start(bf16[64,2048]{1,0:T(8,128)(2,1)S(1)} %get-tuple-element.23), channel_id=1, source_target_pairs={{0,1},{1,0},{2,3},{3,2},{4,5},{5,4},{6,7},{7,6},{8,9},{9,8},{10,11... | collective-permute-start | bytes 786440 | tf_op jit(solution)/shard_map/ppermute | solution.py:338
  22.7 13.5 %collective-permute-start.4 = (bf16[64,2048]{1,0:T(8,128)(2,1)S(1)}, bf16[64,2048]{1,0:T(8,128)(2,1)S(1)}, u32[]{:S(2)}, u32[]{:S(2)}) collective-permute-start(bf16[64,2048]{1,0:T(8,128)(2,1)S(1)} %add_convert_fusion.1.refs_1_), channel_id=1, source_target_pairs={{0,4},{1,5},{2,6},{3,7},{4,0},{5,1},{6,2},{7,3},{8,12},{9,13},{10,... | collective-permute-start | bytes 786440 | tf_op jit(solution)/shard_map/ppermute | solution.py:356
  26.8 12.2 %collective-permute-start.6 = (bf16[64,2048]{1,0:T(8,128)(2,1)S(1)}, bf16[64,2048]{1,0:T(8,128)(2,1)S(1)}, u32[]{:S(2)}, u32[]{:S(2)}) collective-permute-start(bf16[64,2048]{1,0:T(8,128)(2,1)S(1)} %add_convert_fusion.refs_0_), channel_id=1, source_target_pairs={{0,2},{1,3},{2,0},{3,1},{4,6},{5,7},{6,4},{7,5},{8,10},{9,11},{10,... | collective-permute-start | bytes 786440 | tf_op jit(solution)/shard_map/ppermute | solution.py:356
  28.4 10.5 %collective-permute-start.3 = (bf16[64,2048]{1,0:T(8,128)(2,1)S(1)}, bf16[64,2048]{1,0:T(8,128)(2,1)S(1)}, u32[]{:S(2)}, u32[]{:S(2)}) collective-permute-start(bf16[64,2048]{1,0:T(8,128)(2,1)S(1)} %unchanged.7.refs_1_), channel_id=1, source_target_pairs={{0,1},{1,0},{2,3},{3,2},{4,5},{5,4},{6,7},{7,6},{8,9},{9,8},{10,11... | collective-permute-start | bytes 786440 | tf_op jit(solution)/shard_map/ppermute | solution.py:354
  31.9 7.0 %copy-start.1 = (bf16[64,2048]{1,0:T(8,128)(2,1)S(1)}, bf16[64,2048]{1,0:T(8,128)(2,1)}, u32[]{:S(2)}) copy-start(bf16[64,2048]{1,0:T(8,128)(2,1)} %residual_ref.1) | copy-start | bytes 786436
  31.9 7.0 %copy-start.2 = (bf16[2048]{0:T(1024)(128)(2,1)S(1)}, bf16[2048]{0:T(1024)(128)(2,1)}, u32[]{:S(2)}) copy-start(bf16[2048]{0:T(1024)(128)(2,1)} %param.8) | copy-start | bytes 12292
  32.0 7.0 %copy-start.3 = (bf16[2048]{0:T(1024)(128)(2,1)S(1)}, bf16[2048]{0:T(1024)(128)(2,1)}, u32[]{:S(2)}) copy-start(bf16[2048]{0:T(1024)(128)(2,1)} %param.9) | copy-start | bytes 12292
  40.0 11.1 %collective-permute-start.8 = (bf16[64,2176]{1,0:T(8,128)(2,1)S(1)}, bf16[64,2176]{1,0:T(8,128)(2,1)S(1)}, u32[]{:S(2)}, u32[]{:S(2)}) collective-permute-start(bf16[64,2176]{1,0:T(8,128)(2,1)S(1)} %get-tuple-element.28.sent_ref.refs_0_), channel_id=1, source_target_pairs={{0,2},{1,3},{2,0},{3,1},{4,6},{5,7},{6,4},{7,5},{8,10},{9,11},{10,... | collective-permute-start | bytes 835592 | tf_op jit(solution)/shard_map/ppermute | solution.py:368
  40.0 11.1 %collective-permute-start.7 = (bf16[64,1024]{1,0:T(8,128)(2,1)S(1)}, bf16[64,1024]{1,0:T(8,128)(2,1)S(1)}, u32[]{:S(2)}, u32[]{:S(2)}) collective-permute-start(bf16[64,1024]{1,0:T(8,128)(2,1)S(1)} %get-tuple-element.27), channel_id=1, source_target_pairs={{0,4},{1,5},{2,6},{3,7},{4,0},{5,1},{6,2},{7,3},{8,12},{9,13},{10,... | collective-permute-start | bytes 393224 | tf_op jit(solution)/shard_map/ppermute | solution.py:373
  43.4 3.7 %collective-permute-start.9 = (bf16[16,128]{1,0:T(8,128)(2,1)S(1)}, bf16[16,128]{1,0:T(8,128)(2,1)S(1)}, u32[]{:S(2)}, u32[]{:S(2)}) collective-permute-start(bf16[16,128]{1,0:T(8,128)(2,1)S(1)} %get-tuple-element.29), channel_id=1, source_target_pairs={{0,1},{1,0},{2,3},{3,2},{4,5},{5,4},{6,7},{7,6},{8,9},{9,8},{10,11... | collective-permute-start | bytes 12296 | tf_op jit(solution)/shard_map/ppermute | solution.py:365
  44.5 14.5 %collective-permute-start.13 = (bf16[64,2176]{1,0:T(8,128)(2,1)S(1)}, bf16[64,2176]{1,0:T(8,128)(2,1)S(1)}, u32[]{:S(2)}, u32[]{:S(2)}) collective-permute-start(bf16[64,2176]{1,0:T(8,128)(2,1)S(1)} %get-tuple-element.28.sent_ref.refs_0_), channel_id=1, source_target_pairs={{0,1},{1,0},{2,3},{3,2},{4,5},{5,4},{6,7},{7,6},{8,9},{9,8},{10,11... | collective-permute-start | bytes 835592 | tf_op jit(solution)/shard_map/ppermute | solution.py:372
  47.1 11.9 %collective-permute-start.12 = (bf16[64,1152]{1,0:T(8,128)(2,1)S(1)}, bf16[64,1152]{1,0:T(8,128)(2,1)S(1)}, u32[]{:S(2)}, u32[]{:S(2)}) collective-permute-start(bf16[64,1152]{1,0:T(8,128)(2,1)S(1)} %merge.1.refs_1_.refs_10_), channel_id=1, source_target_pairs={{0,4},{1,5},{2,6},{3,7},{4,0},{5,1},{6,2},{7,3},{8,12},{9,13},{10,... | collective-permute-start | bytes 442376 | tf_op jit(solution)/shard_map/ppermute | solution.py:373
  51.0 9.5 %collective-permute-start.14 = (bf16[64,2176]{1,0:T(8,128)(2,1)S(1)}, bf16[64,2176]{1,0:T(8,128)(2,1)S(1)}, u32[]{:S(2)}, u32[]{:S(2)}) collective-permute-start(bf16[64,2176]{1,0:T(8,128)(2,1)S(1)} %unchanged.9.refs_1_.refs_2_.refs_13_), channel_id=1, source_target_pairs={{0,1},{1,0},{2,3},{3,2},{4,5},{5,4},{6,7},{7,6},{8,9},{9,8},{10,11... | collective-permute-start | bytes 835592 | tf_op jit(solution)/shard_map/ppermute | solution.py:372
  51.1 6.9 %collective-permute-start.10 = (bf16[64,1024]{1,0:T(8,128)(2,1)S(1)}, bf16[64,1024]{1,0:T(8,128)(2,1)S(1)}, u32[]{:S(2)}, u32[]{:S(2)}) collective-permute-start(bf16[64,1024]{1,0:T(8,128)(2,1)S(1)} %unchanged.10.refs_1_.refs_4_), channel_id=1, source_target_pairs={{0,2},{1,3},{2,0},{3,1},{4,6},{5,7},{6,4},{7,5},{8,10},{9,11},{10,... | collective-permute-start | bytes 393224 | tf_op jit(solution)/shard_map/ppermute | solution.py:381
  53.4 10.0 %collective-permute-start.17 = (bf16[64,1024]{1,0:T(8,128)(2,1)S(1)}, bf16[64,1024]{1,0:T(8,128)(2,1)S(1)}, u32[]{:S(2)}, u32[]{:S(2)}) collective-permute-start(bf16[64,1024]{1,0:T(8,128)(2,1)S(1)} %unchanged.10.refs_1_.refs_4_), channel_id=1, source_target_pairs={{0,1},{1,0},{2,3},{3,2},{4,5},{5,4},{6,7},{7,6},{8,9},{9,8},{10,11... | collective-permute-start | bytes 393224 | tf_op jit(solution)/shard_map/ppermute | solution.py:387
  58.0 7.8 %collective-permute-start.11 = (bf16[64,1024]{1,0:T(8,128)(2,1)S(1)}, bf16[64,1024]{1,0:T(8,128)(2,1)S(1)}, u32[]{:S(2)}, u32[]{:S(2)}) collective-permute-start(bf16[64,1024]{1,0:T(8,128)(2,1)S(1)} %collective-permute-done.10.refs_8_), channel_id=1, source_target_pairs={{0,1},{1,0},{2,3},{3,2},{4,5},{5,4},{6,7},{7,6},{8,9},{9,8},{10,11... | collective-permute-start | bytes 393224 | tf_op jit(solution)/shard_map/ppermute | solution.py:387
  60.6 5.1 %collective-permute-start.15 = (bf16[64,1152]{1,0:T(8,128)(2,1)S(1)}, bf16[64,1152]{1,0:T(8,128)(2,1)S(1)}, u32[]{:S(2)}, u32[]{:S(2)}) collective-permute-start(bf16[64,1152]{1,0:T(8,128)(2,1)S(1)} %unchanged.12.refs_5_.refs_11_), channel_id=1, source_target_pairs={{0,2},{1,3},{2,0},{3,1},{4,6},{5,7},{6,4},{7,5},{8,10},{9,11},{10,... | collective-permute-start | bytes 442376 | tf_op jit(solution)/shard_map/ppermute | solution.py:381
  63.4 5.1 %collective-permute-start.18 = (bf16[64,1152]{1,0:T(8,128)(2,1)S(1)}, bf16[64,1152]{1,0:T(8,128)(2,1)S(1)}, u32[]{:S(2)}, u32[]{:S(2)}) collective-permute-start(bf16[64,1152]{1,0:T(8,128)(2,1)S(1)} %unchanged.12.refs_5_.refs_11_), channel_id=1, source_target_pairs={{0,1},{1,0},{2,3},{3,2},{4,5},{5,4},{6,7},{7,6},{8,9},{9,8},{10,11... | collective-permute-start | bytes 442376 | tf_op jit(solution)/shard_map/ppermute | solution.py:387
  65.7 7.5 %collective-permute-start.16 = (bf16[64,1152]{1,0:T(8,128)(2,1)S(1)}, bf16[64,1152]{1,0:T(8,128)(2,1)S(1)}, u32[]{:S(2)}, u32[]{:S(2)}) collective-permute-start(bf16[64,1152]{1,0:T(8,128)(2,1)S(1)} %collective-permute-done.15.refs_9_.refs_12_), channel_id=1, source_target_pairs={{0,1},{1,0},{2,3},{3,2},{4,5},{5,4},{6,7},{7,6},{8,9},{9,8},{10,11... | collective-permute-start | bytes 442376 | tf_op jit(solution)/shard_map/ppermute | solution.py:387

commit v10 on v9

--- a/solution.py
+++ b/solution.py
@@ -37,9 +37,7 @@
 def product_kernel(targets, splits, local, tile, rows_ref, weight_ref, *refs):
     count = len(targets)
     held, scratch, semaphores = refs[-3:]
-    token = refs[-4]
-    outs = refs[-4 - count : -4]
-    token[...] = jnp.zeros_like(token)
+    outs = refs[-3 - count : -3]
     nx, per = splits[1], local // tile
     me = lax.axis_index("tensor")
     outer, inner = me // nx, lax.rem(me, nx)
@@ -76,18 +74,17 @@
         out_shape=[
             jax.ShapeDtypeStruct((rows, local), jnp.bfloat16 if j else jnp.float32)
             for _, j in targets
-        ]
-        + [jax.ShapeDtypeStruct((8, LANES), jnp.float32)],
+        ],
         in_specs=[pl.BlockSpec(memory_space=pltpu.HBM)] * 2
         + [pl.BlockSpec(memory_space=pl.ANY)] * len(after),
-        out_specs=[vmem] * (len(targets) + 1),
+        out_specs=[vmem] * len(targets),
         scratch_shapes=[
             pltpu.VMEM((rows, depth), jnp.bfloat16),
             pltpu.VMEM((slots, depth, tile), jnp.bfloat16),
             pltpu.SemaphoreType.DMA((slots + 1,)),
         ],
         compiler_params=pltpu.CompilerParams(
-            vmem_limit_bytes=(40 if after else 60) * MIB
+            vmem_limit_bytes=40 * MIB
         ),
         cost_estimate=pl.CostEstimate(
             flops=2 * rows * depth * local * len(targets),
@@ -108,7 +105,7 @@
 
 
 def stream_kernel(count, residual_ref, gain_ref, bias_ref, *refs):
-    terms, (half_ref, sent_ref, stats_ref, *head) = refs[:count], refs[count:]
+    terms, (half_ref, sent_ref, tail_ref, *head) = refs[:count], refs[count:]
     stream = residual_ref[...].astype(jnp.float32)
     for term in terms:
         stream = stream + term[...].astype(jnp.float32)
@@ -129,12 +126,15 @@
             [table, jnp.zeros((LANES - rows, LANES), jnp.float32)], axis=0
         )
     stats = jnp.transpose(table)
-    stats_ref[...] = stats[: stats_ref.shape[0]].astype(stats_ref.dtype)
     stats = stats[: rows - 2 * gain_ref.shape[0]]
-    sent_ref[:, width:] = jnp.concatenate(
+    shared = jnp.concatenate(
         [stats, gain_ref[...].astype(jnp.float32), bias_ref[...].astype(jnp.float32)],
         axis=0,
     ).astype(sent_ref.dtype)
+    sent_ref[:, width:] = shared
+    rest = tail_ref.shape[1] - LANES
+    tail_ref[:, :rest] = half[:, width - rest :]
+    tail_ref[:, rest:] = shared
 
 
 def own_stream(residual, gain, bias, terms, first):
@@ -145,7 +145,7 @@
         out_shape=(
             jax.ShapeDtypeStruct((rows, local), jnp.bfloat16),
             jax.ShapeDtypeStruct((rows, local + LANES), jnp.bfloat16),
-            jax.ShapeDtypeStruct((16, LANES), jnp.bfloat16),
+            jax.ShapeDtypeStruct((rows, local + LANES - first), jnp.bfloat16),
         )
         + (jax.ShapeDtypeStruct((rows, first), jnp.bfloat16),) * bool(first),
         compiler_params=pltpu.CompilerParams(vmem_limit_bytes=8 * MIB),
@@ -189,27 +189,26 @@
     return centre, squares
 
 
-def merge_kernel(first, sent_ref, *refs):
-    out_ref = refs[-1]
-    rows = out_ref.shape[0]
-    local = sent_ref.shape[1] - LANES
-    tables = [sent_ref[0:8, local:]] + [ref[0:8] for ref in refs[:-1]]
+def merge_kernel(local, *refs):
+    tail_ref, out_ref = refs[0], refs[-1]
+    rest = out_ref.shape[1] - LANES
+    tables = [ref[0:8, rest:] for ref in refs[:-1]]
     centre, squares = moments(tables, [local] * len(tables))
-    row = lax.broadcasted_iota(jnp.int32, (rows, LANES), 0)
-    table = sent_ref[:, local:].astype(jnp.float32)
+    row = lax.broadcasted_iota(jnp.int32, (out_ref.shape[0], LANES), 0)
+    table = tail_ref[:, rest:].astype(jnp.float32)
     for place, part in enumerate(in_three(centre) + in_three(squares)):
         table = jnp.where(row == place, part, table)
-    out_ref[:, : local - first] = sent_ref[:, first:local]
-    out_ref[:, local - first :] = table.astype(out_ref.dtype)
-
-
-def merge(sent, others, first):
+    out_ref[:, :rest] = tail_ref[:, :rest]
+    out_ref[:, rest:] = table.astype(out_ref.dtype)
+
+
+def merge(tails, local):
     return pl.pallas_call(
-        functools.partial(merge_kernel, first),
-        out_shape=jax.ShapeDtypeStruct((sent.shape[0], sent.shape[1] - first), sent.dtype),
+        functools.partial(merge_kernel, local),
+        out_shape=jax.ShapeDtypeStruct(tails[0].shape, tails[0].dtype),
         compiler_params=pltpu.CompilerParams(vmem_limit_bytes=4 * MIB),
         name="merge",
-    )(sent, *others)
+    )(*tails)
 
 
 def coded_rows(parts, local, centre, inverse, table):
@@ -329,10 +328,10 @@
     terms = {k: [] for k in range(nz)}
     after, held, released = [], [], []
     for targets, joined in zip(calls, joins):
-        *results, token = products(
+        results = products(
             attended, out_weight, targets, splits, local, after + released
         )
-        after = [token]
+        after = [results[-1]]
         for (k, j), result in zip(targets, results):
             if j and k:
                 result = lax.ppermute(result, "tensor", swap[j])
@@ -359,20 +358,25 @@
             terms[k ^ bit].append(joined_to)
 
     first = local // 2 if local % (2 * LANES) == 0 else 0
-    stream_out, sent, stats, *head = own_stream(
+    stream_out, sent, tail, *head = own_stream(
         residual, norm_gain, norm_bias, terms[0], first
     )
-    others = [lax.ppermute(stats, "tensor", swap[j]) for j in range(1, nx)]
-    base = head + [merge(sent, others, first)]
+    crossed, waited = {}, []
+    for p in away[0]:
+        crossed[p] = [lax.ppermute(part, "tensor", swap[p[1]]) for part in [tail] + head][::-1]
+        waited += crossed[p][:-1]
+    tails = [crossed[p][-1] for p in away[0]]
+    base = [unchanged(part, *tails, cost=0) for part in head]
+    base.append(merge([tail] + tails, local))
     top = nz // 2
-    near = unchanged(lax.ppermute(sent, "tensor", jump[1]), base[-1], cost=0)
-    have = {0: [sent], 1: [near]}
-    crossed = {}
-    for k, j in away[0] + away[1]:
-        crossed[k, j] = [lax.ppermute(have[k][0], "tensor", swap[j])]
+    near = lax.ppermute(sent, "tensor", jump[1])
+    near = unchanged(near, base[-1], *waited, cost=0)
+    have = {0: head + [tail], 1: [near]}
+    for p in away[1]:
+        crossed[p] = [lax.ppermute(near, "tensor", swap[p[1]])]
     far = [lax.ppermute(part, "tensor", jump[top]) for part in base]
     far[:-1] = [unchanged(part, near) for part in far[:-1]]
-    far[-1] = unchanged(far[-1], *far[:-1], *[crossed[p][0] for p in away[0] + away[1]])
+    far[-1] = unchanged(far[-1], *far[:-1], *[crossed[p][0] for p in away[1]])
     have[top] = far
     for k in sorted(range(2, nz), key=lambda k: (k & (k - 1), k)):
         if k != top:

time: 74.8 us -> 75.6 us (1.011)
  Pallas kernels: 24.6 us -> 22.8 us
  starting transfers between devices: 21.5 us -> 23 us
  waiting for transfers between devices: 26.8 us -> 27.7 us
    ppermute x2, waiting for transfers between devices: 0.01 us -> 6.86 us  [body(): far = [lax.ppermute(part, 'tensor', jump[top]) for part in base]]
    ppermute x4, waiting for transfers between devices: 5.52 us -> 0.01 us  [body(): parts = [lax.ppermute(part, 'tensor', swap[j]) for part in have[k]]]
    ppermute x4, waiting for transfers between devices: 7.1 us -> 3.11 us  [the longest x2 3.11 us: body(): lax.ppermute(part, 'tensor', swap[p[1]])]
    ppermute x2, waiting for transfers between devices: 5.73 us -> 8.55 us  [body(): lax.ppermute(part, 'tensor', jump[k & -k])]
    ppermute x2, starting transfers between devices: 2.35 us -> 0.29 us  [body(): lax.ppermute(part, 'tensor', jump[k & -k])]
    ppermute x4, starting transfers between devices: 2.27 us -> 4.01 us  [body(): parts = [lax.ppermute(part, 'tensor', swap[j]) for part in have[k]]]
    pallas_call x4, Pallas kernels: 17.4 us -> 15.8 us  [products(): pl.pallas_call(functools.partial(product_kernel, targets, splits, local,...]
    ppermute x4, starting transfers between devices: 2.03 us -> 3.34 us  [the longest x2 2.03 us: body(): lax.ppermute(part, 'tensor', swap[p[1]])]
  transfers between devices with their start and end apart: 19 -> 19, of which waited for: 11 -> 8; matrix products, arithmetic and copies ran while one was open for 0% -> 0% of each run, Pallas kernels for 25% -> 24%
where the time goes in v10:
time: 75.6 us; the launch traced here: 75.5 us
  waiting for transfers between devices  27.7 us (37%)
  starting transfers between devices  23 us (30%)
  Pallas kernels  22.8 us (30%)
  local copies, waits for them, and re-layouts  0.93 us (1%)
  between operations  0.81 us (1%)
    pallas_call x4, Pallas kernels, products(): pl.pallas_call(functools.partial(product_kernel, targets, splits, local,...  15.8 us
    ppermute x2, waiting for transfers between devices, body(): lax.ppermute(part, 'tensor', jump[k & -k])  8.55 us
    ppermute x3, waiting for transfers between devices, body(): joined_to = lax.ppermute(total, 'tensor', jump[bit])  7.29 us
    ppermute x2, waiting for transfers between devices, body(): far = [lax.ppermute(part, 'tensor', jump[top]) for part in base]  6.86 us
    ppermute x3, starting transfers between devices, body(): joined_to = lax.ppermute(total, 'tensor', jump[bit])  6.19 us
    pallas_call x2, Pallas kernels, finish(): pl.pallas_call(functools.partial(finish_kernel, places, splits, lengths,...  6.11 us
    ppermute x3, starting transfers between devices, body(): result = lax.ppermute(result, 'tensor', swap[j])  4.62 us
    ppermute x4, starting transfers between devices, body(): parts = [lax.ppermute(part, 'tensor', swap[j]) for part in have[k]]  4.01 us
  transfers between devices with their start and end apart: 19, of which 8 were waited for; matrix products, arithmetic and copies ran while one was open for 0% of the time, Pallas kernels for 24%

profile of v10, /device:TPU:0, one launch (start us, length us, event | category | flops | bytes accessed | tf_op | source)
XLA Modules:
  0.0 75.5 jit_solution(2172671654362269322)
XLA Ops:
  0.6 0.9 %copy-done = bf16[64,1024]{1,0:T(8,128)(2,1)S(1)} copy-done((bf16[64,1024]{1,0:T(8,128)(2,1)S(1)}, bf16[64,1024]{1,0:T(8,128)(2,1)}, u32[]{:S(2)}) %copy-start) | copy-done | bytes 131096
  1.5 2.7 %products.4.refs_0_ = bf16[64,2048]{1,0:T(8,128)(2,1)S(1)} custom-call(bf16[64,1024]{1,0:T(8,128)(2,1)S(1)} %copy-done, bf16[1024,16384]{1,0:T(8,128)(2,1)} %weight_ref.7), custom_call_target="tpu_custom_call" | custom-call | flops 268435456 | bytes 4194304 | tf_op jit(solution)/shard_map/products/pallas_call | solution.py:72
  4.2 3.0 %collective-permute-start = (bf16[64,2048]{1,0:T(8,128)(2,1)S(1)}, bf16[64,2048]{1,0:T(8,128)(2,1)S(1)}, u32[]{:S(2)}, u32[]{:S(2)}) collective-permute-start(bf16[64,2048]{1,0:T(8,128)(2,1)S(1)} %products.4.refs_0_), channel_id=1, source_target_pairs={{0,1},{1,0},{2,3},{3,2},{4,5},{5,4},{6,7},{7,6},{8,9},{9,8},{10,11... | collective-permute-start | bytes 786440 | tf_op jit(solution)/shard_map/ppermute | solution.py:337
  7.2 5.2 %products.5 = (bf16[64,2048]{1,0:T(8,128)(2,1)S(1)}, bf16[64,2048]{1,0:T(8,128)(2,1)S(1)}, f32[64,2048]{1,0:T(8,128)S(1)}) custom-call(bf16[64,1024]{1,0:T(8,128)(2,1)S(1)} %copy-done, bf16[1024,16384]{1,0:T(8,128)(2,1)} %weight_ref.7, bf16[64,2048]{1,0:T(8,128)(2,1)S(1)} %products.4.refs_0_), custom_call_target="tpu_custom_call" | custom-call | flops 805306368 | bytes 12582912 | tf_op jit(solution)/shard_map/products/pallas_call | solution.py:72
  12.5 0.1 collective-permute-start.1
  12.6 0.9 %collective-permute-done = bf16[64,2048]{1,0:T(8,128)(2,1)S(1)} collective-permute-done((bf16[64,2048]{1,0:T(8,128)(2,1)S(1)}, bf16[64,2048]{1,0:T(8,128)(2,1)S(1)}, u32[]{:S(2)}, u32[]{:S(2)}) %collective-permute-start) | collective-permute-done | bytes 262176 | tf_op jit(solution)/shard_map/ppermute | solution.py:337
  13.6 1.9 %collective-permute-start.2 = (bf16[64,2048]{1,0:T(8,128)(2,1)S(1)}, bf16[64,2048]{1,0:T(8,128)(2,1)S(1)}, u32[]{:S(2)}, u32[]{:S(2)}) collective-permute-start(bf16[64,2048]{1,0:T(8,128)(2,1)S(1)} %add_convert_fusion.2.refs_0_), channel_id=1, source_target_pairs={{0,2},{1,3},{2,0},{3,1},{4,6},{5,7},{6,4},{7,5},{8,10},{9,11},{10,... | collective-permute-start | bytes 786440 | tf_op jit(solution)/shard_map/ppermute | solution.py:355
  15.5 1.5 %collective-permute-start.5 = (bf16[64,2048]{1,0:T(8,128)(2,1)S(1)}, bf16[64,2048]{1,0:T(8,128)(2,1)S(1)}, u32[]{:S(2)}, u32[]{:S(2)}) collective-permute-start(bf16[64,2048]{1,0:T(8,128)(2,1)S(1)} %get-tuple-element.18), channel_id=1, source_target_pairs={{0,1},{1,0},{2,3},{3,2},{4,5},{5,4},{6,7},{7,6},{8,9},{9,8},{10,11... | collective-permute-start | bytes 786440 | tf_op jit(solution)/shard_map/ppermute | solution.py:337
  17.0 5.2 %products.6 = (bf16[64,2048]{1,0:T(8,128)(2,1)S(1)}, f32[64,2048]{1,0:T(8,128)S(1)}, f32[64,2048]{1,0:T(8,128)S(1)}) custom-call(bf16[64,1024]{1,0:T(8,128)(2,1)S(1)} %copy-done, bf16[1024,16384]{1,0:T(8,128)(2,1)} %weight_ref.7, bf16[64,2048]{1,0:T(8,128)(2,1)S(1)} %add_convert_fusion.2.refs_0_), custom_call_target="tpu_custom_call" | custom-call | flops 805306368 | bytes 12582912 | tf_op jit(solution)/shard_map/products/pallas_call | solution.py:72
  22.2 0.0 collective-permute-done.1
  22.2 0.0 collective-permute-done.2
  22.2 0.1 add_convert_fusion.1.refs_1_
  22.3 2.7 %collective-permute-start.4 = (bf16[64,2048]{1,0:T(8,128)(2,1)S(1)}, bf16[64,2048]{1,0:T(8,128)(2,1)S(1)}, u32[]{:S(2)}, u32[]{:S(2)}) collective-permute-start(bf16[64,2048]{1,0:T(8,128)(2,1)S(1)} %add_convert_fusion.1.refs_1_), channel_id=1, source_target_pairs={{0,4},{1,5},{2,6},{3,7},{4,0},{5,1},{6,2},{7,3},{8,12},{9,13},{10,... | collective-permute-start | bytes 786440 | tf_op jit(solution)/shard_map/ppermute | solution.py:355
  25.0 0.9 %collective-permute-done.5 = bf16[64,2048]{1,0:T(8,128)(2,1)S(1)} collective-permute-done((bf16[64,2048]{1,0:T(8,128)(2,1)S(1)}, bf16[64,2048]{1,0:T(8,128)(2,1)S(1)}, u32[]{:S(2)}, u32[]{:S(2)}) %collective-permute-start.5) | collective-permute-done | bytes 262176 | tf_op jit(solution)/shard_map/ppermute | solution.py:337
  26.0 1.6 %collective-permute-start.6 = (bf16[64,2048]{1,0:T(8,128)(2,1)S(1)}, bf16[64,2048]{1,0:T(8,128)(2,1)S(1)}, u32[]{:S(2)}, u32[]{:S(2)}) collective-permute-start(bf16[64,2048]{1,0:T(8,128)(2,1)S(1)} %add_convert_fusion.refs_0_), channel_id=1, source_target_pairs={{0,2},{1,3},{2,0},{3,1},{4,6},{5,7},{6,4},{7,5},{8,10},{9,11},{10,... | collective-permute-start | bytes 786440 | tf_op jit(solution)/shard_map/ppermute | solution.py:355
  27.6 0.6 collective-permute-start.3
  28.2 2.7 %products.7.refs_3_ = f32[64,2048]{1,0:T(8,128)S(1)} custom-call(bf16[64,1024]{1,0:T(8,128)(2,1)S(1)} %copy-done, bf16[1024,16384]{1,0:T(8,128)(2,1)} %weight_ref.7, bf16[64,2048]{1,0:T(8,128)(2,1)S(1)} %add_convert_fusion.refs_0_, bf16[64,2048]{1,0:T(8,128)(2,1)S(1)} %unchanged.8.refs_1_), custom_call_target="tpu_custom_call" | custom-call | flops 268435456 | bytes 4194304 | tf_op jit(solution)/shard_map/products/pallas_call | solution.py:72
  30.9 0.0 copy-start.1
  30.9 0.0 copy-start.2
  30.9 0.0 copy-start.3
  30.9 4.6 %collective-permute-done.4.refs_0_ = bf16[64,2048]{1,0:T(8,128)(2,1)S(1)} collective-permute-done((bf16[64,2048]{1,0:T(8,128)(2,1)S(1)}, bf16[64,2048]{1,0:T(8,128)(2,1)S(1)}, u32[]{:S(2)}, u32[]{:S(2)}) %collective-permute-start.4) | collective-permute-done | bytes 262176 | tf_op jit(solution)/shard_map/ppermute | solution.py:355
  35.5 2.7 %collective-permute-done.6.refs_2_ = bf16[64,2048]{1,0:T(8,128)(2,1)S(1)} collective-permute-done((bf16[64,2048]{1,0:T(8,128)(2,1)S(1)}, bf16[64,2048]{1,0:T(8,128)(2,1)S(1)}, u32[]{:S(2)}, u32[]{:S(2)}) %collective-permute-start.6) | collective-permute-done | bytes 262176 | tf_op jit(solution)/shard_map/ppermute | solution.py:355
  38.2 0.0 collective-permute-done.3.refs_0_
  38.2 0.9 %own_stream.1 = (bf16[64,2048]{1,0:T(8,128)(2,1)}, bf16[64,2176]{1,0:T(8,128)(2,1)S(1)}, bf16[64,1152]{1,0:T(8,128)(2,1)S(1)}, bf16[64,1024]{1,0:T(8,128)(2,1)S(1)}) custom-call(bf16[64,2048]{1,0:T(8,128)(2,1)S(1)} %copy-done.1, bf16[16,128]{1,0:T(8,128)(2,1)S(1)} %bitcast.2, bf16[16,128]{1,0:T(8,128)(2,1)S(1)} %bitcast.3, ...), custom_call_target="tpu_custom_call" | custom-call | flops 2621440 | bytes 2097152 | tf_op jit(solution)/shard_map/own_stream/pallas_call | solution.py:143
  39.1 0.0 collective-permute-start.9
  39.1 0.9 %collective-permute-start.7 = (bf16[64,1152]{1,0:T(8,128)(2,1)S(1)}, bf16[64,1152]{1,0:T(8,128)(2,1)S(1)}, u32[]{:S(2)}, u32[]{:S(2)}) collective-permute-start(bf16[64,1152]{1,0:T(8,128)(2,1)S(1)} %get-tuple-element.22.refs_0_.refs_1_), channel_id=1, source_target_pairs={{0,1},{1,0},{2,3},{3,2},{4,5},{5,4},{6,7},{7,6},{8,9},{9,8},{10,11... | collective-permute-start | bytes 442376 | tf_op jit(solution)/shard_map/ppermute | solution.py:366
  40.0 1.1 %collective-permute-start.10 = (bf16[64,1024]{1,0:T(8,128)(2,1)S(1)}, bf16[64,1024]{1,0:T(8,128)(2,1)S(1)}, u32[]{:S(2)}, u32[]{:S(2)}) collective-permute-start(bf16[64,1024]{1,0:T(8,128)(2,1)S(1)} %get-tuple-element.21.refs_0_), channel_id=1, source_target_pairs={{0,1},{1,0},{2,3},{3,2},{4,5},{5,4},{6,7},{7,6},{8,9},{9,8},{10,11... | collective-permute-start | bytes 393224 | tf_op jit(solution)/shard_map/ppermute | solution.py:366
  41.1 3.1 %collective-permute-done.7.refs_1_.refs_3_ = bf16[64,1152]{1,0:T(8,128)(2,1)S(1)} collective-permute-done((bf16[64,1152]{1,0:T(8,128)(2,1)S(1)}, bf16[64,1152]{1,0:T(8,128)(2,1)S(1)}, u32[]{:S(2)}, u32[]{:S(2)}) %collective-permute-start.7) | collective-permute-done | bytes 147488 | tf_op jit(solution)/shard_map/ppermute | solution.py:366
  44.3 3.9 %collective-permute-start.8 = (bf16[64,1024]{1,0:T(8,128)(2,1)S(1)}, bf16[64,1024]{1,0:T(8,128)(2,1)S(1)}, u32[]{:S(2)}, u32[]{:S(2)}) collective-permute-start(bf16[64,1024]{1,0:T(8,128)(2,1)S(1)} %unchanged.10), channel_id=1, source_target_pairs={{0,4},{1,5},{2,6},{3,7},{4,0},{5,1},{6,2},{7,3},{8,12},{9,13},{10,... | collective-permute-start | bytes 393224 | tf_op jit(solution)/shard_map/ppermute | solution.py:377
  48.2 0.1 collective-permute-start.13
  48.3 0.0 collective-permute-done.10.refs_2_
  48.3 0.0 collective-permute-done.9.refs_0_
  48.3 1.3 %collective-permute-start.14 = (bf16[64,2176]{1,0:T(8,128)(2,1)S(1)}, bf16[64,2176]{1,0:T(8,128)(2,1)S(1)}, u32[]{:S(2)}, u32[]{:S(2)}) collective-permute-start(bf16[64,2176]{1,0:T(8,128)(2,1)S(1)} %unchanged.11.refs_1_.refs_4_.refs_15_), channel_id=1, source_target_pairs={{0,1},{1,0},{2,3},{3,2},{4,5},{5,4},{6,7},{7,6},{8,9},{9,8},{10,11... | collective-permute-start | bytes 835592 | tf_op jit(solution)/shard_map/ppermute | solution.py:376
  49.6 6.9 %collective-permute-done.8.refs_0_ = bf16[64,1024]{1,0:T(8,128)(2,1)S(1)} collective-permute-done((bf16[64,1024]{1,0:T(8,128)(2,1)S(1)}, bf16[64,1024]{1,0:T(8,128)(2,1)S(1)}, u32[]{:S(2)}, u32[]{:S(2)}) %collective-permute-start.8) | collective-permute-done | bytes 131104 | tf_op jit(solution)/shard_map/ppermute | solution.py:377
  56.5 0.0 collective-permute-start.11
  56.5 1.3 %collective-permute-start.17 = (bf16[64,1024]{1,0:T(8,128)(2,1)S(1)}, bf16[64,1024]{1,0:T(8,128)(2,1)S(1)}, u32[]{:S(2)}, u32[]{:S(2)}) collective-permute-start(bf16[64,1024]{1,0:T(8,128)(2,1)S(1)} %unchanged.12.refs_1_.refs_6_), channel_id=1, source_target_pairs={{0,1},{1,0},{2,3},{3,2},{4,5},{5,4},{6,7},{7,6},{8,9},{9,8},{10,11... | collective-permute-start | bytes 393224 | tf_op jit(solution)/shard_map/ppermute | solution.py:391
  57.7 4.4 %collective-permute-done.11.refs_10_ = bf16[64,1024]{1,0:T(8,128)(2,1)S(1)} collective-permute-done((bf16[64,1024]{1,0:T(8,128)(2,1)S(1)}, bf16[64,1024]{1,0:T(8,128)(2,1)S(1)}, u32[]{:S(2)}, u32[]{:S(2)}) %collective-permute-start.11) | collective-permute-done | bytes 131104 | tf_op jit(solution)/shard_map/ppermute | solution.py:385
  62.2 1.3 %collective-permute-start.12 = (bf16[64,1024]{1,0:T(8,128)(2,1)S(1)}, bf16[64,1024]{1,0:T(8,128)(2,1)S(1)}, u32[]{:S(2)}, u32[]{:S(2)}) collective-permute-start(bf16[64,1024]{1,0:T(8,128)(2,1)S(1)} %collective-permute-done.11.refs_10_), channel_id=1, source_target_pairs={{0,1},{1,0},{2,3},{3,2},{4,5},{5,4},{6,7},{7,6},{8,9},{9,8},{10,11... | collective-permute-start | bytes 393224 | tf_op jit(solution)/shard_map/ppermute | solution.py:391
  63.5 0.0 collective-permute-done.13.refs_0_
  63.5 0.0 collective-permute-done.14.refs_2_.refs_5_.refs_16_
  63.5 0.3 collective-permute-start.15
  63.8 0.7 collective-permute-start.18
  64.5 4.1 %collective-permute-done.15.refs_11_.refs_14_ = bf16[64,1152]{1,0:T(8,128)(2,1)S(1)} collective-permute-done((bf16[64,1152]{1,0:T(8,128)(2,1)S(1)}, bf16[64,1152]{1,0:T(8,128)(2,1)S(1)}, u32[]{:S(2)}, u32[]{:S(2)}) %collective-permute-start.15) | collective-permute-done | bytes 147488 | tf_op jit(solution)/shard_map/ppermute | solution.py:385
  68.6 0.7 collective-permute-start.16
  69.4 0.0 collective-permute-done.12.refs_0_
  69.4 4.7 %finish.2 = (bf16[64,16384]{1,0:T(8,128)(2,1)}, f32[64,128]{1,0:T(8,128)S(1)}) custom-call(bf16[64,1024]{1,0:T(8,128)(2,1)S(1)} %get-tuple-element.21.refs_0_, bf16[64,1152]{1,0:T(8,128)(2,1)S(1)} %get-tuple-element.22.refs_0_.refs_1_, bf16[64,1024]{1,0:T(8,128)(2,1)S(1)} %collective-permute-done.10.refs_2_, ...), custom_call_target="tpu_custom_call" | custom-call | flops 939524096 | bytes 3670016 | tf_op jit(solution)/shard_map/finish/pallas_call | solution.py:288
  74.1 0.0 collective-permute-done.16.refs_1_
  74.1 1.4 %finish.3 = bf16[64,16384]{1,0:T(8,128)(2,1)} custom-call(bf16[64,1024]{1,0:T(8,128)(2,1)S(1)} %unchanged.13.refs_0_, bf16[64,1152]{1,0:T(8,128)(2,1)S(1)} %collective-permute-done.16.refs_1_, f32[64,128]{1,0:T(8,128)S(1)} %get-tuple-element.24.refs_2_, bf16[64,16384]{1,0:T(8,128)(2,1)} %get-tuple-element.25.refs_3_), custom_call_target="tpu_custom_call", output_to_operand_aliasing={{}: (3, {})} | custom-call | flops 134217728 | bytes 524288 | tf_op jit(solution)/shard_map/finish/pallas_call | solution.py:288
  (18 shorter events, 0.2 us)
Async XLA Ops:
  0.6 0.9 %copy-start = (bf16[64,1024]{1,0:T(8,128)(2,1)S(1)}, bf16[64,1024]{1,0:T(8,128)(2,1)}, u32[]{:S(2)}) copy-start(bf16[64,1024]{1,0:T(8,128)(2,1)} %rows_ref.7) | copy-start | bytes 393220
  4.2 9.3 %collective-permute-start = (bf16[64,2048]{1,0:T(8,128)(2,1)S(1)}, bf16[64,2048]{1,0:T(8,128)(2,1)S(1)}, u32[]{:S(2)}, u32[]{:S(2)}) collective-permute-start(bf16[64,2048]{1,0:T(8,128)(2,1)S(1)} %products.4.refs_0_), channel_id=1, source_target_pairs={{0,1},{1,0},{2,3},{3,2},{4,5},{5,4},{6,7},{7,6},{8,9},{9,8},{10,11... | collective-permute-start | bytes 786440 | tf_op jit(solution)/shard_map/ppermute | solution.py:337
  12.5 9.7 %collective-permute-start.1 = (bf16[64,2048]{1,0:T(8,128)(2,1)S(1)}, bf16[64,2048]{1,0:T(8,128)(2,1)S(1)}, u32[]{:S(2)}, u32[]{:S(2)}) collective-permute-start(bf16[64,2048]{1,0:T(8,128)(2,1)S(1)} %get-tuple-element.16), channel_id=1, source_target_pairs={{0,1},{1,0},{2,3},{3,2},{4,5},{5,4},{6,7},{7,6},{8,9},{9,8},{10,11... | collective-permute-start | bytes 786440 | tf_op jit(solution)/shard_map/ppermute | solution.py:337
  13.6 8.6 %collective-permute-start.2 = (bf16[64,2048]{1,0:T(8,128)(2,1)S(1)}, bf16[64,2048]{1,0:T(8,128)(2,1)S(1)}, u32[]{:S(2)}, u32[]{:S(2)}) collective-permute-start(bf16[64,2048]{1,0:T(8,128)(2,1)S(1)} %add_convert_fusion.2.refs_0_), channel_id=1, source_target_pairs={{0,2},{1,3},{2,0},{3,1},{4,6},{5,7},{6,4},{7,5},{8,10},{9,11},{10,... | collective-permute-start | bytes 786440 | tf_op jit(solution)/shard_map/ppermute | solution.py:355
  15.5 10.4 %collective-permute-start.5 = (bf16[64,2048]{1,0:T(8,128)(2,1)S(1)}, bf16[64,2048]{1,0:T(8,128)(2,1)S(1)}, u32[]{:S(2)}, u32[]{:S(2)}) collective-permute-start(bf16[64,2048]{1,0:T(8,128)(2,1)S(1)} %get-tuple-element.18), channel_id=1, source_target_pairs={{0,1},{1,0},{2,3},{3,2},{4,5},{5,4},{6,7},{7,6},{8,9},{9,8},{10,11... | collective-permute-start | bytes 786440 | tf_op jit(solution)/shard_map/ppermute | solution.py:337
  22.3 13.2 %collective-permute-start.4 = (bf16[64,2048]{1,0:T(8,128)(2,1)S(1)}, bf16[64,2048]{1,0:T(8,128)(2,1)S(1)}, u32[]{:S(2)}, u32[]{:S(2)}) collective-permute-start(bf16[64,2048]{1,0:T(8,128)(2,1)S(1)} %add_convert_fusion.1.refs_1_), channel_id=1, source_target_pairs={{0,4},{1,5},{2,6},{3,7},{4,0},{5,1},{6,2},{7,3},{8,12},{9,13},{10,... | collective-permute-start | bytes 786440 | tf_op jit(solution)/shard_map/ppermute | solution.py:355
  26.0 12.2 %collective-permute-start.6 = (bf16[64,2048]{1,0:T(8,128)(2,1)S(1)}, bf16[64,2048]{1,0:T(8,128)(2,1)S(1)}, u32[]{:S(2)}, u32[]{:S(2)}) collective-permute-start(bf16[64,2048]{1,0:T(8,128)(2,1)S(1)} %add_convert_fusion.refs_0_), channel_id=1, source_target_pairs={{0,2},{1,3},{2,0},{3,1},{4,6},{5,7},{6,4},{7,5},{8,10},{9,11},{10,... | collective-permute-start | bytes 786440 | tf_op jit(solution)/shard_map/ppermute | solution.py:355
  27.6 10.6 %collective-permute-start.3 = (bf16[64,2048]{1,0:T(8,128)(2,1)S(1)}, bf16[64,2048]{1,0:T(8,128)(2,1)S(1)}, u32[]{:S(2)}, u32[]{:S(2)}) collective-permute-start(bf16[64,2048]{1,0:T(8,128)(2,1)S(1)} %unchanged.8.refs_1_), channel_id=1, source_target_pairs={{0,1},{1,0},{2,3},{3,2},{4,5},{5,4},{6,7},{7,6},{8,9},{9,8},{10,11... | collective-permute-start | bytes 786440 | tf_op jit(solution)/shard_map/ppermute | solution.py:353
  30.9 7.3 %copy-start.1 = (bf16[64,2048]{1,0:T(8,128)(2,1)S(1)}, bf16[64,2048]{1,0:T(8,128)(2,1)}, u32[]{:S(2)}) copy-start(bf16[64,2048]{1,0:T(8,128)(2,1)} %residual_ref.1) | copy-start | bytes 786436
  30.9 7.3 %copy-start.2 = (bf16[2048]{0:T(1024)(128)(2,1)S(1)}, bf16[2048]{0:T(1024)(128)(2,1)}, u32[]{:S(2)}) copy-start(bf16[2048]{0:T(1024)(128)(2,1)} %param.8) | copy-start | bytes 12292
  30.9 7.3 %copy-start.3 = (bf16[2048]{0:T(1024)(128)(2,1)S(1)}, bf16[2048]{0:T(1024)(128)(2,1)}, u32[]{:S(2)}) copy-start(bf16[2048]{0:T(1024)(128)(2,1)} %param.9) | copy-start | bytes 12292
  39.1 9.2 %collective-permute-start.9 = (bf16[64,2176]{1,0:T(8,128)(2,1)S(1)}, bf16[64,2176]{1,0:T(8,128)(2,1)S(1)}, u32[]{:S(2)}, u32[]{:S(2)}) collective-permute-start(bf16[64,2176]{1,0:T(8,128)(2,1)S(1)} %get-tuple-element.23), channel_id=1, source_target_pairs={{0,2},{1,3},{2,0},{3,1},{4,6},{5,7},{6,4},{7,5},{8,10},{9,11},{10,... | collective-permute-start | bytes 835592 | tf_op jit(solution)/shard_map/ppermute | solution.py:372
  39.1 5.1 %collective-permute-start.7 = (bf16[64,1152]{1,0:T(8,128)(2,1)S(1)}, bf16[64,1152]{1,0:T(8,128)(2,1)S(1)}, u32[]{:S(2)}, u32[]{:S(2)}) collective-permute-start(bf16[64,1152]{1,0:T(8,128)(2,1)S(1)} %get-tuple-element.22.refs_0_.refs_1_), channel_id=1, source_target_pairs={{0,1},{1,0},{2,3},{3,2},{4,5},{5,4},{6,7},{7,6},{8,9},{9,8},{10,11... | collective-permute-start | bytes 442376 | tf_op jit(solution)/shard_map/ppermute | solution.py:366
  40.0 8.3 %collective-permute-start.10 = (bf16[64,1024]{1,0:T(8,128)(2,1)S(1)}, bf16[64,1024]{1,0:T(8,128)(2,1)S(1)}, u32[]{:S(2)}, u32[]{:S(2)}) collective-permute-start(bf16[64,1024]{1,0:T(8,128)(2,1)S(1)} %get-tuple-element.21.refs_0_), channel_id=1, source_target_pairs={{0,1},{1,0},{2,3},{3,2},{4,5},{5,4},{6,7},{7,6},{8,9},{9,8},{10,11... | collective-permute-start | bytes 393224 | tf_op jit(solution)/shard_map/ppermute | solution.py:366
  44.3 12.2 %collective-permute-start.8 = (bf16[64,1024]{1,0:T(8,128)(2,1)S(1)}, bf16[64,1024]{1,0:T(8,128)(2,1)S(1)}, u32[]{:S(2)}, u32[]{:S(2)}) collective-permute-start(bf16[64,1024]{1,0:T(8,128)(2,1)S(1)} %unchanged.10), channel_id=1, source_target_pairs={{0,4},{1,5},{2,6},{3,7},{4,0},{5,1},{6,2},{7,3},{8,12},{9,13},{10,... | collective-permute-start | bytes 393224 | tf_op jit(solution)/shard_map/ppermute | solution.py:377
  48.2 15.3 %collective-permute-start.13 = (bf16[64,1152]{1,0:T(8,128)(2,1)S(1)}, bf16[64,1152]{1,0:T(8,128)(2,1)S(1)}, u32[]{:S(2)}, u32[]{:S(2)}) collective-permute-start(bf16[64,1152]{1,0:T(8,128)(2,1)S(1)} %merge.1.refs_1_.refs_12_), channel_id=1, source_target_pairs={{0,4},{1,5},{2,6},{3,7},{4,0},{5,1},{6,2},{7,3},{8,12},{9,13},{10,... | collective-permute-start | bytes 442376 | tf_op jit(solution)/shard_map/ppermute | solution.py:377
  48.3 15.2 %collective-permute-start.14 = (bf16[64,2176]{1,0:T(8,128)(2,1)S(1)}, bf16[64,2176]{1,0:T(8,128)(2,1)S(1)}, u32[]{:S(2)}, u32[]{:S(2)}) collective-permute-start(bf16[64,2176]{1,0:T(8,128)(2,1)S(1)} %unchanged.11.refs_1_.refs_4_.refs_15_), channel_id=1, source_target_pairs={{0,1},{1,0},{2,3},{3,2},{4,5},{5,4},{6,7},{7,6},{8,9},{9,8},{10,11... | collective-permute-start | bytes 835592 | tf_op jit(solution)/shard_map/ppermute | solution.py:376
  56.5 5.7 %collective-permute-start.11 = (bf16[64,1024]{1,0:T(8,128)(2,1)S(1)}, bf16[64,1024]{1,0:T(8,128)(2,1)S(1)}, u32[]{:S(2)}, u32[]{:S(2)}) collective-permute-start(bf16[64,1024]{1,0:T(8,128)(2,1)S(1)} %unchanged.12.refs_1_.refs_6_), channel_id=1, source_target_pairs={{0,2},{1,3},{2,0},{3,1},{4,6},{5,7},{6,4},{7,5},{8,10},{9,11},{10,... | collective-permute-start | bytes 393224 | tf_op jit(solution)/shard_map/ppermute | solution.py:385
  56.5 7.3 %collective-permute-start.17 = (bf16[64,1024]{1,0:T(8,128)(2,1)S(1)}, bf16[64,1024]{1,0:T(8,128)(2,1)S(1)}, u32[]{:S(2)}, u32[]{:S(2)}) collective-permute-start(bf16[64,1024]{1,0:T(8,128)(2,1)S(1)} %unchanged.12.refs_1_.refs_6_), channel_id=1, source_target_pairs={{0,1},{1,0},{2,3},{3,2},{4,5},{5,4},{6,7},{7,6},{8,9},{9,8},{10,11... | collective-permute-start | bytes 393224 | tf_op jit(solution)/shard_map/ppermute | solution.py:391
  62.2 7.2 %collective-permute-start.12 = (bf16[64,1024]{1,0:T(8,128)(2,1)S(1)}, bf16[64,1024]{1,0:T(8,128)(2,1)S(1)}, u32[]{:S(2)}, u32[]{:S(2)}) collective-permute-start(bf16[64,1024]{1,0:T(8,128)(2,1)S(1)} %collective-permute-done.11.refs_10_), channel_id=1, source_target_pairs={{0,1},{1,0},{2,3},{3,2},{4,5},{5,4},{6,7},{7,6},{8,9},{9,8},{10,11... | collective-permute-start | bytes 393224 | tf_op jit(solution)/shard_map/ppermute | solution.py:391
  63.5 5.1 %collective-permute-start.15 = (bf16[64,1152]{1,0:T(8,128)(2,1)S(1)}, bf16[64,1152]{1,0:T(8,128)(2,1)S(1)}, u32[]{:S(2)}, u32[]{:S(2)}) collective-permute-start(bf16[64,1152]{1,0:T(8,128)(2,1)S(1)} %unchanged.14.refs_7_.refs_13_), channel_id=1, source_target_pairs={{0,2},{1,3},{2,0},{3,1},{4,6},{5,7},{6,4},{7,5},{8,10},{9,11},{10,... | collective-permute-start | bytes 442376 | tf_op jit(solution)/shard_map/ppermute | solution.py:385
  63.8 5.6 %collective-permute-start.18 = (bf16[64,1152]{1,0:T(8,128)(2,1)S(1)}, bf16[64,1152]{1,0:T(8,128)(2,1)S(1)}, u32[]{:S(2)}, u32[]{:S(2)}) collective-permute-start(bf16[64,1152]{1,0:T(8,128)(2,1)S(1)} %unchanged.14.refs_7_.refs_13_), channel_id=1, source_target_pairs={{0,1},{1,0},{2,3},{3,2},{4,5},{5,4},{6,7},{7,6},{8,9},{9,8},{10,11... | collective-permute-start | bytes 442376 | tf_op jit(solution)/shard_map/ppermute | solution.py:391
  68.6 5.5 %collective-permute-start.16 = (bf16[64,1152]{1,0:T(8,128)(2,1)S(1)}, bf16[64,1152]{1,0:T(8,128)(2,1)S(1)}, u32[]{:S(2)}, u32[]{:S(2)}) collective-permute-start(bf16[64,1152]{1,0:T(8,128)(2,1)S(1)} %collective-permute-done.15.refs_11_.refs_14_), channel_id=1, source_target_pairs={{0,1},{1,0},{2,3},{3,2},{4,5},{5,4},{6,7},{7,6},{8,9},{9,8},{10,11... | collective-permute-start | bytes 442376 | tf_op jit(solution)/shard_map/ppermute | solution.py:391

commit v11 on v7

--- a/solution.py
+++ b/solution.py
@@ -66,7 +66,7 @@
 
 def products(attended, weight, targets, splits, local, after):
     rows, depth = attended.shape
-    tile = tile_width(local, 512)
+    tile = tile_width(local, 256)
     slots = len(targets) * (local // tile)
     vmem = pl.BlockSpec(memory_space=pltpu.VMEM)
     return pl.pallas_call(
@@ -206,12 +206,12 @@
     )(sent, *others)
 
 
-def coded_rows(piece, local, centre, inverse, table):
+def coded_rows(piece, local, chosen, centre, inverse, table):
     rows, blocks = piece.shape[0], local // BLOCK_LEN
     unit = 1.0 / math.sqrt(BLOCK_LEN)
     scaling = piece[rows - 2 * blocks :, local:].astype(jnp.float32)
     normal = []
-    for b in range(blocks):
+    for b in chosen:
         block = piece[:, b * BLOCK_LEN : (b + 1) * BLOCK_LEN].astype(jnp.float32)
         block = (block - centre) * inverse
         normal.append(block * scaling[b : b + 1] + scaling[blocks + b : blocks + b + 1])
@@ -247,19 +247,28 @@
     me = lax.axis_index("tensor")
     outer, inner = me // splits[1], lax.rem(me, splits[1])
     copies = []
+    blocks = width // BLOCK_LEN
+    step = blocks // 2 if len(places) == 1 and blocks > 1 else blocks
     for p, (k, j) in enumerate(places):
-        back = coded_rows(pieces[p], width, columns[:, 0:1], columns[:, 1:2], table)
-        for b in range(width // BLOCK_LEN):
-            done_ref[p, :, b * BLOCK_LEN : (b + 1) * BLOCK_LEN] = back[
-                b * rows : (b + 1) * rows
-            ]
         owner = jnp.bitwise_xor(outer, k) * splits[1] + jnp.bitwise_xor(inner, j)
-        place = pl.ds(pl.multiple_of(owner * width, LANES), width)
-        copy = pltpu.make_async_copy(
-            done_ref.at[p], out_ref.at[:, place], semaphores.at[p]
-        )
-        copy.start()
-        copies.append(copy)
+        for begin in range(0, blocks, step):
+            chosen = range(begin, begin + step)
+            back = coded_rows(
+                pieces[p], width, chosen, columns[:, 0:1], columns[:, 1:2], table
+            )
+            for i, b in enumerate(chosen):
+                done_ref[p, :, b * BLOCK_LEN : (b + 1) * BLOCK_LEN] = back[
+                    i * rows : (i + 1) * rows
+                ]
+            here = pl.ds(begin * BLOCK_LEN, step * BLOCK_LEN)
+            start = pl.multiple_of(owner * width + begin * BLOCK_LEN, LANES)
+            copy = pltpu.make_async_copy(
+                done_ref.at[p, :, here],
+                out_ref.at[:, pl.ds(start, step * BLOCK_LEN)],
+                semaphores.at[len(copies)],
+            )
+            copy.start()
+            copies.append(copy)
     for copy in copies:
         copy.wait()
 
@@ -281,7 +290,7 @@
         out_specs=[anywhere, vmem][: len(out_shape)],
         scratch_shapes=[
             pltpu.VMEM((count, rows, local), jnp.bfloat16),
-            pltpu.SemaphoreType.DMA((count,)),
+            pltpu.SemaphoreType.DMA((count + 1,)),
         ],
         input_output_aliases={count + len(given) - 1: 0} if earlier else {},
         compiler_params=pltpu.CompilerParams(vmem_limit_bytes=16 * MIB),

time: 71.2 us -> 75.4 us (1.059)
  Pallas kernels: 23 us -> 30.4 us
  starting transfers between devices: 20.7 us -> 16.4 us
  waiting for transfers between devices: 25.5 us -> 26.5 us
    pallas_call x4, Pallas kernels: 15.8 us -> 23.1 us  [products(): pl.pallas_call(functools.partial(product_kernel, targets, splits, local,...]
    ppermute x3, waiting for transfers between devices: 1.88 us -> 0.01 us  [body(): result = lax.ppermute(result, 'tensor', swap[j])]
    ppermute x1, waiting for transfers between devices: 1.71 us -> 3.35 us  [body(): have = {0: merged, 1: lax.ppermute(sent, 'tensor', jump[1])}]
    ppermute x2, starting transfers between devices: 2.56 us -> 1.02 us  [body(): crossed[k, j] = lax.ppermute(have[k], 'tensor', swap[j])]
    ppermute x1, starting transfers between devices: 3.41 us -> 2.01 us  [body(): have[top] = lax.ppermute(merged, 'tensor', jump[top])]
    ppermute x3, starting transfers between devices: 6.19 us -> 5.31 us  [body(): joined_to = lax.ppermute(total, 'tensor', jump[bit])]
    ppermute x1, waiting for transfers between devices: 5.24 us -> 6.01 us  [body(): have[k] = lax.ppermute(have[k ^ k & -k], 'tensor', jump[k & -k])]
    ppermute x2, waiting for transfers between devices: 0.59 us -> 1.35 us  [body(): crossed[k, j] = lax.ppermute(have[k], 'tensor', swap[j])]
  transfers between devices with their start and end apart: 15 -> 15, of which waited for: 9 -> 8; matrix products, arithmetic and copies ran while one was open for 0% -> 0% of each run, Pallas kernels for 25% -> 32%
where the time goes in v11:
time: 75.4 us; the launch traced here: 75.3 us
  Pallas kernels  30.4 us (40%)
  waiting for transfers between devices  26.5 us (35%)
  starting transfers between devices  16.4 us (22%)
  local copies, waits for them, and re-layouts  0.92 us (1%)
  between operations  0.92 us (1%)
    pallas_call x4, Pallas kernels, products(): pl.pallas_call(functools.partial(product_kernel, targets, splits, local,...  23.1 us
    ppermute x3, waiting for transfers between devices, body(): joined_to = lax.ppermute(total, 'tensor', jump[bit])  7.49 us
    ppermute x1, waiting for transfers between devices, body(): have[top] = lax.ppermute(merged, 'tensor', jump[top])  6.62 us
    pallas_call x2, Pallas kernels, finish(): pl.pallas_call(functools.partial(finish_kernel, places, splits, counts, t...  6.29 us
    ppermute x1, waiting for transfers between devices, body(): have[k] = lax.ppermute(have[k ^ k & -k], 'tensor', jump[k & -k])  6.01 us
    ppermute x3, starting transfers between devices, body(): joined_to = lax.ppermute(total, 'tensor', jump[bit])  5.31 us
    ppermute x3, starting transfers between devices, body(): result = lax.ppermute(result, 'tensor', swap[j])  4.62 us
    ppermute x1, waiting for transfers between devices, body(): have = {0: merged, 1: lax.ppermute(sent, 'tensor', jump[1])}  3.35 us
  transfers between devices with their start and end apart: 15, of which 8 were waited for; matrix products, arithmetic and copies ran while one was open for 0% of the time, Pallas kernels for 32%

profile of v11, /device:TPU:0, one launch (start us, length us, event | category | flops | bytes accessed | tf_op | source)
XLA Modules:
  0.0 75.3 jit_solution(6589042648221902824)
XLA Ops:
  0.6 0.0 copy-start
  0.6 0.9 %copy-done = bf16[64,1024]{1,0:T(8,128)(2,1)S(1)} copy-done((bf16[64,1024]{1,0:T(8,128)(2,1)S(1)}, bf16[64,1024]{1,0:T(8,128)(2,1)}, u32[]{:S(2)}) %copy-start) | copy-done | bytes 131096
  1.5 3.5 %products.4.refs_0_ = bf16[64,2048]{1,0:T(8,128)(2,1)S(1)} custom-call(bf16[64,1024]{1,0:T(8,128)(2,1)S(1)} %copy-done, bf16[1024,16384]{1,0:T(8,128)(2,1)} %weight_ref.7), custom_call_target="tpu_custom_call" | custom-call | flops 268435456 | bytes 4194304 | tf_op jit(solution)/shard_map/products/pallas_call | solution.py:72
  5.0 3.0 %collective-permute-start = (bf16[64,2048]{1,0:T(8,128)(2,1)S(1)}, bf16[64,2048]{1,0:T(8,128)(2,1)S(1)}, u32[]{:S(2)}, u32[]{:S(2)}) collective-permute-start(bf16[64,2048]{1,0:T(8,128)(2,1)S(1)} %products.4.refs_0_), channel_id=1, source_target_pairs={{0,1},{1,0},{2,3},{3,2},{4,5},{5,4},{6,7},{7,6},{8,9},{9,8},{10,11... | collective-permute-start | bytes 786440 | tf_op jit(solution)/shard_map/ppermute | solution.py:334
  8.0 8.0 %products.5 = (bf16[64,2048]{1,0:T(8,128)(2,1)S(1)}, bf16[64,2048]{1,0:T(8,128)(2,1)S(1)}, f32[64,2048]{1,0:T(8,128)S(1)}) custom-call(bf16[64,1024]{1,0:T(8,128)(2,1)S(1)} %copy-done, bf16[1024,16384]{1,0:T(8,128)(2,1)} %weight_ref.7, bf16[64,2048]{1,0:T(8,128)(2,1)S(1)} %products.4.refs_0_), custom_call_target="tpu_custom_call" | custom-call | flops 805306368 | bytes 12582912 | tf_op jit(solution)/shard_map/products/pallas_call | solution.py:72
  16.0 0.1 collective-permute-start.1
  16.1 0.0 collective-permute-done
  16.2 2.1 %collective-permute-start.2 = (bf16[64,2048]{1,0:T(8,128)(2,1)S(1)}, bf16[64,2048]{1,0:T(8,128)(2,1)S(1)}, u32[]{:S(2)}, u32[]{:S(2)}) collective-permute-start(bf16[64,2048]{1,0:T(8,128)(2,1)S(1)} %add_convert_fusion.2.refs_0_), channel_id=1, source_target_pairs={{0,2},{1,3},{2,0},{3,1},{4,6},{5,7},{6,4},{7,5},{8,10},{9,11},{10,... | collective-permute-start | bytes 786440 | tf_op jit(solution)/shard_map/ppermute | solution.py:352
  18.3 1.5 %collective-permute-start.5 = (bf16[64,2048]{1,0:T(8,128)(2,1)S(1)}, bf16[64,2048]{1,0:T(8,128)(2,1)S(1)}, u32[]{:S(2)}, u32[]{:S(2)}) collective-permute-start(bf16[64,2048]{1,0:T(8,128)(2,1)S(1)} %get-tuple-element.17), channel_id=1, source_target_pairs={{0,1},{1,0},{2,3},{3,2},{4,5},{5,4},{6,7},{7,6},{8,9},{9,8},{10,11... | collective-permute-start | bytes 786440 | tf_op jit(solution)/shard_map/ppermute | solution.py:334
  19.8 8.0 %products.6 = (bf16[64,2048]{1,0:T(8,128)(2,1)S(1)}, f32[64,2048]{1,0:T(8,128)S(1)}, f32[64,2048]{1,0:T(8,128)S(1)}) custom-call(bf16[64,1024]{1,0:T(8,128)(2,1)S(1)} %copy-done, bf16[1024,16384]{1,0:T(8,128)(2,1)} %weight_ref.7, bf16[64,2048]{1,0:T(8,128)(2,1)S(1)} %add_convert_fusion.2.refs_0_), custom_call_target="tpu_custom_call" | custom-call | flops 805306368 | bytes 12582912 | tf_op jit(solution)/shard_map/products/pallas_call | solution.py:72
  27.8 0.0 collective-permute-done.1
  27.8 0.0 collective-permute-done.2
  27.8 0.1 add_convert_fusion.1.refs_1_
  27.9 2.7 %collective-permute-start.4 = (bf16[64,2048]{1,0:T(8,128)(2,1)S(1)}, bf16[64,2048]{1,0:T(8,128)(2,1)S(1)}, u32[]{:S(2)}, u32[]{:S(2)}) collective-permute-start(bf16[64,2048]{1,0:T(8,128)(2,1)S(1)} %add_convert_fusion.1.refs_1_), channel_id=1, source_target_pairs={{0,4},{1,5},{2,6},{3,7},{4,0},{5,1},{6,2},{7,3},{8,12},{9,13},{10,... | collective-permute-start | bytes 786440 | tf_op jit(solution)/shard_map/ppermute | solution.py:352
  30.6 0.0 collective-permute-done.5
  30.6 0.5 collective-permute-start.6
  31.2 0.5 collective-permute-start.3
  31.7 3.6 %products.7.refs_3_ = f32[64,2048]{1,0:T(8,128)S(1)} custom-call(bf16[64,1024]{1,0:T(8,128)(2,1)S(1)} %copy-done, bf16[1024,16384]{1,0:T(8,128)(2,1)} %weight_ref.7, bf16[64,2048]{1,0:T(8,128)(2,1)S(1)} %add_convert_fusion.refs_0_, bf16[64,2048]{1,0:T(8,128)(2,1)S(1)} %unchanged.3.refs_1_), custom_call_target="tpu_custom_call" | custom-call | flops 268435456 | bytes 4194304 | tf_op jit(solution)/shard_map/products/pallas_call | solution.py:72
  35.3 0.0 copy-start.1
  35.3 0.0 copy-start.2
  35.4 0.0 copy-start.3
  35.4 6.0 %collective-permute-done.4.refs_0_ = bf16[64,2048]{1,0:T(8,128)(2,1)S(1)} collective-permute-done((bf16[64,2048]{1,0:T(8,128)(2,1)S(1)}, bf16[64,2048]{1,0:T(8,128)(2,1)S(1)}, u32[]{:S(2)}, u32[]{:S(2)}) %collective-permute-start.4) | collective-permute-done | bytes 262176 | tf_op jit(solution)/shard_map/ppermute | solution.py:352
  41.4 1.4 %collective-permute-done.6.refs_2_ = bf16[64,2048]{1,0:T(8,128)(2,1)S(1)} collective-permute-done((bf16[64,2048]{1,0:T(8,128)(2,1)S(1)}, bf16[64,2048]{1,0:T(8,128)(2,1)S(1)}, u32[]{:S(2)}, u32[]{:S(2)}) %collective-permute-start.6) | collective-permute-done | bytes 262176 | tf_op jit(solution)/shard_map/ppermute | solution.py:352
  42.9 0.0 collective-permute-done.3.refs_0_
  42.9 0.0 copy-done.1
  42.9 0.0 copy-done.2
  42.9 0.0 copy-done.3
  42.9 1.0 %own_stream.1 = (bf16[64,2048]{1,0:T(8,128)(2,1)}, bf16[64,2176]{1,0:T(8,128)(2,1)S(1)}, bf16[16,128]{1,0:T(8,128)(2,1)S(1)}) custom-call(bf16[64,2048]{1,0:T(8,128)(2,1)S(1)} %copy-done.1, bf16[16,128]{1,0:T(8,128)(2,1)S(1)} %bitcast.2, bf16[16,128]{1,0:T(8,128)(2,1)S(1)} %bitcast.3, bf16[64,2048]{1,0:T(8,128)(2,1)S(1)} %collective-permute-done.3.refs_0_, ...), custom_call_target="tpu_custom_call" | custom-call | flops 2621440 | bytes 2097152 | tf_op jit(solution)/shard_map/own_stream/pallas_call | solution.py:138
  43.9 0.3 collective-permute-start.10
  44.2 0.5 collective-permute-start.7
  44.7 1.5 %collective-permute-start.9 = (bf16[64,2176]{1,0:T(8,128)(2,1)S(1)}, bf16[64,2176]{1,0:T(8,128)(2,1)S(1)}, u32[]{:S(2)}, u32[]{:S(2)}) collective-permute-start(bf16[64,2176]{1,0:T(8,128)(2,1)S(1)} %get-tuple-element.20.sent_ref), channel_id=1, source_target_pairs={{0,1},{1,0},{2,3},{3,2},{4,5},{5,4},{6,7},{7,6},{8,9},{9,8},{10,11... | collective-permute-start | bytes 835592 | tf_op jit(solution)/shard_map/ppermute | solution.py:365
  46.2 1.7 %collective-permute-done.7.refs_0_ = bf16[16,128]{1,0:T(8,128)(2,1)S(1)} collective-permute-done((bf16[16,128]{1,0:T(8,128)(2,1)S(1)}, bf16[16,128]{1,0:T(8,128)(2,1)S(1)}, u32[]{:S(2)}, u32[]{:S(2)}) %collective-permute-start.7) | collective-permute-done | bytes 4128 | tf_op jit(solution)/shard_map/ppermute | solution.py:358
  47.9 2.0 %collective-permute-start.8 = (bf16[64,2176]{1,0:T(8,128)(2,1)S(1)}, bf16[64,2176]{1,0:T(8,128)(2,1)S(1)}, u32[]{:S(2)}, u32[]{:S(2)}) collective-permute-start(bf16[64,2176]{1,0:T(8,128)(2,1)S(1)} %merge.1.refs_0_.refs_7_), channel_id=1, source_target_pairs={{0,4},{1,5},{2,6},{3,7},{4,0},{5,1},{6,2},{7,3},{8,12},{9,13},{10,... | collective-permute-start | bytes 835592 | tf_op jit(solution)/shard_map/ppermute | solution.py:363
  49.9 3.3 %collective-permute-done.10.refs_2_.refs_10_ = bf16[64,2176]{1,0:T(8,128)(2,1)S(1)} collective-permute-done((bf16[64,2176]{1,0:T(8,128)(2,1)S(1)}, bf16[64,2176]{1,0:T(8,128)(2,1)S(1)}, u32[]{:S(2)}, u32[]{:S(2)}) %collective-permute-start.10) | collective-permute-done | bytes 278560 | tf_op jit(solution)/shard_map/ppermute | solution.py:360
  53.3 0.5 collective-permute-start.11
  53.8 0.0 collective-permute-done.9.refs_1_
  53.8 6.6 %collective-permute-done.8.refs_0_ = bf16[64,2176]{1,0:T(8,128)(2,1)S(1)} collective-permute-done((bf16[64,2176]{1,0:T(8,128)(2,1)S(1)}, bf16[64,2176]{1,0:T(8,128)(2,1)S(1)}, u32[]{:S(2)}, u32[]{:S(2)}) %collective-permute-start.8) | collective-permute-done | bytes 278560 | tf_op jit(solution)/shard_map/ppermute | solution.py:363
  60.4 0.0 collective-permute-done.11.refs_2_.refs_3_.refs_11_
  60.4 0.0 collective-permute-start.12
  60.4 0.5 collective-permute-start.14
  61.0 6.0 %collective-permute-done.12.refs_6_.refs_9_ = bf16[64,2176]{1,0:T(8,128)(2,1)S(1)} collective-permute-done((bf16[64,2176]{1,0:T(8,128)(2,1)S(1)}, bf16[64,2176]{1,0:T(8,128)(2,1)S(1)}, u32[]{:S(2)}, u32[]{:S(2)}) %collective-permute-start.12) | collective-permute-done | bytes 278560 | tf_op jit(solution)/shard_map/ppermute | solution.py:369
  67.0 0.5 collective-permute-start.13
  67.5 0.4 collective-permute-done.14.refs_5_
  67.9 4.7 %finish.2 = (bf16[64,16384]{1,0:T(8,128)(2,1)}, f32[64,128]{1,0:T(8,128)S(1)}) custom-call(bf16[64,2176]{1,0:T(8,128)(2,1)S(1)} %merge.1.refs_0_.refs_7_, bf16[64,2176]{1,0:T(8,128)(2,1)S(1)} %collective-permute-done.9.refs_1_, bf16[64,2176]{1,0:T(8,128)(2,1)S(1)} %collective-permute-done.10.refs_2_.refs_10_, ...), custom_call_target="tpu_custom_call" | custom-call | flops 939524096 | bytes 3670016 | tf_op jit(solution)/shard_map/finish/pallas_call | solution.py:285
  72.6 0.9 %collective-permute-done.13.refs_0_ = bf16[64,2176]{1,0:T(8,128)(2,1)S(1)} collective-permute-done((bf16[64,2176]{1,0:T(8,128)(2,1)S(1)}, bf16[64,2176]{1,0:T(8,128)(2,1)S(1)}, u32[]{:S(2)}, u32[]{:S(2)}) %collective-permute-start.13) | collective-permute-done | bytes 278560 | tf_op jit(solution)/shard_map/ppermute | solution.py:373
  73.5 1.6 %finish.3 = bf16[64,16384]{1,0:T(8,128)(2,1)} custom-call(bf16[64,2176]{1,0:T(8,128)(2,1)S(1)} %collective-permute-done.13.refs_0_, f32[64,128]{1,0:T(8,128)S(1)} %get-tuple-element.22.refs_1_, bf16[64,16384]{1,0:T(8,128)(2,1)} %get-tuple-element.23.refs_2_), custom_call_target="tpu_custom_call", output_to_operand_aliasing={{}: (2, {})} | custom-call | flops 134217728 | bytes 524288 | tf_op jit(solution)/shard_map/finish/pallas_call | solution.py:285
  (6 shorter events, 0.1 us)
Async XLA Ops:
  0.6 0.9 %copy-start = (bf16[64,1024]{1,0:T(8,128)(2,1)S(1)}, bf16[64,1024]{1,0:T(8,128)(2,1)}, u32[]{:S(2)}) copy-start(bf16[64,1024]{1,0:T(8,128)(2,1)} %rows_ref.7) | copy-start | bytes 393220
  5.0 11.1 %collective-permute-start = (bf16[64,2048]{1,0:T(8,128)(2,1)S(1)}, bf16[64,2048]{1,0:T(8,128)(2,1)S(1)}, u32[]{:S(2)}, u32[]{:S(2)}) collective-permute-start(bf16[64,2048]{1,0:T(8,128)(2,1)S(1)} %products.4.refs_0_), channel_id=1, source_target_pairs={{0,1},{1,0},{2,3},{3,2},{4,5},{5,4},{6,7},{7,6},{8,9},{9,8},{10,11... | collective-permute-start | bytes 786440 | tf_op jit(solution)/shard_map/ppermute | solution.py:334
  16.0 11.8 %collective-permute-start.1 = (bf16[64,2048]{1,0:T(8,128)(2,1)S(1)}, bf16[64,2048]{1,0:T(8,128)(2,1)S(1)}, u32[]{:S(2)}, u32[]{:S(2)}) collective-permute-start(bf16[64,2048]{1,0:T(8,128)(2,1)S(1)} %get-tuple-element.15), channel_id=1, source_target_pairs={{0,1},{1,0},{2,3},{3,2},{4,5},{5,4},{6,7},{7,6},{8,9},{9,8},{10,11... | collective-permute-start | bytes 786440 | tf_op jit(solution)/shard_map/ppermute | solution.py:334
  16.2 11.6 %collective-permute-start.2 = (bf16[64,2048]{1,0:T(8,128)(2,1)S(1)}, bf16[64,2048]{1,0:T(8,128)(2,1)S(1)}, u32[]{:S(2)}, u32[]{:S(2)}) collective-permute-start(bf16[64,2048]{1,0:T(8,128)(2,1)S(1)} %add_convert_fusion.2.refs_0_), channel_id=1, source_target_pairs={{0,2},{1,3},{2,0},{3,1},{4,6},{5,7},{6,4},{7,5},{8,10},{9,11},{10,... | collective-permute-start | bytes 786440 | tf_op jit(solution)/shard_map/ppermute | solution.py:352
  18.3 12.3 %collective-permute-start.5 = (bf16[64,2048]{1,0:T(8,128)(2,1)S(1)}, bf16[64,2048]{1,0:T(8,128)(2,1)S(1)}, u32[]{:S(2)}, u32[]{:S(2)}) collective-permute-start(bf16[64,2048]{1,0:T(8,128)(2,1)S(1)} %get-tuple-element.17), channel_id=1, source_target_pairs={{0,1},{1,0},{2,3},{3,2},{4,5},{5,4},{6,7},{7,6},{8,9},{9,8},{10,11... | collective-permute-start | bytes 786440 | tf_op jit(solution)/shard_map/ppermute | solution.py:334
  27.9 13.5 %collective-permute-start.4 = (bf16[64,2048]{1,0:T(8,128)(2,1)S(1)}, bf16[64,2048]{1,0:T(8,128)(2,1)S(1)}, u32[]{:S(2)}, u32[]{:S(2)}) collective-permute-start(bf16[64,2048]{1,0:T(8,128)(2,1)S(1)} %add_convert_fusion.1.refs_1_), channel_id=1, source_target_pairs={{0,4},{1,5},{2,6},{3,7},{4,0},{5,1},{6,2},{7,3},{8,12},{9,13},{10,... | collective-permute-start | bytes 786440 | tf_op jit(solution)/shard_map/ppermute | solution.py:352
  30.6 12.2 %collective-permute-start.6 = (bf16[64,2048]{1,0:T(8,128)(2,1)S(1)}, bf16[64,2048]{1,0:T(8,128)(2,1)S(1)}, u32[]{:S(2)}, u32[]{:S(2)}) collective-permute-start(bf16[64,2048]{1,0:T(8,128)(2,1)S(1)} %add_convert_fusion.refs_0_), channel_id=1, source_target_pairs={{0,2},{1,3},{2,0},{3,1},{4,6},{5,7},{6,4},{7,5},{8,10},{9,11},{10,... | collective-permute-start | bytes 786440 | tf_op jit(solution)/shard_map/ppermute | solution.py:352
  31.2 11.7 %collective-permute-start.3 = (bf16[64,2048]{1,0:T(8,128)(2,1)S(1)}, bf16[64,2048]{1,0:T(8,128)(2,1)S(1)}, u32[]{:S(2)}, u32[]{:S(2)}) collective-permute-start(bf16[64,2048]{1,0:T(8,128)(2,1)S(1)} %unchanged.3.refs_1_), channel_id=1, source_target_pairs={{0,1},{1,0},{2,3},{3,2},{4,5},{5,4},{6,7},{7,6},{8,9},{9,8},{10,11... | collective-permute-start | bytes 786440 | tf_op jit(solution)/shard_map/ppermute | solution.py:350
  35.3 7.5 %copy-start.1 = (bf16[64,2048]{1,0:T(8,128)(2,1)S(1)}, bf16[64,2048]{1,0:T(8,128)(2,1)}, u32[]{:S(2)}) copy-start(bf16[64,2048]{1,0:T(8,128)(2,1)} %residual_ref.1) | copy-start | bytes 786436
  35.3 7.5 %copy-start.2 = (bf16[2048]{0:T(1024)(128)(2,1)S(1)}, bf16[2048]{0:T(1024)(128)(2,1)}, u32[]{:S(2)}) copy-start(bf16[2048]{0:T(1024)(128)(2,1)} %param.8) | copy-start | bytes 12292
  35.4 7.5 %copy-start.3 = (bf16[2048]{0:T(1024)(128)(2,1)S(1)}, bf16[2048]{0:T(1024)(128)(2,1)}, u32[]{:S(2)}) copy-start(bf16[2048]{0:T(1024)(128)(2,1)} %param.9) | copy-start | bytes 12292
  43.9 9.4 %collective-permute-start.10 = (bf16[64,2176]{1,0:T(8,128)(2,1)S(1)}, bf16[64,2176]{1,0:T(8,128)(2,1)S(1)}, u32[]{:S(2)}, u32[]{:S(2)}) collective-permute-start(bf16[64,2176]{1,0:T(8,128)(2,1)S(1)} %get-tuple-element.20.sent_ref), channel_id=1, source_target_pairs={{0,2},{1,3},{2,0},{3,1},{4,6},{5,7},{6,4},{7,5},{8,10},{9,11},{10,... | collective-permute-start | bytes 835592 | tf_op jit(solution)/shard_map/ppermute | solution.py:360
  44.2 3.7 %collective-permute-start.7 = (bf16[16,128]{1,0:T(8,128)(2,1)S(1)}, bf16[16,128]{1,0:T(8,128)(2,1)S(1)}, u32[]{:S(2)}, u32[]{:S(2)}) collective-permute-start(bf16[16,128]{1,0:T(8,128)(2,1)S(1)} %get-tuple-element.21), channel_id=1, source_target_pairs={{0,1},{1,0},{2,3},{3,2},{4,5},{5,4},{6,7},{7,6},{8,9},{9,8},{10,11... | collective-permute-start | bytes 12296 | tf_op jit(solution)/shard_map/ppermute | solution.py:358
  44.7 9.1 %collective-permute-start.9 = (bf16[64,2176]{1,0:T(8,128)(2,1)S(1)}, bf16[64,2176]{1,0:T(8,128)(2,1)S(1)}, u32[]{:S(2)}, u32[]{:S(2)}) collective-permute-start(bf16[64,2176]{1,0:T(8,128)(2,1)S(1)} %get-tuple-element.20.sent_ref), channel_id=1, source_target_pairs={{0,1},{1,0},{2,3},{3,2},{4,5},{5,4},{6,7},{7,6},{8,9},{9,8},{10,11... | collective-permute-start | bytes 835592 | tf_op jit(solution)/shard_map/ppermute | solution.py:365
  47.9 12.5 %collective-permute-start.8 = (bf16[64,2176]{1,0:T(8,128)(2,1)S(1)}, bf16[64,2176]{1,0:T(8,128)(2,1)S(1)}, u32[]{:S(2)}, u32[]{:S(2)}) collective-permute-start(bf16[64,2176]{1,0:T(8,128)(2,1)S(1)} %merge.1.refs_0_.refs_7_), channel_id=1, source_target_pairs={{0,4},{1,5},{2,6},{3,7},{4,0},{5,1},{6,2},{7,3},{8,12},{9,13},{10,... | collective-permute-start | bytes 835592 | tf_op jit(solution)/shard_map/ppermute | solution.py:363
  53.3 7.2 %collective-permute-start.11 = (bf16[64,2176]{1,0:T(8,128)(2,1)S(1)}, bf16[64,2176]{1,0:T(8,128)(2,1)S(1)}, u32[]{:S(2)}, u32[]{:S(2)}) collective-permute-start(bf16[64,2176]{1,0:T(8,128)(2,1)S(1)} %collective-permute-done.10.refs_2_.refs_10_), channel_id=1, source_target_pairs={{0,1},{1,0},{2,3},{3,2},{4,5},{5,4},{6,7},{7,6},{8,9},{9,8},{10,11... | collective-permute-start | bytes 835592 | tf_op jit(solution)/shard_map/ppermute | solution.py:365
  60.4 6.5 %collective-permute-start.12 = (bf16[64,2176]{1,0:T(8,128)(2,1)S(1)}, bf16[64,2176]{1,0:T(8,128)(2,1)S(1)}, u32[]{:S(2)}, u32[]{:S(2)}) collective-permute-start(bf16[64,2176]{1,0:T(8,128)(2,1)S(1)} %unchanged.5.refs_4_.refs_8_), channel_id=1, source_target_pairs={{0,2},{1,3},{2,0},{3,1},{4,6},{5,7},{6,4},{7,5},{8,10},{9,11},{10,... | collective-permute-start | bytes 835592 | tf_op jit(solution)/shard_map/ppermute | solution.py:369
  60.4 7.4 %collective-permute-start.14 = (bf16[64,2176]{1,0:T(8,128)(2,1)S(1)}, bf16[64,2176]{1,0:T(8,128)(2,1)S(1)}, u32[]{:S(2)}, u32[]{:S(2)}) collective-permute-start(bf16[64,2176]{1,0:T(8,128)(2,1)S(1)} %unchanged.5.refs_4_.refs_8_), channel_id=1, source_target_pairs={{0,1},{1,0},{2,3},{3,2},{4,5},{5,4},{6,7},{7,6},{8,9},{9,8},{10,11... | collective-permute-start | bytes 835592 | tf_op jit(solution)/shard_map/ppermute | solution.py:373
  67.0 6.5 %collective-permute-start.13 = (bf16[64,2176]{1,0:T(8,128)(2,1)S(1)}, bf16[64,2176]{1,0:T(8,128)(2,1)S(1)}, u32[]{:S(2)}, u32[]{:S(2)}) collective-permute-start(bf16[64,2176]{1,0:T(8,128)(2,1)S(1)} %collective-permute-done.12.refs_6_.refs_9_), channel_id=1, source_target_pairs={{0,1},{1,0},{2,3},{3,2},{4,5},{5,4},{6,7},{7,6},{8,9},{9,8},{10,11... | collective-permute-start | bytes 835592 | tf_op jit(solution)/shard_map/ppermute | solution.py:373

commit v12 on v7

--- a/solution.py
+++ b/solution.py
@@ -66,7 +66,7 @@
 
 def products(attended, weight, targets, splits, local, after):
     rows, depth = attended.shape
-    tile = tile_width(local, 512)
+    tile = tile_width(local, 1024 if len(targets) > 1 else 512)
     slots = len(targets) * (local // tile)
     vmem = pl.BlockSpec(memory_space=pltpu.VMEM)
     return pl.pallas_call(

time: 71.2 us -> 71.3 us (level)
  starting transfers between devices: 20.7 us -> 19.7 us
  waiting for transfers between devices: 25.5 us -> 26.3 us
  transfers between devices with their start and end apart: 15 -> 15, of which waited for: 9 -> 9; matrix products, arithmetic and copies ran while one was open for 0% -> 0% of each run, Pallas kernels for 25% -> 26%
where the time goes in v12:
time: 71.3 us; the launch traced here: 71.2 us
  waiting for transfers between devices  26.3 us (37%)
  Pallas kernels  23.2 us (33%)
  starting transfers between devices  19.7 us (28%)
  local copies, waits for them, and re-layouts  0.92 us (1%)
  between operations  0.76 us (1%)
    pallas_call x4, Pallas kernels, products(): pl.pallas_call(functools.partial(product_kernel, targets, splits, local,...  16.1 us
    ppermute x1, waiting for transfers between devices, body(): have[top] = lax.ppermute(merged, 'tensor', jump[top])  7.44 us
    ppermute x3, waiting for transfers between devices, body(): joined_to = lax.ppermute(total, 'tensor', jump[bit])  7.34 us
    ppermute x3, starting transfers between devices, body(): joined_to = lax.ppermute(total, 'tensor', jump[bit])  6.19 us
    pallas_call x2, Pallas kernels, finish(): pl.pallas_call(functools.partial(finish_kernel, places, splits, counts, t...  6.11 us
    ppermute x1, waiting for transfers between devices, body(): have[k] = lax.ppermute(have[k ^ k & -k], 'tensor', jump[k & -k])  5.53 us
    ppermute x3, starting transfers between devices, body(): result = lax.ppermute(result, 'tensor', swap[j])  4.62 us
    ppermute x1, starting transfers between devices, body(): have[top] = lax.ppermute(merged, 'tensor', jump[top])  3.41 us
  transfers between devices with their start and end apart: 15, of which 9 were waited for; matrix products, arithmetic and copies ran while one was open for 0% of the time, Pallas kernels for 26%

profile of v12, /device:TPU:0, one launch (start us, length us, event | category | flops | bytes accessed | tf_op | source)
XLA Modules:
  0.0 71.2 jit_solution(17308789421062679087)
XLA Ops:
  0.6 0.0 copy-start
  0.6 0.9 %copy-done = bf16[64,1024]{1,0:T(8,128)(2,1)S(1)} copy-done((bf16[64,1024]{1,0:T(8,128)(2,1)S(1)}, bf16[64,1024]{1,0:T(8,128)(2,1)}, u32[]{:S(2)}) %copy-start) | copy-done | bytes 131096
  1.5 2.7 %products.4.refs_0_ = bf16[64,2048]{1,0:T(8,128)(2,1)S(1)} custom-call(bf16[64,1024]{1,0:T(8,128)(2,1)S(1)} %copy-done, bf16[1024,16384]{1,0:T(8,128)(2,1)} %weight_ref.7), custom_call_target="tpu_custom_call" | custom-call | flops 268435456 | bytes 4194304 | tf_op jit(solution)/shard_map/products/pallas_call | solution.py:72
  4.2 3.0 %collective-permute-start = (bf16[64,2048]{1,0:T(8,128)(2,1)S(1)}, bf16[64,2048]{1,0:T(8,128)(2,1)S(1)}, u32[]{:S(2)}, u32[]{:S(2)}) collective-permute-start(bf16[64,2048]{1,0:T(8,128)(2,1)S(1)} %products.4.refs_0_), channel_id=1, source_target_pairs={{0,1},{1,0},{2,3},{3,2},{4,5},{5,4},{6,7},{7,6},{8,9},{9,8},{10,11... | collective-permute-start | bytes 786440 | tf_op jit(solution)/shard_map/ppermute | solution.py:325
  7.2 5.4 %products.5 = (bf16[64,2048]{1,0:T(8,128)(2,1)S(1)}, bf16[64,2048]{1,0:T(8,128)(2,1)S(1)}, f32[64,2048]{1,0:T(8,128)S(1)}) custom-call(bf16[64,1024]{1,0:T(8,128)(2,1)S(1)} %copy-done, bf16[1024,16384]{1,0:T(8,128)(2,1)} %weight_ref.7, bf16[64,2048]{1,0:T(8,128)(2,1)S(1)} %products.4.refs_0_), custom_call_target="tpu_custom_call" | custom-call | flops 805306368 | bytes 12582912 | tf_op jit(solution)/shard_map/products/pallas_call | solution.py:72
  12.6 0.1 collective-permute-start.1
  12.7 0.8 %collective-permute-done = bf16[64,2048]{1,0:T(8,128)(2,1)S(1)} collective-permute-done((bf16[64,2048]{1,0:T(8,128)(2,1)S(1)}, bf16[64,2048]{1,0:T(8,128)(2,1)S(1)}, u32[]{:S(2)}, u32[]{:S(2)}) %collective-permute-start) | collective-permute-done | bytes 262176 | tf_op jit(solution)/shard_map/ppermute | solution.py:325
  13.6 1.9 %collective-permute-start.2 = (bf16[64,2048]{1,0:T(8,128)(2,1)S(1)}, bf16[64,2048]{1,0:T(8,128)(2,1)S(1)}, u32[]{:S(2)}, u32[]{:S(2)}) collective-permute-start(bf16[64,2048]{1,0:T(8,128)(2,1)S(1)} %add_convert_fusion.2.refs_0_), channel_id=1, source_target_pairs={{0,2},{1,3},{2,0},{3,1},{4,6},{5,7},{6,4},{7,5},{8,10},{9,11},{10,... | collective-permute-start | bytes 786440 | tf_op jit(solution)/shard_map/ppermute | solution.py:343
  15.5 1.5 %collective-permute-start.5 = (bf16[64,2048]{1,0:T(8,128)(2,1)S(1)}, bf16[64,2048]{1,0:T(8,128)(2,1)S(1)}, u32[]{:S(2)}, u32[]{:S(2)}) collective-permute-start(bf16[64,2048]{1,0:T(8,128)(2,1)S(1)} %get-tuple-element.17), channel_id=1, source_target_pairs={{0,1},{1,0},{2,3},{3,2},{4,5},{5,4},{6,7},{7,6},{8,9},{9,8},{10,11... | collective-permute-start | bytes 786440 | tf_op jit(solution)/shard_map/ppermute | solution.py:325
  17.0 5.4 %products.6 = (bf16[64,2048]{1,0:T(8,128)(2,1)S(1)}, f32[64,2048]{1,0:T(8,128)S(1)}, f32[64,2048]{1,0:T(8,128)S(1)}) custom-call(bf16[64,1024]{1,0:T(8,128)(2,1)S(1)} %copy-done, bf16[1024,16384]{1,0:T(8,128)(2,1)} %weight_ref.7, bf16[64,2048]{1,0:T(8,128)(2,1)S(1)} %add_convert_fusion.2.refs_0_), custom_call_target="tpu_custom_call" | custom-call | flops 805306368 | bytes 12582912 | tf_op jit(solution)/shard_map/products/pallas_call | solution.py:72
  22.3 0.0 collective-permute-done.1
  22.4 0.0 collective-permute-done.2
  22.4 0.1 add_convert_fusion.1.refs_1_
  22.5 2.7 %collective-permute-start.4 = (bf16[64,2048]{1,0:T(8,128)(2,1)S(1)}, bf16[64,2048]{1,0:T(8,128)(2,1)S(1)}, u32[]{:S(2)}, u32[]{:S(2)}) collective-permute-start(bf16[64,2048]{1,0:T(8,128)(2,1)S(1)} %add_convert_fusion.1.refs_1_), channel_id=1, source_target_pairs={{0,4},{1,5},{2,6},{3,7},{4,0},{5,1},{6,2},{7,3},{8,12},{9,13},{10,... | collective-permute-start | bytes 786440 | tf_op jit(solution)/shard_map/ppermute | solution.py:343
  25.1 0.9 %collective-permute-done.5 = bf16[64,2048]{1,0:T(8,128)(2,1)S(1)} collective-permute-done((bf16[64,2048]{1,0:T(8,128)(2,1)S(1)}, bf16[64,2048]{1,0:T(8,128)(2,1)S(1)}, u32[]{:S(2)}, u32[]{:S(2)}) %collective-permute-start.5) | collective-permute-done | bytes 262176 | tf_op jit(solution)/shard_map/ppermute | solution.py:325
  26.1 1.6 %collective-permute-start.6 = (bf16[64,2048]{1,0:T(8,128)(2,1)S(1)}, bf16[64,2048]{1,0:T(8,128)(2,1)S(1)}, u32[]{:S(2)}, u32[]{:S(2)}) collective-permute-start(bf16[64,2048]{1,0:T(8,128)(2,1)S(1)} %add_convert_fusion.refs_0_), channel_id=1, source_target_pairs={{0,2},{1,3},{2,0},{3,1},{4,6},{5,7},{6,4},{7,5},{8,10},{9,11},{10,... | collective-permute-start | bytes 786440 | tf_op jit(solution)/shard_map/ppermute | solution.py:343
  27.8 0.5 collective-permute-start.3
  28.3 2.7 %products.7.refs_3_ = f32[64,2048]{1,0:T(8,128)S(1)} custom-call(bf16[64,1024]{1,0:T(8,128)(2,1)S(1)} %copy-done, bf16[1024,16384]{1,0:T(8,128)(2,1)} %weight_ref.7, bf16[64,2048]{1,0:T(8,128)(2,1)S(1)} %add_convert_fusion.refs_0_, bf16[64,2048]{1,0:T(8,128)(2,1)S(1)} %unchanged.3.refs_1_), custom_call_target="tpu_custom_call" | custom-call | flops 268435456 | bytes 4194304 | tf_op jit(solution)/shard_map/products/pallas_call | solution.py:72
  31.0 0.0 copy-start.1
  31.0 0.0 copy-start.2
  31.0 0.0 copy-start.3
  31.0 4.6 %collective-permute-done.4.refs_0_ = bf16[64,2048]{1,0:T(8,128)(2,1)S(1)} collective-permute-done((bf16[64,2048]{1,0:T(8,128)(2,1)S(1)}, bf16[64,2048]{1,0:T(8,128)(2,1)S(1)}, u32[]{:S(2)}, u32[]{:S(2)}) %collective-permute-start.4) | collective-permute-done | bytes 262176 | tf_op jit(solution)/shard_map/ppermute | solution.py:343
  35.6 2.7 %collective-permute-done.6.refs_2_ = bf16[64,2048]{1,0:T(8,128)(2,1)S(1)} collective-permute-done((bf16[64,2048]{1,0:T(8,128)(2,1)S(1)}, bf16[64,2048]{1,0:T(8,128)(2,1)S(1)}, u32[]{:S(2)}, u32[]{:S(2)}) %collective-permute-start.6) | collective-permute-done | bytes 262176 | tf_op jit(solution)/shard_map/ppermute | solution.py:343
  38.3 0.0 collective-permute-done.3.refs_0_
  38.3 0.0 copy-done.1
  38.4 0.0 copy-done.2
  38.4 0.0 copy-done.3
  38.4 1.0 %own_stream.1 = (bf16[64,2048]{1,0:T(8,128)(2,1)}, bf16[64,2176]{1,0:T(8,128)(2,1)S(1)}, bf16[16,128]{1,0:T(8,128)(2,1)S(1)}) custom-call(bf16[64,2048]{1,0:T(8,128)(2,1)S(1)} %copy-done.1, bf16[16,128]{1,0:T(8,128)(2,1)S(1)} %bitcast.2, bf16[16,128]{1,0:T(8,128)(2,1)S(1)} %bitcast.3, bf16[64,2048]{1,0:T(8,128)(2,1)S(1)} %collective-permute-done.3.refs_0_, ...), custom_call_target="tpu_custom_call" | custom-call | flops 2621440 | bytes 2097152 | tf_op jit(solution)/shard_map/own_stream/pallas_call | solution.py:138
  39.4 0.0 collective-permute-start.10
  39.4 0.7 %collective-permute-start.7 = (bf16[16,128]{1,0:T(8,128)(2,1)S(1)}, bf16[16,128]{1,0:T(8,128)(2,1)S(1)}, u32[]{:S(2)}, u32[]{:S(2)}) collective-permute-start(bf16[16,128]{1,0:T(8,128)(2,1)S(1)} %get-tuple-element.21), channel_id=1, source_target_pairs={{0,1},{1,0},{2,3},{3,2},{4,5},{5,4},{6,7},{7,6},{8,9},{9,8},{10,11... | collective-permute-start | bytes 12296 | tf_op jit(solution)/shard_map/ppermute | solution.py:349
  40.1 1.3 %collective-permute-start.9 = (bf16[64,2176]{1,0:T(8,128)(2,1)S(1)}, bf16[64,2176]{1,0:T(8,128)(2,1)S(1)}, u32[]{:S(2)}, u32[]{:S(2)}) collective-permute-start(bf16[64,2176]{1,0:T(8,128)(2,1)S(1)} %get-tuple-element.20.sent_ref), channel_id=1, source_target_pairs={{0,1},{1,0},{2,3},{3,2},{4,5},{5,4},{6,7},{7,6},{8,9},{9,8},{10,11... | collective-permute-start | bytes 835592 | tf_op jit(solution)/shard_map/ppermute | solution.py:356
  41.4 1.7 %collective-permute-done.7.refs_0_ = bf16[16,128]{1,0:T(8,128)(2,1)S(1)} collective-permute-done((bf16[16,128]{1,0:T(8,128)(2,1)S(1)}, bf16[16,128]{1,0:T(8,128)(2,1)S(1)}, u32[]{:S(2)}, u32[]{:S(2)}) %collective-permute-start.7) | collective-permute-done | bytes 4128 | tf_op jit(solution)/shard_map/ppermute | solution.py:349
  43.1 3.4 %collective-permute-start.8 = (bf16[64,2176]{1,0:T(8,128)(2,1)S(1)}, bf16[64,2176]{1,0:T(8,128)(2,1)S(1)}, u32[]{:S(2)}, u32[]{:S(2)}) collective-permute-start(bf16[64,2176]{1,0:T(8,128)(2,1)S(1)} %merge.1.refs_0_.refs_7_), channel_id=1, source_target_pairs={{0,4},{1,5},{2,6},{3,7},{4,0},{5,1},{6,2},{7,3},{8,12},{9,13},{10,... | collective-permute-start | bytes 835592 | tf_op jit(solution)/shard_map/ppermute | solution.py:354
  46.5 1.7 %collective-permute-done.10.refs_2_.refs_10_ = bf16[64,2176]{1,0:T(8,128)(2,1)S(1)} collective-permute-done((bf16[64,2176]{1,0:T(8,128)(2,1)S(1)}, bf16[64,2176]{1,0:T(8,128)(2,1)S(1)}, u32[]{:S(2)}, u32[]{:S(2)}) %collective-permute-start.10) | collective-permute-done | bytes 278560 | tf_op jit(solution)/shard_map/ppermute | solution.py:351
  48.2 1.0 %collective-permute-start.11 = (bf16[64,2176]{1,0:T(8,128)(2,1)S(1)}, bf16[64,2176]{1,0:T(8,128)(2,1)S(1)}, u32[]{:S(2)}, u32[]{:S(2)}) collective-permute-start(bf16[64,2176]{1,0:T(8,128)(2,1)S(1)} %collective-permute-done.10.refs_2_.refs_10_), channel_id=1, source_target_pairs={{0,1},{1,0},{2,3},{3,2},{4,5},{5,4},{6,7},{7,6},{8,9},{9,8},{10,11... | collective-permute-start | bytes 835592 | tf_op jit(solution)/shard_map/ppermute | solution.py:356
  49.2 0.0 collective-permute-done.9.refs_1_
  49.2 7.4 %collective-permute-done.8.refs_0_ = bf16[64,2176]{1,0:T(8,128)(2,1)S(1)} collective-permute-done((bf16[64,2176]{1,0:T(8,128)(2,1)S(1)}, bf16[64,2176]{1,0:T(8,128)(2,1)S(1)}, u32[]{:S(2)}, u32[]{:S(2)}) %collective-permute-start.8) | collective-permute-done | bytes 278560 | tf_op jit(solution)/shard_map/ppermute | solution.py:354
  56.7 0.0 collective-permute-done.11.refs_2_.refs_3_.refs_11_
  56.7 0.0 collective-permute-start.12
  56.7 1.0 %collective-permute-start.14 = (bf16[64,2176]{1,0:T(8,128)(2,1)S(1)}, bf16[64,2176]{1,0:T(8,128)(2,1)S(1)}, u32[]{:S(2)}, u32[]{:S(2)}) collective-permute-start(bf16[64,2176]{1,0:T(8,128)(2,1)S(1)} %unchanged.5.refs_4_.refs_8_), channel_id=1, source_target_pairs={{0,1},{1,0},{2,3},{3,2},{4,5},{5,4},{6,7},{7,6},{8,9},{9,8},{10,11... | collective-permute-start | bytes 835592 | tf_op jit(solution)/shard_map/ppermute | solution.py:364
  57.7 5.5 %collective-permute-done.12.refs_6_.refs_9_ = bf16[64,2176]{1,0:T(8,128)(2,1)S(1)} collective-permute-done((bf16[64,2176]{1,0:T(8,128)(2,1)S(1)}, bf16[64,2176]{1,0:T(8,128)(2,1)S(1)}, u32[]{:S(2)}, u32[]{:S(2)}) %collective-permute-start.12) | collective-permute-done | bytes 278560 | tf_op jit(solution)/shard_map/ppermute | solution.py:360
  63.2 1.0 %collective-permute-start.13 = (bf16[64,2176]{1,0:T(8,128)(2,1)S(1)}, bf16[64,2176]{1,0:T(8,128)(2,1)S(1)}, u32[]{:S(2)}, u32[]{:S(2)}) collective-permute-start(bf16[64,2176]{1,0:T(8,128)(2,1)S(1)} %collective-permute-done.12.refs_6_.refs_9_), channel_id=1, source_target_pairs={{0,1},{1,0},{2,3},{3,2},{4,5},{5,4},{6,7},{7,6},{8,9},{9,8},{10,11... | collective-permute-start | bytes 835592 | tf_op jit(solution)/shard_map/ppermute | solution.py:364
  64.2 0.0 collective-permute-done.14.refs_5_
  64.2 4.7 %finish.2 = (bf16[64,16384]{1,0:T(8,128)(2,1)}, f32[64,128]{1,0:T(8,128)S(1)}) custom-call(bf16[64,2176]{1,0:T(8,128)(2,1)S(1)} %merge.1.refs_0_.refs_7_, bf16[64,2176]{1,0:T(8,128)(2,1)S(1)} %collective-permute-done.9.refs_1_, bf16[64,2176]{1,0:T(8,128)(2,1)S(1)} %collective-permute-done.10.refs_2_.refs_10_, ...), custom_call_target="tpu_custom_call" | custom-call | flops 939524096 | bytes 3670016 | tf_op jit(solution)/shard_map/finish/pallas_call | solution.py:276
  68.9 0.9 %collective-permute-done.13.refs_0_ = bf16[64,2176]{1,0:T(8,128)(2,1)S(1)} collective-permute-done((bf16[64,2176]{1,0:T(8,128)(2,1)S(1)}, bf16[64,2176]{1,0:T(8,128)(2,1)S(1)}, u32[]{:S(2)}, u32[]{:S(2)}) %collective-permute-start.13) | collective-permute-done | bytes 278560 | tf_op jit(solution)/shard_map/ppermute | solution.py:364
  69.8 1.4 %finish.3 = bf16[64,16384]{1,0:T(8,128)(2,1)} custom-call(bf16[64,2176]{1,0:T(8,128)(2,1)S(1)} %collective-permute-done.13.refs_0_, f32[64,128]{1,0:T(8,128)S(1)} %get-tuple-element.22.refs_1_, bf16[64,16384]{1,0:T(8,128)(2,1)} %get-tuple-element.23.refs_2_), custom_call_target="tpu_custom_call", output_to_operand_aliasing={{}: (2, {})} | custom-call | flops 134217728 | bytes 524288 | tf_op jit(solution)/shard_map/finish/pallas_call | solution.py:276
  (6 shorter events, 0.1 us)
Async XLA Ops:
  0.6 0.9 %copy-start = (bf16[64,1024]{1,0:T(8,128)(2,1)S(1)}, bf16[64,1024]{1,0:T(8,128)(2,1)}, u32[]{:S(2)}) copy-start(bf16[64,1024]{1,0:T(8,128)(2,1)} %rows_ref.7) | copy-start | bytes 393220
  4.2 9.3 %collective-permute-start = (bf16[64,2048]{1,0:T(8,128)(2,1)S(1)}, bf16[64,2048]{1,0:T(8,128)(2,1)S(1)}, u32[]{:S(2)}, u32[]{:S(2)}) collective-permute-start(bf16[64,2048]{1,0:T(8,128)(2,1)S(1)} %products.4.refs_0_), channel_id=1, source_target_pairs={{0,1},{1,0},{2,3},{3,2},{4,5},{5,4},{6,7},{7,6},{8,9},{9,8},{10,11... | collective-permute-start | bytes 786440 | tf_op jit(solution)/shard_map/ppermute | solution.py:325
  12.6 9.7 %collective-permute-start.1 = (bf16[64,2048]{1,0:T(8,128)(2,1)S(1)}, bf16[64,2048]{1,0:T(8,128)(2,1)S(1)}, u32[]{:S(2)}, u32[]{:S(2)}) collective-permute-start(bf16[64,2048]{1,0:T(8,128)(2,1)S(1)} %get-tuple-element.15), channel_id=1, source_target_pairs={{0,1},{1,0},{2,3},{3,2},{4,5},{5,4},{6,7},{7,6},{8,9},{9,8},{10,11... | collective-permute-start | bytes 786440 | tf_op jit(solution)/shard_map/ppermute | solution.py:325
  13.6 8.8 %collective-permute-start.2 = (bf16[64,2048]{1,0:T(8,128)(2,1)S(1)}, bf16[64,2048]{1,0:T(8,128)(2,1)S(1)}, u32[]{:S(2)}, u32[]{:S(2)}) collective-permute-start(bf16[64,2048]{1,0:T(8,128)(2,1)S(1)} %add_convert_fusion.2.refs_0_), channel_id=1, source_target_pairs={{0,2},{1,3},{2,0},{3,1},{4,6},{5,7},{6,4},{7,5},{8,10},{9,11},{10,... | collective-permute-start | bytes 786440 | tf_op jit(solution)/shard_map/ppermute | solution.py:343
  15.5 10.6 %collective-permute-start.5 = (bf16[64,2048]{1,0:T(8,128)(2,1)S(1)}, bf16[64,2048]{1,0:T(8,128)(2,1)S(1)}, u32[]{:S(2)}, u32[]{:S(2)}) collective-permute-start(bf16[64,2048]{1,0:T(8,128)(2,1)S(1)} %get-tuple-element.17), channel_id=1, source_target_pairs={{0,1},{1,0},{2,3},{3,2},{4,5},{5,4},{6,7},{7,6},{8,9},{9,8},{10,11... | collective-permute-start | bytes 786440 | tf_op jit(solution)/shard_map/ppermute | solution.py:325
  22.5 13.2 %collective-permute-start.4 = (bf16[64,2048]{1,0:T(8,128)(2,1)S(1)}, bf16[64,2048]{1,0:T(8,128)(2,1)S(1)}, u32[]{:S(2)}, u32[]{:S(2)}) collective-permute-start(bf16[64,2048]{1,0:T(8,128)(2,1)S(1)} %add_convert_fusion.1.refs_1_), channel_id=1, source_target_pairs={{0,4},{1,5},{2,6},{3,7},{4,0},{5,1},{6,2},{7,3},{8,12},{9,13},{10,... | collective-permute-start | bytes 786440 | tf_op jit(solution)/shard_map/ppermute | solution.py:343
  26.1 12.2 %collective-permute-start.6 = (bf16[64,2048]{1,0:T(8,128)(2,1)S(1)}, bf16[64,2048]{1,0:T(8,128)(2,1)S(1)}, u32[]{:S(2)}, u32[]{:S(2)}) collective-permute-start(bf16[64,2048]{1,0:T(8,128)(2,1)S(1)} %add_convert_fusion.refs_0_), channel_id=1, source_target_pairs={{0,2},{1,3},{2,0},{3,1},{4,6},{5,7},{6,4},{7,5},{8,10},{9,11},{10,... | collective-permute-start | bytes 786440 | tf_op jit(solution)/shard_map/ppermute | solution.py:343
  27.8 10.6 %collective-permute-start.3 = (bf16[64,2048]{1,0:T(8,128)(2,1)S(1)}, bf16[64,2048]{1,0:T(8,128)(2,1)S(1)}, u32[]{:S(2)}, u32[]{:S(2)}) collective-permute-start(bf16[64,2048]{1,0:T(8,128)(2,1)S(1)} %unchanged.3.refs_1_), channel_id=1, source_target_pairs={{0,1},{1,0},{2,3},{3,2},{4,5},{5,4},{6,7},{7,6},{8,9},{9,8},{10,11... | collective-permute-start | bytes 786440 | tf_op jit(solution)/shard_map/ppermute | solution.py:341
  31.0 7.4 %copy-start.1 = (bf16[64,2048]{1,0:T(8,128)(2,1)S(1)}, bf16[64,2048]{1,0:T(8,128)(2,1)}, u32[]{:S(2)}) copy-start(bf16[64,2048]{1,0:T(8,128)(2,1)} %residual_ref.1) | copy-start | bytes 786436
  31.0 7.4 %copy-start.2 = (bf16[2048]{0:T(1024)(128)(2,1)S(1)}, bf16[2048]{0:T(1024)(128)(2,1)}, u32[]{:S(2)}) copy-start(bf16[2048]{0:T(1024)(128)(2,1)} %param.8) | copy-start | bytes 12292
  31.0 7.4 %copy-start.3 = (bf16[2048]{0:T(1024)(128)(2,1)S(1)}, bf16[2048]{0:T(1024)(128)(2,1)}, u32[]{:S(2)}) copy-start(bf16[2048]{0:T(1024)(128)(2,1)} %param.9) | copy-start | bytes 12292
  39.4 8.9 %collective-permute-start.10 = (bf16[64,2176]{1,0:T(8,128)(2,1)S(1)}, bf16[64,2176]{1,0:T(8,128)(2,1)S(1)}, u32[]{:S(2)}, u32[]{:S(2)}) collective-permute-start(bf16[64,2176]{1,0:T(8,128)(2,1)S(1)} %get-tuple-element.20.sent_ref), channel_id=1, source_target_pairs={{0,2},{1,3},{2,0},{3,1},{4,6},{5,7},{6,4},{7,5},{8,10},{9,11},{10,... | collective-permute-start | bytes 835592 | tf_op jit(solution)/shard_map/ppermute | solution.py:351
  39.4 3.7 %collective-permute-start.7 = (bf16[16,128]{1,0:T(8,128)(2,1)S(1)}, bf16[16,128]{1,0:T(8,128)(2,1)S(1)}, u32[]{:S(2)}, u32[]{:S(2)}) collective-permute-start(bf16[16,128]{1,0:T(8,128)(2,1)S(1)} %get-tuple-element.21), channel_id=1, source_target_pairs={{0,1},{1,0},{2,3},{3,2},{4,5},{5,4},{6,7},{7,6},{8,9},{9,8},{10,11... | collective-permute-start | bytes 12296 | tf_op jit(solution)/shard_map/ppermute | solution.py:349
  40.1 9.1 %collective-permute-start.9 = (bf16[64,2176]{1,0:T(8,128)(2,1)S(1)}, bf16[64,2176]{1,0:T(8,128)(2,1)S(1)}, u32[]{:S(2)}, u32[]{:S(2)}) collective-permute-start(bf16[64,2176]{1,0:T(8,128)(2,1)S(1)} %get-tuple-element.20.sent_ref), channel_id=1, source_target_pairs={{0,1},{1,0},{2,3},{3,2},{4,5},{5,4},{6,7},{7,6},{8,9},{9,8},{10,11... | collective-permute-start | bytes 835592 | tf_op jit(solution)/shard_map/ppermute | solution.py:356
  43.1 13.5 %collective-permute-start.8 = (bf16[64,2176]{1,0:T(8,128)(2,1)S(1)}, bf16[64,2176]{1,0:T(8,128)(2,1)S(1)}, u32[]{:S(2)}, u32[]{:S(2)}) collective-permute-start(bf16[64,2176]{1,0:T(8,128)(2,1)S(1)} %merge.1.refs_0_.refs_7_), channel_id=1, source_target_pairs={{0,4},{1,5},{2,6},{3,7},{4,0},{5,1},{6,2},{7,3},{8,12},{9,13},{10,... | collective-permute-start | bytes 835592 | tf_op jit(solution)/shard_map/ppermute | solution.py:354
  48.2 8.4 %collective-permute-start.11 = (bf16[64,2176]{1,0:T(8,128)(2,1)S(1)}, bf16[64,2176]{1,0:T(8,128)(2,1)S(1)}, u32[]{:S(2)}, u32[]{:S(2)}) collective-permute-start(bf16[64,2176]{1,0:T(8,128)(2,1)S(1)} %collective-permute-done.10.refs_2_.refs_10_), channel_id=1, source_target_pairs={{0,1},{1,0},{2,3},{3,2},{4,5},{5,4},{6,7},{7,6},{8,9},{9,8},{10,11... | collective-permute-start | bytes 835592 | tf_op jit(solution)/shard_map/ppermute | solution.py:356
  56.7 6.5 %collective-permute-start.12 = (bf16[64,2176]{1,0:T(8,128)(2,1)S(1)}, bf16[64,2176]{1,0:T(8,128)(2,1)S(1)}, u32[]{:S(2)}, u32[]{:S(2)}) collective-permute-start(bf16[64,2176]{1,0:T(8,128)(2,1)S(1)} %unchanged.5.refs_4_.refs_8_), channel_id=1, source_target_pairs={{0,2},{1,3},{2,0},{3,1},{4,6},{5,7},{6,4},{7,5},{8,10},{9,11},{10,... | collective-permute-start | bytes 835592 | tf_op jit(solution)/shard_map/ppermute | solution.py:360
  56.7 7.5 %collective-permute-start.14 = (bf16[64,2176]{1,0:T(8,128)(2,1)S(1)}, bf16[64,2176]{1,0:T(8,128)(2,1)S(1)}, u32[]{:S(2)}, u32[]{:S(2)}) collective-permute-start(bf16[64,2176]{1,0:T(8,128)(2,1)S(1)} %unchanged.5.refs_4_.refs_8_), channel_id=1, source_target_pairs={{0,1},{1,0},{2,3},{3,2},{4,5},{5,4},{6,7},{7,6},{8,9},{9,8},{10,11... | collective-permute-start | bytes 835592 | tf_op jit(solution)/shard_map/ppermute | solution.py:364
  63.2 6.5 %collective-permute-start.13 = (bf16[64,2176]{1,0:T(8,128)(2,1)S(1)}, bf16[64,2176]{1,0:T(8,128)(2,1)S(1)}, u32[]{:S(2)}, u32[]{:S(2)}) collective-permute-start(bf16[64,2176]{1,0:T(8,128)(2,1)S(1)} %collective-permute-done.12.refs_6_.refs_9_), channel_id=1, source_target_pairs={{0,1},{1,0},{2,3},{3,2},{4,5},{5,4},{6,7},{7,6},{8,9},{9,8},{10,11... | collective-permute-start | bytes 835592 | tf_op jit(solution)/shard_map/ppermute | solution.py:364

commit v13 on v7

--- a/solution.py
+++ b/solution.py
@@ -354,7 +354,9 @@
     have[top] = lax.ppermute(merged, "tensor", jump[top])
     for k, j in away[0] + away[1]:
         crossed[k, j] = lax.ppermute(have[k] if k else sent, "tensor", swap[j])
-    have[top] = unchanged(have[top], *crossed.values())
+    have[top] = unchanged(have[top], have[1], *[crossed[p] for p in away[0]])
+    for p in away[1]:
+        crossed[p] = unchanged(unchanged(crossed[p]))
     for k in sorted(range(2, nz), key=lambda k: (k & (k - 1), k)):
         if k != top:
             have[k] = lax.ppermute(have[k ^ (k & -k)], "tensor", jump[k & -k])

time: 71.2 us -> 71.8 us (level)
  waiting for transfers between devices: 25.5 us -> 28.1 us
  starting transfers between devices: 20.7 us -> 18.8 us
    ppermute x1, waiting for transfers between devices: 1.71 us -> 7.64 us  [body(): have = {0: merged, 1: lax.ppermute(sent, 'tensor', jump[1])}]
    ppermute x1, waiting for transfers between devices: 7.08 us -> 2.24 us  [body(): have[top] = lax.ppermute(merged, 'tensor', jump[top])]
    ppermute x2, waiting for transfers between devices: 0.01 us -> 2.35 us  [body(): crossed[k, j] = lax.ppermute(have[k] if k else sent, 'tensor', swap[j])]
    ppermute x1, starting transfers between devices: 3.41 us -> 1.73 us  [body(): have[top] = lax.ppermute(merged, 'tensor', jump[top])]
    ppermute x1, waiting for transfers between devices: 5.24 us -> 4.07 us  [body(): have[k] = lax.ppermute(have[k ^ k & -k], 'tensor', jump[k & -k])]
  transfers between devices with their start and end apart: 15 -> 15, of which waited for: 9 -> 10; matrix products, arithmetic and copies ran while one was open for 0% -> 0% of each run, Pallas kernels for 25% -> 25%
where the time goes in v13:
time: 71.8 us; the launch traced here: 71.6 us
  waiting for transfers between devices  28.1 us (39%)
  Pallas kernels  23 us (32%)
  starting transfers between devices  18.8 us (26%)
  local copies, waits for them, and re-layouts  0.92 us (1%)
  between operations  0.76 us (1%)
    pallas_call x4, Pallas kernels, products(): pl.pallas_call(functools.partial(product_kernel, targets, splits, local,...  15.8 us
    ppermute x1, waiting for transfers between devices, body(): have = {0: merged, 1: lax.ppermute(sent, 'tensor', jump[1])}  7.64 us
    ppermute x3, waiting for transfers between devices, body(): joined_to = lax.ppermute(total, 'tensor', jump[bit])  7.29 us
    ppermute x3, starting transfers between devices, body(): joined_to = lax.ppermute(total, 'tensor', jump[bit])  6.19 us
    pallas_call x2, Pallas kernels, finish(): pl.pallas_call(functools.partial(finish_kernel, places, splits, counts, t...  6.11 us
    ppermute x3, starting transfers between devices, body(): result = lax.ppermute(result, 'tensor', swap[j])  4.62 us
    ppermute x1, waiting for transfers between devices, body(): have[k] = lax.ppermute(have[k ^ k & -k], 'tensor', jump[k & -k])  4.07 us
    ppermute x2, starting transfers between devices, body(): crossed[k, j] = lax.ppermute(have[k] if k else sent, 'tensor', swap[j])  2.59 us
  transfers between devices with their start and end apart: 15, of which 10 were waited for; matrix products, arithmetic and copies ran while one was open for 0% of the time, Pallas kernels for 25%

profile of v13, /device:TPU:0, one launch (start us, length us, event | category | flops | bytes accessed | tf_op | source)
XLA Modules:
  0.0 71.6 jit_solution(11693413710700289894)
XLA Ops:
  0.6 0.0 copy-start
  0.6 0.9 %copy-done = bf16[64,1024]{1,0:T(8,128)(2,1)S(1)} copy-done((bf16[64,1024]{1,0:T(8,128)(2,1)S(1)}, bf16[64,1024]{1,0:T(8,128)(2,1)}, u32[]{:S(2)}) %copy-start) | copy-done | bytes 131096
  1.5 2.7 %products.4.refs_0_ = bf16[64,2048]{1,0:T(8,128)(2,1)S(1)} custom-call(bf16[64,1024]{1,0:T(8,128)(2,1)S(1)} %copy-done, bf16[1024,16384]{1,0:T(8,128)(2,1)} %weight_ref.7), custom_call_target="tpu_custom_call" | custom-call | flops 268435456 | bytes 4194304 | tf_op jit(solution)/shard_map/products/pallas_call | solution.py:72
  4.2 3.0 %collective-permute-start = (bf16[64,2048]{1,0:T(8,128)(2,1)S(1)}, bf16[64,2048]{1,0:T(8,128)(2,1)S(1)}, u32[]{:S(2)}, u32[]{:S(2)}) collective-permute-start(bf16[64,2048]{1,0:T(8,128)(2,1)S(1)} %products.4.refs_0_), channel_id=1, source_target_pairs={{0,1},{1,0},{2,3},{3,2},{4,5},{5,4},{6,7},{7,6},{8,9},{9,8},{10,11... | collective-permute-start | bytes 786440 | tf_op jit(solution)/shard_map/ppermute | solution.py:325
  7.2 5.2 %products.5 = (bf16[64,2048]{1,0:T(8,128)(2,1)S(1)}, bf16[64,2048]{1,0:T(8,128)(2,1)S(1)}, f32[64,2048]{1,0:T(8,128)S(1)}) custom-call(bf16[64,1024]{1,0:T(8,128)(2,1)S(1)} %copy-done, bf16[1024,16384]{1,0:T(8,128)(2,1)} %weight_ref.7, bf16[64,2048]{1,0:T(8,128)(2,1)S(1)} %products.4.refs_0_), custom_call_target="tpu_custom_call" | custom-call | flops 805306368 | bytes 12582912 | tf_op jit(solution)/shard_map/products/pallas_call | solution.py:72
  12.5 0.1 collective-permute-start.1
  12.6 0.9 %collective-permute-done = bf16[64,2048]{1,0:T(8,128)(2,1)S(1)} collective-permute-done((bf16[64,2048]{1,0:T(8,128)(2,1)S(1)}, bf16[64,2048]{1,0:T(8,128)(2,1)S(1)}, u32[]{:S(2)}, u32[]{:S(2)}) %collective-permute-start) | collective-permute-done | bytes 262176 | tf_op jit(solution)/shard_map/ppermute | solution.py:325
  13.6 1.9 %collective-permute-start.2 = (bf16[64,2048]{1,0:T(8,128)(2,1)S(1)}, bf16[64,2048]{1,0:T(8,128)(2,1)S(1)}, u32[]{:S(2)}, u32[]{:S(2)}) collective-permute-start(bf16[64,2048]{1,0:T(8,128)(2,1)S(1)} %add_convert_fusion.2.refs_0_), channel_id=1, source_target_pairs={{0,2},{1,3},{2,0},{3,1},{4,6},{5,7},{6,4},{7,5},{8,10},{9,11},{10,... | collective-permute-start | bytes 786440 | tf_op jit(solution)/shard_map/ppermute | solution.py:343
  15.5 1.5 %collective-permute-start.5 = (bf16[64,2048]{1,0:T(8,128)(2,1)S(1)}, bf16[64,2048]{1,0:T(8,128)(2,1)S(1)}, u32[]{:S(2)}, u32[]{:S(2)}) collective-permute-start(bf16[64,2048]{1,0:T(8,128)(2,1)S(1)} %get-tuple-element.17), channel_id=1, source_target_pairs={{0,1},{1,0},{2,3},{3,2},{4,5},{5,4},{6,7},{7,6},{8,9},{9,8},{10,11... | collective-permute-start | bytes 786440 | tf_op jit(solution)/shard_map/ppermute | solution.py:325
  17.0 5.2 %products.6 = (bf16[64,2048]{1,0:T(8,128)(2,1)S(1)}, f32[64,2048]{1,0:T(8,128)S(1)}, f32[64,2048]{1,0:T(8,128)S(1)}) custom-call(bf16[64,1024]{1,0:T(8,128)(2,1)S(1)} %copy-done, bf16[1024,16384]{1,0:T(8,128)(2,1)} %weight_ref.7, bf16[64,2048]{1,0:T(8,128)(2,1)S(1)} %add_convert_fusion.2.refs_0_), custom_call_target="tpu_custom_call" | custom-call | flops 805306368 | bytes 12582912 | tf_op jit(solution)/shard_map/products/pallas_call | solution.py:72
  22.2 0.0 collective-permute-done.1
  22.2 0.0 collective-permute-done.2
  22.2 0.1 add_convert_fusion.1.refs_1_
  22.3 2.7 %collective-permute-start.4 = (bf16[64,2048]{1,0:T(8,128)(2,1)S(1)}, bf16[64,2048]{1,0:T(8,128)(2,1)S(1)}, u32[]{:S(2)}, u32[]{:S(2)}) collective-permute-start(bf16[64,2048]{1,0:T(8,128)(2,1)S(1)} %add_convert_fusion.1.refs_1_), channel_id=1, source_target_pairs={{0,4},{1,5},{2,6},{3,7},{4,0},{5,1},{6,2},{7,3},{8,12},{9,13},{10,... | collective-permute-start | bytes 786440 | tf_op jit(solution)/shard_map/ppermute | solution.py:343
  25.0 0.9 %collective-permute-done.5 = bf16[64,2048]{1,0:T(8,128)(2,1)S(1)} collective-permute-done((bf16[64,2048]{1,0:T(8,128)(2,1)S(1)}, bf16[64,2048]{1,0:T(8,128)(2,1)S(1)}, u32[]{:S(2)}, u32[]{:S(2)}) %collective-permute-start.5) | collective-permute-done | bytes 262176 | tf_op jit(solution)/shard_map/ppermute | solution.py:325
  26.0 1.6 %collective-permute-start.6 = (bf16[64,2048]{1,0:T(8,128)(2,1)S(1)}, bf16[64,2048]{1,0:T(8,128)(2,1)S(1)}, u32[]{:S(2)}, u32[]{:S(2)}) collective-permute-start(bf16[64,2048]{1,0:T(8,128)(2,1)S(1)} %add_convert_fusion.refs_0_), channel_id=1, source_target_pairs={{0,2},{1,3},{2,0},{3,1},{4,6},{5,7},{6,4},{7,5},{8,10},{9,11},{10,... | collective-permute-start | bytes 786440 | tf_op jit(solution)/shard_map/ppermute | solution.py:343
  27.6 0.6 collective-permute-start.3
  28.2 2.7 %products.7.refs_3_ = f32[64,2048]{1,0:T(8,128)S(1)} custom-call(bf16[64,1024]{1,0:T(8,128)(2,1)S(1)} %copy-done, bf16[1024,16384]{1,0:T(8,128)(2,1)} %weight_ref.7, bf16[64,2048]{1,0:T(8,128)(2,1)S(1)} %add_convert_fusion.refs_0_, bf16[64,2048]{1,0:T(8,128)(2,1)S(1)} %unchanged.5.refs_1_), custom_call_target="tpu_custom_call" | custom-call | flops 268435456 | bytes 4194304 | tf_op jit(solution)/shard_map/products/pallas_call | solution.py:72
  30.9 0.0 copy-start.1
  30.9 0.0 copy-start.2
  30.9 0.0 copy-start.3
  30.9 4.6 %collective-permute-done.4.refs_0_ = bf16[64,2048]{1,0:T(8,128)(2,1)S(1)} collective-permute-done((bf16[64,2048]{1,0:T(8,128)(2,1)S(1)}, bf16[64,2048]{1,0:T(8,128)(2,1)S(1)}, u32[]{:S(2)}, u32[]{:S(2)}) %collective-permute-start.4) | collective-permute-done | bytes 262176 | tf_op jit(solution)/shard_map/ppermute | solution.py:343
  35.5 2.7 %collective-permute-done.6.refs_2_ = bf16[64,2048]{1,0:T(8,128)(2,1)S(1)} collective-permute-done((bf16[64,2048]{1,0:T(8,128)(2,1)S(1)}, bf16[64,2048]{1,0:T(8,128)(2,1)S(1)}, u32[]{:S(2)}, u32[]{:S(2)}) %collective-permute-start.6) | collective-permute-done | bytes 262176 | tf_op jit(solution)/shard_map/ppermute | solution.py:343
  38.2 0.0 collective-permute-done.3.refs_0_
  38.2 0.0 copy-done.1
  38.2 0.0 copy-done.2
  38.2 0.0 copy-done.3
  38.2 1.0 %own_stream.1 = (bf16[64,2048]{1,0:T(8,128)(2,1)}, bf16[64,2176]{1,0:T(8,128)(2,1)S(1)}, bf16[16,128]{1,0:T(8,128)(2,1)S(1)}) custom-call(bf16[64,2048]{1,0:T(8,128)(2,1)S(1)} %copy-done.1, bf16[16,128]{1,0:T(8,128)(2,1)S(1)} %bitcast.2, bf16[16,128]{1,0:T(8,128)(2,1)S(1)} %bitcast.3, bf16[64,2048]{1,0:T(8,128)(2,1)S(1)} %collective-permute-done.3.refs_0_, ...), custom_call_target="tpu_custom_call" | custom-call | flops 2621440 | bytes 2097152 | tf_op jit(solution)/shard_map/own_stream/pallas_call | solution.py:138
  39.2 0.9 %collective-permute-start.7 = (bf16[16,128]{1,0:T(8,128)(2,1)S(1)}, bf16[16,128]{1,0:T(8,128)(2,1)S(1)}, u32[]{:S(2)}, u32[]{:S(2)}) collective-permute-start(bf16[16,128]{1,0:T(8,128)(2,1)S(1)} %get-tuple-element.21), channel_id=1, source_target_pairs={{0,1},{1,0},{2,3},{3,2},{4,5},{5,4},{6,7},{7,6},{8,9},{9,8},{10,11... | collective-permute-start | bytes 12296 | tf_op jit(solution)/shard_map/ppermute | solution.py:349
  40.1 1.1 %collective-permute-start.10 = (bf16[64,2176]{1,0:T(8,128)(2,1)S(1)}, bf16[64,2176]{1,0:T(8,128)(2,1)S(1)}, u32[]{:S(2)}, u32[]{:S(2)}) collective-permute-start(bf16[64,2176]{1,0:T(8,128)(2,1)S(1)} %get-tuple-element.20.sent_ref), channel_id=1, source_target_pairs={{0,1},{1,0},{2,3},{3,2},{4,5},{5,4},{6,7},{7,6},{8,9},{9,8},{10,11... | collective-permute-start | bytes 835592 | tf_op jit(solution)/shard_map/ppermute | solution.py:356
  41.2 0.0 collective-permute-start.9
  41.2 1.7 %collective-permute-done.7.refs_0_ = bf16[16,128]{1,0:T(8,128)(2,1)S(1)} collective-permute-done((bf16[16,128]{1,0:T(8,128)(2,1)S(1)}, bf16[16,128]{1,0:T(8,128)(2,1)S(1)}, u32[]{:S(2)}, u32[]{:S(2)}) %collective-permute-start.7) | collective-permute-done | bytes 4128 | tf_op jit(solution)/shard_map/ppermute | solution.py:349
  43.0 1.7 %collective-permute-start.8 = (bf16[64,2176]{1,0:T(8,128)(2,1)S(1)}, bf16[64,2176]{1,0:T(8,128)(2,1)S(1)}, u32[]{:S(2)}, u32[]{:S(2)}) collective-permute-start(bf16[64,2176]{1,0:T(8,128)(2,1)S(1)} %merge.1.refs_0_.refs_7_), channel_id=1, source_target_pairs={{0,4},{1,5},{2,6},{3,7},{4,0},{5,1},{6,2},{7,3},{8,12},{9,13},{10,... | collective-permute-start | bytes 835592 | tf_op jit(solution)/shard_map/ppermute | solution.py:354
  44.7 7.6 %collective-permute-done.9.refs_1_.refs_2_.refs_10_ = bf16[64,2176]{1,0:T(8,128)(2,1)S(1)} collective-permute-done((bf16[64,2176]{1,0:T(8,128)(2,1)S(1)}, bf16[64,2176]{1,0:T(8,128)(2,1)S(1)}, u32[]{:S(2)}, u32[]{:S(2)}) %collective-permute-start.9) | collective-permute-done | bytes 278560 | tf_op jit(solution)/shard_map/ppermute | solution.py:351
  52.3 1.4 %collective-permute-start.13 = (bf16[64,2176]{1,0:T(8,128)(2,1)S(1)}, bf16[64,2176]{1,0:T(8,128)(2,1)S(1)}, u32[]{:S(2)}, u32[]{:S(2)}) collective-permute-start(bf16[64,2176]{1,0:T(8,128)(2,1)S(1)} %collective-permute-done.9.refs_1_.refs_2_.refs_10_), channel_id=1, source_target_pairs={{0,1},{1,0},{2,3},{3,2},{4,5},{5,4},{6,7},{7,6},{8,9},{9,8},{10,11... | collective-permute-start | bytes 835592 | tf_op jit(solution)/shard_map/ppermute | solution.py:356
  53.8 0.0 collective-permute-done.10.refs_2_.refs_1_
  53.8 2.2 %collective-permute-done.8.refs_0_ = bf16[64,2176]{1,0:T(8,128)(2,1)S(1)} collective-permute-done((bf16[64,2176]{1,0:T(8,128)(2,1)S(1)}, bf16[64,2176]{1,0:T(8,128)(2,1)S(1)}, u32[]{:S(2)}, u32[]{:S(2)}) %collective-permute-start.8) | collective-permute-done | bytes 278560 | tf_op jit(solution)/shard_map/ppermute | solution.py:354
  56.0 1.1 %collective-permute-start.14 = (bf16[64,2176]{1,0:T(8,128)(2,1)S(1)}, bf16[64,2176]{1,0:T(8,128)(2,1)S(1)}, u32[]{:S(2)}, u32[]{:S(2)}) collective-permute-start(bf16[64,2176]{1,0:T(8,128)(2,1)S(1)} %unchanged.7.refs_4_.refs_8_), channel_id=1, source_target_pairs={{0,1},{1,0},{2,3},{3,2},{4,5},{5,4},{6,7},{7,6},{8,9},{9,8},{10,11... | collective-permute-start | bytes 835592 | tf_op jit(solution)/shard_map/ppermute | solution.py:366
  57.1 0.1 collective-permute-start.11
  57.3 2.3 %collective-permute-done.13.refs_0_ = bf16[64,2176]{1,0:T(8,128)(2,1)S(1)} collective-permute-done((bf16[64,2176]{1,0:T(8,128)(2,1)S(1)}, bf16[64,2176]{1,0:T(8,128)(2,1)S(1)}, u32[]{:S(2)}, u32[]{:S(2)}) %collective-permute-start.13) | collective-permute-done | bytes 278560 | tf_op jit(solution)/shard_map/ppermute | solution.py:356
  59.6 4.1 %collective-permute-done.11.refs_6_.refs_9_ = bf16[64,2176]{1,0:T(8,128)(2,1)S(1)} collective-permute-done((bf16[64,2176]{1,0:T(8,128)(2,1)S(1)}, bf16[64,2176]{1,0:T(8,128)(2,1)S(1)}, u32[]{:S(2)}, u32[]{:S(2)}) %collective-permute-start.11) | collective-permute-done | bytes 278560 | tf_op jit(solution)/shard_map/ppermute | solution.py:362
  63.7 0.9 %collective-permute-start.12 = (bf16[64,2176]{1,0:T(8,128)(2,1)S(1)}, bf16[64,2176]{1,0:T(8,128)(2,1)S(1)}, u32[]{:S(2)}, u32[]{:S(2)}) collective-permute-start(bf16[64,2176]{1,0:T(8,128)(2,1)S(1)} %collective-permute-done.11.refs_6_.refs_9_), channel_id=1, source_target_pairs={{0,1},{1,0},{2,3},{3,2},{4,5},{5,4},{6,7},{7,6},{8,9},{9,8},{10,11... | collective-permute-start | bytes 835592 | tf_op jit(solution)/shard_map/ppermute | solution.py:366
  64.6 0.0 collective-permute-done.14.refs_5_
  64.6 4.7 %finish.2 = (bf16[64,16384]{1,0:T(8,128)(2,1)}, f32[64,128]{1,0:T(8,128)S(1)}) custom-call(bf16[64,2176]{1,0:T(8,128)(2,1)S(1)} %merge.1.refs_0_.refs_7_, bf16[64,2176]{1,0:T(8,128)(2,1)S(1)} %collective-permute-done.10.refs_2_.refs_1_, bf16[64,2176]{1,0:T(8,128)(2,1)S(1)} %collective-permute-done.9.refs_1_.refs_2_.refs_10_, ...), custom_call_target="tpu_custom_call" | custom-call | flops 939524096 | bytes 3670016 | tf_op jit(solution)/shard_map/finish/pallas_call | solution.py:276
  69.3 0.9 %collective-permute-done.12.refs_0_ = bf16[64,2176]{1,0:T(8,128)(2,1)S(1)} collective-permute-done((bf16[64,2176]{1,0:T(8,128)(2,1)S(1)}, bf16[64,2176]{1,0:T(8,128)(2,1)S(1)}, u32[]{:S(2)}, u32[]{:S(2)}) %collective-permute-start.12) | collective-permute-done | bytes 278560 | tf_op jit(solution)/shard_map/ppermute | solution.py:366
  70.2 1.4 %finish.3 = bf16[64,16384]{1,0:T(8,128)(2,1)} custom-call(bf16[64,2176]{1,0:T(8,128)(2,1)S(1)} %collective-permute-done.12.refs_0_, f32[64,128]{1,0:T(8,128)S(1)} %get-tuple-element.22.refs_1_, bf16[64,16384]{1,0:T(8,128)(2,1)} %get-tuple-element.23.refs_2_), custom_call_target="tpu_custom_call", output_to_operand_aliasing={{}: (2, {})} | custom-call | flops 134217728 | bytes 524288 | tf_op jit(solution)/shard_map/finish/pallas_call | solution.py:276
  (8 shorter events, 0.1 us)
Async XLA Ops:
  0.6 0.9 %copy-start = (bf16[64,1024]{1,0:T(8,128)(2,1)S(1)}, bf16[64,1024]{1,0:T(8,128)(2,1)}, u32[]{:S(2)}) copy-start(bf16[64,1024]{1,0:T(8,128)(2,1)} %rows_ref.7) | copy-start | bytes 393220
  4.2 9.3 %collective-permute-start = (bf16[64,2048]{1,0:T(8,128)(2,1)S(1)}, bf16[64,2048]{1,0:T(8,128)(2,1)S(1)}, u32[]{:S(2)}, u32[]{:S(2)}) collective-permute-start(bf16[64,2048]{1,0:T(8,128)(2,1)S(1)} %products.4.refs_0_), channel_id=1, source_target_pairs={{0,1},{1,0},{2,3},{3,2},{4,5},{5,4},{6,7},{7,6},{8,9},{9,8},{10,11... | collective-permute-start | bytes 786440 | tf_op jit(solution)/shard_map/ppermute | solution.py:325
  12.5 9.7 %collective-permute-start.1 = (bf16[64,2048]{1,0:T(8,128)(2,1)S(1)}, bf16[64,2048]{1,0:T(8,128)(2,1)S(1)}, u32[]{:S(2)}, u32[]{:S(2)}) collective-permute-start(bf16[64,2048]{1,0:T(8,128)(2,1)S(1)} %get-tuple-element.15), channel_id=1, source_target_pairs={{0,1},{1,0},{2,3},{3,2},{4,5},{5,4},{6,7},{7,6},{8,9},{9,8},{10,11... | collective-permute-start | bytes 786440 | tf_op jit(solution)/shard_map/ppermute | solution.py:325
  13.6 8.6 %collective-permute-start.2 = (bf16[64,2048]{1,0:T(8,128)(2,1)S(1)}, bf16[64,2048]{1,0:T(8,128)(2,1)S(1)}, u32[]{:S(2)}, u32[]{:S(2)}) collective-permute-start(bf16[64,2048]{1,0:T(8,128)(2,1)S(1)} %add_convert_fusion.2.refs_0_), channel_id=1, source_target_pairs={{0,2},{1,3},{2,0},{3,1},{4,6},{5,7},{6,4},{7,5},{8,10},{9,11},{10,... | collective-permute-start | bytes 786440 | tf_op jit(solution)/shard_map/ppermute | solution.py:343
  15.5 10.4 %collective-permute-start.5 = (bf16[64,2048]{1,0:T(8,128)(2,1)S(1)}, bf16[64,2048]{1,0:T(8,128)(2,1)S(1)}, u32[]{:S(2)}, u32[]{:S(2)}) collective-permute-start(bf16[64,2048]{1,0:T(8,128)(2,1)S(1)} %get-tuple-element.17), channel_id=1, source_target_pairs={{0,1},{1,0},{2,3},{3,2},{4,5},{5,4},{6,7},{7,6},{8,9},{9,8},{10,11... | collective-permute-start | bytes 786440 | tf_op jit(solution)/shard_map/ppermute | solution.py:325
  22.3 13.2 %collective-permute-start.4 = (bf16[64,2048]{1,0:T(8,128)(2,1)S(1)}, bf16[64,2048]{1,0:T(8,128)(2,1)S(1)}, u32[]{:S(2)}, u32[]{:S(2)}) collective-permute-start(bf16[64,2048]{1,0:T(8,128)(2,1)S(1)} %add_convert_fusion.1.refs_1_), channel_id=1, source_target_pairs={{0,4},{1,5},{2,6},{3,7},{4,0},{5,1},{6,2},{7,3},{8,12},{9,13},{10,... | collective-permute-start | bytes 786440 | tf_op jit(solution)/shard_map/ppermute | solution.py:343
  26.0 12.2 %collective-permute-start.6 = (bf16[64,2048]{1,0:T(8,128)(2,1)S(1)}, bf16[64,2048]{1,0:T(8,128)(2,1)S(1)}, u32[]{:S(2)}, u32[]{:S(2)}) collective-permute-start(bf16[64,2048]{1,0:T(8,128)(2,1)S(1)} %add_convert_fusion.refs_0_), channel_id=1, source_target_pairs={{0,2},{1,3},{2,0},{3,1},{4,6},{5,7},{6,4},{7,5},{8,10},{9,11},{10,... | collective-permute-start | bytes 786440 | tf_op jit(solution)/shard_map/ppermute | solution.py:343
  27.6 10.6 %collective-permute-start.3 = (bf16[64,2048]{1,0:T(8,128)(2,1)S(1)}, bf16[64,2048]{1,0:T(8,128)(2,1)S(1)}, u32[]{:S(2)}, u32[]{:S(2)}) collective-permute-start(bf16[64,2048]{1,0:T(8,128)(2,1)S(1)} %unchanged.5.refs_1_), channel_id=1, source_target_pairs={{0,1},{1,0},{2,3},{3,2},{4,5},{5,4},{6,7},{7,6},{8,9},{9,8},{10,11... | collective-permute-start | bytes 786440 | tf_op jit(solution)/shard_map/ppermute | solution.py:341
  30.9 7.3 %copy-start.1 = (bf16[64,2048]{1,0:T(8,128)(2,1)S(1)}, bf16[64,2048]{1,0:T(8,128)(2,1)}, u32[]{:S(2)}) copy-start(bf16[64,2048]{1,0:T(8,128)(2,1)} %residual_ref.1) | copy-start | bytes 786436
  30.9 7.3 %copy-start.2 = (bf16[2048]{0:T(1024)(128)(2,1)S(1)}, bf16[2048]{0:T(1024)(128)(2,1)}, u32[]{:S(2)}) copy-start(bf16[2048]{0:T(1024)(128)(2,1)} %param.8) | copy-start | bytes 12292
  30.9 7.3 %copy-start.3 = (bf16[2048]{0:T(1024)(128)(2,1)S(1)}, bf16[2048]{0:T(1024)(128)(2,1)}, u32[]{:S(2)}) copy-start(bf16[2048]{0:T(1024)(128)(2,1)} %param.9) | copy-start | bytes 12292
  39.2 3.7 %collective-permute-start.7 = (bf16[16,128]{1,0:T(8,128)(2,1)S(1)}, bf16[16,128]{1,0:T(8,128)(2,1)S(1)}, u32[]{:S(2)}, u32[]{:S(2)}) collective-permute-start(bf16[16,128]{1,0:T(8,128)(2,1)S(1)} %get-tuple-element.21), channel_id=1, source_target_pairs={{0,1},{1,0},{2,3},{3,2},{4,5},{5,4},{6,7},{7,6},{8,9},{9,8},{10,11... | collective-permute-start | bytes 12296 | tf_op jit(solution)/shard_map/ppermute | solution.py:349
  40.1 13.7 %collective-permute-start.10 = (bf16[64,2176]{1,0:T(8,128)(2,1)S(1)}, bf16[64,2176]{1,0:T(8,128)(2,1)S(1)}, u32[]{:S(2)}, u32[]{:S(2)}) collective-permute-start(bf16[64,2176]{1,0:T(8,128)(2,1)S(1)} %get-tuple-element.20.sent_ref), channel_id=1, source_target_pairs={{0,1},{1,0},{2,3},{3,2},{4,5},{5,4},{6,7},{7,6},{8,9},{9,8},{10,11... | collective-permute-start | bytes 835592 | tf_op jit(solution)/shard_map/ppermute | solution.py:356
  41.2 11.1 %collective-permute-start.9 = (bf16[64,2176]{1,0:T(8,128)(2,1)S(1)}, bf16[64,2176]{1,0:T(8,128)(2,1)S(1)}, u32[]{:S(2)}, u32[]{:S(2)}) collective-permute-start(bf16[64,2176]{1,0:T(8,128)(2,1)S(1)} %get-tuple-element.20.sent_ref), channel_id=1, source_target_pairs={{0,2},{1,3},{2,0},{3,1},{4,6},{5,7},{6,4},{7,5},{8,10},{9,11},{10,... | collective-permute-start | bytes 835592 | tf_op jit(solution)/shard_map/ppermute | solution.py:351
  43.0 13.1 %collective-permute-start.8 = (bf16[64,2176]{1,0:T(8,128)(2,1)S(1)}, bf16[64,2176]{1,0:T(8,128)(2,1)S(1)}, u32[]{:S(2)}, u32[]{:S(2)}) collective-permute-start(bf16[64,2176]{1,0:T(8,128)(2,1)S(1)} %merge.1.refs_0_.refs_7_), channel_id=1, source_target_pairs={{0,4},{1,5},{2,6},{3,7},{4,0},{5,1},{6,2},{7,3},{8,12},{9,13},{10,... | collective-permute-start | bytes 835592 | tf_op jit(solution)/shard_map/ppermute | solution.py:354
  52.3 7.3 %collective-permute-start.13 = (bf16[64,2176]{1,0:T(8,128)(2,1)S(1)}, bf16[64,2176]{1,0:T(8,128)(2,1)S(1)}, u32[]{:S(2)}, u32[]{:S(2)}) collective-permute-start(bf16[64,2176]{1,0:T(8,128)(2,1)S(1)} %collective-permute-done.9.refs_1_.refs_2_.refs_10_), channel_id=1, source_target_pairs={{0,1},{1,0},{2,3},{3,2},{4,5},{5,4},{6,7},{7,6},{8,9},{9,8},{10,11... | collective-permute-start | bytes 835592 | tf_op jit(solution)/shard_map/ppermute | solution.py:356
  56.0 8.6 %collective-permute-start.14 = (bf16[64,2176]{1,0:T(8,128)(2,1)S(1)}, bf16[64,2176]{1,0:T(8,128)(2,1)S(1)}, u32[]{:S(2)}, u32[]{:S(2)}) collective-permute-start(bf16[64,2176]{1,0:T(8,128)(2,1)S(1)} %unchanged.7.refs_4_.refs_8_), channel_id=1, source_target_pairs={{0,1},{1,0},{2,3},{3,2},{4,5},{5,4},{6,7},{7,6},{8,9},{9,8},{10,11... | collective-permute-start | bytes 835592 | tf_op jit(solution)/shard_map/ppermute | solution.py:366
  57.1 6.5 %collective-permute-start.11 = (bf16[64,2176]{1,0:T(8,128)(2,1)S(1)}, bf16[64,2176]{1,0:T(8,128)(2,1)S(1)}, u32[]{:S(2)}, u32[]{:S(2)}) collective-permute-start(bf16[64,2176]{1,0:T(8,128)(2,1)S(1)} %unchanged.7.refs_4_.refs_8_), channel_id=1, source_target_pairs={{0,2},{1,3},{2,0},{3,1},{4,6},{5,7},{6,4},{7,5},{8,10},{9,11},{10,... | collective-permute-start | bytes 835592 | tf_op jit(solution)/shard_map/ppermute | solution.py:362
  63.7 6.5 %collective-permute-start.12 = (bf16[64,2176]{1,0:T(8,128)(2,1)S(1)}, bf16[64,2176]{1,0:T(8,128)(2,1)S(1)}, u32[]{:S(2)}, u32[]{:S(2)}) collective-permute-start(bf16[64,2176]{1,0:T(8,128)(2,1)S(1)} %collective-permute-done.11.refs_6_.refs_9_), channel_id=1, source_target_pairs={{0,1},{1,0},{2,3},{3,2},{4,5},{5,4},{6,7},{7,6},{8,9},{9,8},{10,11... | collective-permute-start | bytes 835592 | tf_op jit(solution)/shard_map/ppermute | solution.py:366

commit v14 on v7

--- a/solution.py
+++ b/solution.py
@@ -36,13 +36,11 @@
 
 def product_kernel(targets, splits, local, tile, rows_ref, weight_ref, *refs):
     count = len(targets)
-    held, scratch, semaphores = refs[-3:]
-    outs = refs[-3 - count : -3]
+    scratch, semaphores = refs[-2:]
+    outs = refs[-2 - count : -2]
     nx, per = splits[1], local // tile
     me = lax.axis_index("tensor")
     outer, inner = me // nx, lax.rem(me, nx)
-    first = pltpu.make_async_copy(rows_ref, held, semaphores.at[count * per])
-    first.start()
     copies = []
     for t, (k, j) in enumerate(targets):
         owner = jnp.bitwise_xor(outer, k) * nx + jnp.bitwise_xor(inner, j)
@@ -55,12 +53,11 @@
             )
             copy.start()
             copies.append(copy)
-    first.wait()
     for t in range(count):
         for i in range(per):
             copies[t * per + i].wait()
             outs[t][:, i * tile : (i + 1) * tile] = jnp.dot(
-                held[...], scratch[t * per + i], preferred_element_type=jnp.float32
+                rows_ref[...], scratch[t * per + i], preferred_element_type=jnp.float32
             ).astype(outs[t].dtype)
 
 
@@ -75,13 +72,12 @@
             jax.ShapeDtypeStruct((rows, local), jnp.bfloat16 if j else jnp.float32)
             for _, j in targets
         ],
-        in_specs=[pl.BlockSpec(memory_space=pltpu.HBM)] * 2
+        in_specs=[vmem, pl.BlockSpec(memory_space=pltpu.HBM)]
         + [pl.BlockSpec(memory_space=pl.ANY)] * len(after),
         out_specs=[vmem] * len(targets),
         scratch_shapes=[
-            pltpu.VMEM((rows, depth), jnp.bfloat16),
             pltpu.VMEM((slots, depth, tile), jnp.bfloat16),
-            pltpu.SemaphoreType.DMA((slots + 1,)),
+            pltpu.SemaphoreType.DMA((slots,)),
         ],
         compiler_params=pltpu.CompilerParams(
             vmem_limit_bytes=40 * MIB

time: 71.2 us -> 70.9 us (level)
  starting transfers between devices: 20.7 us -> 21.8 us
  waiting for transfers between devices: 25.5 us -> 24.7 us
where the time goes in v14:
time: 70.9 us; the launch traced here: 70.8 us
  waiting for transfers between devices  24.7 us (35%)
  Pallas kernels  22.4 us (32%)
  starting transfers between devices  21.8 us (31%)
  local copies, waits for them, and re-layouts  0.92 us (1%)
  between operations  0.76 us (1%)
    pallas_call x4, Pallas kernels, products(): pl.pallas_call(functools.partial(product_kernel, targets, splits, local,...  15.2 us
    ppermute x3, waiting for transfers between devices, body(): joined_to = lax.ppermute(total, 'tensor', jump[bit])  7.29 us
    ppermute x1, waiting for transfers between devices, body(): have[top] = lax.ppermute(merged, 'tensor', jump[top])  6.78 us
    ppermute x3, starting transfers between devices, body(): joined_to = lax.ppermute(total, 'tensor', jump[bit])  6.19 us
    pallas_call x2, Pallas kernels, finish(): pl.pallas_call(functools.partial(finish_kernel, places, splits, counts, t...  6.11 us
    ppermute x1, waiting for transfers between devices, body(): have[k] = lax.ppermute(have[k ^ k & -k], 'tensor', jump[k & -k])  4.92 us
    ppermute x3, starting transfers between devices, body(): result = lax.ppermute(result, 'tensor', swap[j])  4.73 us
    ppermute x1, starting transfers between devices, body(): have[top] = lax.ppermute(merged, 'tensor', jump[top])  3.32 us
  transfers between devices with their start and end apart: 15, of which 9 were waited for; matrix products, arithmetic and copies ran while one was open for 0% of the time, Pallas kernels for 25%

profile of v14, /device:TPU:0, one launch (start us, length us, event | category | flops | bytes accessed | tf_op | source)
XLA Modules:
  0.0 70.8 jit_solution(7484801075838277818)
XLA Ops:
  0.6 0.0 copy-start
  0.6 0.9 %copy-done = bf16[64,1024]{1,0:T(8,128)(2,1)S(1)} copy-done((bf16[64,1024]{1,0:T(8,128)(2,1)S(1)}, bf16[64,1024]{1,0:T(8,128)(2,1)}, u32[]{:S(2)}) %copy-start) | copy-done | bytes 131096
  1.5 2.5 %products.4.refs_0_ = bf16[64,2048]{1,0:T(8,128)(2,1)S(1)} custom-call(bf16[64,1024]{1,0:T(8,128)(2,1)S(1)} %copy-done, bf16[1024,16384]{1,0:T(8,128)(2,1)} %weight_ref.7), custom_call_target="tpu_custom_call" | custom-call | flops 268435456 | bytes 4194304 | tf_op jit(solution)/shard_map/products/pallas_call | solution.py:69
  4.1 3.0 %collective-permute-start = (bf16[64,2048]{1,0:T(8,128)(2,1)S(1)}, bf16[64,2048]{1,0:T(8,128)(2,1)S(1)}, u32[]{:S(2)}, u32[]{:S(2)}) collective-permute-start(bf16[64,2048]{1,0:T(8,128)(2,1)S(1)} %products.4.refs_0_), channel_id=1, source_target_pairs={{0,1},{1,0},{2,3},{3,2},{4,5},{5,4},{6,7},{7,6},{8,9},{9,8},{10,11... | collective-permute-start | bytes 786440 | tf_op jit(solution)/shard_map/ppermute | solution.py:321
  7.1 5.1 %products.5 = (bf16[64,2048]{1,0:T(8,128)(2,1)S(1)}, bf16[64,2048]{1,0:T(8,128)(2,1)S(1)}, f32[64,2048]{1,0:T(8,128)S(1)}) custom-call(bf16[64,1024]{1,0:T(8,128)(2,1)S(1)} %copy-done, bf16[1024,16384]{1,0:T(8,128)(2,1)} %weight_ref.7, bf16[64,2048]{1,0:T(8,128)(2,1)S(1)} %products.4.refs_0_), custom_call_target="tpu_custom_call" | custom-call | flops 805306368 | bytes 12582912 | tf_op jit(solution)/shard_map/products/pallas_call | solution.py:69
  12.2 0.1 collective-permute-start.1
  12.3 1.1 %collective-permute-done = bf16[64,2048]{1,0:T(8,128)(2,1)S(1)} collective-permute-done((bf16[64,2048]{1,0:T(8,128)(2,1)S(1)}, bf16[64,2048]{1,0:T(8,128)(2,1)S(1)}, u32[]{:S(2)}, u32[]{:S(2)}) %collective-permute-start) | collective-permute-done | bytes 262176 | tf_op jit(solution)/shard_map/ppermute | solution.py:321
  13.4 1.9 %collective-permute-start.2 = (bf16[64,2048]{1,0:T(8,128)(2,1)S(1)}, bf16[64,2048]{1,0:T(8,128)(2,1)S(1)}, u32[]{:S(2)}, u32[]{:S(2)}) collective-permute-start(bf16[64,2048]{1,0:T(8,128)(2,1)S(1)} %add_convert_fusion.2.refs_0_), channel_id=1, source_target_pairs={{0,2},{1,3},{2,0},{3,1},{4,6},{5,7},{6,4},{7,5},{8,10},{9,11},{10,... | collective-permute-start | bytes 786440 | tf_op jit(solution)/shard_map/ppermute | solution.py:339
  15.3 1.6 %collective-permute-start.5 = (bf16[64,2048]{1,0:T(8,128)(2,1)S(1)}, bf16[64,2048]{1,0:T(8,128)(2,1)S(1)}, u32[]{:S(2)}, u32[]{:S(2)}) collective-permute-start(bf16[64,2048]{1,0:T(8,128)(2,1)S(1)} %get-tuple-element.17), channel_id=1, source_target_pairs={{0,1},{1,0},{2,3},{3,2},{4,5},{5,4},{6,7},{7,6},{8,9},{9,8},{10,11... | collective-permute-start | bytes 786440 | tf_op jit(solution)/shard_map/ppermute | solution.py:321
  16.9 5.1 %products.6 = (bf16[64,2048]{1,0:T(8,128)(2,1)S(1)}, f32[64,2048]{1,0:T(8,128)S(1)}, f32[64,2048]{1,0:T(8,128)S(1)}) custom-call(bf16[64,1024]{1,0:T(8,128)(2,1)S(1)} %copy-done, bf16[1024,16384]{1,0:T(8,128)(2,1)} %weight_ref.7, bf16[64,2048]{1,0:T(8,128)(2,1)S(1)} %add_convert_fusion.2.refs_0_), custom_call_target="tpu_custom_call" | custom-call | flops 805306368 | bytes 12582912 | tf_op jit(solution)/shard_map/products/pallas_call | solution.py:69
  22.0 0.0 collective-permute-done.1
  22.1 0.0 collective-permute-done.2
  22.1 0.1 add_convert_fusion.1.refs_1_
  22.2 2.7 %collective-permute-start.4 = (bf16[64,2048]{1,0:T(8,128)(2,1)S(1)}, bf16[64,2048]{1,0:T(8,128)(2,1)S(1)}, u32[]{:S(2)}, u32[]{:S(2)}) collective-permute-start(bf16[64,2048]{1,0:T(8,128)(2,1)S(1)} %add_convert_fusion.1.refs_1_), channel_id=1, source_target_pairs={{0,4},{1,5},{2,6},{3,7},{4,0},{5,1},{6,2},{7,3},{8,12},{9,13},{10,... | collective-permute-start | bytes 786440 | tf_op jit(solution)/shard_map/ppermute | solution.py:339
  24.8 0.8 %collective-permute-done.5 = bf16[64,2048]{1,0:T(8,128)(2,1)S(1)} collective-permute-done((bf16[64,2048]{1,0:T(8,128)(2,1)S(1)}, bf16[64,2048]{1,0:T(8,128)(2,1)S(1)}, u32[]{:S(2)}, u32[]{:S(2)}) %collective-permute-start.5) | collective-permute-done | bytes 262176 | tf_op jit(solution)/shard_map/ppermute | solution.py:321
  25.7 1.6 %collective-permute-start.6 = (bf16[64,2048]{1,0:T(8,128)(2,1)S(1)}, bf16[64,2048]{1,0:T(8,128)(2,1)S(1)}, u32[]{:S(2)}, u32[]{:S(2)}) collective-permute-start(bf16[64,2048]{1,0:T(8,128)(2,1)S(1)} %add_convert_fusion.refs_0_), channel_id=1, source_target_pairs={{0,2},{1,3},{2,0},{3,1},{4,6},{5,7},{6,4},{7,5},{8,10},{9,11},{10,... | collective-permute-start | bytes 786440 | tf_op jit(solution)/shard_map/ppermute | solution.py:339
  27.3 0.7 %collective-permute-start.3 = (bf16[64,2048]{1,0:T(8,128)(2,1)S(1)}, bf16[64,2048]{1,0:T(8,128)(2,1)S(1)}, u32[]{:S(2)}, u32[]{:S(2)}) collective-permute-start(bf16[64,2048]{1,0:T(8,128)(2,1)S(1)} %unchanged.3.refs_1_), channel_id=1, source_target_pairs={{0,1},{1,0},{2,3},{3,2},{4,5},{5,4},{6,7},{7,6},{8,9},{9,8},{10,11... | collective-permute-start | bytes 786440 | tf_op jit(solution)/shard_map/ppermute | solution.py:337
  28.1 2.5 %products.7.refs_3_ = f32[64,2048]{1,0:T(8,128)S(1)} custom-call(bf16[64,1024]{1,0:T(8,128)(2,1)S(1)} %copy-done, bf16[1024,16384]{1,0:T(8,128)(2,1)} %weight_ref.7, bf16[64,2048]{1,0:T(8,128)(2,1)S(1)} %add_convert_fusion.refs_0_, bf16[64,2048]{1,0:T(8,128)(2,1)S(1)} %unchanged.3.refs_1_), custom_call_target="tpu_custom_call" | custom-call | flops 268435456 | bytes 4194304 | tf_op jit(solution)/shard_map/products/pallas_call | solution.py:69
  30.6 0.0 copy-start.1
  30.6 0.0 copy-start.2
  30.6 0.0 copy-start.3
  30.6 4.6 %collective-permute-done.4.refs_0_ = bf16[64,2048]{1,0:T(8,128)(2,1)S(1)} collective-permute-done((bf16[64,2048]{1,0:T(8,128)(2,1)S(1)}, bf16[64,2048]{1,0:T(8,128)(2,1)S(1)}, u32[]{:S(2)}, u32[]{:S(2)}) %collective-permute-start.4) | collective-permute-done | bytes 262176 | tf_op jit(solution)/shard_map/ppermute | solution.py:339
  35.2 2.7 %collective-permute-done.6.refs_2_ = bf16[64,2048]{1,0:T(8,128)(2,1)S(1)} collective-permute-done((bf16[64,2048]{1,0:T(8,128)(2,1)S(1)}, bf16[64,2048]{1,0:T(8,128)(2,1)S(1)}, u32[]{:S(2)}, u32[]{:S(2)}) %collective-permute-start.6) | collective-permute-done | bytes 262176 | tf_op jit(solution)/shard_map/ppermute | solution.py:339
  37.9 0.0 collective-permute-done.3.refs_0_
  37.9 0.0 copy-done.1
  37.9 0.0 copy-done.2
  37.9 0.0 copy-done.3
  37.9 1.0 %own_stream.1 = (bf16[64,2048]{1,0:T(8,128)(2,1)}, bf16[64,2176]{1,0:T(8,128)(2,1)S(1)}, bf16[16,128]{1,0:T(8,128)(2,1)S(1)}) custom-call(bf16[64,2048]{1,0:T(8,128)(2,1)S(1)} %copy-done.1, bf16[16,128]{1,0:T(8,128)(2,1)S(1)} %bitcast.2, bf16[16,128]{1,0:T(8,128)(2,1)S(1)} %bitcast.3, bf16[64,2048]{1,0:T(8,128)(2,1)S(1)} %collective-permute-done.3.refs_0_, ...), custom_call_target="tpu_custom_call" | custom-call | flops 2621440 | bytes 2097152 | tf_op jit(solution)/shard_map/own_stream/pallas_call | solution.py:134
  38.9 0.0 collective-permute-start.10
  38.9 1.1 %collective-permute-start.7 = (bf16[16,128]{1,0:T(8,128)(2,1)S(1)}, bf16[16,128]{1,0:T(8,128)(2,1)S(1)}, u32[]{:S(2)}, u32[]{:S(2)}) collective-permute-start(bf16[16,128]{1,0:T(8,128)(2,1)S(1)} %get-tuple-element.21), channel_id=1, source_target_pairs={{0,1},{1,0},{2,3},{3,2},{4,5},{5,4},{6,7},{7,6},{8,9},{9,8},{10,11... | collective-permute-start | bytes 12296 | tf_op jit(solution)/shard_map/ppermute | solution.py:345
  40.0 1.0 %collective-permute-start.9 = (bf16[64,2176]{1,0:T(8,128)(2,1)S(1)}, bf16[64,2176]{1,0:T(8,128)(2,1)S(1)}, u32[]{:S(2)}, u32[]{:S(2)}) collective-permute-start(bf16[64,2176]{1,0:T(8,128)(2,1)S(1)} %get-tuple-element.20.sent_ref), channel_id=1, source_target_pairs={{0,1},{1,0},{2,3},{3,2},{4,5},{5,4},{6,7},{7,6},{8,9},{9,8},{10,11... | collective-permute-start | bytes 835592 | tf_op jit(solution)/shard_map/ppermute | solution.py:352
  41.0 1.7 %collective-permute-done.7.refs_0_ = bf16[16,128]{1,0:T(8,128)(2,1)S(1)} collective-permute-done((bf16[16,128]{1,0:T(8,128)(2,1)S(1)}, bf16[16,128]{1,0:T(8,128)(2,1)S(1)}, u32[]{:S(2)}, u32[]{:S(2)}) %collective-permute-start.7) | collective-permute-done | bytes 4128 | tf_op jit(solution)/shard_map/ppermute | solution.py:345
  42.7 3.3 %collective-permute-start.8 = (bf16[64,2176]{1,0:T(8,128)(2,1)S(1)}, bf16[64,2176]{1,0:T(8,128)(2,1)S(1)}, u32[]{:S(2)}, u32[]{:S(2)}) collective-permute-start(bf16[64,2176]{1,0:T(8,128)(2,1)S(1)} %merge.1.refs_0_.refs_7_), channel_id=1, source_target_pairs={{0,4},{1,5},{2,6},{3,7},{4,0},{5,1},{6,2},{7,3},{8,12},{9,13},{10,... | collective-permute-start | bytes 835592 | tf_op jit(solution)/shard_map/ppermute | solution.py:350
  46.0 1.8 %collective-permute-done.10.refs_2_.refs_10_ = bf16[64,2176]{1,0:T(8,128)(2,1)S(1)} collective-permute-done((bf16[64,2176]{1,0:T(8,128)(2,1)S(1)}, bf16[64,2176]{1,0:T(8,128)(2,1)S(1)}, u32[]{:S(2)}, u32[]{:S(2)}) %collective-permute-start.10) | collective-permute-done | bytes 278560 | tf_op jit(solution)/shard_map/ppermute | solution.py:347
  47.8 1.6 %collective-permute-start.11 = (bf16[64,2176]{1,0:T(8,128)(2,1)S(1)}, bf16[64,2176]{1,0:T(8,128)(2,1)S(1)}, u32[]{:S(2)}, u32[]{:S(2)}) collective-permute-start(bf16[64,2176]{1,0:T(8,128)(2,1)S(1)} %collective-permute-done.10.refs_2_.refs_10_), channel_id=1, source_target_pairs={{0,1},{1,0},{2,3},{3,2},{4,5},{5,4},{6,7},{7,6},{8,9},{9,8},{10,11... | collective-permute-start | bytes 835592 | tf_op jit(solution)/shard_map/ppermute | solution.py:352
  49.5 0.0 collective-permute-done.9.refs_1_
  49.5 6.8 %collective-permute-done.8.refs_0_ = bf16[64,2176]{1,0:T(8,128)(2,1)S(1)} collective-permute-done((bf16[64,2176]{1,0:T(8,128)(2,1)S(1)}, bf16[64,2176]{1,0:T(8,128)(2,1)S(1)}, u32[]{:S(2)}, u32[]{:S(2)}) %collective-permute-start.8) | collective-permute-done | bytes 278560 | tf_op jit(solution)/shard_map/ppermute | solution.py:350
  56.3 0.0 collective-permute-done.11.refs_2_.refs_3_.refs_11_
  56.3 0.0 collective-permute-start.12
  56.3 1.6 %collective-permute-start.14 = (bf16[64,2176]{1,0:T(8,128)(2,1)S(1)}, bf16[64,2176]{1,0:T(8,128)(2,1)S(1)}, u32[]{:S(2)}, u32[]{:S(2)}) collective-permute-start(bf16[64,2176]{1,0:T(8,128)(2,1)S(1)} %unchanged.5.refs_4_.refs_8_), channel_id=1, source_target_pairs={{0,1},{1,0},{2,3},{3,2},{4,5},{5,4},{6,7},{7,6},{8,9},{9,8},{10,11... | collective-permute-start | bytes 835592 | tf_op jit(solution)/shard_map/ppermute | solution.py:360
  57.9 4.9 %collective-permute-done.12.refs_6_.refs_9_ = bf16[64,2176]{1,0:T(8,128)(2,1)S(1)} collective-permute-done((bf16[64,2176]{1,0:T(8,128)(2,1)S(1)}, bf16[64,2176]{1,0:T(8,128)(2,1)S(1)}, u32[]{:S(2)}, u32[]{:S(2)}) %collective-permute-start.12) | collective-permute-done | bytes 278560 | tf_op jit(solution)/shard_map/ppermute | solution.py:356
  62.8 1.6 %collective-permute-start.13 = (bf16[64,2176]{1,0:T(8,128)(2,1)S(1)}, bf16[64,2176]{1,0:T(8,128)(2,1)S(1)}, u32[]{:S(2)}, u32[]{:S(2)}) collective-permute-start(bf16[64,2176]{1,0:T(8,128)(2,1)S(1)} %collective-permute-done.12.refs_6_.refs_9_), channel_id=1, source_target_pairs={{0,1},{1,0},{2,3},{3,2},{4,5},{5,4},{6,7},{7,6},{8,9},{9,8},{10,11... | collective-permute-start | bytes 835592 | tf_op jit(solution)/shard_map/ppermute | solution.py:360
  64.4 0.0 collective-permute-done.14.refs_5_
  64.4 4.7 %finish.2 = (bf16[64,16384]{1,0:T(8,128)(2,1)}, f32[64,128]{1,0:T(8,128)S(1)}) custom-call(bf16[64,2176]{1,0:T(8,128)(2,1)S(1)} %merge.1.refs_0_.refs_7_, bf16[64,2176]{1,0:T(8,128)(2,1)S(1)} %collective-permute-done.9.refs_1_, bf16[64,2176]{1,0:T(8,128)(2,1)S(1)} %collective-permute-done.10.refs_2_.refs_10_, ...), custom_call_target="tpu_custom_call" | custom-call | flops 939524096 | bytes 3670016 | tf_op jit(solution)/shard_map/finish/pallas_call | solution.py:272
  69.1 0.3 collective-permute-done.13.refs_0_
  69.4 1.4 %finish.3 = bf16[64,16384]{1,0:T(8,128)(2,1)} custom-call(bf16[64,2176]{1,0:T(8,128)(2,1)S(1)} %collective-permute-done.13.refs_0_, f32[64,128]{1,0:T(8,128)S(1)} %get-tuple-element.22.refs_1_, bf16[64,16384]{1,0:T(8,128)(2,1)} %get-tuple-element.23.refs_2_), custom_call_target="tpu_custom_call", output_to_operand_aliasing={{}: (2, {})} | custom-call | flops 134217728 | bytes 524288 | tf_op jit(solution)/shard_map/finish/pallas_call | solution.py:272
  (6 shorter events, 0.1 us)
Async XLA Ops:
  0.6 0.9 %copy-start = (bf16[64,1024]{1,0:T(8,128)(2,1)S(1)}, bf16[64,1024]{1,0:T(8,128)(2,1)}, u32[]{:S(2)}) copy-start(bf16[64,1024]{1,0:T(8,128)(2,1)} %rows_ref.7) | copy-start | bytes 393220
  4.1 9.3 %collective-permute-start = (bf16[64,2048]{1,0:T(8,128)(2,1)S(1)}, bf16[64,2048]{1,0:T(8,128)(2,1)S(1)}, u32[]{:S(2)}, u32[]{:S(2)}) collective-permute-start(bf16[64,2048]{1,0:T(8,128)(2,1)S(1)} %products.4.refs_0_), channel_id=1, source_target_pairs={{0,1},{1,0},{2,3},{3,2},{4,5},{5,4},{6,7},{7,6},{8,9},{9,8},{10,11... | collective-permute-start | bytes 786440 | tf_op jit(solution)/shard_map/ppermute | solution.py:321
  12.2 9.9 %collective-permute-start.1 = (bf16[64,2048]{1,0:T(8,128)(2,1)S(1)}, bf16[64,2048]{1,0:T(8,128)(2,1)S(1)}, u32[]{:S(2)}, u32[]{:S(2)}) collective-permute-start(bf16[64,2048]{1,0:T(8,128)(2,1)S(1)} %get-tuple-element.15), channel_id=1, source_target_pairs={{0,1},{1,0},{2,3},{3,2},{4,5},{5,4},{6,7},{7,6},{8,9},{9,8},{10,11... | collective-permute-start | bytes 786440 | tf_op jit(solution)/shard_map/ppermute | solution.py:321
  13.4 8.6 %collective-permute-start.2 = (bf16[64,2048]{1,0:T(8,128)(2,1)S(1)}, bf16[64,2048]{1,0:T(8,128)(2,1)S(1)}, u32[]{:S(2)}, u32[]{:S(2)}) collective-permute-start(bf16[64,2048]{1,0:T(8,128)(2,1)S(1)} %add_convert_fusion.2.refs_0_), channel_id=1, source_target_pairs={{0,2},{1,3},{2,0},{3,1},{4,6},{5,7},{6,4},{7,5},{8,10},{9,11},{10,... | collective-permute-start | bytes 786440 | tf_op jit(solution)/shard_map/ppermute | solution.py:339
  15.3 10.3 %collective-permute-start.5 = (bf16[64,2048]{1,0:T(8,128)(2,1)S(1)}, bf16[64,2048]{1,0:T(8,128)(2,1)S(1)}, u32[]{:S(2)}, u32[]{:S(2)}) collective-permute-start(bf16[64,2048]{1,0:T(8,128)(2,1)S(1)} %get-tuple-element.17), channel_id=1, source_target_pairs={{0,1},{1,0},{2,3},{3,2},{4,5},{5,4},{6,7},{7,6},{8,9},{9,8},{10,11... | collective-permute-start | bytes 786440 | tf_op jit(solution)/shard_map/ppermute | solution.py:321
  22.2 13.1 %collective-permute-start.4 = (bf16[64,2048]{1,0:T(8,128)(2,1)S(1)}, bf16[64,2048]{1,0:T(8,128)(2,1)S(1)}, u32[]{:S(2)}, u32[]{:S(2)}) collective-permute-start(bf16[64,2048]{1,0:T(8,128)(2,1)S(1)} %add_convert_fusion.1.refs_1_), channel_id=1, source_target_pairs={{0,4},{1,5},{2,6},{3,7},{4,0},{5,1},{6,2},{7,3},{8,12},{9,13},{10,... | collective-permute-start | bytes 786440 | tf_op jit(solution)/shard_map/ppermute | solution.py:339
  25.7 12.2 %collective-permute-start.6 = (bf16[64,2048]{1,0:T(8,128)(2,1)S(1)}, bf16[64,2048]{1,0:T(8,128)(2,1)S(1)}, u32[]{:S(2)}, u32[]{:S(2)}) collective-permute-start(bf16[64,2048]{1,0:T(8,128)(2,1)S(1)} %add_convert_fusion.refs_0_), channel_id=1, source_target_pairs={{0,2},{1,3},{2,0},{3,1},{4,6},{5,7},{6,4},{7,5},{8,10},{9,11},{10,... | collective-permute-start | bytes 786440 | tf_op jit(solution)/shard_map/ppermute | solution.py:339
  27.3 10.6 %collective-permute-start.3 = (bf16[64,2048]{1,0:T(8,128)(2,1)S(1)}, bf16[64,2048]{1,0:T(8,128)(2,1)S(1)}, u32[]{:S(2)}, u32[]{:S(2)}) collective-permute-start(bf16[64,2048]{1,0:T(8,128)(2,1)S(1)} %unchanged.3.refs_1_), channel_id=1, source_target_pairs={{0,1},{1,0},{2,3},{3,2},{4,5},{5,4},{6,7},{7,6},{8,9},{9,8},{10,11... | collective-permute-start | bytes 786440 | tf_op jit(solution)/shard_map/ppermute | solution.py:337
  30.6 7.3 %copy-start.1 = (bf16[64,2048]{1,0:T(8,128)(2,1)S(1)}, bf16[64,2048]{1,0:T(8,128)(2,1)}, u32[]{:S(2)}) copy-start(bf16[64,2048]{1,0:T(8,128)(2,1)} %residual_ref.1) | copy-start | bytes 786436
  30.6 7.3 %copy-start.2 = (bf16[2048]{0:T(1024)(128)(2,1)S(1)}, bf16[2048]{0:T(1024)(128)(2,1)}, u32[]{:S(2)}) copy-start(bf16[2048]{0:T(1024)(128)(2,1)} %param.8) | copy-start | bytes 12292
  30.6 7.3 %copy-start.3 = (bf16[2048]{0:T(1024)(128)(2,1)S(1)}, bf16[2048]{0:T(1024)(128)(2,1)}, u32[]{:S(2)}) copy-start(bf16[2048]{0:T(1024)(128)(2,1)} %param.9) | copy-start | bytes 12292
  38.9 8.9 %collective-permute-start.10 = (bf16[64,2176]{1,0:T(8,128)(2,1)S(1)}, bf16[64,2176]{1,0:T(8,128)(2,1)S(1)}, u32[]{:S(2)}, u32[]{:S(2)}) collective-permute-start(bf16[64,2176]{1,0:T(8,128)(2,1)S(1)} %get-tuple-element.20.sent_ref), channel_id=1, source_target_pairs={{0,2},{1,3},{2,0},{3,1},{4,6},{5,7},{6,4},{7,5},{8,10},{9,11},{10,... | collective-permute-start | bytes 835592 | tf_op jit(solution)/shard_map/ppermute | solution.py:347
  38.9 3.7 %collective-permute-start.7 = (bf16[16,128]{1,0:T(8,128)(2,1)S(1)}, bf16[16,128]{1,0:T(8,128)(2,1)S(1)}, u32[]{:S(2)}, u32[]{:S(2)}) collective-permute-start(bf16[16,128]{1,0:T(8,128)(2,1)S(1)} %get-tuple-element.21), channel_id=1, source_target_pairs={{0,1},{1,0},{2,3},{3,2},{4,5},{5,4},{6,7},{7,6},{8,9},{9,8},{10,11... | collective-permute-start | bytes 12296 | tf_op jit(solution)/shard_map/ppermute | solution.py:345
  40.0 9.5 %collective-permute-start.9 = (bf16[64,2176]{1,0:T(8,128)(2,1)S(1)}, bf16[64,2176]{1,0:T(8,128)(2,1)S(1)}, u32[]{:S(2)}, u32[]{:S(2)}) collective-permute-start(bf16[64,2176]{1,0:T(8,128)(2,1)S(1)} %get-tuple-element.20.sent_ref), channel_id=1, source_target_pairs={{0,1},{1,0},{2,3},{3,2},{4,5},{5,4},{6,7},{7,6},{8,9},{9,8},{10,11... | collective-permute-start | bytes 835592 | tf_op jit(solution)/shard_map/ppermute | solution.py:352
  42.7 13.6 %collective-permute-start.8 = (bf16[64,2176]{1,0:T(8,128)(2,1)S(1)}, bf16[64,2176]{1,0:T(8,128)(2,1)S(1)}, u32[]{:S(2)}, u32[]{:S(2)}) collective-permute-start(bf16[64,2176]{1,0:T(8,128)(2,1)S(1)} %merge.1.refs_0_.refs_7_), channel_id=1, source_target_pairs={{0,4},{1,5},{2,6},{3,7},{4,0},{5,1},{6,2},{7,3},{8,12},{9,13},{10,... | collective-permute-start | bytes 835592 | tf_op jit(solution)/shard_map/ppermute | solution.py:350
  47.8 8.4 %collective-permute-start.11 = (bf16[64,2176]{1,0:T(8,128)(2,1)S(1)}, bf16[64,2176]{1,0:T(8,128)(2,1)S(1)}, u32[]{:S(2)}, u32[]{:S(2)}) collective-permute-start(bf16[64,2176]{1,0:T(8,128)(2,1)S(1)} %collective-permute-done.10.refs_2_.refs_10_), channel_id=1, source_target_pairs={{0,1},{1,0},{2,3},{3,2},{4,5},{5,4},{6,7},{7,6},{8,9},{9,8},{10,11... | collective-permute-start | bytes 835592 | tf_op jit(solution)/shard_map/ppermute | solution.py:352
  56.3 6.5 %collective-permute-start.12 = (bf16[64,2176]{1,0:T(8,128)(2,1)S(1)}, bf16[64,2176]{1,0:T(8,128)(2,1)S(1)}, u32[]{:S(2)}, u32[]{:S(2)}) collective-permute-start(bf16[64,2176]{1,0:T(8,128)(2,1)S(1)} %unchanged.5.refs_4_.refs_8_), channel_id=1, source_target_pairs={{0,2},{1,3},{2,0},{3,1},{4,6},{5,7},{6,4},{7,5},{8,10},{9,11},{10,... | collective-permute-start | bytes 835592 | tf_op jit(solution)/shard_map/ppermute | solution.py:356
  56.3 8.1 %collective-permute-start.14 = (bf16[64,2176]{1,0:T(8,128)(2,1)S(1)}, bf16[64,2176]{1,0:T(8,128)(2,1)S(1)}, u32[]{:S(2)}, u32[]{:S(2)}) collective-permute-start(bf16[64,2176]{1,0:T(8,128)(2,1)S(1)} %unchanged.5.refs_4_.refs_8_), channel_id=1, source_target_pairs={{0,1},{1,0},{2,3},{3,2},{4,5},{5,4},{6,7},{7,6},{8,9},{9,8},{10,11... | collective-permute-start | bytes 835592 | tf_op jit(solution)/shard_map/ppermute | solution.py:360
  62.8 6.5 %collective-permute-start.13 = (bf16[64,2176]{1,0:T(8,128)(2,1)S(1)}, bf16[64,2176]{1,0:T(8,128)(2,1)S(1)}, u32[]{:S(2)}, u32[]{:S(2)}) collective-permute-start(bf16[64,2176]{1,0:T(8,128)(2,1)S(1)} %collective-permute-done.12.refs_6_.refs_9_), channel_id=1, source_target_pairs={{0,1},{1,0},{2,3},{3,2},{4,5},{5,4},{6,7},{7,6},{8,9},{9,8},{10,11... | collective-permute-start | bytes 835592 | tf_op jit(solution)/shard_map/ppermute | solution.py:360
